TPU v7x, 256 devices: a whole 4x4x8 slice. The times are simulated.
256 devices in a mesh: blk: 32 (over y_lo, z, core), rep: 8 (over y_hi, x).
Axes of the slice: x: 4, y: 4 (y_hi: 2, y_lo: 2; y = y_hi * 2 + y_lo), z: 8, core: 2. Of those that a mesh axis runs over, the one named last changes fastest.
Arguments:
- query_act: bfloat16 [16384, 16384], P('blk', 'rep'), may hold values from -8 to 8
- passage_act: bfloat16 [1024, 16384], P('blk', 'rep'), may hold values from -8 to 8
- positive: int32 [16384], P('blk'), may hold values from 0 to 1023
- normalizer: float32 [16384], P('blk'), as said below
Outputs:
- query_grad: bfloat16 [16384, 16384], P('blk', 'rep')
- passage_grad: bfloat16 [1024, 16384], P('blk', 'rep')
Inputs may be any that keep to these rules, and one draw needn't show every extreme that they name: `normalizer`: close to the log of the sum over passages of exp(scores).
All inputs are finite; a program needn't handle non-finite values.
Results may differ from a plain program's by a relative error of at most 0.009.
The roundings to bfloat16 on the way count: a program that leaves them out, or rounds other values in their place, can miss the bound.
Values may be sent and summed in bfloat16 or wider, within the bound.
No kernel may reach another device: no remote copies, remote signals or barrier semaphores. Data moves between devices by JAX's collectives and lax.ppermute only.
A program may use at most 64 MiB of HBM per device.

v0:
```python
import math

import jax
import jax.numpy as jnp
from jax import lax
from jax.sharding import PartitionSpec as P

VOCAB = 16384


def saturate(act):
    wide = act.astype(jnp.float32)
    return jnp.log1p(jnp.maximum(wide, 0.0))


def slope(act):
    wide = act.astype(jnp.float32)
    return jnp.where(wide > 0.0, 1.0 / (1.0 + jnp.maximum(wide, 0.0)), 0.0)


def grad_block(scores, normalizer, positive, width, factor):
    columns = jnp.arange(width, dtype=jnp.int32)
    onehot = (positive[:, None] == columns[None, :]).astype(jnp.float32)
    return ((jnp.exp(scores - normalizer[:, None]) - onehot) * (8.0 * factor)).astype(jnp.bfloat16)


def shards(query_act, passage_act, positive, normalizer):
    factor = 8.0 / math.sqrt(VOCAB)
    query_rep = saturate(query_act).astype(jnp.bfloat16)
    passage_rep = saturate(passage_act).astype(jnp.bfloat16)
    contract_last = (((1,), (1,)), ((), ()))
    contract_first = (((0,), (0,)), ((), ()))
    all_passages = lax.all_gather(passage_rep, "blk", axis=0, tiled=True)
    partial_value = lax.dot_general(
        query_rep, all_passages, contract_last, preferred_element_type=jnp.float32
    )
    scores = lax.psum(partial_value, "rep") * factor
    score_grad = grad_block(scores, normalizer, positive, all_passages.shape[0], factor)
    query_sum = jnp.dot(score_grad, all_passages, preferred_element_type=jnp.float32)
    passage_sum = lax.psum_scatter(
        lax.dot_general(score_grad, query_rep, contract_first, preferred_element_type=jnp.float32),
        "blk",
        scatter_dimension=0,
        tiled=True,
    )
    query_grad = (query_sum * slope(query_act)).astype(jnp.bfloat16)
    passage_grad = (passage_sum * slope(passage_act)).astype(jnp.bfloat16)
    return (query_grad, passage_grad)


def solution(mesh):
    placed = (P("blk", "rep"), P("blk", "rep"), P("blk"), P("blk"))
    return jax.shard_map(
        shards,
        mesh=mesh,
        in_specs=placed,
        out_specs=(P("blk", "rep"), P("blk", "rep")),
        check_vma=False,
    )
```

profile of v0, /device:TPU:8, one launch (start us, length us, event | category | flops | bytes accessed | tf_op | source)
XLA Modules:
  0.0 328.1 jit_solution(1416489800357393725)
XLA Ops:
  7.2 0.0 all-gather.2.cloned.1.call-start
  7.2 1.7 fusion.13
  8.9 0.0 all-gather.2.cloned.1.call-update
  8.9 0.0 all-reduce.2.cloned.1.call-start
  8.9 70.6 %all-gather.2.cloned.1.call-done = bf16[1024,2048]{1,0:T(8,128)(2,1)} async-done(((bf16[32,2048]{1,0:T(8,128)(2,1)}), bf16[1024,2048]{1,0:T(8,128)(2,1)}) %all-gather.2.cloned.1.call-update) | async-done | bytes 4194320 | tf_op jit(solution)/shard_map/all_gather | solution.py:33
  79.6 0.0 copy-start.3
  79.6 7.0 %fusion.9 = f32[512,1024]{1,0:T(8,128)} fusion(bf16[1024,2048]{1,0:T(8,128)(2,1)} %all-gather.2.cloned.1.call-done, bf16[512,2048]{1,0:T(8,128)(2,1)} %param.4), kind=kOutput, calls=%fused_computation.12 | convolution fusion | flops 2150629376 | bytes 8388608 | tf_op jit(solution)/shard_map/dot_general | solution.py:34
  86.6 0.0 copy-start.1
  86.6 0.0 copy-start.2
  86.6 0.0 all-reduce.2.cloned.1.call-update
  86.6 0.0 reduce-scatter.2.cloned.1.call-start
  86.7 96.8 %all-reduce.2.cloned.1.call-done = f32[512,1024]{1,0:T(8,128)} async-done(((f32[512,1024]{1,0:T(8,128)}), f32[512,1024]{1,0:T(8,128)}) %all-reduce.2.cloned.1.call-update) | async-done | bytes 2097168 | tf_op jit(solution)/shard_map/psum | solution.py:37
  183.5 0.0 copy-done.3
  183.5 0.0 copy-done.1
  183.5 0.0 copy-done.2
  183.5 7.9 %fusion.7 = f32[1024,2048]{1,0:T(8,128)} fusion(bf16[512,2048]{1,0:T(8,128)(2,1)S(1)} %copy-done.1, f32[512,1024]{1,0:T(8,128)} %all-reduce.2.cloned.1.call-done, s32[512]{0:T(512)S(1)} %copy-done.2, f32[512]{0:T(512)S(1)} %copy-done.3), kind=kOutput, calls=%fused_computation.11 | convolution fusion | flops 2154299392 | bytes 12587008 | tf_op jit(solution)/shard_map/dot_general | solution.py:41
  191.5 0.0 reduce-scatter.2.cloned.1.call-update
  191.5 0.0 copy-start
  191.5 7.4 %fusion.6 = bf16[512,2048]{1,0:T(8,128)(2,1)} fusion(bf16[512,2048]{1,0:T(8,128)(2,1)S(1)} %copy-done.1, bf16[1024,2048]{1,0:T(8,128)(2,1)} %all-gather.2.cloned.1.call-done, f32[512,1024]{1,0:T(8,128)} %all-reduce.2.cloned.1.call-done, s32[512]{0:T(512)S(1)} %copy-done.2, f32[512]{0:T(512)S(1)} %copy-done.3), kind=kOutput, calls=%fused_computation.8 | convolution fusion | flops 2159542272 | bytes 10489856 | tf_op jit(solution)/shard_map/dot_general | solution.py:39
  198.9 120.9 %reduce-scatter.2.cloned.1.call-done = f32[32,2048]{1,0:T(8,128)} async-done(((f32[1024,2048]{1,0:T(8,128)}), f32[32,2048]{1,0:T(8,128)}) %reduce-scatter.2.cloned.1.call-update) | async-done | bytes 262160 | tf_op jit(solution)/shard_map/reduce_scatter | solution.py:40
  319.9 0.0 copy-done
  319.9 1.7 fusion.17
Async XLA Ops:
  7.2 72.4 %all-gather.2.cloned.1.call-start = ((), (), s32[]{:S(2)}) async-start(), calls=%async_computation.1 | async-start | bytes 4325376 | tf_op jit(solution)/shard_map/all_gather | solution.py:33
  8.9 174.6 %all-reduce.2.cloned.1.call-start = ((), (), s32[]{:S(2)}) async-start(), calls=%async_computation.2 | async-start | bytes 4194304 | tf_op jit(solution)/shard_map/psum | solution.py:37
  79.6 104.0 %copy-start.3 = (f32[512]{0:T(512)S(1)}, f32[512]{0:T(512)}, u32[]{:S(2)}) copy-start(f32[512]{0:T(512)} %param.7) | copy-start | bytes 6148
  86.6 96.9 %copy-start.1 = (bf16[512,2048]{1,0:T(8,128)(2,1)S(1)}, bf16[512,2048]{1,0:T(8,128)(2,1)}, u32[]{:S(2)}) copy-start(bf16[512,2048]{1,0:T(8,128)(2,1)} %param.4) | copy-start | bytes 6291460
  86.6 96.9 %copy-start.2 = (s32[512]{0:T(512)S(1)}, s32[512]{0:T(512)}, u32[]{:S(2)}) copy-start(s32[512]{0:T(512)} %param.6) | copy-start | bytes 6148
  86.6 233.2 %reduce-scatter.2.cloned.1.call-start = ((), (), s32[]{:S(2)}) async-start(), calls=%async_computation.3 | async-start | bytes 8650752 | tf_op jit(solution)/shard_map/reduce_scatter | solution.py:40
  191.5 128.4 %copy-start = (bf16[32,2048]{1,0:T(8,128)(2,1)S(1)}, bf16[32,2048]{1,0:T(8,128)(2,1)}, u32[]{:S(2)}) copy-start(bf16[32,2048]{1,0:T(8,128)(2,1)} %param.5) | copy-start | bytes 393220
Sparse Core Ops, SparseCore 0:
  10.4 69.0 all-gather.1
  86.8 96.7 all-reduce.1
  191.6 128.2 reduce-scatter.1
where the time goes:
time: 329 us; the launch traced here: 328 us
  waiting for transfers between devices  288 us (88%)
  matrix products  22.4 us (7%)
  between operations  13.8 us (4%)
  other arithmetic  3.34 us (1%)
    reduce_scatter x1, waiting for transfers between devices, shards(): lax.psum_scatter(lax.dot_general(score_grad, query_rep, contract_first, p...  121 us
    psum x1, waiting for transfers between devices, shards(): scores = lax.psum(partial_value, 'rep') * factor  96.8 us
    all_gather x1, waiting for transfers between devices, shards(): all_passages = lax.all_gather(passage_rep, 'blk', axis=0, tiled=True)  70.6 us
    dot_general x1, matrix products, shards(): lax.dot_general(score_grad, query_rep, contract_first, preferred_element_...  7.93 us
    dot_general x1, matrix products, shards(): jnp.dot(score_grad, all_passages, preferred_element_type=jnp.float32)  7.43 us
    dot_general x1, matrix products, shards(): lax.dot_general(query_rep, all_passages, contract_last, preferred_element...  7.04 us
  transfers between devices with their start and end apart: 3, of which 3 were waited for; matrix products, arithmetic and copies ran while one was open for 2% of the time, Pallas kernels for 0%

commit v1 on v0

v1 whole, which is shorter than its diff:
```python
import math

import jax
import jax.numpy as jnp
from jax import lax
from jax.sharding import Mesh, PartitionSpec as P

VOCAB = 16384
REP = ("yhi", "x")


def saturate(act):
    wide = act.astype(jnp.float32)
    return jnp.log1p(jnp.maximum(wide, 0.0)).astype(jnp.bfloat16)


def slope(act):
    wide = act.astype(jnp.float32)
    return jnp.where(wide > 0.0, 1.0 / (1.0 + jnp.maximum(wide, 0.0)), 0.0)


def swap(value, axis):
    return lax.ppermute(value, axis, [(0, 1), (1, 0)])


def shift(value, step):
    return lax.ppermute(value, "z", [(i, (i + step) % 8) for i in range(8)])


def shards(query_act, passage_act, positive, normalizer):
    factor = 8.0 / math.sqrt(VOCAB)
    core, y, z = lax.axis_index("core"), lax.axis_index("ylo"), lax.axis_index("z")
    rep = lax.axis_index(REP)
    bf16, f32 = jnp.bfloat16, jnp.float32

    own = saturate(passage_act)
    blocks = {0: jnp.concatenate([own, swap(own, "ylo")], axis=0)}
    for d in range(1, 4):
        blocks[-d] = shift(blocks[1 - d], 1)
        blocks[d] = shift(blocks[d - 1], -1)
    blocks[4] = jnp.concatenate([shift(blocks[-3][:32], 1), shift(blocks[3][32:], -1)], axis=0)
    order = [0, 1, -1, 2, -2, 3, -3, 4]
    half = jnp.concatenate([blocks[d] for d in order], axis=0)

    query_rep = saturate(query_act)
    queries = jnp.concatenate([query_rep, swap(query_rep, "core")], axis=0)
    row_info = jnp.stack([normalizer, positive.astype(f32)])
    row_info = jnp.concatenate([row_info, swap(row_info, "core")], axis=1)
    row_info = lax.dynamic_slice_in_dim(row_info, rep * 128, 128, axis=1)

    part = lax.dot_general(queries, half, (((1,), (1,)), ((), ())), preferred_element_type=f32)
    pieces = lax.all_to_all(part.reshape(8, 128, 512), REP, split_axis=0, concat_axis=0)
    scores = jnp.sum(pieces, axis=0) * factor

    place = jnp.arange(512, dtype=jnp.int32)
    where = jnp.array(order, dtype=jnp.int32)[place // 64]
    ident = jnp.where(place % 64 < 32, y, 1 - y) * 16 + ((z + where + 8) % 8) * 2 + core
    ident = ident * 32 + place % 32
    onehot = (row_info[1].astype(jnp.int32)[:, None] == ident[None, :]).astype(f32)
    score_grad = ((jnp.exp(scores - row_info[0][:, None]) - onehot) * (8.0 * factor)).astype(bf16)
    spread = lax.all_to_all(
        jnp.broadcast_to(score_grad[None], (8, 128, 512)), REP, split_axis=0, concat_axis=0
    ).reshape(1024, 512)

    def term(d):
        at = order.index(d) * 64
        return lax.dot_general(
            spread[:, at : at + 64], queries, (((0,), (0,)), ((), ())), preferred_element_type=f32
        )

    far = term(4).astype(bf16)
    up, down = shift(far[:32], 1), shift(far[32:], -1)
    for d in (3, 2, 1):
        mine_up, mine_down = term(d), term(-d)
        if d == 3:
            pad = jnp.zeros((32, mine_up.shape[1]), f32)
            up = jnp.concatenate([up.astype(f32), pad], axis=0)
            down = jnp.concatenate([pad, down.astype(f32)], axis=0)
        up = shift((mine_up + up.astype(f32)).astype(bf16), 1)
        down = shift((mine_down + down.astype(f32)).astype(bf16), -1)
    total = term(0) + up.astype(f32) + down.astype(f32)
    passage_sum = total[:32] + swap(total[32:].astype(bf16), "ylo").astype(f32)
    passage_grad = (passage_sum * slope(passage_act)).astype(bf16)

    other_half = swap(half, "core")
    other_grad = swap(spread[512:], "core")
    query_sum = jnp.dot(spread[:512], half, preferred_element_type=f32) + jnp.dot(
        other_grad, other_half, preferred_element_type=f32
    )
    query_grad = (query_sum * slope(query_act)).astype(bf16)
    return (query_grad, passage_grad)


def solution(mesh):
    split = Mesh(mesh.devices.reshape(2, 8, 2, 2, 4), ("ylo", "z", "core", "yhi", "x"))
    rows, columns = ("ylo", "z", "core"), ("yhi", "x")
    return jax.shard_map(
        shards,
        mesh=split,
        in_specs=(P(rows, columns), P(rows, columns), P(rows), P(rows)),
        out_specs=(P(rows, columns), P(rows, columns)),
        check_vma=False,
    )
```

time: 329 us -> 144 us (0.44)
  waiting for transfers between devices: 288 us -> 70.6 us
  starting transfers between devices: 0.12 us -> 46 us
  between operations: 13.8 us -> 1.08 us
  matrix products: 22.4 us -> 18.7 us
    reduce_scatter x1 -> x0, waiting for transfers between devices: 121 us -> none  [shards(): lax.psum_scatter(lax.dot_general(score_grad, query_rep, contract_first, p...]
    psum x1 -> x0, waiting for transfers between devices: 96.8 us -> none  [shards(): scores = lax.psum(partial_value, 'rep') * factor]
    all_gather x1 -> x0, waiting for transfers between devices: 70.6 us -> none  [shards(): all_passages = lax.all_gather(passage_rep, 'blk', axis=0, tiled=True)]
    all_to_all x0 -> x2, waiting for transfers between devices: none -> 38.9 us  [the longest x1 22.5 us: shards(): lax.all_to_all(part.reshape(8, 128, 512), REP, split_axis=0, concat_axis=0)]
    ppermute x0 -> x22, starting transfers between devices: none -> 36 us  [the longest x16 30.1 us: shift(): return lax.ppermute(value, 'z', [(i, (i + step) % 8) for i in range(8)])]
    ppermute x0 -> x22, waiting for transfers between devices: none -> 31.6 us  [the longest x16 30.6 us: shift(): return lax.ppermute(value, 'z', [(i, (i + step) % 8) for i in range(8)])]
    all_to_all x0 -> x2, starting transfers between devices: none -> 9.98 us  [the longest x1 6.12 us: shards(): lax.all_to_all(part.reshape(8, 128, 512), REP, split_axis=0, concat_axis=0)]
    dot_general x3 -> x11, matrix products: 22.4 us -> 18.7 us  [the longest x8 8.86 us: term(): lax.dot_general(spread[:, at:at + 64], queries, (((0,), (0,)), ((), ())),...]
  transfers between devices with their start and end apart: 3 -> 24, of which waited for: 3 -> 12; matrix products, arithmetic and copies ran while one was open for 2% -> 12% of each run, Pallas kernels for 0% -> 0%
where the time goes in v1:
time: 144 us; the launch traced here: 143 us
  waiting for transfers between devices  70.6 us (49%)
  starting transfers between devices  46 us (32%)
  matrix products  18.7 us (13%)
  other arithmetic  5.54 us (4%)
    ppermute x16, waiting for transfers between devices, shift(): return lax.ppermute(value, 'z', [(i, (i + step) % 8) for i in range(8)])  30.6 us
    ppermute x16, starting transfers between devices, shift(): return lax.ppermute(value, 'z', [(i, (i + step) % 8) for i in range(8)])  30.1 us
    all_to_all x1, waiting for transfers between devices, shards(): lax.all_to_all(part.reshape(8, 128, 512), REP, split_axis=0, concat_axis=0)  22.5 us
    all_to_all x1, waiting for transfers between devices, shards(): lax.all_to_all(jnp.broadcast_to(score_grad[None], (8, 128, 512)), REP, sp...  16.4 us
    dot_general x8, matrix products, term(): lax.dot_general(spread[:, at:at + 64], queries, (((0,), (0,)), ((), ())),...  8.86 us
    all_to_all x1, starting transfers between devices, shards(): lax.all_to_all(part.reshape(8, 128, 512), REP, split_axis=0, concat_axis=0)  6.12 us
    ppermute x6, starting transfers between devices, swap(): return lax.ppermute(value, axis, [(0, 1), (1, 0)])  5.89 us
    convert_element_type x2, other arithmetic, saturate(): return jnp.log1p(jnp.maximum(wide, 0.0)).astype(jnp.bfloat16)  4.15 us
  transfers between devices with their start and end apart: 24, of which 12 were waited for; matrix products, arithmetic and copies ran while one was open for 12% of the time, Pallas kernels for 0%

profile of v1, /device:TPU:8, one launch (start us, length us, event | category | flops | bytes accessed | tf_op | source)
XLA Modules:
  0.0 143.2 jit_solution(4418281278188374822)
XLA Ops:
  0.6 1.0 fusion.16
  1.7 2.3 %collective-permute-start.1 = (bf16[32,2048]{1,0:T(8,128)(2,1)S(1)}, bf16[32,2048]{1,0:T(8,128)(2,1)S(1)}, u32[]{:S(2)}, u32[]{:S(2)}) collective-permute-start(bf16[32,2048]{1,0:T(8,128)(2,1)S(1)} %fusion.16), channel_id=1, source_target_pairs={{0,128},{128,0},{1,129},{129,1},{2,130},{130,2},{3,131},{131,3},{4... | collective-permute-start | bytes 393224 | tf_op jit(solution)/shard_map/ppermute | solution.py:23
  3.9 3.1 %fusion.2 = bf16[512,2048]{1,0:T(8,128)(2,1)S(1)} fusion(bf16[512,2048]{1,0:T(8,128)(2,1)} %param.5), kind=kLoop, calls=%fused_computation.4 | loop fusion | flops 3145728 | bytes 4194304 | tf_op jit(solution)/shard_map/convert_element_type | solution.py:14
  7.1 0.1 collective-permute-start
  7.2 5.7 %collective-permute-start.2 = (bf16[64,2048]{1,0:T(8,128)(2,1)S(1)}, bf16[64,2048]{1,0:T(8,128)(2,1)S(1)}, u32[]{:S(2)}, u32[]{:S(2)}) collective-permute-start(bf16[64,2048]{1,0:T(8,128)(2,1)S(1)} %pad_maximum_fusion.1), channel_id=1, source_target_pairs={{0,112},{16,0},{32,16},{48,32},{64,48},{80,64},{96,80},{112,96},{1... | collective-permute-start | bytes 786440 | tf_op jit(solution)/shard_map/ppermute | solution.py:27
  12.9 0.1 constant_dynamic-update-slice_fusion.9
  13.1 4.6 %collective-permute-done.2 = bf16[64,2048]{1,0:T(8,128)(2,1)S(1)} collective-permute-done((bf16[64,2048]{1,0:T(8,128)(2,1)S(1)}, bf16[64,2048]{1,0:T(8,128)(2,1)S(1)}, u32[]{:S(2)}, u32[]{:S(2)}) %collective-permute-start.2) | collective-permute-done | bytes 262176 | tf_op jit(solution)/shard_map/ppermute | solution.py:27
  17.6 3.7 %collective-permute-start.4 = (bf16[64,2048]{1,0:T(8,128)(2,1)S(1)}, bf16[64,2048]{1,0:T(8,128)(2,1)S(1)}, u32[]{:S(2)}, u32[]{:S(2)}) collective-permute-start(bf16[64,2048]{1,0:T(8,128)(2,1)S(1)} %collective-permute-done.2), channel_id=1, source_target_pairs={{0,112},{16,0},{32,16},{48,32},{64,48},{80,64},{96,80},{112,96},{1... | collective-permute-start | bytes 786440 | tf_op jit(solution)/shard_map/ppermute | solution.py:27
  21.4 3.8 %collective-permute-done.4 = bf16[64,2048]{1,0:T(8,128)(2,1)S(1)} collective-permute-done((bf16[64,2048]{1,0:T(8,128)(2,1)S(1)}, bf16[64,2048]{1,0:T(8,128)(2,1)S(1)}, u32[]{:S(2)}, u32[]{:S(2)}) %collective-permute-start.4) | collective-permute-done | bytes 262176 | tf_op jit(solution)/shard_map/ppermute | solution.py:27
  25.2 3.7 %collective-permute-start.6 = (bf16[64,2048]{1,0:T(8,128)(2,1)S(1)}, bf16[64,2048]{1,0:T(8,128)(2,1)S(1)}, u32[]{:S(2)}, u32[]{:S(2)}) collective-permute-start(bf16[64,2048]{1,0:T(8,128)(2,1)S(1)} %collective-permute-done.4), channel_id=1, source_target_pairs={{0,112},{16,0},{32,16},{48,32},{64,48},{80,64},{96,80},{112,96},{1... | collective-permute-start | bytes 786440 | tf_op jit(solution)/shard_map/ppermute | solution.py:27
  29.0 8.1 %collective-permute-done.7 = bf16[64,2048]{1,0:T(8,128)(2,1)S(1)} collective-permute-done((bf16[64,2048]{1,0:T(8,128)(2,1)S(1)}, bf16[64,2048]{1,0:T(8,128)(2,1)S(1)}, u32[]{:S(2)}, u32[]{:S(2)}) %collective-permute-start.7) | collective-permute-done | bytes 262176 | tf_op jit(solution)/shard_map/ppermute | solution.py:27
  37.1 0.1 collective-permute-start.8
  37.2 3.3 %collective-permute-start.9 = (bf16[32,2048]{1,0:T(8,128)(2,1)S(1)}, bf16[32,2048]{1,0:T(8,128)(2,1)S(1)}, u32[]{:S(2)}, u32[]{:S(2)}) collective-permute-start(bf16[32,2048]{1,0:T(8,128)(2,1)S(1)} %slice.91), channel_id=1, source_target_pairs={{0,112},{16,0},{32,16},{48,32},{64,48},{80,64},{96,80},{112,96},{1... | collective-permute-start | bytes 393224 | tf_op jit(solution)/shard_map/ppermute | solution.py:27
  40.5 2.8 %collective-permute-done.8 = bf16[32,2048]{1,0:T(8,128)(2,1)S(1)} collective-permute-done((bf16[32,2048]{1,0:T(8,128)(2,1)S(1)}, bf16[32,2048]{1,0:T(8,128)(2,1)S(1)}, u32[]{:S(2)}, u32[]{:S(2)}) %collective-permute-start.8) | collective-permute-done | bytes 131104 | tf_op jit(solution)/shard_map/ppermute | solution.py:27
  43.4 3.7 %fusion.45 = f32[1024,512]{1,0:T(8,128)} fusion(bf16[512,2048]{1,0:T(8,128)(2,1)S(1)} %constant_dynamic-update-slice_fusion, bf16[512,2048]{1,0:T(8,128)(2,1)S(1)} %collective-permute-done, bf16[512,2048]{1,0:T(8,128)(2,1)S(1)} %fusion.2), kind=kOutput, calls=%fused_computation.98 | convolution fusion | flops 2155872256 | bytes 8388608 | tf_op jit(solution)/shard_map/dot_general | solution.py:51
  47.1 6.1 %all-to-all-start = ((f32[8,128,512]{2,1,0:T(8,128)}), f32[8,128,512]{2,1,0:T(8,128)S(1)}, u32[]{:S(2)}, u32[]{:S(2)}) async-start(f32[8,128,512]{2,1,0:T(8,128)} %bitcast.24), calls=%async_computation | async-start | bytes 4194304 | tf_op jit(solution)/shard_map/all_to_all | solution.py:52
  53.3 0.3 collective-permute-start.10
  53.7 1.1 collective-permute-done.10
  54.8 22.5 %all-to-all-done = f32[8,128,512]{2,1,0:T(8,128)S(1)} async-done(((f32[8,128,512]{2,1,0:T(8,128)}), f32[8,128,512]{2,1,0:T(8,128)S(1)}, u32[]{:S(2)}, u32[]{:S(2)}) %all-to-all-start) | async-done | bytes 2097184 | tf_op jit(solution)/shard_map/all_to_all | solution.py:52
  77.3 0.2 reduce_sum.9
  77.5 0.1 multiply_convert_fusion
  77.6 1.1 broadcast_in_dim.23
  78.7 3.9 %all-to-all-start.1 = ((bf16[8,128,512]{2,1,0:T(8,128)(2,1)}), bf16[8,128,512]{2,1,0:T(8,128)(2,1)S(1)}, u32[]{:S(2)}, u32[]{:S(2)}) async-start(bf16[8,128,512]{2,1,0:T(8,128)(2,1)} %broadcast_in_dim.23), calls=%async_computation.1 | async-start | bytes 2097152 | tf_op jit(solution)/shard_map/all_to_all | solution.py:61
  82.6 16.4 %all-to-all-done.1 = bf16[8,128,512]{2,1,0:T(8,128)(2,1)S(1)} async-done(((bf16[8,128,512]{2,1,0:T(8,128)(2,1)}), bf16[8,128,512]{2,1,0:T(8,128)(2,1)S(1)}, u32[]{:S(2)}, u32[]{:S(2)}) %all-to-all-start.1) | async-done | bytes 1048608 | tf_op jit(solution)/shard_map/all_to_all | solution.py:61
  99.0 2.5 %convolution_convert_fusion = bf16[64,2048]{1,0:T(8,128)(2,1)S(1)} fusion(bf16[1024,512]{1,0:T(8,128)(2,1)S(1)} %bitcast.16, bf16[512,2048]{1,0:T(8,128)(2,1)} %copy-done.8, bf16[512,2048]{1,0:T(8,128)(2,1)S(1)} %copy-done.2), kind=kOutput, calls=%fused_computation.24 | convolution fusion | flops 276955136 | bytes 4718592 | tf_op jit(solution)/shard_map/dot_general | solution.py:67
  101.6 0.1 collective-permute-start.13
  101.7 3.2 %collective-permute-start.17 = (bf16[32,2048]{1,0:T(8,128)(2,1)S(1)}, bf16[32,2048]{1,0:T(8,128)(2,1)S(1)}, u32[]{:S(2)}, u32[]{:S(2)}) collective-permute-start(bf16[32,2048]{1,0:T(8,128)(2,1)S(1)} %get-tuple-element.5), channel_id=1, source_target_pairs={{0,112},{16,0},{32,16},{48,32},{64,48},{80,64},{96,80},{112,96},{1... | collective-permute-start | bytes 393224 | tf_op jit(solution)/shard_map/ppermute | solution.py:27
  105.0 0.1 collective-permute-start.11
  105.1 2.9 %collective-permute-done.13 = bf16[32,2048]{1,0:T(8,128)(2,1)S(1)} collective-permute-done((bf16[32,2048]{1,0:T(8,128)(2,1)S(1)}, bf16[32,2048]{1,0:T(8,128)(2,1)S(1)}, u32[]{:S(2)}, u32[]{:S(2)}) %collective-permute-start.13) | collective-permute-done | bytes 131104 | tf_op jit(solution)/shard_map/ppermute | solution.py:27
  107.9 0.9 fusion.10
  108.9 0.1 collective-permute-start.14
  109.0 0.9 fusion.13
  109.9 3.3 %collective-permute-start.18 = (bf16[64,2048]{1,0:T(8,128)(2,1)S(1)}, bf16[64,2048]{1,0:T(8,128)(2,1)S(1)}, u32[]{:S(2)}, u32[]{:S(2)}) collective-permute-start(bf16[64,2048]{1,0:T(8,128)(2,1)S(1)} %fusion.13), channel_id=1, source_target_pairs={{0,112},{16,0},{32,16},{48,32},{64,48},{80,64},{96,80},{112,96},{1... | collective-permute-start | bytes 786440 | tf_op jit(solution)/shard_map/ppermute | solution.py:27
  113.2 4.0 %collective-permute-done.14 = bf16[64,2048]{1,0:T(8,128)(2,1)S(1)} collective-permute-done((bf16[64,2048]{1,0:T(8,128)(2,1)S(1)}, bf16[64,2048]{1,0:T(8,128)(2,1)S(1)}, u32[]{:S(2)}, u32[]{:S(2)}) %collective-permute-start.14) | collective-permute-done | bytes 262176 | tf_op jit(solution)/shard_map/ppermute | solution.py:27
  117.2 0.9 fusion.9
  118.2 0.9 fusion.12
  119.1 3.3 %collective-permute-start.19 = (bf16[64,2048]{1,0:T(8,128)(2,1)S(1)}, bf16[64,2048]{1,0:T(8,128)(2,1)S(1)}, u32[]{:S(2)}, u32[]{:S(2)}) collective-permute-start(bf16[64,2048]{1,0:T(8,128)(2,1)S(1)} %fusion.12), channel_id=1, source_target_pairs={{0,112},{16,0},{32,16},{48,32},{64,48},{80,64},{96,80},{112,96},{1... | collective-permute-start | bytes 786440 | tf_op jit(solution)/shard_map/ppermute | solution.py:27
  122.4 3.4 %collective-permute-done.15 = bf16[64,2048]{1,0:T(8,128)(2,1)S(1)} collective-permute-done((bf16[64,2048]{1,0:T(8,128)(2,1)S(1)}, bf16[64,2048]{1,0:T(8,128)(2,1)S(1)}, u32[]{:S(2)}, u32[]{:S(2)}) %collective-permute-start.15) | collective-permute-done | bytes 262176 | tf_op jit(solution)/shard_map/ppermute | solution.py:27
  125.8 0.9 fusion.8
  126.8 0.9 fusion.11
  127.7 3.5 %collective-permute-start.20 = (bf16[64,2048]{1,0:T(8,128)(2,1)S(1)}, bf16[64,2048]{1,0:T(8,128)(2,1)S(1)}, u32[]{:S(2)}, u32[]{:S(2)}) collective-permute-start(bf16[64,2048]{1,0:T(8,128)(2,1)S(1)} %fusion.11), channel_id=1, source_target_pairs={{0,112},{16,0},{32,16},{48,32},{64,48},{80,64},{96,80},{112,96},{1... | collective-permute-start | bytes 786440 | tf_op jit(solution)/shard_map/ppermute | solution.py:27
  131.2 2.8 %fusion.48 = f32[512,2048]{1,0:T(8,128)S(1)} fusion(bf16[512,512]{1,0:T(8,128)(2,1)S(1)} %collective-permute-done.11, bf16[512,2048]{1,0:T(8,128)(2,1)} %collective-permute-done.12), kind=kOutput, calls=%fused_computation.101 | convolution fusion | flops 1073741824 | bytes 6815744 | tf_op jit(solution)/shard_map/dot_general | solution.py:87
  134.1 0.3 collective-permute-done.16
  134.4 0.7 collective-permute-done.20
  135.1 0.9 fusion.7
  136.0 3.2 %collective-permute-start.21 = (bf16[32,2048]{1,0:T(8,128)(2,1)S(1)}, bf16[32,2048]{1,0:T(8,128)(2,1)S(1)}, u32[]{:S(2)}, u32[]{:S(2)}) collective-permute-start(bf16[32,2048]{1,0:T(8,128)(2,1)S(1)} %slice.130), channel_id=1, source_target_pairs={{0,128},{128,0},{1,129},{129,1},{2,130},{130,2},{3,131},{131,3},{4... | collective-permute-start | bytes 393224 | tf_op jit(solution)/shard_map/ppermute | solution.py:23
  139.2 3.3 %fusion.6 = bf16[512,2048]{1,0:T(8,128)(2,1)} fusion(bf16[512,2048]{1,0:T(8,128)(2,1)S(1)} %copy-done, f32[512,2048]{1,0:T(8,128)S(1)} %fusion.48, bf16[512,512]{1,0:T(8,128)(2,1)S(1)} %bitcast.25, bf16[512,2048]{1,0:T(8,128)(2,1)S(1)} %copy-done.5), kind=kOutput, calls=%fused_computation.9 | convolution fusion | flops 1083179008 | bytes 11010048 | tf_op jit(solution)/shard_map/dot_general | solution.py:87
  142.5 0.7 fusion.28
  (60 shorter events, 0.7 us)
Async XLA Ops:
  1.6 11.3 %copy-start.3 = (bf16[32,2048]{1,0:T(8,128)(2,1)S(1)}, bf16[32,2048]{1,0:T(8,128)(2,1)}, u32[]{:S(2)}) copy-start(bf16[32,2048]{1,0:T(8,128)(2,1)} %param.6) | copy-start | bytes 393220
  1.7 5.5 %collective-permute-start.1 = (bf16[32,2048]{1,0:T(8,128)(2,1)S(1)}, bf16[32,2048]{1,0:T(8,128)(2,1)S(1)}, u32[]{:S(2)}, u32[]{:S(2)}) collective-permute-start(bf16[32,2048]{1,0:T(8,128)(2,1)S(1)} %fusion.16), channel_id=1, source_target_pairs={{0,128},{128,0},{1,129},{129,1},{2,130},{130,2},{3,131},{131,3},{4... | collective-permute-start | bytes 393224 | tf_op jit(solution)/shard_map/ppermute | solution.py:23
  7.1 36.3 %copy-start.1 = (bf16[512,2048]{1,0:T(8,128)(2,1)}, bf16[512,2048]{1,0:T(8,128)(2,1)S(1)}, u32[]{:S(2)}) copy-start(bf16[512,2048]{1,0:T(8,128)(2,1)S(1)} %fusion.2) | copy-start | bytes 6291460
  7.1 36.3 %collective-permute-start = (bf16[512,2048]{1,0:T(8,128)(2,1)S(1)}, bf16[512,2048]{1,0:T(8,128)(2,1)S(1)}, u32[]{:S(2)}, u32[]{:S(2)}) collective-permute-start(bf16[512,2048]{1,0:T(8,128)(2,1)S(1)} %fusion.2), channel_id=1, source_target_pairs={{0,8},{8,0},{1,9},{9,1},{2,10},{10,2},{3,11},{11,3},{4,12},{12,4},... | collective-permute-start | bytes 6291464 | tf_op jit(solution)/shard_map/ppermute | solution.py:23
  7.2 10.4 %collective-permute-start.2 = (bf16[64,2048]{1,0:T(8,128)(2,1)S(1)}, bf16[64,2048]{1,0:T(8,128)(2,1)S(1)}, u32[]{:S(2)}, u32[]{:S(2)}) collective-permute-start(bf16[64,2048]{1,0:T(8,128)(2,1)S(1)} %pad_maximum_fusion.1), channel_id=1, source_target_pairs={{0,112},{16,0},{32,16},{48,32},{64,48},{80,64},{96,80},{112,96},{1... | collective-permute-start | bytes 786440 | tf_op jit(solution)/shard_map/ppermute | solution.py:27
  12.9 8.4 %collective-permute-start.3 = (bf16[64,2048]{1,0:T(8,128)(2,1)S(1)}, bf16[64,2048]{1,0:T(8,128)(2,1)S(1)}, u32[]{:S(2)}, u32[]{:S(2)}) collective-permute-start(bf16[64,2048]{1,0:T(8,128)(2,1)S(1)} %pad_maximum_fusion.1), channel_id=1, source_target_pairs={{0,16},{16,32},{32,48},{48,64},{64,80},{80,96},{96,112},{112,0},{1... | collective-permute-start | bytes 786440 | tf_op jit(solution)/shard_map/ppermute | solution.py:27
  17.6 7.6 %collective-permute-start.4 = (bf16[64,2048]{1,0:T(8,128)(2,1)S(1)}, bf16[64,2048]{1,0:T(8,128)(2,1)S(1)}, u32[]{:S(2)}, u32[]{:S(2)}) collective-permute-start(bf16[64,2048]{1,0:T(8,128)(2,1)S(1)} %collective-permute-done.2), channel_id=1, source_target_pairs={{0,112},{16,0},{32,16},{48,32},{64,48},{80,64},{96,80},{112,96},{1... | collective-permute-start | bytes 786440 | tf_op jit(solution)/shard_map/ppermute | solution.py:27
  21.3 7.6 %collective-permute-start.5 = (bf16[64,2048]{1,0:T(8,128)(2,1)S(1)}, bf16[64,2048]{1,0:T(8,128)(2,1)S(1)}, u32[]{:S(2)}, u32[]{:S(2)}) collective-permute-start(bf16[64,2048]{1,0:T(8,128)(2,1)S(1)} %collective-permute-done.3), channel_id=1, source_target_pairs={{0,16},{16,32},{32,48},{48,64},{64,80},{80,96},{96,112},{112,0},{1... | collective-permute-start | bytes 786440 | tf_op jit(solution)/shard_map/ppermute | solution.py:27
  25.2 12.0 %collective-permute-start.6 = (bf16[64,2048]{1,0:T(8,128)(2,1)S(1)}, bf16[64,2048]{1,0:T(8,128)(2,1)S(1)}, u32[]{:S(2)}, u32[]{:S(2)}) collective-permute-start(bf16[64,2048]{1,0:T(8,128)(2,1)S(1)} %collective-permute-done.4), channel_id=1, source_target_pairs={{0,112},{16,0},{32,16},{48,32},{64,48},{80,64},{96,80},{112,96},{1... | collective-permute-start | bytes 786440 | tf_op jit(solution)/shard_map/ppermute | solution.py:27
  28.9 8.2 %collective-permute-start.7 = (bf16[64,2048]{1,0:T(8,128)(2,1)S(1)}, bf16[64,2048]{1,0:T(8,128)(2,1)S(1)}, u32[]{:S(2)}, u32[]{:S(2)}) collective-permute-start(bf16[64,2048]{1,0:T(8,128)(2,1)S(1)} %collective-permute-done.5), channel_id=1, source_target_pairs={{0,16},{16,32},{32,48},{48,64},{64,80},{80,96},{96,112},{112,0},{1... | collective-permute-start | bytes 786440 | tf_op jit(solution)/shard_map/ppermute | solution.py:27
  37.1 6.3 %collective-permute-start.8 = (bf16[32,2048]{1,0:T(8,128)(2,1)S(1)}, bf16[32,2048]{1,0:T(8,128)(2,1)S(1)}, u32[]{:S(2)}, u32[]{:S(2)}) collective-permute-start(bf16[32,2048]{1,0:T(8,128)(2,1)S(1)} %slice.90), channel_id=1, source_target_pairs={{0,16},{16,32},{32,48},{48,64},{64,80},{80,96},{96,112},{112,0},{1... | collective-permute-start | bytes 393224 | tf_op jit(solution)/shard_map/ppermute | solution.py:27
  37.2 6.2 %collective-permute-start.9 = (bf16[32,2048]{1,0:T(8,128)(2,1)S(1)}, bf16[32,2048]{1,0:T(8,128)(2,1)S(1)}, u32[]{:S(2)}, u32[]{:S(2)}) collective-permute-start(bf16[32,2048]{1,0:T(8,128)(2,1)S(1)} %slice.91), channel_id=1, source_target_pairs={{0,112},{16,0},{32,16},{48,32},{64,48},{80,64},{96,80},{112,96},{1... | collective-permute-start | bytes 393224 | tf_op jit(solution)/shard_map/ppermute | solution.py:27
  43.4 3.7 %copy-start.4 = (bf16[512,2048]{1,0:T(8,128)(2,1)}, bf16[512,2048]{1,0:T(8,128)(2,1)S(1)}, u32[]{:S(2)}) copy-start(bf16[512,2048]{1,0:T(8,128)(2,1)S(1)} %constant_dynamic-update-slice_fusion) | copy-start | bytes 6291460
  43.4 3.7 %copy-start.8 = (bf16[512,2048]{1,0:T(8,128)(2,1)}, bf16[512,2048]{1,0:T(8,128)(2,1)S(1)}, u32[]{:S(2)}) copy-start(bf16[512,2048]{1,0:T(8,128)(2,1)S(1)} %collective-permute-done) | copy-start | bytes 6291460
  47.1 6.1 %copy-start.7 = (s32[512]{0:T(512)S(1)}, s32[512]{0:T(512)}, u32[]{:S(2)}) copy-start(s32[512]{0:T(512)} %param.7) | copy-start | bytes 6148
  47.1 6.2 %copy-start.6 = (f32[512]{0:T(512)S(1)}, f32[512]{0:T(512)}, u32[]{:S(2)}) copy-start(f32[512]{0:T(512)} %param.8) | copy-start | bytes 6148
  47.1 30.2 %all-to-all-start = ((f32[8,128,512]{2,1,0:T(8,128)}), f32[8,128,512]{2,1,0:T(8,128)S(1)}, u32[]{:S(2)}, u32[]{:S(2)}) async-start(f32[8,128,512]{2,1,0:T(8,128)} %bitcast.24), calls=%async_computation | async-start | bytes 4194304 | tf_op jit(solution)/shard_map/all_to_all | solution.py:52
  53.3 1.4 %collective-permute-start.10 = (f32[2,512]{1,0:T(2,128)S(1)}, f32[2,512]{1,0:T(2,128)S(1)}, u32[]{:S(2)}, u32[]{:S(2)}) collective-permute-start(f32[2,512]{1,0:T(2,128)S(1)} %pad_maximum_fusion.2), channel_id=1, source_target_pairs={{0,8},{8,0},{1,9},{9,1},{2,10},{10,2},{3,11},{11,3},{4,12},{12,4},... | collective-permute-start | bytes 12296 | tf_op jit(solution)/shard_map/ppermute | solution.py:23
  77.5 21.5 %copy-start.2 = (bf16[512,2048]{1,0:T(8,128)(2,1)S(1)}, bf16[512,2048]{1,0:T(8,128)(2,1)}, u32[]{:S(2)}) copy-start(bf16[512,2048]{1,0:T(8,128)(2,1)} %copy-done.1) | copy-start | bytes 6291460
  78.7 20.3 %all-to-all-start.1 = ((bf16[8,128,512]{2,1,0:T(8,128)(2,1)}), bf16[8,128,512]{2,1,0:T(8,128)(2,1)S(1)}, u32[]{:S(2)}, u32[]{:S(2)}) async-start(bf16[8,128,512]{2,1,0:T(8,128)(2,1)} %broadcast_in_dim.23), calls=%async_computation.1 | async-start | bytes 2097152 | tf_op jit(solution)/shard_map/all_to_all | solution.py:61
  82.6 48.7 %collective-permute-start.12 = (bf16[512,2048]{1,0:T(8,128)(2,1)}, bf16[512,2048]{1,0:T(8,128)(2,1)}, u32[]{:S(2)}, u32[]{:S(2)}) collective-permute-start(bf16[512,2048]{1,0:T(8,128)(2,1)} %copy-done.4), channel_id=1, source_target_pairs={{0,8},{8,0},{1,9},{9,1},{2,10},{10,2},{3,11},{11,3},{4,12},{12,4},... | collective-permute-start | bytes 6291464 | tf_op jit(solution)/shard_map/ppermute | solution.py:23
  101.6 6.4 %copy-start.9 = (bf16[512,2048]{1,0:T(8,128)(2,1)S(1)}, bf16[512,2048]{1,0:T(8,128)(2,1)}, u32[]{:S(2)}) copy-start(bf16[512,2048]{1,0:T(8,128)(2,1)} %copy-done.8) | copy-start | bytes 6291460
  101.6 6.4 %collective-permute-start.13 = (bf16[32,2048]{1,0:T(8,128)(2,1)S(1)}, bf16[32,2048]{1,0:T(8,128)(2,1)S(1)}, u32[]{:S(2)}, u32[]{:S(2)}) collective-permute-start(bf16[32,2048]{1,0:T(8,128)(2,1)S(1)} %get-tuple-element.4), channel_id=1, source_target_pairs={{0,16},{16,32},{32,48},{48,64},{64,80},{80,96},{96,112},{112,0},{1... | collective-permute-start | bytes 393224 | tf_op jit(solution)/shard_map/ppermute | solution.py:27
  101.7 7.3 %collective-permute-start.17 = (bf16[32,2048]{1,0:T(8,128)(2,1)S(1)}, bf16[32,2048]{1,0:T(8,128)(2,1)S(1)}, u32[]{:S(2)}, u32[]{:S(2)}) collective-permute-start(bf16[32,2048]{1,0:T(8,128)(2,1)S(1)} %get-tuple-element.5), channel_id=1, source_target_pairs={{0,112},{16,0},{32,16},{48,32},{64,48},{80,64},{96,80},{112,96},{1... | collective-permute-start | bytes 393224 | tf_op jit(solution)/shard_map/ppermute | solution.py:27
  105.0 26.2 %collective-permute-start.11 = (bf16[512,512]{1,0:T(8,128)(2,1)S(1)}, bf16[512,512]{1,0:T(8,128)(2,1)S(1)}, u32[]{:S(2)}, u32[]{:S(2)}) collective-permute-start(bf16[512,512]{1,0:T(8,128)(2,1)S(1)} %bitcast.26), channel_id=1, source_target_pairs={{0,8},{8,0},{1,9},{9,1},{2,10},{10,2},{3,11},{11,3},{4,12},{12,4},... | collective-permute-start | bytes 1572872 | tf_op jit(solution)/shard_map/ppermute | solution.py:23
  108.9 8.3 %collective-permute-start.14 = (bf16[64,2048]{1,0:T(8,128)(2,1)S(1)}, bf16[64,2048]{1,0:T(8,128)(2,1)S(1)}, u32[]{:S(2)}, u32[]{:S(2)}) collective-permute-start(bf16[64,2048]{1,0:T(8,128)(2,1)S(1)} %fusion.10), channel_id=1, source_target_pairs={{0,16},{16,32},{32,48},{48,64},{64,80},{80,96},{96,112},{112,0},{1... | collective-permute-start | bytes 786440 | tf_op jit(solution)/shard_map/ppermute | solution.py:27
  109.9 8.3 %collective-permute-start.18 = (bf16[64,2048]{1,0:T(8,128)(2,1)S(1)}, bf16[64,2048]{1,0:T(8,128)(2,1)S(1)}, u32[]{:S(2)}, u32[]{:S(2)}) collective-permute-start(bf16[64,2048]{1,0:T(8,128)(2,1)S(1)} %fusion.13), channel_id=1, source_target_pairs={{0,112},{16,0},{32,16},{48,32},{64,48},{80,64},{96,80},{112,96},{1... | collective-permute-start | bytes 786440 | tf_op jit(solution)/shard_map/ppermute | solution.py:27
  118.1 7.7 %collective-permute-start.15 = (bf16[64,2048]{1,0:T(8,128)(2,1)S(1)}, bf16[64,2048]{1,0:T(8,128)(2,1)S(1)}, u32[]{:S(2)}, u32[]{:S(2)}) collective-permute-start(bf16[64,2048]{1,0:T(8,128)(2,1)S(1)} %fusion.9), channel_id=1, source_target_pairs={{0,16},{16,32},{32,48},{48,64},{64,80},{80,96},{96,112},{112,0},{1... | collective-permute-start | bytes 786440 | tf_op jit(solution)/shard_map/ppermute | solution.py:27
  119.1 7.7 %collective-permute-start.19 = (bf16[64,2048]{1,0:T(8,128)(2,1)S(1)}, bf16[64,2048]{1,0:T(8,128)(2,1)S(1)}, u32[]{:S(2)}, u32[]{:S(2)}) collective-permute-start(bf16[64,2048]{1,0:T(8,128)(2,1)S(1)} %fusion.12), channel_id=1, source_target_pairs={{0,112},{16,0},{32,16},{48,32},{64,48},{80,64},{96,80},{112,96},{1... | collective-permute-start | bytes 786440 | tf_op jit(solution)/shard_map/ppermute | solution.py:27
  126.7 7.7 %collective-permute-start.16 = (bf16[64,2048]{1,0:T(8,128)(2,1)S(1)}, bf16[64,2048]{1,0:T(8,128)(2,1)S(1)}, u32[]{:S(2)}, u32[]{:S(2)}) collective-permute-start(bf16[64,2048]{1,0:T(8,128)(2,1)S(1)} %fusion.8), channel_id=1, source_target_pairs={{0,16},{16,32},{32,48},{48,64},{64,80},{80,96},{96,112},{112,0},{1... | collective-permute-start | bytes 786440 | tf_op jit(solution)/shard_map/ppermute | solution.py:27
  127.7 7.4 %collective-permute-start.20 = (bf16[64,2048]{1,0:T(8,128)(2,1)S(1)}, bf16[64,2048]{1,0:T(8,128)(2,1)S(1)}, u32[]{:S(2)}, u32[]{:S(2)}) collective-permute-start(bf16[64,2048]{1,0:T(8,128)(2,1)S(1)} %fusion.11), channel_id=1, source_target_pairs={{0,112},{16,0},{32,16},{48,32},{64,48},{80,64},{96,80},{112,96},{1... | collective-permute-start | bytes 786440 | tf_op jit(solution)/shard_map/ppermute | solution.py:27
  134.1 5.1 %copy-start = (bf16[512,2048]{1,0:T(8,128)(2,1)S(1)}, bf16[512,2048]{1,0:T(8,128)(2,1)}, u32[]{:S(2)}) copy-start(bf16[512,2048]{1,0:T(8,128)(2,1)} %param.5) | copy-start | bytes 6291460
  134.1 5.1 %copy-start.5 = (bf16[512,2048]{1,0:T(8,128)(2,1)S(1)}, bf16[512,2048]{1,0:T(8,128)(2,1)}, u32[]{:S(2)}) copy-start(bf16[512,2048]{1,0:T(8,128)(2,1)} %copy-done.4) | copy-start | bytes 6291460
  136.0 6.4 %collective-permute-start.21 = (bf16[32,2048]{1,0:T(8,128)(2,1)S(1)}, bf16[32,2048]{1,0:T(8,128)(2,1)S(1)}, u32[]{:S(2)}, u32[]{:S(2)}) collective-permute-start(bf16[32,2048]{1,0:T(8,128)(2,1)S(1)} %slice.130), channel_id=1, source_target_pairs={{0,128},{128,0},{1,129},{129,1},{2,130},{130,2},{3,131},{131,3},{4... | collective-permute-start | bytes 393224 | tf_op jit(solution)/shard_map/ppermute | solution.py:23

commit v2 on v1

v2 whole, which is shorter than its diff:
```python
import math

import jax
import jax.numpy as jnp
from jax import lax
from jax.sharding import Mesh, PartitionSpec as P

VOCAB = 16384
REP = ("yhi", "x")
NEAR = [(0, 0), (1, 0), (0, 1), (1, 1), (0, -1), (1, -1), (0, 2), (0, -2)]
FAR = [(1, 2), (1, -2), (0, 3), (0, -3), (1, 3), (1, -3), (0, 4), (1, 4)]


def saturate(act):
    wide = act.astype(jnp.float32)
    return jnp.log1p(jnp.maximum(wide, 0.0)).astype(jnp.bfloat16)


def slope(act):
    wide = act.astype(jnp.float32)
    return jnp.where(wide > 0.0, 1.0 / (1.0 + jnp.maximum(wide, 0.0)), 0.0)


def swap(value, axis):
    return lax.ppermute(value, axis, [(0, 1), (1, 0)])


def shift(value, step):
    return lax.ppermute(value, "z", [(i, (i + step) % 8) for i in range(8)])


def shards(query_act, passage_act, positive, normalizer):
    factor = 8.0 / math.sqrt(VOCAB)
    core, y, z = lax.axis_index("core"), lax.axis_index("ylo"), lax.axis_index("z")
    rep = lax.axis_index(REP)
    bf16, f32 = jnp.bfloat16, jnp.float32

    own = saturate(passage_act)
    blocks = {(0, 0): own, (1, 0): swap(own, "ylo")}
    for d in range(1, 4):
        for s in (0, 1):
            blocks[s, -d] = shift(blocks[s, 1 - d], 1)
            blocks[s, d] = shift(blocks[s, d - 1], -1)
    blocks[0, 4] = shift(blocks[0, -3], 1)
    blocks[1, 4] = shift(blocks[1, 3], -1)

    query_rep = saturate(query_act)
    queries = jnp.concatenate([query_rep, swap(query_rep, "core")], axis=0)
    row_info = jnp.stack([normalizer, positive.astype(f32)])
    row_info = jnp.concatenate([row_info, swap(row_info, "core")], axis=1)
    row_info = lax.dynamic_slice_in_dim(row_info, rep * 128, 128, axis=1)
    row_norm, row_positive = row_info[0][:, None], row_info[1].astype(jnp.int32)[:, None]

    def spread_grad(keys, passages):
        part = lax.dot_general(queries, passages, (((1,), (1,)), ((), ())), preferred_element_type=f32)
        pieces = lax.all_to_all(part.reshape(8, 128, 256), REP, split_axis=0, concat_axis=0)
        scores = jnp.sum(pieces, axis=0) * factor
        place = jnp.arange(256, dtype=jnp.int32)
        stream = jnp.array([s for s, _ in keys], dtype=jnp.int32)[place // 32]
        where = jnp.array([d for _, d in keys], dtype=jnp.int32)[place // 32]
        ident = ((y + stream) % 2) * 16 + ((z + where + 8) % 8) * 2 + core
        ident = ident * 32 + place % 32
        onehot = (row_positive == ident[None, :]).astype(f32)
        grad = ((jnp.exp(scores - row_norm) - onehot) * (8.0 * factor)).astype(bf16)
        return lax.all_to_all(
            jnp.broadcast_to(grad[None], (8, 128, 256)), REP, split_axis=0, concat_axis=0
        ).reshape(1024, 256)

    near = jnp.concatenate([blocks[k] for k in NEAR], axis=0)
    far = jnp.concatenate([blocks[k] for k in FAR], axis=0)
    near_grad = spread_grad(NEAR, near)
    far_grad = spread_grad(FAR, far)

    def sums(grad):
        return lax.dot_general(grad, queries, (((0,), (0,)), ((), ())), preferred_element_type=f32)

    terms = {}
    for keys, block in ((FAR, sums(far_grad)), (NEAR, sums(near_grad))):
        block = lax.optimization_barrier(block)
        for i, k in enumerate(keys):
            terms[k] = block[i * 32 : i * 32 + 32]

    up, down = {}, {}
    up[0] = shift(terms[0, 4].astype(bf16), 1).astype(f32)
    down[1] = shift(terms[1, 4].astype(bf16), -1).astype(f32)
    up[1] = down[0] = 0.0
    for d in (3, 2, 1):
        for s in (1, 0):
            up[s] = shift((terms[s, d] + up[s]).astype(bf16), 1).astype(f32)
            down[s] = shift((terms[s, -d] + down[s]).astype(bf16), -1).astype(f32)
    partner = swap((terms[1, 0] + up[1] + down[1]).astype(bf16), "ylo").astype(f32)
    passage_sum = terms[0, 0] + up[0] + down[0] + partner
    passage_grad = (passage_sum * slope(passage_act)).astype(bf16)

    passages = jnp.concatenate([near, far, swap(near, "core"), swap(far, "core")], axis=0)
    grads = jnp.concatenate(
        [near_grad[:512], far_grad[:512], swap(near_grad[512:], "core"), swap(far_grad[512:], "core")],
        axis=1,
    )
    query_sum = jnp.dot(grads, passages, preferred_element_type=f32)
    query_grad = (query_sum * slope(query_act)).astype(bf16)
    return (query_grad, passage_grad)


def solution(mesh):
    split = Mesh(mesh.devices.reshape(2, 8, 2, 2, 4), ("ylo", "z", "core", "yhi", "x"))
    rows, columns = ("ylo", "z", "core"), ("yhi", "x")
    return jax.shard_map(
        shards,
        mesh=split,
        in_specs=(P(rows, columns), P(rows, columns), P(rows), P(rows)),
        out_specs=(P(rows, columns), P(rows, columns)),
        check_vma=False,
    )
```

time: 144 us -> 165 us (1.15)
  waiting for transfers between devices: 70.6 us -> 46.9 us
  local copies, waits for them, and re-layouts: 1.37 us -> 22 us
  starting transfers between devices: 46 us -> 65 us
  other arithmetic: 5.54 us -> 9.49 us
    ppermute x16 -> x28, waiting for transfers between devices: 30.6 us -> 8.43 us  [shift(): return lax.ppermute(value, 'z', [(i, (i + step) % 8) for i in range(8)])]
    unnamed x28 -> x36, local copies, waits for them, and re-layouts: 0.18 us -> 14.9 us
    ppermute x16 -> x28, starting transfers between devices: 30.1 us -> 42.9 us  [shift(): return lax.ppermute(value, 'z', [(i, (i + step) % 8) for i in range(8)])]
    all_to_all x2 -> x4, starting transfers between devices: 9.98 us -> 16.9 us  [the longest x2 9.88 us: spread_grad(): lax.all_to_all(part.reshape(8, 128, 256), REP, split_axis=0, concat_axis=0)]
    concatenate x1 -> x3, local copies, waits for them, and re-layouts: 0.01 us -> 4.6 us  [the longest x1 2.3 us: shards(): jnp.concatenate([near, far, swap(near, 'core'), swap(far, 'core')], axis=0)]
    convert_element_type x2 -> x7, other arithmetic: 0.14 us -> 3.03 us  [the longest x3 2.8 us: shards(): up[s] = shift((terms[s, d] + up[s]).astype(bf16), 1).astype(f32)]
    dot_general x11 -> x5, matrix products: 18.7 us -> 19.8 us  [the longest x2 7.01 us: sums(): lax.dot_general(grad, queries, (((0,), (0,)), ((), ())), preferred_elemen...]
    all_to_all x2 -> x4, waiting for transfers between devices: 38.9 us -> 38 us  [the longest x2 19.6 us: spread_grad(): lax.all_to_all(part.reshape(8, 128, 256), REP, split_axis=0, concat_axis=0)]
  transfers between devices with their start and end apart: 24 -> 40, of which waited for: 12 -> 11; matrix products, arithmetic and copies ran while one was open for 12% -> 29% of each run, Pallas kernels for 0% -> 0%
where the time goes in v2:
time: 165 us; the launch traced here: 164 us
  starting transfers between devices  65 us (39%)
  waiting for transfers between devices  46.9 us (28%)
  local copies, waits for them, and re-layouts  22 us (13%)
  matrix products  19.8 us (12%)
  other arithmetic  9.49 us (6%)
    ppermute x28, starting transfers between devices, shift(): return lax.ppermute(value, 'z', [(i, (i + step) % 8) for i in range(8)])  42.9 us
    all_to_all x2, waiting for transfers between devices, spread_grad(): lax.all_to_all(part.reshape(8, 128, 256), REP, split_axis=0, concat_axis=0)  19.6 us
    all_to_all x2, waiting for transfers between devices, spread_grad(): lax.all_to_all(jnp.broadcast_to(grad[None], (8, 128, 256)), REP, split_ax...  18.4 us
    unnamed x36, local copies, waits for them, and re-layouts  14.9 us
    all_to_all x2, starting transfers between devices, spread_grad(): lax.all_to_all(part.reshape(8, 128, 256), REP, split_axis=0, concat_axis=0)  9.88 us
    ppermute x28, waiting for transfers between devices, shift(): return lax.ppermute(value, 'z', [(i, (i + step) % 8) for i in range(8)])  8.43 us
    dot_general x2, matrix products, sums(): lax.dot_general(grad, queries, (((0,), (0,)), ((), ())), preferred_elemen...  7.01 us
    all_to_all x2, starting transfers between devices, spread_grad(): lax.all_to_all(jnp.broadcast_to(grad[None], (8, 128, 256)), REP, split_ax...  6.98 us
  transfers between devices with their start and end apart: 40, of which 11 were waited for; matrix products, arithmetic and copies ran while one was open for 29% of the time, Pallas kernels for 0%

profile of v2, /device:TPU:8, one launch (start us, length us, event | category | flops | bytes accessed | tf_op | source)
XLA Modules:
  0.0 164.2 jit_solution(3760332235410681471)
XLA Ops:
  0.6 1.1 fusion.16
  1.7 2.3 %collective-permute-start.1 = (bf16[32,2048]{1,0:T(8,128)(2,1)S(1)}, bf16[32,2048]{1,0:T(8,128)(2,1)S(1)}, u32[]{:S(2)}, u32[]{:S(2)}) collective-permute-start(bf16[32,2048]{1,0:T(8,128)(2,1)S(1)} %fusion.16), channel_id=1, source_target_pairs={{0,128},{128,0},{1,129},{129,1},{2,130},{130,2},{3,131},{131,3},{4... | collective-permute-start | bytes 393224 | tf_op jit(solution)/shard_map/ppermute | solution.py:25
  4.0 4.1 %collective-permute-start.2 = (bf16[32,2048]{1,0:T(8,128)(2,1)S(1)}, bf16[32,2048]{1,0:T(8,128)(2,1)S(1)}, u32[]{:S(2)}, u32[]{:S(2)}) collective-permute-start(bf16[32,2048]{1,0:T(8,128)(2,1)S(1)} %fusion.16), channel_id=1, source_target_pairs={{0,112},{16,0},{32,16},{48,32},{64,48},{80,64},{96,80},{112,96},{1... | collective-permute-start | bytes 393224 | tf_op jit(solution)/shard_map/ppermute | solution.py:29
  8.1 3.1 %fusion.2 = bf16[512,2048]{1,0:T(8,128)(2,1)S(1)} fusion(bf16[512,2048]{1,0:T(8,128)(2,1)} %param.8), kind=kLoop, calls=%fused_computation.4 | loop fusion | flops 3145728 | bytes 4194304 | tf_op jit(solution)/shard_map/convert_element_type | solution.py:16
  11.4 1.0 constant_dynamic-update-slice_fusion.7
  12.4 3.2 %collective-permute-start.3 = (bf16[32,2048]{1,0:T(8,128)(2,1)S(1)}, bf16[32,2048]{1,0:T(8,128)(2,1)S(1)}, u32[]{:S(2)}, u32[]{:S(2)}) collective-permute-start(bf16[32,2048]{1,0:T(8,128)(2,1)S(1)} %collective-permute-done.1), channel_id=1, source_target_pairs={{0,112},{16,0},{32,16},{48,32},{64,48},{80,64},{96,80},{112,96},{1... | collective-permute-start | bytes 393224 | tf_op jit(solution)/shard_map/ppermute | solution.py:29
  15.6 3.2 %collective-permute-start.6 = (bf16[32,2048]{1,0:T(8,128)(2,1)S(1)}, bf16[32,2048]{1,0:T(8,128)(2,1)S(1)}, u32[]{:S(2)}, u32[]{:S(2)}) collective-permute-start(bf16[32,2048]{1,0:T(8,128)(2,1)S(1)} %collective-permute-done.2), channel_id=1, source_target_pairs={{0,112},{16,0},{32,16},{48,32},{64,48},{80,64},{96,80},{112,96},{1... | collective-permute-start | bytes 393224 | tf_op jit(solution)/shard_map/ppermute | solution.py:29
  20.2 3.2 %collective-permute-start.9 = (bf16[32,2048]{1,0:T(8,128)(2,1)S(1)}, bf16[32,2048]{1,0:T(8,128)(2,1)S(1)}, u32[]{:S(2)}, u32[]{:S(2)}) collective-permute-start(bf16[32,2048]{1,0:T(8,128)(2,1)S(1)} %collective-permute-done.3), channel_id=1, source_target_pairs={{0,112},{16,0},{32,16},{48,32},{64,48},{80,64},{96,80},{112,96},{1... | collective-permute-start | bytes 393224 | tf_op jit(solution)/shard_map/ppermute | solution.py:29
  23.5 3.2 %collective-permute-start.11 = (bf16[32,2048]{1,0:T(8,128)(2,1)S(1)}, bf16[32,2048]{1,0:T(8,128)(2,1)S(1)}, u32[]{:S(2)}, u32[]{:S(2)}) collective-permute-start(bf16[32,2048]{1,0:T(8,128)(2,1)S(1)} %collective-permute-done.6), channel_id=1, source_target_pairs={{0,112},{16,0},{32,16},{48,32},{64,48},{80,64},{96,80},{112,96},{1... | collective-permute-start | bytes 393224 | tf_op jit(solution)/shard_map/ppermute | solution.py:29
  30.0 3.2 %collective-permute-start.13 = (bf16[32,2048]{1,0:T(8,128)(2,1)S(1)}, bf16[32,2048]{1,0:T(8,128)(2,1)}, u32[]{:S(2)}, u32[]{:S(2)}) collective-permute-start(bf16[32,2048]{1,0:T(8,128)(2,1)S(1)} %collective-permute-done.9), channel_id=1, source_target_pairs={{0,112},{16,0},{32,16},{48,32},{64,48},{80,64},{96,80},{112,96},{1... | collective-permute-start | bytes 393224 | tf_op jit(solution)/shard_map/ppermute | solution.py:29
  36.1 3.5 %collective-permute-start.16 = (bf16[32,2048]{1,0:T(8,128)(2,1)}, bf16[32,2048]{1,0:T(8,128)(2,1)}, u32[]{:S(2)}, u32[]{:S(2)}) collective-permute-start(bf16[32,2048]{1,0:T(8,128)(2,1)} %collective-permute-done.13), channel_id=1, source_target_pairs={{0,112},{16,0},{32,16},{48,32},{64,48},{80,64},{96,80},{112,96},{1... | collective-permute-start | bytes 393224 | tf_op jit(solution)/shard_map/ppermute | solution.py:29
  39.6 1.6 constant_dynamic-update-slice_fusion.11
  41.2 1.0 copy-done.7
  42.1 2.3 %fusion.57 = f32[1024,256]{1,0:T(8,128)} fusion(bf16[256,2048]{1,0:T(8,128)(2,1)S(1)} %get-tuple-element.35, bf16[512,2048]{1,0:T(8,128)(2,1)S(1)} %collective-permute-done, bf16[512,2048]{1,0:T(8,128)(2,1)S(1)} %fusion.2), kind=kOutput, calls=%fused_computation.152 | convolution fusion | flops 1082130432 | bytes 6291456 | tf_op jit(solution)/shard_map/dot_general | solution.py:55
  44.5 6.3 %all-to-all-start = ((f32[8,128,256]{2,1,0:T(8,128)}), f32[8,128,256]{2,1,0:T(8,128)S(1)}, u32[]{:S(2)}, u32[]{:S(2)}) async-start(f32[8,128,256]{2,1,0:T(8,128)} %bitcast.26), calls=%async_computation | async-start | bytes 2097152 | tf_op jit(solution)/shard_map/all_to_all | solution.py:56
  50.8 1.6 constant_dynamic-update-slice_fusion.10
  52.4 1.6 constant_dynamic-update-slice_fusion.9
  54.1 1.6 constant_dynamic-update-slice_fusion.8
  55.7 4.1 %fusion.56 = f32[1024,256]{1,0:T(8,128)} fusion(bf16[256,2048]{1,0:T(8,128)(2,1)} %get-tuple-element.19, bf16[512,2048]{1,0:T(8,128)(2,1)} %copy-done.10, bf16[512,2048]{1,0:T(8,128)(2,1)S(1)} %fusion.2), kind=kOutput, calls=%fused_computation.151 | convolution fusion | flops 1082130432 | bytes 6291456 | tf_op jit(solution)/shard_map/dot_general | solution.py:55
  59.9 5.2 %all-to-all-done = f32[8,128,256]{2,1,0:T(8,128)S(1)} async-done(((f32[8,128,256]{2,1,0:T(8,128)}), f32[8,128,256]{2,1,0:T(8,128)S(1)}, u32[]{:S(2)}, u32[]{:S(2)}) %all-to-all-start) | async-done | bytes 1048608 | tf_op jit(solution)/shard_map/all_to_all | solution.py:56
  65.1 3.6 %all-to-all-start.2 = ((f32[8,128,256]{2,1,0:T(8,128)}), f32[8,128,256]{2,1,0:T(8,128)S(1)}, u32[]{:S(2)}, u32[]{:S(2)}) async-start(f32[8,128,256]{2,1,0:T(8,128)} %bitcast.25), calls=%async_computation.2 | async-start | bytes 2097152 | tf_op jit(solution)/shard_map/all_to_all | solution.py:56
  70.1 14.3 %all-to-all-done.2 = f32[8,128,256]{2,1,0:T(8,128)S(1)} async-done(((f32[8,128,256]{2,1,0:T(8,128)}), f32[8,128,256]{2,1,0:T(8,128)S(1)}, u32[]{:S(2)}, u32[]{:S(2)}) %all-to-all-start.2) | async-done | bytes 1048608 | tf_op jit(solution)/shard_map/all_to_all | solution.py:56
  84.6 0.8 broadcast_in_dim.7
  85.5 3.5 %all-to-all-start.3 = ((bf16[8,128,256]{2,1,0:T(8,128)(2,1)}), bf16[8,128,256]{2,1,0:T(8,128)(2,1)S(1)}, u32[]{:S(2)}, u32[]{:S(2)}) async-start(bf16[8,128,256]{2,1,0:T(8,128)(2,1)} %broadcast_in_dim.7), calls=%async_computation.3 | async-start | bytes 1048576 | tf_op jit(solution)/shard_map/all_to_all | solution.py:65
  89.1 1.1 constant_dynamic-update-slice_fusion.17
  90.2 10.5 %all-to-all-done.3 = bf16[8,128,256]{2,1,0:T(8,128)(2,1)S(1)} async-done(((bf16[8,128,256]{2,1,0:T(8,128)(2,1)}), bf16[8,128,256]{2,1,0:T(8,128)(2,1)S(1)}, u32[]{:S(2)}, u32[]{:S(2)}) %all-to-all-start.3) | async-done | bytes 524320 | tf_op jit(solution)/shard_map/all_to_all | solution.py:65
  100.6 3.5 %fusion.54 = f32[256,2048]{1,0:T(8,128)S(1)} fusion(bf16[1024,256]{1,0:T(8,128)(2,1)S(1)} %bitcast.23, bf16[512,2048]{1,0:T(8,128)(2,1)} %copy-done.10, bf16[512,2048]{1,0:T(8,128)(2,1)} %copy-done.1), kind=kOutput, calls=%fused_computation.149 | convolution fusion | flops 1082130432 | bytes 6815744 | tf_op jit(solution)/shard_map/dot_general | solution.py:75
  104.3 0.8 fusion.58
  105.1 3.2 %collective-permute-start.31 = (bf16[32,2048]{1,0:T(8,128)(2,1)}, bf16[32,2048]{1,0:T(8,128)(2,1)S(1)}, u32[]{:S(2)}, u32[]{:S(2)}) collective-permute-start(bf16[32,2048]{1,0:T(8,128)(2,1)} %get-tuple-element.12), channel_id=1, source_target_pairs={{0,112},{16,0},{32,16},{48,32},{64,48},{80,64},{96,80},{112,96},{1... | collective-permute-start | bytes 393224 | tf_op jit(solution)/shard_map/ppermute | solution.py:29
  108.3 2.3 %constant_dynamic-update-slice_fusion.16 = bf16[1024,2048]{1,0:T(8,128)(2,1)} fusion(bf16[1024,2048]{1,0:T(8,128)(2,1)} %constant_dynamic-update-slice_fusion.17, bf16[256,2048]{1,0:T(8,128)(2,1)} %collective-permute-done.20), kind=kLoop, calls=%fused_computation.70 | loop fusion | bytes 2097152 | tf_op jit(solution)/shard_map/concatenate | solution.py:95
  110.6 0.8 broadcast_in_dim.6
  111.4 3.5 %all-to-all-start.1 = ((bf16[8,128,256]{2,1,0:T(8,128)(2,1)}), bf16[8,128,256]{2,1,0:T(8,128)(2,1)S(1)}, u32[]{:S(2)}, u32[]{:S(2)}) async-start(bf16[8,128,256]{2,1,0:T(8,128)(2,1)} %broadcast_in_dim.6), calls=%async_computation.1 | async-start | bytes 1048576 | tf_op jit(solution)/shard_map/all_to_all | solution.py:65
  116.3 1.8 %fusion.29 = (bf16[32,2048]{1,0:T(8,128)(2,1)}, bf16[32,2048]{1,0:T(8,128)(2,1)S(1)}, bf16[32,2048]{1,0:T(8,128)(2,1)S(1)}) fusion(f32[256,2048]{1,0:T(8,128)S(1)} %fusion.54, bf16[32,2048]{1,0:T(8,128)(2,1)} %copy-done.3, bf16[32,2048]{1,0:T(8,128)(2,1)} %copy-done.4, bf16[32,2048]{1,0:T(8,128)(2,1)} %collective-permute-done.28), kind=kLoop, calls=%fused_computation.43 | loop fusion | flops 589824 | bytes 1572864 | tf_op jit(solution)/shard_map/convert_element_type | solution.py:89
  118.0 8.0 %all-to-all-done.1 = bf16[8,128,256]{2,1,0:T(8,128)(2,1)S(1)} async-done(((bf16[8,128,256]{2,1,0:T(8,128)(2,1)}), bf16[8,128,256]{2,1,0:T(8,128)(2,1)S(1)}, u32[]{:S(2)}, u32[]{:S(2)}) %all-to-all-start.1) | async-done | bytes 524320 | tf_op jit(solution)/shard_map/all_to_all | solution.py:65
  126.0 3.5 %fusion.55 = f32[256,2048]{1,0:T(8,128)S(1)} fusion(bf16[1024,256]{1,0:T(8,128)(2,1)S(1)} %bitcast.24, bf16[512,2048]{1,0:T(8,128)(2,1)} %copy-done.10, bf16[512,2048]{1,0:T(8,128)(2,1)} %copy-done.1), kind=kOutput, calls=%fused_computation.150 | convolution fusion | flops 1082130432 | bytes 6815744 | tf_op jit(solution)/shard_map/dot_general | solution.py:75
  129.6 3.0 %collective-permute-start.25 = (bf16[32,2048]{1,0:T(8,128)(2,1)S(1)}, bf16[32,2048]{1,0:T(8,128)(2,1)S(1)}, u32[]{:S(2)}, u32[]{:S(2)}) collective-permute-start(bf16[32,2048]{1,0:T(8,128)(2,1)S(1)} %copy-done.5), channel_id=1, source_target_pairs={{0,112},{16,0},{32,16},{48,32},{64,48},{80,64},{96,80},{112,96},{1... | collective-permute-start | bytes 393224 | tf_op jit(solution)/shard_map/ppermute | solution.py:29
  132.7 1.9 %collective-permute-start.29 = (bf16[32,2048]{1,0:T(8,128)(2,1)S(1)}, bf16[32,2048]{1,0:T(8,128)(2,1)S(1)}, u32[]{:S(2)}, u32[]{:S(2)}) collective-permute-start(bf16[32,2048]{1,0:T(8,128)(2,1)S(1)} %get-tuple-element.8), channel_id=1, source_target_pairs={{0,16},{16,32},{32,48},{48,64},{64,80},{80,96},{96,112},{112,0},{1... | collective-permute-start | bytes 393224 | tf_op jit(solution)/shard_map/ppermute | solution.py:29
  134.6 0.9 fusion.30
  135.6 1.9 %collective-permute-done.32 = bf16[32,2048]{1,0:T(8,128)(2,1)S(1)} collective-permute-done((bf16[32,2048]{1,0:T(8,128)(2,1)S(1)}, bf16[32,2048]{1,0:T(8,128)(2,1)S(1)}, u32[]{:S(2)}, u32[]{:S(2)}) %collective-permute-start.32) | collective-permute-done | bytes 131104 | tf_op jit(solution)/shard_map/ppermute | solution.py:29
  137.6 3.6 %collective-permute-start.33 = (bf16[32,2048]{1,0:T(8,128)(2,1)S(1)}, bf16[32,2048]{1,0:T(8,128)(2,1)S(1)}, u32[]{:S(2)}, u32[]{:S(2)}) collective-permute-start(bf16[32,2048]{1,0:T(8,128)(2,1)S(1)} %fusion.21), channel_id=1, source_target_pairs={{0,112},{16,0},{32,16},{48,32},{64,48},{80,64},{96,80},{112,96},{1... | collective-permute-start | bytes 393224 | tf_op jit(solution)/shard_map/ppermute | solution.py:29
  141.8 1.9 %collective-permute-done.33 = bf16[32,2048]{1,0:T(8,128)(2,1)S(1)} collective-permute-done((bf16[32,2048]{1,0:T(8,128)(2,1)S(1)}, bf16[32,2048]{1,0:T(8,128)(2,1)S(1)}, u32[]{:S(2)}, u32[]{:S(2)}) %collective-permute-start.33) | collective-permute-done | bytes 131104 | tf_op jit(solution)/shard_map/ppermute | solution.py:29
  143.8 3.7 %collective-permute-start.26 = (bf16[32,2048]{1,0:T(8,128)(2,1)S(1)}, bf16[32,2048]{1,0:T(8,128)(2,1)S(1)}, u32[]{:S(2)}, u32[]{:S(2)}) collective-permute-start(bf16[32,2048]{1,0:T(8,128)(2,1)S(1)} %get-tuple-element.5), channel_id=1, source_target_pairs={{0,112},{16,0},{32,16},{48,32},{64,48},{80,64},{96,80},{112,96},{1... | collective-permute-start | bytes 393224 | tf_op jit(solution)/shard_map/ppermute | solution.py:29
  147.6 1.9 %collective-permute-start.30 = (bf16[32,2048]{1,0:T(8,128)(2,1)S(1)}, bf16[32,2048]{1,0:T(8,128)(2,1)S(1)}, u32[]{:S(2)}, u32[]{:S(2)}) collective-permute-start(bf16[32,2048]{1,0:T(8,128)(2,1)S(1)} %get-tuple-element.4), channel_id=1, source_target_pairs={{0,16},{16,32},{32,48},{48,64},{64,80},{80,96},{96,112},{112,0},{1... | collective-permute-start | bytes 393224 | tf_op jit(solution)/shard_map/ppermute | solution.py:29
  150.1 2.4 %collective-permute-done.34 = bf16[32,2048]{1,0:T(8,128)(2,1)S(1)} collective-permute-done((bf16[32,2048]{1,0:T(8,128)(2,1)S(1)}, bf16[32,2048]{1,0:T(8,128)(2,1)S(1)}, u32[]{:S(2)}, u32[]{:S(2)}) %collective-permute-start.34) | collective-permute-done | bytes 131104 | tf_op jit(solution)/shard_map/ppermute | solution.py:29
  152.5 1.3 collective-permute-done.30
  153.9 2.0 %collective-permute-start.35 = (bf16[32,2048]{1,0:T(8,128)(2,1)S(1)}, bf16[32,2048]{1,0:T(8,128)(2,1)S(1)}, u32[]{:S(2)}, u32[]{:S(2)}) collective-permute-start(bf16[32,2048]{1,0:T(8,128)(2,1)S(1)} %get-tuple-element.10), channel_id=1, source_target_pairs={{0,128},{128,0},{1,129},{129,1},{2,130},{130,2},{3,131},{131,3},{4... | collective-permute-start | bytes 393224 | tf_op jit(solution)/shard_map/ppermute | solution.py:25
  155.8 1.3 collective-permute-start.27
  157.2 6.2 %fusion.6 = bf16[512,2048]{1,0:T(8,128)(2,1)} fusion(bf16[512,2048]{1,0:T(8,128)(2,1)S(1)} %copy-done, bf16[1024,2048]{1,0:T(8,128)(2,1)} %constant_dynamic-update-slice_fusion.16, bf16[512,256]{1,0:T(8,128)(2,1)S(1)} %collective-permute-done.18, bf16[512,256]{1,0:T(8,128)(2,1)S(1)} %collective-permute-done.17, bf16[512,256]{1,0:T(8,128)(2,1)S(1)} %bitcast.27, ...), kind=kOutput, calls=%fused_computation.9 | convolution fusion | flops 2160066560 | bytes 9437184 | tf_op jit(solution)/shard_map/dot_general | solution.py:100
  (102 shorter events, 13.1 us)
Async XLA Ops:
  0.6 10.7 %copy-start.2 = (bf16[32,2048]{1,0:T(8,128)(2,1)S(1)}, bf16[32,2048]{1,0:T(8,128)(2,1)}, u32[]{:S(2)}) copy-start(bf16[32,2048]{1,0:T(8,128)(2,1)} %param.9) | copy-start | bytes 393220
  1.7 10.7 %collective-permute-start.1 = (bf16[32,2048]{1,0:T(8,128)(2,1)S(1)}, bf16[32,2048]{1,0:T(8,128)(2,1)S(1)}, u32[]{:S(2)}, u32[]{:S(2)}) collective-permute-start(bf16[32,2048]{1,0:T(8,128)(2,1)S(1)} %fusion.16), channel_id=1, source_target_pairs={{0,128},{128,0},{1,129},{129,1},{2,130},{130,2},{3,131},{131,3},{4... | collective-permute-start | bytes 393224 | tf_op jit(solution)/shard_map/ppermute | solution.py:25
  4.0 11.6 %collective-permute-start.2 = (bf16[32,2048]{1,0:T(8,128)(2,1)S(1)}, bf16[32,2048]{1,0:T(8,128)(2,1)S(1)}, u32[]{:S(2)}, u32[]{:S(2)}) collective-permute-start(bf16[32,2048]{1,0:T(8,128)(2,1)S(1)} %fusion.16), channel_id=1, source_target_pairs={{0,112},{16,0},{32,16},{48,32},{64,48},{80,64},{96,80},{112,96},{1... | collective-permute-start | bytes 393224 | tf_op jit(solution)/shard_map/ppermute | solution.py:29
  8.1 10.8 %collective-permute-start.4 = (bf16[32,2048]{1,0:T(8,128)(2,1)S(1)}, bf16[32,2048]{1,0:T(8,128)(2,1)S(1)}, u32[]{:S(2)}, u32[]{:S(2)}) collective-permute-start(bf16[32,2048]{1,0:T(8,128)(2,1)S(1)} %fusion.16), channel_id=1, source_target_pairs={{0,16},{16,32},{32,48},{48,64},{64,80},{80,96},{96,112},{112,0},{1... | collective-permute-start | bytes 393224 | tf_op jit(solution)/shard_map/ppermute | solution.py:29
  11.3 44.4 %copy-start.1 = (bf16[512,2048]{1,0:T(8,128)(2,1)}, bf16[512,2048]{1,0:T(8,128)(2,1)S(1)}, u32[]{:S(2)}) copy-start(bf16[512,2048]{1,0:T(8,128)(2,1)S(1)} %fusion.2) | copy-start | bytes 6291460
  11.3 29.9 %collective-permute-start = (bf16[512,2048]{1,0:T(8,128)(2,1)S(1)}, bf16[512,2048]{1,0:T(8,128)(2,1)S(1)}, u32[]{:S(2)}, u32[]{:S(2)}) collective-permute-start(bf16[512,2048]{1,0:T(8,128)(2,1)S(1)} %fusion.2), channel_id=1, source_target_pairs={{0,8},{8,0},{1,9},{9,1},{2,10},{10,2},{3,11},{11,3},{4,12},{12,4},... | collective-permute-start | bytes 6291464 | tf_op jit(solution)/shard_map/ppermute | solution.py:25
  12.4 7.8 %collective-permute-start.3 = (bf16[32,2048]{1,0:T(8,128)(2,1)S(1)}, bf16[32,2048]{1,0:T(8,128)(2,1)S(1)}, u32[]{:S(2)}, u32[]{:S(2)}) collective-permute-start(bf16[32,2048]{1,0:T(8,128)(2,1)S(1)} %collective-permute-done.1), channel_id=1, source_target_pairs={{0,112},{16,0},{32,16},{48,32},{64,48},{80,64},{96,80},{112,96},{1... | collective-permute-start | bytes 393224 | tf_op jit(solution)/shard_map/ppermute | solution.py:29
  15.6 7.8 %collective-permute-start.5 = (bf16[32,2048]{1,0:T(8,128)(2,1)S(1)}, bf16[32,2048]{1,0:T(8,128)(2,1)S(1)}, u32[]{:S(2)}, u32[]{:S(2)}) collective-permute-start(bf16[32,2048]{1,0:T(8,128)(2,1)S(1)} %collective-permute-done.1), channel_id=1, source_target_pairs={{0,16},{16,32},{32,48},{48,64},{64,80},{80,96},{96,112},{112,0},{1... | collective-permute-start | bytes 393224 | tf_op jit(solution)/shard_map/ppermute | solution.py:29
  15.6 7.8 %collective-permute-start.6 = (bf16[32,2048]{1,0:T(8,128)(2,1)S(1)}, bf16[32,2048]{1,0:T(8,128)(2,1)S(1)}, u32[]{:S(2)}, u32[]{:S(2)}) collective-permute-start(bf16[32,2048]{1,0:T(8,128)(2,1)S(1)} %collective-permute-done.2), channel_id=1, source_target_pairs={{0,112},{16,0},{32,16},{48,32},{64,48},{80,64},{96,80},{112,96},{1... | collective-permute-start | bytes 393224 | tf_op jit(solution)/shard_map/ppermute | solution.py:29
  18.9 7.8 %collective-permute-start.7 = (bf16[32,2048]{1,0:T(8,128)(2,1)S(1)}, bf16[32,2048]{1,0:T(8,128)(2,1)S(1)}, u32[]{:S(2)}, u32[]{:S(2)}) collective-permute-start(bf16[32,2048]{1,0:T(8,128)(2,1)S(1)} %collective-permute-done.4), channel_id=1, source_target_pairs={{0,16},{16,32},{32,48},{48,64},{64,80},{80,96},{96,112},{112,0},{1... | collective-permute-start | bytes 393224 | tf_op jit(solution)/shard_map/ppermute | solution.py:29
  20.2 9.8 %collective-permute-start.9 = (bf16[32,2048]{1,0:T(8,128)(2,1)S(1)}, bf16[32,2048]{1,0:T(8,128)(2,1)S(1)}, u32[]{:S(2)}, u32[]{:S(2)}) collective-permute-start(bf16[32,2048]{1,0:T(8,128)(2,1)S(1)} %collective-permute-done.3), channel_id=1, source_target_pairs={{0,112},{16,0},{32,16},{48,32},{64,48},{80,64},{96,80},{112,96},{1... | collective-permute-start | bytes 393224 | tf_op jit(solution)/shard_map/ppermute | solution.py:29
  23.5 9.8 %collective-permute-start.10 = (bf16[32,2048]{1,0:T(8,128)(2,1)S(1)}, bf16[32,2048]{1,0:T(8,128)(2,1)S(1)}, u32[]{:S(2)}, u32[]{:S(2)}) collective-permute-start(bf16[32,2048]{1,0:T(8,128)(2,1)S(1)} %collective-permute-done.5), channel_id=1, source_target_pairs={{0,16},{16,32},{32,48},{48,64},{64,80},{80,96},{96,112},{112,0},{1... | collective-permute-start | bytes 393224 | tf_op jit(solution)/shard_map/ppermute | solution.py:29
  23.5 11.3 %collective-permute-start.11 = (bf16[32,2048]{1,0:T(8,128)(2,1)S(1)}, bf16[32,2048]{1,0:T(8,128)(2,1)S(1)}, u32[]{:S(2)}, u32[]{:S(2)}) collective-permute-start(bf16[32,2048]{1,0:T(8,128)(2,1)S(1)} %collective-permute-done.6), channel_id=1, source_target_pairs={{0,112},{16,0},{32,16},{48,32},{64,48},{80,64},{96,80},{112,96},{1... | collective-permute-start | bytes 393224 | tf_op jit(solution)/shard_map/ppermute | solution.py:29
  26.7 6.6 %collective-permute-start.12 = (bf16[32,2048]{1,0:T(8,128)(2,1)S(1)}, bf16[32,2048]{1,0:T(8,128)(2,1)S(1)}, u32[]{:S(2)}, u32[]{:S(2)}) collective-permute-start(bf16[32,2048]{1,0:T(8,128)(2,1)S(1)} %collective-permute-done.7), channel_id=1, source_target_pairs={{0,16},{16,32},{32,48},{48,64},{64,80},{80,96},{96,112},{112,0},{1... | collective-permute-start | bytes 393224 | tf_op jit(solution)/shard_map/ppermute | solution.py:29
  30.0 14.4 %copy-start.6 = (bf16[256,2048]{1,0:T(8,128)(2,1)}, bf16[256,2048]{1,0:T(8,128)(2,1)S(1)}, u32[]{:S(2)}) copy-start(bf16[256,2048]{1,0:T(8,128)(2,1)S(1)} %get-tuple-element.35) | copy-start | bytes 3145732
  30.0 6.0 %collective-permute-start.13 = (bf16[32,2048]{1,0:T(8,128)(2,1)S(1)}, bf16[32,2048]{1,0:T(8,128)(2,1)}, u32[]{:S(2)}, u32[]{:S(2)}) collective-permute-start(bf16[32,2048]{1,0:T(8,128)(2,1)S(1)} %collective-permute-done.9), channel_id=1, source_target_pairs={{0,112},{16,0},{32,16},{48,32},{64,48},{80,64},{96,80},{112,96},{1... | collective-permute-start | bytes 393224 | tf_op jit(solution)/shard_map/ppermute | solution.py:29
  33.3 17.5 %collective-permute-start.14 = (bf16[32,2048]{1,0:T(8,128)(2,1)S(1)}, bf16[32,2048]{1,0:T(8,128)(2,1)}, u32[]{:S(2)}, u32[]{:S(2)}) collective-permute-start(bf16[32,2048]{1,0:T(8,128)(2,1)S(1)} %collective-permute-done.10), channel_id=1, source_target_pairs={{0,16},{16,32},{32,48},{48,64},{64,80},{80,96},{96,112},{112,0},{1... | collective-permute-start | bytes 393224 | tf_op jit(solution)/shard_map/ppermute | solution.py:29
  33.3 19.2 %collective-permute-start.15 = (bf16[32,2048]{1,0:T(8,128)(2,1)S(1)}, bf16[32,2048]{1,0:T(8,128)(2,1)}, u32[]{:S(2)}, u32[]{:S(2)}) collective-permute-start(bf16[32,2048]{1,0:T(8,128)(2,1)S(1)} %collective-permute-done.12), channel_id=1, source_target_pairs={{0,16},{16,32},{32,48},{48,64},{64,80},{80,96},{96,112},{112,0},{1... | collective-permute-start | bytes 393224 | tf_op jit(solution)/shard_map/ppermute | solution.py:29
  36.1 18.0 %collective-permute-start.16 = (bf16[32,2048]{1,0:T(8,128)(2,1)}, bf16[32,2048]{1,0:T(8,128)(2,1)}, u32[]{:S(2)}, u32[]{:S(2)}) collective-permute-start(bf16[32,2048]{1,0:T(8,128)(2,1)} %collective-permute-done.13), channel_id=1, source_target_pairs={{0,112},{16,0},{32,16},{48,32},{64,48},{80,64},{96,80},{112,96},{1... | collective-permute-start | bytes 393224 | tf_op jit(solution)/shard_map/ppermute | solution.py:29
  42.1 2.4 %copy-start.10 = (bf16[512,2048]{1,0:T(8,128)(2,1)}, bf16[512,2048]{1,0:T(8,128)(2,1)S(1)}, u32[]{:S(2)}) copy-start(bf16[512,2048]{1,0:T(8,128)(2,1)S(1)} %collective-permute-done) | copy-start | bytes 6291460
  44.5 20.6 %all-to-all-start = ((f32[8,128,256]{2,1,0:T(8,128)}), f32[8,128,256]{2,1,0:T(8,128)S(1)}, u32[]{:S(2)}, u32[]{:S(2)}) async-start(f32[8,128,256]{2,1,0:T(8,128)} %bitcast.26), calls=%async_computation | async-start | bytes 2097152 | tf_op jit(solution)/shard_map/all_to_all | solution.py:56
  55.7 12.9 %copy-start.9 = (s32[512]{0:T(512)S(1)}, s32[512]{0:T(512)}, u32[]{:S(2)}) copy-start(s32[512]{0:T(512)} %param.10) | copy-start | bytes 6148
  55.7 13.0 %copy-start.8 = (f32[512]{0:T(512)S(1)}, f32[512]{0:T(512)}, u32[]{:S(2)}) copy-start(f32[512]{0:T(512)} %param.11) | copy-start | bytes 6148
  65.1 19.4 %all-to-all-start.2 = ((f32[8,128,256]{2,1,0:T(8,128)}), f32[8,128,256]{2,1,0:T(8,128)S(1)}, u32[]{:S(2)}, u32[]{:S(2)}) async-start(f32[8,128,256]{2,1,0:T(8,128)} %bitcast.25), calls=%async_computation.2 | async-start | bytes 2097152 | tf_op jit(solution)/shard_map/all_to_all | solution.py:56
  68.7 1.3 collective-permute-start.8
  68.8 20.3 %collective-permute-start.19 = (bf16[256,2048]{1,0:T(8,128)(2,1)}, bf16[256,2048]{1,0:T(8,128)(2,1)S(1)}, u32[]{:S(2)}, u32[]{:S(2)}) collective-permute-start(bf16[256,2048]{1,0:T(8,128)(2,1)} %copy-done.6), channel_id=1, source_target_pairs={{0,8},{8,0},{1,9},{9,1},{2,10},{10,2},{3,11},{11,3},{4,12},{12,4},... | collective-permute-start | bytes 3145736 | tf_op jit(solution)/shard_map/ppermute | solution.py:25
  85.5 15.1 %all-to-all-start.3 = ((bf16[8,128,256]{2,1,0:T(8,128)(2,1)}), bf16[8,128,256]{2,1,0:T(8,128)(2,1)S(1)}, u32[]{:S(2)}, u32[]{:S(2)}) async-start(bf16[8,128,256]{2,1,0:T(8,128)(2,1)} %broadcast_in_dim.7), calls=%async_computation.3 | async-start | bytes 1048576 | tf_op jit(solution)/shard_map/all_to_all | solution.py:65
  89.0 19.3 %collective-permute-start.20 = (bf16[256,2048]{1,0:T(8,128)(2,1)}, bf16[256,2048]{1,0:T(8,128)(2,1)}, u32[]{:S(2)}, u32[]{:S(2)}) collective-permute-start(bf16[256,2048]{1,0:T(8,128)(2,1)} %get-tuple-element.19), channel_id=1, source_target_pairs={{0,8},{8,0},{1,9},{9,1},{2,10},{10,2},{3,11},{11,3},{4,12},{12,4},... | collective-permute-start | bytes 3145736 | tf_op jit(solution)/shard_map/ppermute | solution.py:25
  105.1 9.9 %collective-permute-start.21 = (bf16[32,2048]{1,0:T(8,128)(2,1)}, bf16[32,2048]{1,0:T(8,128)(2,1)S(1)}, u32[]{:S(2)}, u32[]{:S(2)}) collective-permute-start(bf16[32,2048]{1,0:T(8,128)(2,1)} %get-tuple-element.11), channel_id=1, source_target_pairs={{0,16},{16,32},{32,48},{48,64},{64,80},{80,96},{96,112},{112,0},{1... | collective-permute-start | bytes 393224 | tf_op jit(solution)/shard_map/ppermute | solution.py:29
  105.1 9.9 %collective-permute-start.31 = (bf16[32,2048]{1,0:T(8,128)(2,1)}, bf16[32,2048]{1,0:T(8,128)(2,1)S(1)}, u32[]{:S(2)}, u32[]{:S(2)}) collective-permute-start(bf16[32,2048]{1,0:T(8,128)(2,1)} %get-tuple-element.12), channel_id=1, source_target_pairs={{0,112},{16,0},{32,16},{48,32},{64,48},{80,64},{96,80},{112,96},{1... | collective-permute-start | bytes 393224 | tf_op jit(solution)/shard_map/ppermute | solution.py:29
  108.3 8.0 %collective-permute-start.28 = (bf16[32,2048]{1,0:T(8,128)(2,1)}, bf16[32,2048]{1,0:T(8,128)(2,1)}, u32[]{:S(2)}, u32[]{:S(2)}) collective-permute-start(bf16[32,2048]{1,0:T(8,128)(2,1)} %get-tuple-element.13), channel_id=1, source_target_pairs={{0,16},{16,32},{32,48},{48,64},{64,80},{80,96},{96,112},{112,0},{1... | collective-permute-start | bytes 393224 | tf_op jit(solution)/shard_map/ppermute | solution.py:29
  111.4 14.6 %all-to-all-start.1 = ((bf16[8,128,256]{2,1,0:T(8,128)(2,1)}), bf16[8,128,256]{2,1,0:T(8,128)(2,1)S(1)}, u32[]{:S(2)}, u32[]{:S(2)}) async-start(bf16[8,128,256]{2,1,0:T(8,128)(2,1)} %broadcast_in_dim.6), calls=%async_computation.1 | async-start | bytes 1048576 | tf_op jit(solution)/shard_map/all_to_all | solution.py:65
  118.0 16.6 %collective-permute-start.22 = (bf16[32,2048]{1,0:T(8,128)(2,1)}, bf16[32,2048]{1,0:T(8,128)(2,1)}, u32[]{:S(2)}, u32[]{:S(2)}) collective-permute-start(bf16[32,2048]{1,0:T(8,128)(2,1)} %get-tuple-element.6), channel_id=1, source_target_pairs={{0,16},{16,32},{32,48},{48,64},{64,80},{80,96},{96,112},{112,0},{1... | collective-permute-start | bytes 393224 | tf_op jit(solution)/shard_map/ppermute | solution.py:29
  126.0 3.5 %copy-start.5 = (bf16[32,2048]{1,0:T(8,128)(2,1)S(1)}, bf16[32,2048]{1,0:T(8,128)(2,1)}, u32[]{:S(2)}) copy-start(bf16[32,2048]{1,0:T(8,128)(2,1)} %get-tuple-element.14) | copy-start | bytes 393220
  129.5 27.6 %copy-start = (bf16[512,2048]{1,0:T(8,128)(2,1)S(1)}, bf16[512,2048]{1,0:T(8,128)(2,1)}, u32[]{:S(2)}) copy-start(bf16[512,2048]{1,0:T(8,128)(2,1)} %param.8) | copy-start | bytes 6291460
  129.6 11.7 %collective-permute-start.25 = (bf16[32,2048]{1,0:T(8,128)(2,1)S(1)}, bf16[32,2048]{1,0:T(8,128)(2,1)S(1)}, u32[]{:S(2)}, u32[]{:S(2)}) collective-permute-start(bf16[32,2048]{1,0:T(8,128)(2,1)S(1)} %copy-done.5), channel_id=1, source_target_pairs={{0,112},{16,0},{32,16},{48,32},{64,48},{80,64},{96,80},{112,96},{1... | collective-permute-start | bytes 393224 | tf_op jit(solution)/shard_map/ppermute | solution.py:29
  132.6 5.0 %collective-permute-start.32 = (bf16[32,2048]{1,0:T(8,128)(2,1)S(1)}, bf16[32,2048]{1,0:T(8,128)(2,1)S(1)}, u32[]{:S(2)}, u32[]{:S(2)}) collective-permute-start(bf16[32,2048]{1,0:T(8,128)(2,1)S(1)} %get-tuple-element.7), channel_id=1, source_target_pairs={{0,112},{16,0},{32,16},{48,32},{64,48},{80,64},{96,80},{112,96},{1... | collective-permute-start | bytes 393224 | tf_op jit(solution)/shard_map/ppermute | solution.py:29
  132.7 8.6 %collective-permute-start.29 = (bf16[32,2048]{1,0:T(8,128)(2,1)S(1)}, bf16[32,2048]{1,0:T(8,128)(2,1)S(1)}, u32[]{:S(2)}, u32[]{:S(2)}) collective-permute-start(bf16[32,2048]{1,0:T(8,128)(2,1)S(1)} %get-tuple-element.8), channel_id=1, source_target_pairs={{0,16},{16,32},{32,48},{48,64},{64,80},{80,96},{96,112},{112,0},{1... | collective-permute-start | bytes 393224 | tf_op jit(solution)/shard_map/ppermute | solution.py:29
  135.6 6.3 %collective-permute-start.23 = (bf16[32,2048]{1,0:T(8,128)(2,1)S(1)}, bf16[32,2048]{1,0:T(8,128)(2,1)S(1)}, u32[]{:S(2)}, u32[]{:S(2)}) collective-permute-start(bf16[32,2048]{1,0:T(8,128)(2,1)S(1)} %fusion.30), channel_id=1, source_target_pairs={{0,16},{16,32},{32,48},{48,64},{64,80},{80,96},{96,112},{112,0},{1... | collective-permute-start | bytes 393224 | tf_op jit(solution)/shard_map/ppermute | solution.py:29
  137.6 6.1 %collective-permute-start.33 = (bf16[32,2048]{1,0:T(8,128)(2,1)S(1)}, bf16[32,2048]{1,0:T(8,128)(2,1)S(1)}, u32[]{:S(2)}, u32[]{:S(2)}) collective-permute-start(bf16[32,2048]{1,0:T(8,128)(2,1)S(1)} %fusion.21), channel_id=1, source_target_pairs={{0,112},{16,0},{32,16},{48,32},{64,48},{80,64},{96,80},{112,96},{1... | collective-permute-start | bytes 393224 | tf_op jit(solution)/shard_map/ppermute | solution.py:29
  141.2 15.9 %collective-permute-start.18 = (bf16[512,256]{1,0:T(8,128)(2,1)S(1)}, bf16[512,256]{1,0:T(8,128)(2,1)S(1)}, u32[]{:S(2)}, u32[]{:S(2)}) collective-permute-start(bf16[512,256]{1,0:T(8,128)(2,1)S(1)} %bitcast.28), channel_id=1, source_target_pairs={{0,8},{8,0},{1,9},{9,1},{2,10},{10,2},{3,11},{11,3},{4,12},{12,4},... | collective-permute-start | bytes 786440 | tf_op jit(solution)/shard_map/ppermute | solution.py:25
  143.8 6.3 %collective-permute-start.26 = (bf16[32,2048]{1,0:T(8,128)(2,1)S(1)}, bf16[32,2048]{1,0:T(8,128)(2,1)S(1)}, u32[]{:S(2)}, u32[]{:S(2)}) collective-permute-start(bf16[32,2048]{1,0:T(8,128)(2,1)S(1)} %get-tuple-element.5), channel_id=1, source_target_pairs={{0,112},{16,0},{32,16},{48,32},{64,48},{80,64},{96,80},{112,96},{1... | collective-permute-start | bytes 393224 | tf_op jit(solution)/shard_map/ppermute | solution.py:29
  147.5 5.0 %collective-permute-start.34 = (bf16[32,2048]{1,0:T(8,128)(2,1)S(1)}, bf16[32,2048]{1,0:T(8,128)(2,1)S(1)}, u32[]{:S(2)}, u32[]{:S(2)}) collective-permute-start(bf16[32,2048]{1,0:T(8,128)(2,1)S(1)} %get-tuple-element.3), channel_id=1, source_target_pairs={{0,112},{16,0},{32,16},{48,32},{64,48},{80,64},{96,80},{112,96},{1... | collective-permute-start | bytes 393224 | tf_op jit(solution)/shard_map/ppermute | solution.py:29
  147.6 6.2 %collective-permute-start.30 = (bf16[32,2048]{1,0:T(8,128)(2,1)S(1)}, bf16[32,2048]{1,0:T(8,128)(2,1)S(1)}, u32[]{:S(2)}, u32[]{:S(2)}) collective-permute-start(bf16[32,2048]{1,0:T(8,128)(2,1)S(1)} %get-tuple-element.4), channel_id=1, source_target_pairs={{0,16},{16,32},{32,48},{48,64},{64,80},{80,96},{96,112},{112,0},{1... | collective-permute-start | bytes 393224 | tf_op jit(solution)/shard_map/ppermute | solution.py:29
  149.6 7.6 %collective-permute-start.17 = (bf16[512,256]{1,0:T(8,128)(2,1)S(1)}, bf16[512,256]{1,0:T(8,128)(2,1)S(1)}, u32[]{:S(2)}, u32[]{:S(2)}) collective-permute-start(bf16[512,256]{1,0:T(8,128)(2,1)S(1)} %bitcast.30), channel_id=1, source_target_pairs={{0,8},{8,0},{1,9},{9,1},{2,10},{10,2},{3,11},{11,3},{4,12},{12,4},... | collective-permute-start | bytes 786440 | tf_op jit(solution)/shard_map/ppermute | solution.py:25
  150.1 13.4 %collective-permute-start.24 = (bf16[32,2048]{1,0:T(8,128)(2,1)S(1)}, bf16[32,2048]{1,0:T(8,128)(2,1)S(1)}, u32[]{:S(2)}, u32[]{:S(2)}) collective-permute-start(bf16[32,2048]{1,0:T(8,128)(2,1)S(1)} %get-tuple-element.2), channel_id=1, source_target_pairs={{0,16},{16,32},{32,48},{48,64},{64,80},{80,96},{96,112},{112,0},{1... | collective-permute-start | bytes 393224 | tf_op jit(solution)/shard_map/ppermute | solution.py:29
  153.9 9.5 %collective-permute-start.35 = (bf16[32,2048]{1,0:T(8,128)(2,1)S(1)}, bf16[32,2048]{1,0:T(8,128)(2,1)S(1)}, u32[]{:S(2)}, u32[]{:S(2)}) collective-permute-start(bf16[32,2048]{1,0:T(8,128)(2,1)S(1)} %get-tuple-element.10), channel_id=1, source_target_pairs={{0,128},{128,0},{1,129},{129,1},{2,130},{130,2},{3,131},{131,3},{4... | collective-permute-start | bytes 393224 | tf_op jit(solution)/shard_map/ppermute | solution.py:25
  155.8 7.6 %collective-permute-start.27 = (bf16[32,2048]{1,0:T(8,128)(2,1)S(1)}, bf16[32,2048]{1,0:T(8,128)(2,1)S(1)}, u32[]{:S(2)}, u32[]{:S(2)}) collective-permute-start(bf16[32,2048]{1,0:T(8,128)(2,1)S(1)} %get-tuple-element.9), channel_id=1, source_target_pairs={{0,112},{16,0},{32,16},{48,32},{64,48},{80,64},{96,80},{112,96},{1... | collective-permute-start | bytes 393224 | tf_op jit(solution)/shard_map/ppermute | solution.py:29
  (3 other events, 2.3 us)

commit v3 on v0

v3 whole, which is shorter than its diff:
```python
import functools
import math

import jax
import jax.numpy as jnp
from jax import lax
from jax.experimental import pallas as pl
from jax.experimental.pallas import tpu as pltpu
from jax.sharding import Mesh, PartitionSpec as P

VOCAB = 16384
REP = ("x", "yhi")
FACTOR = 8.0 / math.sqrt(VOCAB)
BF16, F32 = jnp.bfloat16, jnp.float32
ORDER = [4, 3, -3, 2, -2, 1, -1, 0]
KEYS = [(s, d) for d in ORDER for s in (0, 1)]
VMEM = pl.BlockSpec(memory_space=pltpu.VMEM)
ANY = pl.BlockSpec(memory_space=pl.ANY)
PARAMS = pltpu.CompilerParams(vmem_limit_bytes=16 * 1024 * 1024)


def shape(dims, dtype):
    return jax.ShapeDtypeStruct(dims, dtype)


def saturate(act):
    wide = jnp.maximum(act.astype(F32), 0.0)
    small = wide - 0.5 * wide * wide
    return jnp.where(wide < 2.0**-8, small, jnp.log(1.0 + wide)).astype(BF16)


def slope(act):
    wide = act.astype(F32)
    return jnp.where(wide > 0.0, 1.0 / (1.0 + jnp.maximum(wide, 0.0)), 0.0)


def swap(value, axis):
    return lax.ppermute(value, axis, [(0, 1), (1, 0)])


def shift(value, step):
    return lax.ppermute(value, "z", [(i, (i + step) % 8) for i in range(8)])


def exchange(value):
    return lax.all_to_all(value, REP, split_axis=0, concat_axis=0)


def after(value, *others):
    return lax.optimization_barrier((value, *others))[0]


def score_kernel(mine_ref, other_ref, *refs):
    blocks, out_ref, joined_ref = refs[:16], refs[-2], refs[-1]
    for i in range(16):
        joined_ref[i * 32 : i * 32 + 32, :] = blocks[i][...]
    for i, ref in enumerate((mine_ref, other_ref)):
        for k in range(2):
            part = lax.dot_general(
                joined_ref[...],
                ref[k * 256 : k * 256 + 256, :],
                (((1,), (1,)), ((), ())),
                preferred_element_type=F32,
            )
            most, least = jnp.max(part, axis=0, keepdims=True), jnp.min(part, axis=0, keepdims=True)
            halves = jnp.round(most + least)
            centre = halves * 0.5
            reach = jnp.maximum(most - centre, centre - least)
            step = jnp.maximum(jnp.ceil(reach * (2.0**17 / 32767)), 1.0)
            code = jnp.round((part - centre) * (2.0**17 / step))
            row = lax.broadcasted_iota(jnp.int32, (16, 256), 0)
            extra = jnp.where(row == 0, halves, jnp.where(row == 1, step, 0.0))
            for n in range(2):
                columns = slice(n * 128, n * 128 + 128)
                at = i * 4 + k * 2 + n
                out_ref[at, :512, :] = code[:, columns].astype(jnp.int32).astype(jnp.int16)
                out_ref[at, 512:, :] = extra[:, columns].astype(jnp.int32).astype(jnp.int16)


def partial_scores(mine, other, blocks):
    return pl.pallas_call(
        score_kernel,
        out_shape=(shape((8, 528, 128), jnp.int16), shape((512, 2048), BF16)),
        in_specs=[VMEM] * 18,
        out_specs=(VMEM, VMEM),
        compiler_params=PARAMS,
    )(mine, other, *blocks)


def grad_kernel(pieces_ref, norm_ref, other_norm_ref, at_ref, other_at_ref, out_ref):
    core, y, z = lax.axis_index("core"), lax.axis_index("ylo"), lax.axis_index("z")
    rep = lax.axis_index("x") * 2 + lax.axis_index("yhi")
    norm = jnp.where(rep < 4, norm_ref[...], other_norm_ref[...])
    positive = jnp.where(rep < 4, at_ref[...], other_at_ref[...])
    turn = lax.broadcasted_iota(jnp.int32, (4, 128), 0) == lax.rem(rep, 4)
    norm = jnp.sum(jnp.where(turn, norm, 0.0), axis=0, keepdims=True)
    positive = jnp.sum(jnp.where(turn, positive, 0), axis=0, keepdims=True)
    scores = 0.0
    for k in range(8):
        extra = pieces_ref[k, 512:, :].astype(jnp.int32).astype(F32)
        code = pieces_ref[k, :512, :].astype(jnp.int32).astype(F32)
        scores = scores + (code * (extra[1:2] * 2.0**-17) + extra[0:1] * 0.5)
    place = lax.broadcasted_iota(jnp.int32, (512, 128), 0)
    turn = place >> 6
    ahead = jnp.where((turn & 1) == 0, 4 + (turn >> 1), (7 - turn) >> 1)
    ident = ((y + (place >> 5)) & 1) * 512 + ((z + ahead) & 7) * 64 + core * 32 + (place & 31)
    onehot = (positive == ident).astype(F32)
    grad = (jnp.exp(scores * FACTOR - norm) - onehot) * (8.0 * FACTOR)
    grad = grad.astype(BF16)
    for k in range(8):
        out_ref[k] = grad


def score_grad(pieces, *rows):
    return pl.pallas_call(
        grad_kernel,
        out_shape=shape((8, 512, 128), BF16),
        in_specs=[VMEM] * 5,
        out_specs=VMEM,
        compiler_params=PARAMS,
    )(pieces, *rows)


def sum_kernel(at, grad_ref, mine_ref, other_ref, *refs):
    left = jnp.concatenate([grad_ref[k, at : at + 256, :] for k in range(8)], axis=1)
    for j in range(4):
        columns = slice(j * 512, j * 512 + 512)
        total = jnp.dot(left[:, :512], mine_ref[:, columns], preferred_element_type=F32)
        total += jnp.dot(left[:, 512:], other_ref[:, columns], preferred_element_type=F32)
        refs[-1][:, :, columns] = total.reshape(8, 32, 512)


def passage_sums(grad, mine, other, at, first):
    out = pl.pallas_call(
        functools.partial(sum_kernel, at),
        out_shape=shape((8, 32, 2048), F32),
        in_specs=[VMEM] * 3 + [ANY] * len(first),
        out_specs=VMEM,
        compiler_params=PARAMS,
    )(grad, mine, other, *first)
    return {k: out[i] for i, k in enumerate(KEYS[at // 32 : at // 32 + 8])}


def query_kernel(act_ref, own_grad_ref, other_grad_ref, own_ref, other_ref, out_ref, turned_ref):
    @pl.when(pl.program_id(0) == 0)
    def _():
        for i, g in enumerate((own_grad_ref, other_grad_ref)):
            for k in range(4):
                turned_ref[k * 128 : k * 128 + 128, i * 512 : i * 512 + 512] = g[k].T

    total = jnp.dot(turned_ref[:, :512], own_ref[...], preferred_element_type=F32)
    total += jnp.dot(turned_ref[:, 512:], other_ref[...], preferred_element_type=F32)
    wide = act_ref[...].astype(F32)
    below = 1.0 + jnp.maximum(wide, 0.0)
    guess = pl.reciprocal(below, approx=True)
    inverse = guess * (2.0 - below * guess)
    out_ref[...] = jnp.where(wide > 0.0, total * inverse, 0.0).astype(BF16)


def query_grads(act, grad, other_grad, own, other):
    column = pl.BlockSpec((512, 512), lambda j: (0, j))
    half = pl.BlockSpec((4, 512, 128), lambda j: (0, 0, 0))
    return pl.pallas_call(
        query_kernel,
        out_shape=shape((512, 2048), BF16),
        grid=(4,),
        in_specs=[column, half, half, column, column],
        out_specs=column,
        scratch_shapes=[pltpu.VMEM((512, 1024), BF16)],
        compiler_params=PARAMS,
    )(act, grad, other_grad, own, other)


def shards(query_act, passage_act, positive, normalizer):
    own = saturate(passage_act)
    blocks = {(0, 0): own, (1, 0): swap(own, "ylo")}
    for d in range(1, 4):
        for s in (0, 1):
            blocks[s, -d] = shift(blocks[s, 1 - d], 1)
            blocks[s, d] = shift(blocks[s, d - 1], -1)
    blocks[0, 4] = shift(blocks[0, -3], 1)
    blocks[1, 4] = shift(blocks[1, 3], -1)

    mine = saturate(query_act)
    other = swap(mine, "core")
    norm, other_norm = normalizer.reshape(4, 128), swap(normalizer, "core").reshape(4, 128)
    at, other_at = positive.reshape(4, 128), swap(positive, "core").reshape(4, 128)
    other, norm, other_norm, at, other_at = lax.optimization_barrier((other, norm, other_norm, at, other_at))

    part, joined = partial_scores(mine, other, [blocks[k] for k in KEYS])
    grad = exchange(score_grad(exchange(part), norm, other_norm, at, other_at))

    joined = after(joined, grad)
    query_grad = query_grads(query_act, grad, swap(grad[4:], "core"), joined, swap(joined, "core"))

    terms = passage_sums(grad, mine, other, 0, [])
    terms.update(passage_sums(grad, mine, other, 256, []))
    both = {d: jnp.concatenate([terms[0, d], terms[1, d]], axis=0) for d in ORDER}
    pad = jnp.zeros((32, 2048), F32)
    up = jnp.concatenate([shift(terms[0, 4].astype(BF16), 1).astype(F32), pad], axis=0)
    down = jnp.concatenate([pad, shift(terms[1, 4].astype(BF16), -1).astype(F32)], axis=0)
    for d in (3, 2, 1):
        up = shift((both[d] + up).astype(BF16), 1).astype(F32)
        down = shift((both[-d] + down).astype(BF16), -1).astype(F32)
    total = both[0] + up + down
    theirs = swap(total[32:].astype(BF16), "ylo").astype(F32)
    total = after(total[:32], query_grad) + theirs
    passage_grad = (total * slope(passage_act)).astype(BF16)
    return (query_grad, passage_grad)


def solution(mesh):
    split = Mesh(mesh.devices.reshape(2, 8, 2, 2, 4), ("ylo", "z", "core", "yhi", "x"))
    rows, columns = ("ylo", "z", "core"), ("yhi", "x")
    return jax.shard_map(
        shards,
        mesh=split,
        in_specs=(P(rows, columns), P(rows, columns), P(rows), P(rows)),
        out_specs=(P(rows, columns), P(rows, columns)),
        check_vma=False,
    )
```

time: 329 us -> 127 us (0.39)
  waiting for transfers between devices: 288 us -> 36.4 us
  starting transfers between devices: 0.12 us -> 37.4 us
  blocking collectives: 0 us -> 36.6 us
  matrix products: 22.4 us -> 0 us
  between operations: 13.8 us -> 0.9 us
  Pallas kernels: 0 us -> 11.2 us
    reduce_scatter x1 -> x0, waiting for transfers between devices: 121 us -> none  [shards(): lax.psum_scatter(lax.dot_general(score_grad, query_rep, contract_first, p...]
    psum x1 -> x0, waiting for transfers between devices: 96.8 us -> none  [shards(): scores = lax.psum(partial_value, 'rep') * factor]
    all_gather x1 -> x0, waiting for transfers between devices: 70.6 us -> none  [shards(): all_passages = lax.all_gather(passage_rep, 'blk', axis=0, tiled=True)]
    ppermute x0 -> x29, starting transfers between devices: none -> 37.4 us  [the longest x22 32.9 us: shift(): return lax.ppermute(value, 'z', [(i, (i + step) % 8) for i in range(8)])]
    all_to_all x0 -> x2, blocking collectives: none -> 36.6 us  [exchange(): return lax.all_to_all(value, REP, split_axis=0, concat_axis=0)]
    ppermute x0 -> x29, waiting for transfers between devices: none -> 36.4 us  [the longest x22 31.7 us: shift(): return lax.ppermute(value, 'z', [(i, (i + step) % 8) for i in range(8)])]
    dot_general x3 -> x0, matrix products: 22.4 us -> none  [the longest x1 7.93 us: shards(): lax.dot_general(score_grad, query_rep, contract_first, preferred_element_...]
    pallas_call x0 -> x5, Pallas kernels: none -> 11.2 us  [the longest x1 5.31 us: query_grads(): pl.pallas_call(query_kernel, out_shape=shape((512, 2048), BF16), grid=(4,...]
  transfers between devices with their start and end apart: 3 -> 29, of which waited for: 3 -> 15; matrix products, arithmetic and copies ran while one was open for 2% -> 1% of each run, Pallas kernels for 0% -> 5%
where the time goes in v3:
time: 127 us
  starting transfers between devices  37.4 us (29%)
  blocking collectives  36.6 us (29%)
  waiting for transfers between devices  36.4 us (29%)
  Pallas kernels  11.2 us (9%)
  other arithmetic  4.4 us (3%)
    all_to_all x2, blocking collectives, exchange(): return lax.all_to_all(value, REP, split_axis=0, concat_axis=0)  36.6 us
    ppermute x22, starting transfers between devices, shift(): return lax.ppermute(value, 'z', [(i, (i + step) % 8) for i in range(8)])  32.9 us
    ppermute x22, waiting for transfers between devices, shift(): return lax.ppermute(value, 'z', [(i, (i + step) % 8) for i in range(8)])  31.7 us
    pallas_call x1, Pallas kernels, query_grads(): pl.pallas_call(query_kernel, out_shape=shape((512, 2048), BF16), grid=(4,...  5.31 us
    ppermute x7, waiting for transfers between devices, swap(): return lax.ppermute(value, axis, [(0, 1), (1, 0)])  4.62 us
    ppermute x7, starting transfers between devices, swap(): return lax.ppermute(value, axis, [(0, 1), (1, 0)])  4.49 us
    convert_element_type x2, other arithmetic, saturate(): jnp.where(wide < 2.0 ** (-8), small, jnp.log(1.0 + wide)).astype(BF16)  3.17 us
    pallas_call x1, Pallas kernels, partial_scores(): pl.pallas_call(score_kernel, out_shape=(shape((8, 528, 128), jnp.int16),...  2.83 us
  transfers between devices with their start and end apart: 29, of which 15 were waited for; matrix products, arithmetic and copies ran while one was open for 1% of the time, Pallas kernels for 5%

profile of v3, /device:TPU:8, one launch (start us, length us, event | category | flops | bytes accessed | tf_op | source)
XLA Modules:
  0.0 127.2 jit_solution(10988911991884904106)
XLA Ops:
  0.7 3.1 %fusion.1.mine_ref = bf16[512,2048]{1,0:T(8,128)(2,1)S(1)} fusion(bf16[512,2048]{1,0:T(8,128)(2,1)} %act_ref.1), kind=kLoop, calls=%fused_computation.2 | loop fusion | flops 9437184 | bytes 4194304 | tf_op jit(solution)/shard_map/convert_element_type | solution.py:29
  3.7 0.1 collective-permute-start
  3.8 0.1 fusion.15.refs_14_
  4.0 2.3 %collective-permute-start.7 = (bf16[32,2048]{1,0:T(8,128)(2,1)S(1)}, bf16[32,2048]{1,0:T(8,128)(2,1)S(1)}, u32[]{:S(2)}, u32[]{:S(2)}) collective-permute-start(bf16[32,2048]{1,0:T(8,128)(2,1)S(1)} %fusion.15.refs_14_), channel_id=1, source_target_pairs={{0,128},{128,0},{1,129},{129,1},{2,130},{130,2},{3,131},{131,3},{4... | collective-permute-start | bytes 393224 | tf_op jit(solution)/shard_map/ppermute | solution.py:38
  6.2 0.2 collective-permute-start.3
  6.4 4.0 %collective-permute-done.7.refs_15_ = bf16[32,2048]{1,0:T(8,128)(2,1)S(1)} collective-permute-done((bf16[32,2048]{1,0:T(8,128)(2,1)S(1)}, bf16[32,2048]{1,0:T(8,128)(2,1)S(1)}, u32[]{:S(2)}, u32[]{:S(2)}) %collective-permute-start.7) | collective-permute-done | bytes 131104 | tf_op jit(solution)/shard_map/ppermute | solution.py:38
  10.4 5.4 %collective-permute-start.8 = (bf16[32,2048]{1,0:T(8,128)(2,1)S(1)}, bf16[32,2048]{1,0:T(8,128)(2,1)S(1)}, u32[]{:S(2)}, u32[]{:S(2)}) collective-permute-start(bf16[32,2048]{1,0:T(8,128)(2,1)S(1)} %collective-permute-done.7.refs_15_), channel_id=1, source_target_pairs={{0,112},{16,0},{32,16},{48,32},{64,48},{80,64},{96,80},{112,96},{1... | collective-permute-start | bytes 393224 | tf_op jit(solution)/shard_map/ppermute | solution.py:42
  15.8 0.5 collective-permute-start.1
  16.3 0.6 collective-permute-done.2
  16.9 1.0 collective-permute-start.12
  18.0 1.0 collective-permute-start.15
  19.1 3.2 %collective-permute-start.9 = (bf16[32,2048]{1,0:T(8,128)(2,1)S(1)}, bf16[32,2048]{1,0:T(8,128)(2,1)S(1)}, u32[]{:S(2)}, u32[]{:S(2)}) collective-permute-start(bf16[32,2048]{1,0:T(8,128)(2,1)S(1)} %collective-permute-done.8.refs_11_), channel_id=1, source_target_pairs={{0,112},{16,0},{32,16},{48,32},{64,48},{80,64},{96,80},{112,96},{1... | collective-permute-start | bytes 393224 | tf_op jit(solution)/shard_map/ppermute | solution.py:42
  22.2 1.1 collective-permute-done.12.refs_10_
  23.3 1.6 %collective-permute-start.13 = (bf16[32,2048]{1,0:T(8,128)(2,1)S(1)}, bf16[32,2048]{1,0:T(8,128)(2,1)S(1)}, u32[]{:S(2)}, u32[]{:S(2)}) collective-permute-start(bf16[32,2048]{1,0:T(8,128)(2,1)S(1)} %collective-permute-done.12.refs_10_), channel_id=1, source_target_pairs={{0,112},{16,0},{32,16},{48,32},{64,48},{80,64},{96,80},{112,96},{1... | collective-permute-start | bytes 393224 | tf_op jit(solution)/shard_map/ppermute | solution.py:42
  24.9 0.6 collective-permute-done.15.refs_13_
  25.6 1.7 %collective-permute-done.4.refs_8_ = bf16[32,2048]{1,0:T(8,128)(2,1)S(1)} collective-permute-done((bf16[32,2048]{1,0:T(8,128)(2,1)S(1)}, bf16[32,2048]{1,0:T(8,128)(2,1)S(1)}, u32[]{:S(2)}, u32[]{:S(2)}) %collective-permute-start.4) | collective-permute-done | bytes 131104 | tf_op jit(solution)/shard_map/ppermute | solution.py:42
  27.3 3.2 %collective-permute-start.10 = (bf16[32,2048]{1,0:T(8,128)(2,1)S(1)}, bf16[32,2048]{1,0:T(8,128)(2,1)S(1)}, u32[]{:S(2)}, u32[]{:S(2)}) collective-permute-start(bf16[32,2048]{1,0:T(8,128)(2,1)S(1)} %collective-permute-done.9.refs_7_), channel_id=1, source_target_pairs={{0,112},{16,0},{32,16},{48,32},{64,48},{80,64},{96,80},{112,96},{1... | collective-permute-start | bytes 393224 | tf_op jit(solution)/shard_map/ppermute | solution.py:42
  30.5 0.7 collective-permute-start.14
  31.2 1.7 %collective-permute-done.16.refs_9_ = bf16[32,2048]{1,0:T(8,128)(2,1)S(1)} collective-permute-done((bf16[32,2048]{1,0:T(8,128)(2,1)S(1)}, bf16[32,2048]{1,0:T(8,128)(2,1)S(1)}, u32[]{:S(2)}, u32[]{:S(2)}) %collective-permute-start.16) | collective-permute-done | bytes 131104 | tf_op jit(solution)/shard_map/ppermute | solution.py:42
  32.9 2.1 %collective-permute-done.5.refs_4_ = bf16[32,2048]{1,0:T(8,128)(2,1)S(1)} collective-permute-done((bf16[32,2048]{1,0:T(8,128)(2,1)S(1)}, bf16[32,2048]{1,0:T(8,128)(2,1)S(1)}, u32[]{:S(2)}, u32[]{:S(2)}) %collective-permute-start.5) | collective-permute-done | bytes 131104 | tf_op jit(solution)/shard_map/ppermute | solution.py:42
  35.1 3.2 %collective-permute-start.11 = (bf16[32,2048]{1,0:T(8,128)(2,1)S(1)}, bf16[32,2048]{1,0:T(8,128)(2,1)S(1)}, u32[]{:S(2)}, u32[]{:S(2)}) collective-permute-start(bf16[32,2048]{1,0:T(8,128)(2,1)S(1)} %collective-permute-done.10.refs_3_), channel_id=1, source_target_pairs={{0,112},{16,0},{32,16},{48,32},{64,48},{80,64},{96,80},{112,96},{1... | collective-permute-start | bytes 393224 | tf_op jit(solution)/shard_map/ppermute | solution.py:42
  38.3 1.1 collective-permute-done.17.refs_5_
  39.4 1.8 %collective-permute-done.6.refs_0_ = bf16[32,2048]{1,0:T(8,128)(2,1)S(1)} collective-permute-done((bf16[32,2048]{1,0:T(8,128)(2,1)S(1)}, bf16[32,2048]{1,0:T(8,128)(2,1)S(1)}, u32[]{:S(2)}, u32[]{:S(2)}) %collective-permute-start.6) | collective-permute-done | bytes 131104 | tf_op jit(solution)/shard_map/ppermute | solution.py:42
  41.2 2.8 %shard_map.59 = (s16[8,528,128]{2,1,0:T(8,128)(2,1)S(1)}, bf16[512,2048]{1,0:T(8,128)(2,1)S(1)}) custom-call(bf16[512,2048]{1,0:T(8,128)(2,1)S(1)} %fusion.1.mine_ref, bf16[512,2048]{1,0:T(8,128)(2,1)S(1)} %collective-permute-done.other_ref, bf16[32,2048]{1,0:T(8,128)(2,1)S(1)} %collective-permute-done.6.refs_0_, ...), custom_call_target="tpu_custom_call" | custom-call | tf_op jit(solution)/shard_map/pallas_call | solution.py:81
  44.1 20.9 %all_to_all.10.pieces_ref = s16[8,528,128]{2,1,0:T(8,128)(2,1)S(1)} all-to-all(s16[8,528,128]{2,1,0:T(8,128)(2,1)S(1)} %get-tuple-element.12), channel_id=1, replica_groups=mesh['ylo'=2,'z'=8,'core'=2,'yhi'=2,'x'=4] {'x','yhi'}, dimensions={0} | all-to-all | bytes 2162688 | tf_op jit(solution)/shard_map/all_to_all | solution.py:46
  65.0 0.6 shard_map.60
  65.6 15.7 %all_to_all.11.own_grad_ref.grad_ref = bf16[8,512,128]{2,1,0:T(8,128)(2,1)S(1)} all-to-all(bf16[8,512,128]{2,1,0:T(8,128)(2,1)S(1)} %shard_map.60), channel_id=1, replica_groups=mesh['ylo'=2,'z'=8,'core'=2,'yhi'=2,'x'=4] {'x','yhi'}, dimensions={0} | all-to-all | bytes 2097152 | tf_op jit(solution)/shard_map/all_to_all | solution.py:46
  81.3 1.2 shard_map.63
  82.5 0.1 convert.11
  82.7 1.8 %collective-permute-start.24 = (bf16[32,2048]{1,0:T(8,128)(2,1)S(1)}, bf16[32,2048]{1,0:T(8,128)(2,1)S(1)}, u32[]{:S(2)}, u32[]{:S(2)}) collective-permute-start(bf16[32,2048]{1,0:T(8,128)(2,1)S(1)} %get-tuple-element.35), channel_id=1, source_target_pairs={{0,112},{16,0},{32,16},{48,32},{64,48},{80,64},{96,80},{112,96},{1... | collective-permute-start | bytes 393224 | tf_op jit(solution)/shard_map/ppermute | solution.py:42
  84.5 0.1 slice_bitcast_fusion.7
  84.6 0.4 collective-permute-start.20
  85.0 1.2 shard_map.62
  86.2 2.1 %collective-permute-done.24 = bf16[32,2048]{1,0:T(8,128)(2,1)S(1)} collective-permute-done((bf16[32,2048]{1,0:T(8,128)(2,1)S(1)}, bf16[32,2048]{1,0:T(8,128)(2,1)S(1)}, u32[]{:S(2)}, u32[]{:S(2)}) %collective-permute-start.24) | collective-permute-done | bytes 131104 | tf_op jit(solution)/shard_map/ppermute | solution.py:42
  88.4 3.0 %collective-permute-start.25 = (bf16[64,2048]{1,0:T(8,128)(2,1)S(1)}, bf16[64,2048]{1,0:T(8,128)(2,1)S(1)}, u32[]{:S(2)}, u32[]{:S(2)}) collective-permute-start(bf16[64,2048]{1,0:T(8,128)(2,1)S(1)} %fusion.9), channel_id=1, source_target_pairs={{0,112},{16,0},{32,16},{48,32},{64,48},{80,64},{96,80},{112,96},{1... | collective-permute-start | bytes 786440 | tf_op jit(solution)/shard_map/ppermute | solution.py:42
  91.4 0.1 slice_bitcast_fusion.11
  91.6 0.1 collective-permute-start.19
  91.8 3.5 %collective-permute-done.25 = bf16[64,2048]{1,0:T(8,128)(2,1)S(1)} collective-permute-done((bf16[64,2048]{1,0:T(8,128)(2,1)S(1)}, bf16[64,2048]{1,0:T(8,128)(2,1)S(1)}, u32[]{:S(2)}, u32[]{:S(2)}) %collective-permute-start.25) | collective-permute-done | bytes 262176 | tf_op jit(solution)/shard_map/ppermute | solution.py:42
  95.4 3.8 %collective-permute-start.26 = (bf16[64,2048]{1,0:T(8,128)(2,1)S(1)}, bf16[64,2048]{1,0:T(8,128)(2,1)S(1)}, u32[]{:S(2)}, u32[]{:S(2)}) collective-permute-start(bf16[64,2048]{1,0:T(8,128)(2,1)S(1)} %fusion.8), channel_id=1, source_target_pairs={{0,112},{16,0},{32,16},{48,32},{64,48},{80,64},{96,80},{112,96},{1... | collective-permute-start | bytes 786440 | tf_op jit(solution)/shard_map/ppermute | solution.py:42
  99.1 2.6 %collective-permute-done.21 = bf16[64,2048]{1,0:T(8,128)(2,1)S(1)} collective-permute-done((bf16[64,2048]{1,0:T(8,128)(2,1)S(1)}, bf16[64,2048]{1,0:T(8,128)(2,1)S(1)}, u32[]{:S(2)}, u32[]{:S(2)}) %collective-permute-start.21) | collective-permute-done | bytes 262176 | tf_op jit(solution)/shard_map/ppermute | solution.py:42
  101.8 0.3 collective-permute-start.22
  102.1 0.9 collective-permute-done.26
  103.1 3.8 %collective-permute-start.27 = (bf16[64,2048]{1,0:T(8,128)(2,1)S(1)}, bf16[64,2048]{1,0:T(8,128)(2,1)S(1)}, u32[]{:S(2)}, u32[]{:S(2)}) collective-permute-start(bf16[64,2048]{1,0:T(8,128)(2,1)S(1)} %fusion.7), channel_id=1, source_target_pairs={{0,112},{16,0},{32,16},{48,32},{64,48},{80,64},{96,80},{112,96},{1... | collective-permute-start | bytes 786440 | tf_op jit(solution)/shard_map/ppermute | solution.py:42
  106.8 4.4 %collective-permute-done.22 = bf16[64,2048]{1,0:T(8,128)(2,1)S(1)} collective-permute-done((bf16[64,2048]{1,0:T(8,128)(2,1)S(1)}, bf16[64,2048]{1,0:T(8,128)(2,1)S(1)}, u32[]{:S(2)}, u32[]{:S(2)}) %collective-permute-start.22) | collective-permute-done | bytes 262176 | tf_op jit(solution)/shard_map/ppermute | solution.py:42
  111.5 8.1 %collective-permute-done.23 = bf16[64,2048]{1,0:T(8,128)(2,1)S(1)} collective-permute-done((bf16[64,2048]{1,0:T(8,128)(2,1)S(1)}, bf16[64,2048]{1,0:T(8,128)(2,1)S(1)}, u32[]{:S(2)}, u32[]{:S(2)}) %collective-permute-start.23) | collective-permute-done | bytes 262176 | tf_op jit(solution)/shard_map/ppermute | solution.py:42
  119.7 1.4 %collective-permute-start.28 = (bf16[32,2048]{1,0:T(8,128)(2,1)S(1)}, bf16[32,2048]{1,0:T(8,128)(2,1)S(1)}, u32[]{:S(2)}, u32[]{:S(2)}) collective-permute-start(bf16[32,2048]{1,0:T(8,128)(2,1)S(1)} %slice.115), channel_id=1, source_target_pairs={{0,128},{128,0},{1,129},{129,1},{2,130},{130,2},{3,131},{131,3},{4... | collective-permute-start | bytes 393224 | tf_op jit(solution)/shard_map/ppermute | solution.py:38
  121.1 5.3 %shard_map.61 = bf16[512,2048]{1,0:T(8,128)(2,1)} custom-call(bf16[512,2048]{1,0:T(8,128)(2,1)S(1)} %copy-done, bf16[8,512,128]{2,1,0:T(8,128)(2,1)S(1)} %all_to_all.11.own_grad_ref.grad_ref, bf16[4,512,128]{2,1,0:T(8,128)(2,1)S(1)} %collective-permute-done.18.other_grad_ref, bf16[512,2048]{1,0:T(8,128)(2,1)S(1)} %get-tuple-element.18.own_ref, ...), custom_call_target="tpu_custom_call" | custom-call | tf_op jit(solution)/shard_map/pallas_call | solution.py:163
  126.5 0.7 fusion.18
  (42 shorter events, 0.8 us)
Async XLA Ops:
  0.6 3.2 %copy-start.3 = (bf16[32,2048]{1,0:T(8,128)(2,1)S(1)}, bf16[32,2048]{1,0:T(8,128)(2,1)}, u32[]{:S(2)}) copy-start(bf16[32,2048]{1,0:T(8,128)(2,1)} %param.5) | copy-start | bytes 393220
  0.6 15.1 %copy-start.2 = (s32[512]{0:T(512)S(1)}, s32[512]{0:T(512)}, u32[]{:S(2)}) copy-start(s32[512]{0:T(512)} %param.6) | copy-start | bytes 6148
  0.7 15.1 %copy-start.1 = (f32[512]{0:T(512)S(1)}, f32[512]{0:T(512)}, u32[]{:S(2)}) copy-start(f32[512]{0:T(512)} %param.7) | copy-start | bytes 6148
  3.7 34.6 %collective-permute-start = (bf16[512,2048]{1,0:T(8,128)(2,1)S(1)}, bf16[512,2048]{1,0:T(8,128)(2,1)S(1)}, u32[]{:S(2)}, u32[]{:S(2)}) collective-permute-start(bf16[512,2048]{1,0:T(8,128)(2,1)S(1)} %fusion.1.mine_ref), channel_id=1, source_target_pairs={{0,8},{8,0},{1,9},{9,1},{2,10},{10,2},{3,11},{11,3},{4,12},{12,4},... | collective-permute-start | bytes 6291464 | tf_op jit(solution)/shard_map/ppermute | solution.py:38
  4.0 6.4 %collective-permute-start.7 = (bf16[32,2048]{1,0:T(8,128)(2,1)S(1)}, bf16[32,2048]{1,0:T(8,128)(2,1)S(1)}, u32[]{:S(2)}, u32[]{:S(2)}) collective-permute-start(bf16[32,2048]{1,0:T(8,128)(2,1)S(1)} %fusion.15.refs_14_), channel_id=1, source_target_pairs={{0,128},{128,0},{1,129},{129,1},{2,130},{130,2},{3,131},{131,3},{4... | collective-permute-start | bytes 393224 | tf_op jit(solution)/shard_map/ppermute | solution.py:38
  6.2 12.8 %collective-permute-start.3 = (bf16[32,2048]{1,0:T(8,128)(2,1)S(1)}, bf16[32,2048]{1,0:T(8,128)(2,1)S(1)}, u32[]{:S(2)}, u32[]{:S(2)}) collective-permute-start(bf16[32,2048]{1,0:T(8,128)(2,1)S(1)} %fusion.15.refs_14_), channel_id=1, source_target_pairs={{0,16},{16,32},{32,48},{48,64},{64,80},{80,96},{96,112},{112,0},{1... | collective-permute-start | bytes 393224 | tf_op jit(solution)/shard_map/ppermute | solution.py:42
  10.4 8.7 %collective-permute-start.8 = (bf16[32,2048]{1,0:T(8,128)(2,1)S(1)}, bf16[32,2048]{1,0:T(8,128)(2,1)S(1)}, u32[]{:S(2)}, u32[]{:S(2)}) collective-permute-start(bf16[32,2048]{1,0:T(8,128)(2,1)S(1)} %collective-permute-done.7.refs_15_), channel_id=1, source_target_pairs={{0,112},{16,0},{32,16},{48,32},{64,48},{80,64},{96,80},{112,96},{1... | collective-permute-start | bytes 393224 | tf_op jit(solution)/shard_map/ppermute | solution.py:42
  15.8 1.2 collective-permute-start.2
  15.8 2.2 %collective-permute-start.1 = (f32[512]{0:T(512)S(1)}, f32[512]{0:T(512)S(1)}, u32[]{:S(2)}, u32[]{:S(2)}) collective-permute-start(f32[512]{0:T(512)S(1)} %copy-done.1), channel_id=1, source_target_pairs={{0,8},{8,0},{1,9},{9,1},{2,10},{10,2},{3,11},{11,3},{4,12},{12,4},... | collective-permute-start | bytes 6152 | tf_op jit(solution)/shard_map/ppermute | solution.py:38
  16.9 6.3 %collective-permute-start.12 = (bf16[32,2048]{1,0:T(8,128)(2,1)S(1)}, bf16[32,2048]{1,0:T(8,128)(2,1)S(1)}, u32[]{:S(2)}, u32[]{:S(2)}) collective-permute-start(bf16[32,2048]{1,0:T(8,128)(2,1)S(1)} %fusion.15.refs_14_), channel_id=1, source_target_pairs={{0,112},{16,0},{32,16},{48,32},{64,48},{80,64},{96,80},{112,96},{1... | collective-permute-start | bytes 393224 | tf_op jit(solution)/shard_map/ppermute | solution.py:42
  18.0 7.6 %collective-permute-start.15 = (bf16[32,2048]{1,0:T(8,128)(2,1)S(1)}, bf16[32,2048]{1,0:T(8,128)(2,1)S(1)}, u32[]{:S(2)}, u32[]{:S(2)}) collective-permute-start(bf16[32,2048]{1,0:T(8,128)(2,1)S(1)} %collective-permute-done.7.refs_15_), channel_id=1, source_target_pairs={{0,16},{16,32},{32,48},{48,64},{64,80},{80,96},{96,112},{112,0},{1... | collective-permute-start | bytes 393224 | tf_op jit(solution)/shard_map/ppermute | solution.py:42
  19.0 8.3 %collective-permute-start.4 = (bf16[32,2048]{1,0:T(8,128)(2,1)S(1)}, bf16[32,2048]{1,0:T(8,128)(2,1)S(1)}, u32[]{:S(2)}, u32[]{:S(2)}) collective-permute-start(bf16[32,2048]{1,0:T(8,128)(2,1)S(1)} %collective-permute-done.3.refs_12_), channel_id=1, source_target_pairs={{0,16},{16,32},{32,48},{48,64},{64,80},{80,96},{96,112},{112,0},{1... | collective-permute-start | bytes 393224 | tf_op jit(solution)/shard_map/ppermute | solution.py:42
  19.1 8.2 %collective-permute-start.9 = (bf16[32,2048]{1,0:T(8,128)(2,1)S(1)}, bf16[32,2048]{1,0:T(8,128)(2,1)S(1)}, u32[]{:S(2)}, u32[]{:S(2)}) collective-permute-start(bf16[32,2048]{1,0:T(8,128)(2,1)S(1)} %collective-permute-done.8.refs_11_), channel_id=1, source_target_pairs={{0,112},{16,0},{32,16},{48,32},{64,48},{80,64},{96,80},{112,96},{1... | collective-permute-start | bytes 393224 | tf_op jit(solution)/shard_map/ppermute | solution.py:42
  23.3 7.2 %collective-permute-start.13 = (bf16[32,2048]{1,0:T(8,128)(2,1)S(1)}, bf16[32,2048]{1,0:T(8,128)(2,1)S(1)}, u32[]{:S(2)}, u32[]{:S(2)}) collective-permute-start(bf16[32,2048]{1,0:T(8,128)(2,1)S(1)} %collective-permute-done.12.refs_10_), channel_id=1, source_target_pairs={{0,112},{16,0},{32,16},{48,32},{64,48},{80,64},{96,80},{112,96},{1... | collective-permute-start | bytes 393224 | tf_op jit(solution)/shard_map/ppermute | solution.py:42
  25.5 7.4 %collective-permute-start.16 = (bf16[32,2048]{1,0:T(8,128)(2,1)S(1)}, bf16[32,2048]{1,0:T(8,128)(2,1)S(1)}, u32[]{:S(2)}, u32[]{:S(2)}) collective-permute-start(bf16[32,2048]{1,0:T(8,128)(2,1)S(1)} %collective-permute-done.15.refs_13_), channel_id=1, source_target_pairs={{0,16},{16,32},{32,48},{48,64},{64,80},{80,96},{96,112},{112,0},{1... | collective-permute-start | bytes 393224 | tf_op jit(solution)/shard_map/ppermute | solution.py:42
  27.3 7.8 %collective-permute-start.5 = (bf16[32,2048]{1,0:T(8,128)(2,1)S(1)}, bf16[32,2048]{1,0:T(8,128)(2,1)S(1)}, u32[]{:S(2)}, u32[]{:S(2)}) collective-permute-start(bf16[32,2048]{1,0:T(8,128)(2,1)S(1)} %collective-permute-done.4.refs_8_), channel_id=1, source_target_pairs={{0,16},{16,32},{32,48},{48,64},{64,80},{80,96},{96,112},{112,0},{1... | collective-permute-start | bytes 393224 | tf_op jit(solution)/shard_map/ppermute | solution.py:42
  27.3 7.8 %collective-permute-start.10 = (bf16[32,2048]{1,0:T(8,128)(2,1)S(1)}, bf16[32,2048]{1,0:T(8,128)(2,1)S(1)}, u32[]{:S(2)}, u32[]{:S(2)}) collective-permute-start(bf16[32,2048]{1,0:T(8,128)(2,1)S(1)} %collective-permute-done.9.refs_7_), channel_id=1, source_target_pairs={{0,112},{16,0},{32,16},{48,32},{64,48},{80,64},{96,80},{112,96},{1... | collective-permute-start | bytes 393224 | tf_op jit(solution)/shard_map/ppermute | solution.py:42
  30.5 7.8 %collective-permute-start.14 = (bf16[32,2048]{1,0:T(8,128)(2,1)S(1)}, bf16[32,2048]{1,0:T(8,128)(2,1)S(1)}, u32[]{:S(2)}, u32[]{:S(2)}) collective-permute-start(bf16[32,2048]{1,0:T(8,128)(2,1)S(1)} %collective-permute-done.13.refs_6_), channel_id=1, source_target_pairs={{0,112},{16,0},{32,16},{48,32},{64,48},{80,64},{96,80},{112,96},{1... | collective-permute-start | bytes 393224 | tf_op jit(solution)/shard_map/ppermute | solution.py:42
  32.9 6.5 %collective-permute-start.17 = (bf16[32,2048]{1,0:T(8,128)(2,1)S(1)}, bf16[32,2048]{1,0:T(8,128)(2,1)S(1)}, u32[]{:S(2)}, u32[]{:S(2)}) collective-permute-start(bf16[32,2048]{1,0:T(8,128)(2,1)S(1)} %collective-permute-done.16.refs_9_), channel_id=1, source_target_pairs={{0,16},{16,32},{32,48},{48,64},{64,80},{80,96},{96,112},{112,0},{1... | collective-permute-start | bytes 393224 | tf_op jit(solution)/shard_map/ppermute | solution.py:42
  35.1 6.2 %collective-permute-start.6 = (bf16[32,2048]{1,0:T(8,128)(2,1)S(1)}, bf16[32,2048]{1,0:T(8,128)(2,1)S(1)}, u32[]{:S(2)}, u32[]{:S(2)}) collective-permute-start(bf16[32,2048]{1,0:T(8,128)(2,1)S(1)} %collective-permute-done.5.refs_4_), channel_id=1, source_target_pairs={{0,16},{16,32},{32,48},{48,64},{64,80},{80,96},{96,112},{112,0},{1... | collective-permute-start | bytes 393224 | tf_op jit(solution)/shard_map/ppermute | solution.py:42
  35.1 6.2 %collective-permute-start.11 = (bf16[32,2048]{1,0:T(8,128)(2,1)S(1)}, bf16[32,2048]{1,0:T(8,128)(2,1)S(1)}, u32[]{:S(2)}, u32[]{:S(2)}) collective-permute-start(bf16[32,2048]{1,0:T(8,128)(2,1)S(1)} %collective-permute-done.10.refs_3_), channel_id=1, source_target_pairs={{0,112},{16,0},{32,16},{48,32},{64,48},{80,64},{96,80},{112,96},{1... | collective-permute-start | bytes 393224 | tf_op jit(solution)/shard_map/ppermute | solution.py:42
  82.7 5.6 %collective-permute-start.24 = (bf16[32,2048]{1,0:T(8,128)(2,1)S(1)}, bf16[32,2048]{1,0:T(8,128)(2,1)S(1)}, u32[]{:S(2)}, u32[]{:S(2)}) collective-permute-start(bf16[32,2048]{1,0:T(8,128)(2,1)S(1)} %get-tuple-element.35), channel_id=1, source_target_pairs={{0,112},{16,0},{32,16},{48,32},{64,48},{80,64},{96,80},{112,96},{1... | collective-permute-start | bytes 393224 | tf_op jit(solution)/shard_map/ppermute | solution.py:42
  84.6 7.0 %collective-permute-start.20 = (bf16[32,2048]{1,0:T(8,128)(2,1)S(1)}, bf16[32,2048]{1,0:T(8,128)(2,1)S(1)}, u32[]{:S(2)}, u32[]{:S(2)}) collective-permute-start(bf16[32,2048]{1,0:T(8,128)(2,1)S(1)} %get-tuple-element.34), channel_id=1, source_target_pairs={{0,16},{16,32},{32,48},{48,64},{64,80},{80,96},{96,112},{112,0},{1... | collective-permute-start | bytes 393224 | tf_op jit(solution)/shard_map/ppermute | solution.py:42
  88.4 6.9 %collective-permute-start.25 = (bf16[64,2048]{1,0:T(8,128)(2,1)S(1)}, bf16[64,2048]{1,0:T(8,128)(2,1)S(1)}, u32[]{:S(2)}, u32[]{:S(2)}) collective-permute-start(bf16[64,2048]{1,0:T(8,128)(2,1)S(1)} %fusion.9), channel_id=1, source_target_pairs={{0,112},{16,0},{32,16},{48,32},{64,48},{80,64},{96,80},{112,96},{1... | collective-permute-start | bytes 786440 | tf_op jit(solution)/shard_map/ppermute | solution.py:42
  91.6 29.6 %collective-permute-start.19 = (bf16[512,2048]{1,0:T(8,128)(2,1)S(1)}, bf16[512,2048]{1,0:T(8,128)(2,1)S(1)}, u32[]{:S(2)}, u32[]{:S(2)}) collective-permute-start(bf16[512,2048]{1,0:T(8,128)(2,1)S(1)} %get-tuple-element.18.own_ref), channel_id=1, source_target_pairs={{0,8},{8,0},{1,9},{9,1},{2,10},{10,2},{3,11},{11,3},{4,12},{12,4},... | collective-permute-start | bytes 6291464 | tf_op jit(solution)/shard_map/ppermute | solution.py:38
  91.7 10.0 %collective-permute-start.21 = (bf16[64,2048]{1,0:T(8,128)(2,1)S(1)}, bf16[64,2048]{1,0:T(8,128)(2,1)S(1)}, u32[]{:S(2)}, u32[]{:S(2)}) collective-permute-start(bf16[64,2048]{1,0:T(8,128)(2,1)S(1)} %fusion.6), channel_id=1, source_target_pairs={{0,16},{16,32},{32,48},{48,64},{64,80},{80,96},{96,112},{112,0},{1... | collective-permute-start | bytes 786440 | tf_op jit(solution)/shard_map/ppermute | solution.py:42
  95.4 7.7 %collective-permute-start.26 = (bf16[64,2048]{1,0:T(8,128)(2,1)S(1)}, bf16[64,2048]{1,0:T(8,128)(2,1)S(1)}, u32[]{:S(2)}, u32[]{:S(2)}) collective-permute-start(bf16[64,2048]{1,0:T(8,128)(2,1)S(1)} %fusion.8), channel_id=1, source_target_pairs={{0,112},{16,0},{32,16},{48,32},{64,48},{80,64},{96,80},{112,96},{1... | collective-permute-start | bytes 786440 | tf_op jit(solution)/shard_map/ppermute | solution.py:42
  101.8 9.4 %collective-permute-start.22 = (bf16[64,2048]{1,0:T(8,128)(2,1)S(1)}, bf16[64,2048]{1,0:T(8,128)(2,1)S(1)}, u32[]{:S(2)}, u32[]{:S(2)}) collective-permute-start(bf16[64,2048]{1,0:T(8,128)(2,1)S(1)} %fusion.5), channel_id=1, source_target_pairs={{0,16},{16,32},{32,48},{48,64},{64,80},{80,96},{96,112},{112,0},{1... | collective-permute-start | bytes 786440 | tf_op jit(solution)/shard_map/ppermute | solution.py:42
  103.1 8.4 %collective-permute-start.27 = (bf16[64,2048]{1,0:T(8,128)(2,1)S(1)}, bf16[64,2048]{1,0:T(8,128)(2,1)S(1)}, u32[]{:S(2)}, u32[]{:S(2)}) collective-permute-start(bf16[64,2048]{1,0:T(8,128)(2,1)S(1)} %fusion.7), channel_id=1, source_target_pairs={{0,112},{16,0},{32,16},{48,32},{64,48},{80,64},{96,80},{112,96},{1... | collective-permute-start | bytes 786440 | tf_op jit(solution)/shard_map/ppermute | solution.py:42
  111.2 10.0 %copy-start = (bf16[512,2048]{1,0:T(8,128)(2,1)S(1)}, bf16[512,2048]{1,0:T(8,128)(2,1)}, u32[]{:S(2)}) copy-start(bf16[512,2048]{1,0:T(8,128)(2,1)} %act_ref.1) | copy-start | bytes 6291460
  111.2 8.3 %collective-permute-start.23 = (bf16[64,2048]{1,0:T(8,128)(2,1)S(1)}, bf16[64,2048]{1,0:T(8,128)(2,1)S(1)}, u32[]{:S(2)}, u32[]{:S(2)}) collective-permute-start(bf16[64,2048]{1,0:T(8,128)(2,1)S(1)} %fusion.4), channel_id=1, source_target_pairs={{0,16},{16,32},{32,48},{48,64},{64,80},{80,96},{96,112},{112,0},{1... | collective-permute-start | bytes 786440 | tf_op jit(solution)/shard_map/ppermute | solution.py:42
  111.4 9.7 %collective-permute-start.18 = (bf16[4,512,128]{2,1,0:T(8,128)(2,1)S(1)}, bf16[4,512,128]{2,1,0:T(8,128)(2,1)S(1)}, u32[]{:S(2)}, u32[]{:S(2)}) collective-permute-start(bf16[4,512,128]{2,1,0:T(8,128)(2,1)S(1)} %slice.79), channel_id=1, source_target_pairs={{0,8},{8,0},{1,9},{9,1},{2,10},{10,2},{3,11},{11,3},{4,12},{12,4},... | collective-permute-start | bytes 1572872 | tf_op jit(solution)/shard_map/ppermute | solution.py:38
  119.7 6.8 %collective-permute-start.28 = (bf16[32,2048]{1,0:T(8,128)(2,1)S(1)}, bf16[32,2048]{1,0:T(8,128)(2,1)S(1)}, u32[]{:S(2)}, u32[]{:S(2)}) collective-permute-start(bf16[32,2048]{1,0:T(8,128)(2,1)S(1)} %slice.115), channel_id=1, source_target_pairs={{0,128},{128,0},{1,129},{129,1},{2,130},{130,2},{3,131},{131,3},{4... | collective-permute-start | bytes 393224 | tf_op jit(solution)/shard_map/ppermute | solution.py:38

commit v4 on v3

--- a/solution.py
+++ b/solution.py
@@ -121,35 +121,58 @@
     )(pieces, *rows)
 
 
-def sum_kernel(at, grad_ref, mine_ref, other_ref, *refs):
+def sum_kernel(at, sends, grad_ref, mine_ref, other_ref, *refs):
+    out_ref, send_refs = refs[-1 - len(sends)], refs[len(refs) - len(sends) :]
     left = jnp.concatenate([grad_ref[k, at : at + 256, :] for k in range(8)], axis=1)
     for j in range(4):
         columns = slice(j * 512, j * 512 + 512)
         total = jnp.dot(left[:, :512], mine_ref[:, columns], preferred_element_type=F32)
         total += jnp.dot(left[:, 512:], other_ref[:, columns], preferred_element_type=F32)
-        refs[-1][:, :, columns] = total.reshape(8, 32, 512)
-
-
-def passage_sums(grad, mine, other, at, first):
-    out = pl.pallas_call(
-        functools.partial(sum_kernel, at),
-        out_shape=shape((8, 32, 2048), F32),
-        in_specs=[VMEM] * 3 + [ANY] * len(first),
-        out_specs=VMEM,
-        compiler_params=PARAMS,
-    )(grad, mine, other, *first)
-    return {k: out[i] for i, k in enumerate(KEYS[at // 32 : at // 32 + 8])}
-
-
-def query_kernel(act_ref, own_grad_ref, other_grad_ref, own_ref, other_ref, out_ref, turned_ref):
-    @pl.when(pl.program_id(0) == 0)
+        out_ref[:, :, columns] = total.reshape(8, 32, 512)
+        for i, ref in zip(sends, send_refs):
+            ref[:, columns] = total[i * 32 : i * 32 + 32].astype(BF16)
+
+
+def passage_sums(grad, mine, other, at, sends):
+    return pl.pallas_call(
+        functools.partial(sum_kernel, at, sends),
+        out_shape=(shape((8, 32, 2048), F32),) + (shape((32, 2048), BF16),) * len(sends),
+        in_specs=[VMEM] * 3,
+        out_specs=(VMEM,) * (1 + len(sends)),
+        compiler_params=PARAMS,
+    )(grad, mine, other)
+
+
+def add_kernel(places, *refs):
+    n = len(places)
+    for i, place in enumerate(places):
+        total = refs[2 * i][place] + refs[2 * i + 1][...].astype(F32)
+        refs[2 * n + i][...] = total.astype(BF16)
+
+
+def add_blocks(*items):
+    return pl.pallas_call(
+        functools.partial(add_kernel, [place for _, place, _ in items]),
+        out_shape=(shape((32, 2048), BF16),) * len(items),
+        in_specs=[VMEM] * (2 * len(items)),
+        out_specs=(VMEM,) * len(items),
+        compiler_params=PARAMS,
+    )(*[a for sums, _, come in items for a in (sums, come)])
+
+
+def query_kernel(first, act_ref, own_grad_ref, other_grad_ref, own_ref, other_ref, *refs):
+    out_ref, turned_ref = refs[-2:]
+    j = pl.program_id(0)
+
+    @pl.when(j == 0)
     def _():
         for i, g in enumerate((own_grad_ref, other_grad_ref)):
             for k in range(4):
                 turned_ref[k * 128 : k * 128 + 128, i * 512 : i * 512 + 512] = g[k].T
 
-    total = jnp.dot(turned_ref[:, :512], own_ref[...], preferred_element_type=F32)
-    total += jnp.dot(turned_ref[:, 512:], other_ref[...], preferred_element_type=F32)
+    columns = pl.ds(pl.multiple_of((j + first) * 512, 512), 512)
+    total = jnp.dot(turned_ref[:, :512], own_ref[:, columns], preferred_element_type=F32)
+    total += jnp.dot(turned_ref[:, 512:], other_ref[:, columns], preferred_element_type=F32)
     wide = act_ref[...].astype(F32)
     below = 1.0 + jnp.maximum(wide, 0.0)
     guess = pl.reciprocal(below, approx=True)
@@ -157,18 +180,20 @@
     out_ref[...] = jnp.where(wide > 0.0, total * inverse, 0.0).astype(BF16)
 
 
-def query_grads(act, grad, other_grad, own, other):
-    column = pl.BlockSpec((512, 512), lambda j: (0, j))
-    half = pl.BlockSpec((4, 512, 128), lambda j: (0, 0, 0))
-    return pl.pallas_call(
-        query_kernel,
+def query_grads(act, grad, other_grad, own, other, begun=None):
+    first = 0 if begun is None else 2
+    column = pl.BlockSpec((512, 512), lambda j: (0, j + first))
+    rest = () if begun is None else (begun,)
+    return pl.pallas_call(
+        functools.partial(query_kernel, first),
         out_shape=shape((512, 2048), BF16),
-        grid=(4,),
-        in_specs=[column, half, half, column, column],
+        grid=(2,),
+        in_specs=[column] + [VMEM] * 4 + [ANY] * len(rest),
         out_specs=column,
         scratch_shapes=[pltpu.VMEM((512, 1024), BF16)],
-        compiler_params=PARAMS,
-    )(act, grad, other_grad, own, other)
+        input_output_aliases={5: 0} if rest else {},
+        compiler_params=PARAMS,
+    )(act, grad, other_grad, own, other, *rest)
 
 
 def shards(query_act, passage_act, positive, normalizer):
@@ -191,20 +216,24 @@
     grad = exchange(score_grad(exchange(part), norm, other_norm, at, other_at))
 
     joined = after(joined, grad)
-    query_grad = query_grads(query_act, grad, swap(grad[4:], "core"), joined, swap(joined, "core"))
-
-    terms = passage_sums(grad, mine, other, 0, [])
-    terms.update(passage_sums(grad, mine, other, 256, []))
-    both = {d: jnp.concatenate([terms[0, d], terms[1, d]], axis=0) for d in ORDER}
-    pad = jnp.zeros((32, 2048), F32)
-    up = jnp.concatenate([shift(terms[0, 4].astype(BF16), 1).astype(F32), pad], axis=0)
-    down = jnp.concatenate([pad, shift(terms[1, 4].astype(BF16), -1).astype(F32)], axis=0)
+    query_args = (query_act, grad, swap(grad[4:], "core"), joined, swap(joined, "core"))
+    query_begun = query_grads(*query_args)
+
+    far, a0, a1, b0, b1 = passage_sums(grad, mine, other, 0, [0, 1, 4, 3])
+    (near,) = passage_sums(grad, mine, other, 256, [])
+    place = {k: (far, i) if i < 8 else (near, i - 8) for i, k in enumerate(KEYS)}
+    a0, a1, b0, b1 = shift(a0, 1), shift(a1, -1), shift(b0, -1), shift(b1, 1)
     for d in (3, 2, 1):
-        up = shift((both[d] + up).astype(BF16), 1).astype(F32)
-        down = shift((both[-d] + down).astype(BF16), -1).astype(F32)
-    total = both[0] + up + down
-    theirs = swap(total[32:].astype(BF16), "ylo").astype(F32)
-    total = after(total[:32], query_grad) + theirs
+        a0, a1 = add_blocks((*place[0, d], a0), (*place[1, -d], a1))
+        a0, a1 = shift(a0, 1), shift(a1, -1)
+        if d > 1:
+            b0, b1 = add_blocks((*place[0, 1 - d], b0), (*place[1, d - 1], b1))
+            b0, b1 = shift(b0, -1), shift(b1, 1)
+    sums = [near[place[s, 0][1]] for s in (0, 1)]
+    theirs = after(sums[1], query_begun) + a1.astype(F32) + b1.astype(F32)
+    theirs = swap(theirs.astype(BF16), "ylo").astype(F32)
+    query_grad = query_grads(*query_args, query_begun)
+    total = after(sums[0], query_grad) + a0.astype(F32) + b0.astype(F32) + theirs
     passage_grad = (total * slope(passage_act)).astype(BF16)
     return (query_grad, passage_grad)
 

time: 127 us -> 119 us (0.937)
  waiting for transfers between devices: 36.4 us -> 20.3 us
  starting transfers between devices: 37.4 us -> 44.6 us
    ppermute x22 -> x28, waiting for transfers between devices: 31.7 us -> 15.2 us  [shift(): return lax.ppermute(value, 'z', [(i, (i + step) % 8) for i in range(8)])]
    ppermute x22 -> x28, starting transfers between devices: 32.9 us -> 40.2 us  [shift(): return lax.ppermute(value, 'z', [(i, (i + step) % 8) for i in range(8)])]
    pallas_call x3 -> x9, Pallas kernels: 7.8 us -> 8.88 us  [the longest x2 6.16 us: query_grads(): pl.pallas_call(functools.partial(query_kernel, first), out_shape=shape((5...]
  transfers between devices with their start and end apart: 29 -> 35, of which waited for: 15 -> 14; matrix products, arithmetic and copies ran while one was open for 1% -> 0% of each run, Pallas kernels for 5% -> 7%
where the time goes in v4:
time: 119 us
  starting transfers between devices  44.6 us (37%)
  blocking collectives  36.6 us (31%)
  waiting for transfers between devices  20.3 us (17%)
  Pallas kernels  12.3 us (10%)
  other arithmetic  3.99 us (3%)
    ppermute x28, starting transfers between devices, shift(): return lax.ppermute(value, 'z', [(i, (i + step) % 8) for i in range(8)])  40.2 us
    all_to_all x2, blocking collectives, exchange(): return lax.all_to_all(value, REP, split_axis=0, concat_axis=0)  36.6 us
    ppermute x28, waiting for transfers between devices, shift(): return lax.ppermute(value, 'z', [(i, (i + step) % 8) for i in range(8)])  15.2 us
    pallas_call x2, Pallas kernels, query_grads(): pl.pallas_call(functools.partial(query_kernel, first), out_shape=shape((5...  6.16 us
    ppermute x7, waiting for transfers between devices, swap(): return lax.ppermute(value, axis, [(0, 1), (1, 0)])  5.15 us
    ppermute x7, starting transfers between devices, swap(): return lax.ppermute(value, axis, [(0, 1), (1, 0)])  4.4 us
    convert_element_type x2, other arithmetic, saturate(): jnp.where(wide < 2.0 ** (-8), small, jnp.log(1.0 + wide)).astype(BF16)  3.17 us
    pallas_call x1, Pallas kernels, partial_scores(): pl.pallas_call(score_kernel, out_shape=(shape((8, 528, 128), jnp.int16),...  2.83 us
  transfers between devices with their start and end apart: 35, of which 14 were waited for; matrix products, arithmetic and copies ran while one was open for 0% of the time, Pallas kernels for 7%

profile of v4, /device:TPU:8, one launch (start us, length us, event | category | flops | bytes accessed | tf_op | source)
XLA Modules:
  0.0 118.7 jit_solution(16629651708216861107)
XLA Ops:
  0.7 3.1 %fusion.1.mine_ref = bf16[512,2048]{1,0:T(8,128)(2,1)S(1)} fusion(bf16[512,2048]{1,0:T(8,128)(2,1)} %act_ref.3), kind=kLoop, calls=%fused_computation.2 | loop fusion | flops 9437184 | bytes 4194304 | tf_op jit(solution)/shard_map/convert_element_type | solution.py:29
  3.8 0.1 fusion.8.refs_14_
  4.0 2.3 %collective-permute-start.7 = (bf16[32,2048]{1,0:T(8,128)(2,1)S(1)}, bf16[32,2048]{1,0:T(8,128)(2,1)S(1)}, u32[]{:S(2)}, u32[]{:S(2)}) collective-permute-start(bf16[32,2048]{1,0:T(8,128)(2,1)S(1)} %fusion.8.refs_14_), channel_id=1, source_target_pairs={{0,128},{128,0},{1,129},{129,1},{2,130},{130,2},{3,131},{131,3},{4... | collective-permute-start | bytes 393224 | tf_op jit(solution)/shard_map/ppermute | solution.py:38
  6.2 0.2 collective-permute-start.3
  6.4 4.0 %collective-permute-done.7.refs_15_ = bf16[32,2048]{1,0:T(8,128)(2,1)S(1)} collective-permute-done((bf16[32,2048]{1,0:T(8,128)(2,1)S(1)}, bf16[32,2048]{1,0:T(8,128)(2,1)S(1)}, u32[]{:S(2)}, u32[]{:S(2)}) %collective-permute-start.7) | collective-permute-done | bytes 131104 | tf_op jit(solution)/shard_map/ppermute | solution.py:38
  10.4 5.4 %collective-permute-start.8 = (bf16[32,2048]{1,0:T(8,128)(2,1)S(1)}, bf16[32,2048]{1,0:T(8,128)(2,1)S(1)}, u32[]{:S(2)}, u32[]{:S(2)}) collective-permute-start(bf16[32,2048]{1,0:T(8,128)(2,1)S(1)} %collective-permute-done.7.refs_15_), channel_id=1, source_target_pairs={{0,112},{16,0},{32,16},{48,32},{64,48},{80,64},{96,80},{112,96},{1... | collective-permute-start | bytes 393224 | tf_op jit(solution)/shard_map/ppermute | solution.py:42
  15.8 0.5 collective-permute-start.1
  16.3 0.6 collective-permute-done.2
  16.9 1.0 collective-permute-start.12
  18.0 1.0 collective-permute-start.15
  19.1 3.2 %collective-permute-start.9 = (bf16[32,2048]{1,0:T(8,128)(2,1)S(1)}, bf16[32,2048]{1,0:T(8,128)(2,1)S(1)}, u32[]{:S(2)}, u32[]{:S(2)}) collective-permute-start(bf16[32,2048]{1,0:T(8,128)(2,1)S(1)} %collective-permute-done.8.refs_11_), channel_id=1, source_target_pairs={{0,112},{16,0},{32,16},{48,32},{64,48},{80,64},{96,80},{112,96},{1... | collective-permute-start | bytes 393224 | tf_op jit(solution)/shard_map/ppermute | solution.py:42
  22.2 1.1 collective-permute-done.12.refs_10_
  23.3 1.6 %collective-permute-start.13 = (bf16[32,2048]{1,0:T(8,128)(2,1)S(1)}, bf16[32,2048]{1,0:T(8,128)(2,1)S(1)}, u32[]{:S(2)}, u32[]{:S(2)}) collective-permute-start(bf16[32,2048]{1,0:T(8,128)(2,1)S(1)} %collective-permute-done.12.refs_10_), channel_id=1, source_target_pairs={{0,112},{16,0},{32,16},{48,32},{64,48},{80,64},{96,80},{112,96},{1... | collective-permute-start | bytes 393224 | tf_op jit(solution)/shard_map/ppermute | solution.py:42
  24.9 0.6 collective-permute-done.15.refs_13_
  25.6 1.7 %collective-permute-done.4.refs_8_ = bf16[32,2048]{1,0:T(8,128)(2,1)S(1)} collective-permute-done((bf16[32,2048]{1,0:T(8,128)(2,1)S(1)}, bf16[32,2048]{1,0:T(8,128)(2,1)S(1)}, u32[]{:S(2)}, u32[]{:S(2)}) %collective-permute-start.4) | collective-permute-done | bytes 131104 | tf_op jit(solution)/shard_map/ppermute | solution.py:42
  27.3 3.2 %collective-permute-start.10 = (bf16[32,2048]{1,0:T(8,128)(2,1)S(1)}, bf16[32,2048]{1,0:T(8,128)(2,1)S(1)}, u32[]{:S(2)}, u32[]{:S(2)}) collective-permute-start(bf16[32,2048]{1,0:T(8,128)(2,1)S(1)} %collective-permute-done.9.refs_7_), channel_id=1, source_target_pairs={{0,112},{16,0},{32,16},{48,32},{64,48},{80,64},{96,80},{112,96},{1... | collective-permute-start | bytes 393224 | tf_op jit(solution)/shard_map/ppermute | solution.py:42
  30.5 0.7 collective-permute-start.14
  31.2 1.7 %collective-permute-done.16.refs_9_ = bf16[32,2048]{1,0:T(8,128)(2,1)S(1)} collective-permute-done((bf16[32,2048]{1,0:T(8,128)(2,1)S(1)}, bf16[32,2048]{1,0:T(8,128)(2,1)S(1)}, u32[]{:S(2)}, u32[]{:S(2)}) %collective-permute-start.16) | collective-permute-done | bytes 131104 | tf_op jit(solution)/shard_map/ppermute | solution.py:42
  32.9 2.1 %collective-permute-done.5.refs_4_ = bf16[32,2048]{1,0:T(8,128)(2,1)S(1)} collective-permute-done((bf16[32,2048]{1,0:T(8,128)(2,1)S(1)}, bf16[32,2048]{1,0:T(8,128)(2,1)S(1)}, u32[]{:S(2)}, u32[]{:S(2)}) %collective-permute-start.5) | collective-permute-done | bytes 131104 | tf_op jit(solution)/shard_map/ppermute | solution.py:42
  35.1 3.2 %collective-permute-start.11 = (bf16[32,2048]{1,0:T(8,128)(2,1)S(1)}, bf16[32,2048]{1,0:T(8,128)(2,1)S(1)}, u32[]{:S(2)}, u32[]{:S(2)}) collective-permute-start(bf16[32,2048]{1,0:T(8,128)(2,1)S(1)} %collective-permute-done.10.refs_3_), channel_id=1, source_target_pairs={{0,112},{16,0},{32,16},{48,32},{64,48},{80,64},{96,80},{112,96},{1... | collective-permute-start | bytes 393224 | tf_op jit(solution)/shard_map/ppermute | solution.py:42
  38.3 1.1 collective-permute-done.17.refs_5_
  39.4 1.8 %collective-permute-done.6.refs_0_ = bf16[32,2048]{1,0:T(8,128)(2,1)S(1)} collective-permute-done((bf16[32,2048]{1,0:T(8,128)(2,1)S(1)}, bf16[32,2048]{1,0:T(8,128)(2,1)S(1)}, u32[]{:S(2)}, u32[]{:S(2)}) %collective-permute-start.6) | collective-permute-done | bytes 131104 | tf_op jit(solution)/shard_map/ppermute | solution.py:42
  41.2 2.8 %shard_map.59 = (s16[8,528,128]{2,1,0:T(8,128)(2,1)S(1)}, bf16[512,2048]{1,0:T(8,128)(2,1)S(1)}) custom-call(bf16[512,2048]{1,0:T(8,128)(2,1)S(1)} %fusion.1.mine_ref, bf16[512,2048]{1,0:T(8,128)(2,1)S(1)} %collective-permute-done.other_ref, bf16[32,2048]{1,0:T(8,128)(2,1)S(1)} %collective-permute-done.6.refs_0_, ...), custom_call_target="tpu_custom_call" | custom-call | tf_op jit(solution)/shard_map/pallas_call | solution.py:81
  44.1 20.9 %all_to_all.10.pieces_ref = s16[8,528,128]{2,1,0:T(8,128)(2,1)S(1)} all-to-all(s16[8,528,128]{2,1,0:T(8,128)(2,1)S(1)} %get-tuple-element.28), channel_id=1, replica_groups=mesh['ylo'=2,'z'=8,'core'=2,'yhi'=2,'x'=4] {'x','yhi'}, dimensions={0} | all-to-all | bytes 2162688 | tf_op jit(solution)/shard_map/all_to_all | solution.py:46
  65.0 0.6 shard_map.60
  65.6 15.7 %all_to_all.11.own_grad_ref.grad_ref = bf16[8,512,128]{2,1,0:T(8,128)(2,1)S(1)} all-to-all(bf16[8,512,128]{2,1,0:T(8,128)(2,1)S(1)} %shard_map.60), channel_id=1, replica_groups=mesh['ylo'=2,'z'=8,'core'=2,'yhi'=2,'x'=4] {'x','yhi'}, dimensions={0} | all-to-all | bytes 2097152 | tf_op jit(solution)/shard_map/all_to_all | solution.py:46
  81.3 1.2 %shard_map.64 = (f32[8,32,2048]{2,1,0:T(8,128)S(1)}, bf16[32,2048]{1,0:T(8,128)(2,1)S(1)}, bf16[32,2048]{1,0:T(8,128)(2,1)S(1)}, bf16[32,2048]{1,0:T(8,128)(2,1)S(1)}, bf16[32,2048]{1,0:T(8,128)(2,1)S(1)}) custom-call(bf16[8,512,128]{2,1,0:T(8,128)(2,1)S(1)} %all_to_all.11.own_grad_ref.grad_ref, bf16[512,2048]{1,0:T(8,128)(2,1)S(1)} %fusion.1.mine_ref, ...), custom_call_target="tpu_custom_call" | custom-call | tf_op jit(solution)/shard_map/pallas_call | solution.py:137
  82.6 3.2 %collective-permute-start.21 = (bf16[32,2048]{1,0:T(8,128)(2,1)S(1)}, bf16[32,2048]{1,0:T(8,128)(2,1)S(1)}, u32[]{:S(2)}, u32[]{:S(2)}) collective-permute-start(bf16[32,2048]{1,0:T(8,128)(2,1)S(1)} %get-tuple-element.38), channel_id=1, source_target_pairs={{0,112},{16,0},{32,16},{48,32},{64,48},{80,64},{96,80},{112,96},{1... | collective-permute-start | bytes 393224 | tf_op jit(solution)/shard_map/ppermute | solution.py:42
  85.8 0.5 collective-permute-start.27
  86.4 1.5 %collective-permute-start.28 = (bf16[32,2048]{1,0:T(8,128)(2,1)S(1)}, bf16[32,2048]{1,0:T(8,128)(2,1)S(1)}, u32[]{:S(2)}, u32[]{:S(2)}) collective-permute-start(bf16[32,2048]{1,0:T(8,128)(2,1)S(1)} %get-tuple-element.45), channel_id=1, source_target_pairs={{0,16},{16,32},{32,48},{48,64},{64,80},{80,96},{96,112},{112,0},{1... | collective-permute-start | bytes 393224 | tf_op jit(solution)/shard_map/ppermute | solution.py:42
  87.9 1.9 %collective-permute-done.20.refs_1_ = bf16[32,2048]{1,0:T(8,128)(2,1)S(1)} collective-permute-done((bf16[32,2048]{1,0:T(8,128)(2,1)S(1)}, bf16[32,2048]{1,0:T(8,128)(2,1)S(1)}, u32[]{:S(2)}, u32[]{:S(2)}) %collective-permute-start.20) | collective-permute-done | bytes 131104 | tf_op jit(solution)/shard_map/ppermute | solution.py:42
  89.9 4.0 %collective-permute-start.23 = (bf16[32,2048]{1,0:T(8,128)(2,1)S(1)}, bf16[32,2048]{1,0:T(8,128)(2,1)S(1)}, u32[]{:S(2)}, u32[]{:S(2)}) collective-permute-start(bf16[32,2048]{1,0:T(8,128)(2,1)S(1)} %get-tuple-element.40), channel_id=1, source_target_pairs={{0,112},{16,0},{32,16},{48,32},{64,48},{80,64},{96,80},{112,96},{1... | collective-permute-start | bytes 393224 | tf_op jit(solution)/shard_map/ppermute | solution.py:42
  93.8 1.2 %shard_map.63.refs_2_.refs_0_ = f32[8,32,2048]{2,1,0:T(8,128)S(1)} custom-call(bf16[8,512,128]{2,1,0:T(8,128)(2,1)S(1)} %all_to_all.11.own_grad_ref.grad_ref, bf16[512,2048]{1,0:T(8,128)(2,1)S(1)} %fusion.1.mine_ref, bf16[512,2048]{1,0:T(8,128)(2,1)S(1)} %collective-permute-done.other_ref), custom_call_target="tpu_custom_call" | custom-call | tf_op jit(solution)/shard_map/pallas_call | solution.py:137
  95.1 1.8 %collective-permute-start.29 = (bf16[32,2048]{1,0:T(8,128)(2,1)S(1)}, bf16[32,2048]{1,0:T(8,128)(2,1)S(1)}, u32[]{:S(2)}, u32[]{:S(2)}) collective-permute-start(bf16[32,2048]{1,0:T(8,128)(2,1)S(1)} %get-tuple-element.46), channel_id=1, source_target_pairs={{0,112},{16,0},{32,16},{48,32},{64,48},{80,64},{96,80},{112,96},{1... | collective-permute-start | bytes 393224 | tf_op jit(solution)/shard_map/ppermute | solution.py:42
  96.9 0.3 collective-permute-start.30
  97.3 0.2 collective-permute-done.23.refs_3_
  97.5 1.5 %collective-permute-start.24 = (bf16[32,2048]{1,0:T(8,128)(2,1)S(1)}, bf16[32,2048]{1,0:T(8,128)(2,1)S(1)}, u32[]{:S(2)}, u32[]{:S(2)}) collective-permute-start(bf16[32,2048]{1,0:T(8,128)(2,1)S(1)} %get-tuple-element.41), channel_id=1, source_target_pairs={{0,16},{16,32},{32,48},{48,64},{64,80},{80,96},{96,112},{112,0},{1... | collective-permute-start | bytes 393224 | tf_op jit(solution)/shard_map/ppermute | solution.py:42
  98.9 2.4 %collective-permute-start.25 = (bf16[32,2048]{1,0:T(8,128)(2,1)S(1)}, bf16[32,2048]{1,0:T(8,128)(2,1)S(1)}, u32[]{:S(2)}, u32[]{:S(2)}) collective-permute-start(bf16[32,2048]{1,0:T(8,128)(2,1)S(1)} %get-tuple-element.42), channel_id=1, source_target_pairs={{0,112},{16,0},{32,16},{48,32},{64,48},{80,64},{96,80},{112,96},{1... | collective-permute-start | bytes 393224 | tf_op jit(solution)/shard_map/ppermute | solution.py:42
  101.5 1.6 %collective-permute-done.30.refs_3_ = bf16[32,2048]{1,0:T(8,128)(2,1)S(1)} collective-permute-done((bf16[32,2048]{1,0:T(8,128)(2,1)S(1)}, bf16[32,2048]{1,0:T(8,128)(2,1)S(1)}, u32[]{:S(2)}, u32[]{:S(2)}) %collective-permute-start.30) | collective-permute-done | bytes 131104 | tf_op jit(solution)/shard_map/ppermute | solution.py:42
  103.3 1.2 %collective-permute-done.24.refs_1_ = bf16[32,2048]{1,0:T(8,128)(2,1)S(1)} collective-permute-done((bf16[32,2048]{1,0:T(8,128)(2,1)S(1)}, bf16[32,2048]{1,0:T(8,128)(2,1)S(1)}, u32[]{:S(2)}, u32[]{:S(2)}) %collective-permute-start.24) | collective-permute-done | bytes 131104 | tf_op jit(solution)/shard_map/ppermute | solution.py:42
  104.6 3.0 %collective-permute-start.32 = (bf16[32,2048]{1,0:T(8,128)(2,1)S(1)}, bf16[32,2048]{1,0:T(8,128)(2,1)S(1)}, u32[]{:S(2)}, u32[]{:S(2)}) collective-permute-start(bf16[32,2048]{1,0:T(8,128)(2,1)S(1)} %get-tuple-element.50), channel_id=1, source_target_pairs={{0,112},{16,0},{32,16},{48,32},{64,48},{80,64},{96,80},{112,96},{1... | collective-permute-start | bytes 393224 | tf_op jit(solution)/shard_map/ppermute | solution.py:42
  107.7 0.8 collective-permute-start.31
  108.5 1.3 %collective-permute-start.26 = (bf16[32,2048]{1,0:T(8,128)(2,1)S(1)}, bf16[32,2048]{1,0:T(8,128)(2,1)S(1)}, u32[]{:S(2)}, u32[]{:S(2)}) collective-permute-start(bf16[32,2048]{1,0:T(8,128)(2,1)S(1)} %get-tuple-element.43), channel_id=1, source_target_pairs={{0,16},{16,32},{32,48},{48,64},{64,80},{80,96},{96,112},{112,0},{1... | collective-permute-start | bytes 393224 | tf_op jit(solution)/shard_map/ppermute | solution.py:42
  109.8 3.1 %shard_map.61.refs_0_ = bf16[512,2048]{1,0:T(8,128)(2,1)} custom-call(bf16[512,2048]{1,0:T(8,128)(2,1)S(1)} %copy-done, bf16[8,512,128]{2,1,0:T(8,128)(2,1)S(1)} %all_to_all.11.own_grad_ref.grad_ref, bf16[4,512,128]{2,1,0:T(8,128)(2,1)S(1)} %collective-permute-done.18.other_grad_ref, bf16[512,2048]{1,0:T(8,128)(2,1)S(1)} %get-tuple-element.34.own_ref, ...), custom_call_target="tpu_custom_call" | custom-call | tf_op jit(solution)/shard_map/pallas_call | solution.py:187
  112.9 1.4 %collective-permute-start.34 = (bf16[32,2048]{1,0:T(8,128)(2,1)S(1)}, bf16[32,2048]{1,0:T(8,128)(2,1)S(1)}, u32[]{:S(2)}, u32[]{:S(2)}) collective-permute-start(bf16[32,2048]{1,0:T(8,128)(2,1)S(1)} %add_convert_fusion), channel_id=1, source_target_pairs={{0,128},{128,0},{1,129},{129,1},{2,130},{130,2},{3,131},{131,3},{4... | collective-permute-start | bytes 393224 | tf_op jit(solution)/shard_map/ppermute | solution.py:38
  114.3 3.1 %shard_map.62 = bf16[512,2048]{1,0:T(8,128)(2,1)} custom-call(bf16[512,2048]{1,0:T(8,128)(2,1)S(1)} %copy-done, bf16[8,512,128]{2,1,0:T(8,128)(2,1)S(1)} %all_to_all.11.own_grad_ref.grad_ref, bf16[4,512,128]{2,1,0:T(8,128)(2,1)S(1)} %collective-permute-done.18.other_grad_ref, ...), custom_call_target="tpu_custom_call", output_to_operand_aliasing={{}: (5, {})} | custom-call | tf_op jit(solution)/shard_map/pallas_call | solution.py:187
  117.4 0.5 collective-permute-done.34
  118.0 0.8 fusion.11
  (49 shorter events, 1.0 us)
Async XLA Ops:
  0.6 3.2 %copy-start.3 = (bf16[32,2048]{1,0:T(8,128)(2,1)S(1)}, bf16[32,2048]{1,0:T(8,128)(2,1)}, u32[]{:S(2)}) copy-start(bf16[32,2048]{1,0:T(8,128)(2,1)} %param.5) | copy-start | bytes 393220
  0.6 15.1 %copy-start.2 = (s32[512]{0:T(512)S(1)}, s32[512]{0:T(512)}, u32[]{:S(2)}) copy-start(s32[512]{0:T(512)} %param.6) | copy-start | bytes 6148
  0.7 15.1 %copy-start.1 = (f32[512]{0:T(512)S(1)}, f32[512]{0:T(512)}, u32[]{:S(2)}) copy-start(f32[512]{0:T(512)} %param.7) | copy-start | bytes 6148
  3.7 34.6 %collective-permute-start = (bf16[512,2048]{1,0:T(8,128)(2,1)S(1)}, bf16[512,2048]{1,0:T(8,128)(2,1)S(1)}, u32[]{:S(2)}, u32[]{:S(2)}) collective-permute-start(bf16[512,2048]{1,0:T(8,128)(2,1)S(1)} %fusion.1.mine_ref), channel_id=1, source_target_pairs={{0,8},{8,0},{1,9},{9,1},{2,10},{10,2},{3,11},{11,3},{4,12},{12,4},... | collective-permute-start | bytes 6291464 | tf_op jit(solution)/shard_map/ppermute | solution.py:38
  4.0 6.4 %collective-permute-start.7 = (bf16[32,2048]{1,0:T(8,128)(2,1)S(1)}, bf16[32,2048]{1,0:T(8,128)(2,1)S(1)}, u32[]{:S(2)}, u32[]{:S(2)}) collective-permute-start(bf16[32,2048]{1,0:T(8,128)(2,1)S(1)} %fusion.8.refs_14_), channel_id=1, source_target_pairs={{0,128},{128,0},{1,129},{129,1},{2,130},{130,2},{3,131},{131,3},{4... | collective-permute-start | bytes 393224 | tf_op jit(solution)/shard_map/ppermute | solution.py:38
  6.2 12.8 %collective-permute-start.3 = (bf16[32,2048]{1,0:T(8,128)(2,1)S(1)}, bf16[32,2048]{1,0:T(8,128)(2,1)S(1)}, u32[]{:S(2)}, u32[]{:S(2)}) collective-permute-start(bf16[32,2048]{1,0:T(8,128)(2,1)S(1)} %fusion.8.refs_14_), channel_id=1, source_target_pairs={{0,16},{16,32},{32,48},{48,64},{64,80},{80,96},{96,112},{112,0},{1... | collective-permute-start | bytes 393224 | tf_op jit(solution)/shard_map/ppermute | solution.py:42
  10.4 8.7 %collective-permute-start.8 = (bf16[32,2048]{1,0:T(8,128)(2,1)S(1)}, bf16[32,2048]{1,0:T(8,128)(2,1)S(1)}, u32[]{:S(2)}, u32[]{:S(2)}) collective-permute-start(bf16[32,2048]{1,0:T(8,128)(2,1)S(1)} %collective-permute-done.7.refs_15_), channel_id=1, source_target_pairs={{0,112},{16,0},{32,16},{48,32},{64,48},{80,64},{96,80},{112,96},{1... | collective-permute-start | bytes 393224 | tf_op jit(solution)/shard_map/ppermute | solution.py:42
  15.8 1.2 collective-permute-start.2
  15.8 2.2 %collective-permute-start.1 = (f32[512]{0:T(512)S(1)}, f32[512]{0:T(512)S(1)}, u32[]{:S(2)}, u32[]{:S(2)}) collective-permute-start(f32[512]{0:T(512)S(1)} %copy-done.1), channel_id=1, source_target_pairs={{0,8},{8,0},{1,9},{9,1},{2,10},{10,2},{3,11},{11,3},{4,12},{12,4},... | collective-permute-start | bytes 6152 | tf_op jit(solution)/shard_map/ppermute | solution.py:38
  16.9 6.3 %collective-permute-start.12 = (bf16[32,2048]{1,0:T(8,128)(2,1)S(1)}, bf16[32,2048]{1,0:T(8,128)(2,1)S(1)}, u32[]{:S(2)}, u32[]{:S(2)}) collective-permute-start(bf16[32,2048]{1,0:T(8,128)(2,1)S(1)} %fusion.8.refs_14_), channel_id=1, source_target_pairs={{0,112},{16,0},{32,16},{48,32},{64,48},{80,64},{96,80},{112,96},{1... | collective-permute-start | bytes 393224 | tf_op jit(solution)/shard_map/ppermute | solution.py:42
  18.0 7.6 %collective-permute-start.15 = (bf16[32,2048]{1,0:T(8,128)(2,1)S(1)}, bf16[32,2048]{1,0:T(8,128)(2,1)S(1)}, u32[]{:S(2)}, u32[]{:S(2)}) collective-permute-start(bf16[32,2048]{1,0:T(8,128)(2,1)S(1)} %collective-permute-done.7.refs_15_), channel_id=1, source_target_pairs={{0,16},{16,32},{32,48},{48,64},{64,80},{80,96},{96,112},{112,0},{1... | collective-permute-start | bytes 393224 | tf_op jit(solution)/shard_map/ppermute | solution.py:42
  19.0 8.3 %collective-permute-start.4 = (bf16[32,2048]{1,0:T(8,128)(2,1)S(1)}, bf16[32,2048]{1,0:T(8,128)(2,1)S(1)}, u32[]{:S(2)}, u32[]{:S(2)}) collective-permute-start(bf16[32,2048]{1,0:T(8,128)(2,1)S(1)} %collective-permute-done.3.refs_12_), channel_id=1, source_target_pairs={{0,16},{16,32},{32,48},{48,64},{64,80},{80,96},{96,112},{112,0},{1... | collective-permute-start | bytes 393224 | tf_op jit(solution)/shard_map/ppermute | solution.py:42
  19.1 8.2 %collective-permute-start.9 = (bf16[32,2048]{1,0:T(8,128)(2,1)S(1)}, bf16[32,2048]{1,0:T(8,128)(2,1)S(1)}, u32[]{:S(2)}, u32[]{:S(2)}) collective-permute-start(bf16[32,2048]{1,0:T(8,128)(2,1)S(1)} %collective-permute-done.8.refs_11_), channel_id=1, source_target_pairs={{0,112},{16,0},{32,16},{48,32},{64,48},{80,64},{96,80},{112,96},{1... | collective-permute-start | bytes 393224 | tf_op jit(solution)/shard_map/ppermute | solution.py:42
  23.3 7.2 %collective-permute-start.13 = (bf16[32,2048]{1,0:T(8,128)(2,1)S(1)}, bf16[32,2048]{1,0:T(8,128)(2,1)S(1)}, u32[]{:S(2)}, u32[]{:S(2)}) collective-permute-start(bf16[32,2048]{1,0:T(8,128)(2,1)S(1)} %collective-permute-done.12.refs_10_), channel_id=1, source_target_pairs={{0,112},{16,0},{32,16},{48,32},{64,48},{80,64},{96,80},{112,96},{1... | collective-permute-start | bytes 393224 | tf_op jit(solution)/shard_map/ppermute | solution.py:42
  25.5 7.4 %collective-permute-start.16 = (bf16[32,2048]{1,0:T(8,128)(2,1)S(1)}, bf16[32,2048]{1,0:T(8,128)(2,1)S(1)}, u32[]{:S(2)}, u32[]{:S(2)}) collective-permute-start(bf16[32,2048]{1,0:T(8,128)(2,1)S(1)} %collective-permute-done.15.refs_13_), channel_id=1, source_target_pairs={{0,16},{16,32},{32,48},{48,64},{64,80},{80,96},{96,112},{112,0},{1... | collective-permute-start | bytes 393224 | tf_op jit(solution)/shard_map/ppermute | solution.py:42
  27.3 7.8 %collective-permute-start.5 = (bf16[32,2048]{1,0:T(8,128)(2,1)S(1)}, bf16[32,2048]{1,0:T(8,128)(2,1)S(1)}, u32[]{:S(2)}, u32[]{:S(2)}) collective-permute-start(bf16[32,2048]{1,0:T(8,128)(2,1)S(1)} %collective-permute-done.4.refs_8_), channel_id=1, source_target_pairs={{0,16},{16,32},{32,48},{48,64},{64,80},{80,96},{96,112},{112,0},{1... | collective-permute-start | bytes 393224 | tf_op jit(solution)/shard_map/ppermute | solution.py:42
  27.3 7.8 %collective-permute-start.10 = (bf16[32,2048]{1,0:T(8,128)(2,1)S(1)}, bf16[32,2048]{1,0:T(8,128)(2,1)S(1)}, u32[]{:S(2)}, u32[]{:S(2)}) collective-permute-start(bf16[32,2048]{1,0:T(8,128)(2,1)S(1)} %collective-permute-done.9.refs_7_), channel_id=1, source_target_pairs={{0,112},{16,0},{32,16},{48,32},{64,48},{80,64},{96,80},{112,96},{1... | collective-permute-start | bytes 393224 | tf_op jit(solution)/shard_map/ppermute | solution.py:42
  30.5 7.8 %collective-permute-start.14 = (bf16[32,2048]{1,0:T(8,128)(2,1)S(1)}, bf16[32,2048]{1,0:T(8,128)(2,1)S(1)}, u32[]{:S(2)}, u32[]{:S(2)}) collective-permute-start(bf16[32,2048]{1,0:T(8,128)(2,1)S(1)} %collective-permute-done.13.refs_6_), channel_id=1, source_target_pairs={{0,112},{16,0},{32,16},{48,32},{64,48},{80,64},{96,80},{112,96},{1... | collective-permute-start | bytes 393224 | tf_op jit(solution)/shard_map/ppermute | solution.py:42
  32.9 6.5 %collective-permute-start.17 = (bf16[32,2048]{1,0:T(8,128)(2,1)S(1)}, bf16[32,2048]{1,0:T(8,128)(2,1)S(1)}, u32[]{:S(2)}, u32[]{:S(2)}) collective-permute-start(bf16[32,2048]{1,0:T(8,128)(2,1)S(1)} %collective-permute-done.16.refs_9_), channel_id=1, source_target_pairs={{0,16},{16,32},{32,48},{48,64},{64,80},{80,96},{96,112},{112,0},{1... | collective-permute-start | bytes 393224 | tf_op jit(solution)/shard_map/ppermute | solution.py:42
  35.1 6.2 %collective-permute-start.6 = (bf16[32,2048]{1,0:T(8,128)(2,1)S(1)}, bf16[32,2048]{1,0:T(8,128)(2,1)S(1)}, u32[]{:S(2)}, u32[]{:S(2)}) collective-permute-start(bf16[32,2048]{1,0:T(8,128)(2,1)S(1)} %collective-permute-done.5.refs_4_), channel_id=1, source_target_pairs={{0,16},{16,32},{32,48},{48,64},{64,80},{80,96},{96,112},{112,0},{1... | collective-permute-start | bytes 393224 | tf_op jit(solution)/shard_map/ppermute | solution.py:42
  35.1 6.2 %collective-permute-start.11 = (bf16[32,2048]{1,0:T(8,128)(2,1)S(1)}, bf16[32,2048]{1,0:T(8,128)(2,1)S(1)}, u32[]{:S(2)}, u32[]{:S(2)}) collective-permute-start(bf16[32,2048]{1,0:T(8,128)(2,1)S(1)} %collective-permute-done.10.refs_3_), channel_id=1, source_target_pairs={{0,112},{16,0},{32,16},{48,32},{64,48},{80,64},{96,80},{112,96},{1... | collective-permute-start | bytes 393224 | tf_op jit(solution)/shard_map/ppermute | solution.py:42
  81.3 28.5 %collective-permute-start.19 = (bf16[512,2048]{1,0:T(8,128)(2,1)S(1)}, bf16[512,2048]{1,0:T(8,128)(2,1)S(1)}, u32[]{:S(2)}, u32[]{:S(2)}) collective-permute-start(bf16[512,2048]{1,0:T(8,128)(2,1)S(1)} %get-tuple-element.34.own_ref), channel_id=1, source_target_pairs={{0,8},{8,0},{1,9},{9,1},{2,10},{10,2},{3,11},{11,3},{4,12},{12,4},... | collective-permute-start | bytes 6291464 | tf_op jit(solution)/shard_map/ppermute | solution.py:38
  82.5 7.2 %collective-permute-start.20 = (bf16[32,2048]{1,0:T(8,128)(2,1)S(1)}, bf16[32,2048]{1,0:T(8,128)(2,1)S(1)}, u32[]{:S(2)}, u32[]{:S(2)}) collective-permute-start(bf16[32,2048]{1,0:T(8,128)(2,1)S(1)} %get-tuple-element.37), channel_id=1, source_target_pairs={{0,16},{16,32},{32,48},{48,64},{64,80},{80,96},{96,112},{112,0},{1... | collective-permute-start | bytes 393224 | tf_op jit(solution)/shard_map/ppermute | solution.py:42
  82.6 7.1 %collective-permute-start.21 = (bf16[32,2048]{1,0:T(8,128)(2,1)S(1)}, bf16[32,2048]{1,0:T(8,128)(2,1)S(1)}, u32[]{:S(2)}, u32[]{:S(2)}) collective-permute-start(bf16[32,2048]{1,0:T(8,128)(2,1)S(1)} %get-tuple-element.38), channel_id=1, source_target_pairs={{0,112},{16,0},{32,16},{48,32},{64,48},{80,64},{96,80},{112,96},{1... | collective-permute-start | bytes 393224 | tf_op jit(solution)/shard_map/ppermute | solution.py:42
  85.8 9.2 %collective-permute-start.27 = (bf16[32,2048]{1,0:T(8,128)(2,1)S(1)}, bf16[32,2048]{1,0:T(8,128)(2,1)S(1)}, u32[]{:S(2)}, u32[]{:S(2)}) collective-permute-start(bf16[32,2048]{1,0:T(8,128)(2,1)S(1)} %get-tuple-element.44), channel_id=1, source_target_pairs={{0,112},{16,0},{32,16},{48,32},{64,48},{80,64},{96,80},{112,96},{1... | collective-permute-start | bytes 393224 | tf_op jit(solution)/shard_map/ppermute | solution.py:42
  86.4 8.7 %collective-permute-start.28 = (bf16[32,2048]{1,0:T(8,128)(2,1)S(1)}, bf16[32,2048]{1,0:T(8,128)(2,1)S(1)}, u32[]{:S(2)}, u32[]{:S(2)}) collective-permute-start(bf16[32,2048]{1,0:T(8,128)(2,1)S(1)} %get-tuple-element.45), channel_id=1, source_target_pairs={{0,16},{16,32},{32,48},{48,64},{64,80},{80,96},{96,112},{112,0},{1... | collective-permute-start | bytes 393224 | tf_op jit(solution)/shard_map/ppermute | solution.py:42
  89.8 7.5 %collective-permute-start.22 = (bf16[32,2048]{1,0:T(8,128)(2,1)S(1)}, bf16[32,2048]{1,0:T(8,128)(2,1)S(1)}, u32[]{:S(2)}, u32[]{:S(2)}) collective-permute-start(bf16[32,2048]{1,0:T(8,128)(2,1)S(1)} %get-tuple-element.39), channel_id=1, source_target_pairs={{0,16},{16,32},{32,48},{48,64},{64,80},{80,96},{96,112},{112,0},{1... | collective-permute-start | bytes 393224 | tf_op jit(solution)/shard_map/ppermute | solution.py:42
  89.9 7.5 %collective-permute-start.23 = (bf16[32,2048]{1,0:T(8,128)(2,1)S(1)}, bf16[32,2048]{1,0:T(8,128)(2,1)S(1)}, u32[]{:S(2)}, u32[]{:S(2)}) collective-permute-start(bf16[32,2048]{1,0:T(8,128)(2,1)S(1)} %get-tuple-element.40), channel_id=1, source_target_pairs={{0,112},{16,0},{32,16},{48,32},{64,48},{80,64},{96,80},{112,96},{1... | collective-permute-start | bytes 393224 | tf_op jit(solution)/shard_map/ppermute | solution.py:42
  95.1 6.2 %collective-permute-start.29 = (bf16[32,2048]{1,0:T(8,128)(2,1)S(1)}, bf16[32,2048]{1,0:T(8,128)(2,1)S(1)}, u32[]{:S(2)}, u32[]{:S(2)}) collective-permute-start(bf16[32,2048]{1,0:T(8,128)(2,1)S(1)} %get-tuple-element.46), channel_id=1, source_target_pairs={{0,112},{16,0},{32,16},{48,32},{64,48},{80,64},{96,80},{112,96},{1... | collective-permute-start | bytes 393224 | tf_op jit(solution)/shard_map/ppermute | solution.py:42
  96.9 6.2 %collective-permute-start.30 = (bf16[32,2048]{1,0:T(8,128)(2,1)S(1)}, bf16[32,2048]{1,0:T(8,128)(2,1)S(1)}, u32[]{:S(2)}, u32[]{:S(2)}) collective-permute-start(bf16[32,2048]{1,0:T(8,128)(2,1)S(1)} %get-tuple-element.47), channel_id=1, source_target_pairs={{0,16},{16,32},{32,48},{48,64},{64,80},{80,96},{96,112},{112,0},{1... | collective-permute-start | bytes 393224 | tf_op jit(solution)/shard_map/ppermute | solution.py:42
  97.5 7.1 %collective-permute-start.24 = (bf16[32,2048]{1,0:T(8,128)(2,1)S(1)}, bf16[32,2048]{1,0:T(8,128)(2,1)S(1)}, u32[]{:S(2)}, u32[]{:S(2)}) collective-permute-start(bf16[32,2048]{1,0:T(8,128)(2,1)S(1)} %get-tuple-element.41), channel_id=1, source_target_pairs={{0,16},{16,32},{32,48},{48,64},{64,80},{80,96},{96,112},{112,0},{1... | collective-permute-start | bytes 393224 | tf_op jit(solution)/shard_map/ppermute | solution.py:42
  98.9 5.6 %collective-permute-start.25 = (bf16[32,2048]{1,0:T(8,128)(2,1)S(1)}, bf16[32,2048]{1,0:T(8,128)(2,1)S(1)}, u32[]{:S(2)}, u32[]{:S(2)}) collective-permute-start(bf16[32,2048]{1,0:T(8,128)(2,1)S(1)} %get-tuple-element.42), channel_id=1, source_target_pairs={{0,112},{16,0},{32,16},{48,32},{64,48},{80,64},{96,80},{112,96},{1... | collective-permute-start | bytes 393224 | tf_op jit(solution)/shard_map/ppermute | solution.py:42
  101.4 7.1 %collective-permute-start.18 = (bf16[4,512,128]{2,1,0:T(8,128)(2,1)S(1)}, bf16[4,512,128]{2,1,0:T(8,128)(2,1)S(1)}, u32[]{:S(2)}, u32[]{:S(2)}) collective-permute-start(bf16[4,512,128]{2,1,0:T(8,128)(2,1)S(1)} %slice.12), channel_id=1, source_target_pairs={{0,8},{8,0},{1,9},{9,1},{2,10},{10,2},{3,11},{11,3},{4,12},{12,4},... | collective-permute-start | bytes 1572872 | tf_op jit(solution)/shard_map/ppermute | solution.py:38
  103.2 6.6 %copy-start = (bf16[512,2048]{1,0:T(8,128)(2,1)S(1)}, bf16[512,2048]{1,0:T(8,128)(2,1)}, u32[]{:S(2)}) copy-start(bf16[512,2048]{1,0:T(8,128)(2,1)} %act_ref.3) | copy-start | bytes 6291460
  103.2 9.7 %collective-permute-start.33 = (bf16[32,2048]{1,0:T(8,128)(2,1)S(1)}, bf16[32,2048]{1,0:T(8,128)(2,1)S(1)}, u32[]{:S(2)}, u32[]{:S(2)}) collective-permute-start(bf16[32,2048]{1,0:T(8,128)(2,1)S(1)} %get-tuple-element.51), channel_id=1, source_target_pairs={{0,16},{16,32},{32,48},{48,64},{64,80},{80,96},{96,112},{112,0},{1... | collective-permute-start | bytes 393224 | tf_op jit(solution)/shard_map/ppermute | solution.py:42
  104.6 8.3 %collective-permute-start.32 = (bf16[32,2048]{1,0:T(8,128)(2,1)S(1)}, bf16[32,2048]{1,0:T(8,128)(2,1)S(1)}, u32[]{:S(2)}, u32[]{:S(2)}) collective-permute-start(bf16[32,2048]{1,0:T(8,128)(2,1)S(1)} %get-tuple-element.50), channel_id=1, source_target_pairs={{0,112},{16,0},{32,16},{48,32},{64,48},{80,64},{96,80},{112,96},{1... | collective-permute-start | bytes 393224 | tf_op jit(solution)/shard_map/ppermute | solution.py:42
  107.7 9.8 %collective-permute-start.31 = (bf16[32,2048]{1,0:T(8,128)(2,1)S(1)}, bf16[32,2048]{1,0:T(8,128)(2,1)S(1)}, u32[]{:S(2)}, u32[]{:S(2)}) collective-permute-start(bf16[32,2048]{1,0:T(8,128)(2,1)S(1)} %get-tuple-element.48), channel_id=1, source_target_pairs={{0,112},{16,0},{32,16},{48,32},{64,48},{80,64},{96,80},{112,96},{1... | collective-permute-start | bytes 393224 | tf_op jit(solution)/shard_map/ppermute | solution.py:42
  108.5 9.0 %collective-permute-start.26 = (bf16[32,2048]{1,0:T(8,128)(2,1)S(1)}, bf16[32,2048]{1,0:T(8,128)(2,1)S(1)}, u32[]{:S(2)}, u32[]{:S(2)}) collective-permute-start(bf16[32,2048]{1,0:T(8,128)(2,1)S(1)} %get-tuple-element.43), channel_id=1, source_target_pairs={{0,16},{16,32},{32,48},{48,64},{64,80},{80,96},{96,112},{112,0},{1... | collective-permute-start | bytes 393224 | tf_op jit(solution)/shard_map/ppermute | solution.py:42
  112.9 5.1 %collective-permute-start.34 = (bf16[32,2048]{1,0:T(8,128)(2,1)S(1)}, bf16[32,2048]{1,0:T(8,128)(2,1)S(1)}, u32[]{:S(2)}, u32[]{:S(2)}) collective-permute-start(bf16[32,2048]{1,0:T(8,128)(2,1)S(1)} %add_convert_fusion), channel_id=1, source_target_pairs={{0,128},{128,0},{1,129},{129,1},{2,130},{130,2},{3,131},{131,3},{4... | collective-permute-start | bytes 393224 | tf_op jit(solution)/shard_map/ppermute | solution.py:38

commit v5 on v4

--- a/solution.py
+++ b/solution.py
@@ -14,6 +14,7 @@
 BF16, F32 = jnp.bfloat16, jnp.float32
 ORDER = [4, 3, -3, 2, -2, 1, -1, 0]
 KEYS = [(s, d) for d in ORDER for s in (0, 1)]
+LATE = 6
 VMEM = pl.BlockSpec(memory_space=pltpu.VMEM)
 ANY = pl.BlockSpec(memory_space=pl.ANY)
 PARAMS = pltpu.CompilerParams(vmem_limit_bytes=16 * 1024 * 1024)
@@ -38,8 +39,12 @@
     return lax.ppermute(value, axis, [(0, 1), (1, 0)])
 
 
-def shift(value, step):
-    return lax.ppermute(value, "z", [(i, (i + step) % 8) for i in range(8)])
+def even(value):
+    return lax.ppermute(value, "z", [(i, i ^ 1) for i in range(8)])
+
+
+def odd(value):
+    return lax.ppermute(value, "z", [(i, ((i - 1) ^ 1) + 1 & 7) for i in range(8)])
 
 
 def exchange(value):
@@ -50,41 +55,68 @@
     return lax.optimization_barrier((value, *others))[0]
 
 
-def score_kernel(mine_ref, other_ref, *refs):
-    blocks, out_ref, joined_ref = refs[:16], refs[-2], refs[-1]
-    for i in range(16):
-        joined_ref[i * 32 : i * 32 + 32, :] = blocks[i][...]
+def early_kernel(mine_ref, other_ref, *refs):
+    *blocks, part_ref, joined_ref = refs
+    for i, block in enumerate(blocks):
+        joined_ref[LATE * 32 + i * 32 : LATE * 32 + i * 32 + 32, :] = block[...]
     for i, ref in enumerate((mine_ref, other_ref)):
         for k in range(2):
-            part = lax.dot_general(
+            part_ref[i * 2 + k] = lax.dot_general(
+                joined_ref[LATE * 32 :, :],
+                ref[k * 256 : k * 256 + 256, :],
+                (((1,), (1,)), ((), ())),
+                preferred_element_type=F32,
+            )
+
+
+def score_kernel(mine_ref, other_ref, early_ref, _, *refs):
+    *blocks, out_ref, joined_ref = refs
+    for i, block in enumerate(blocks):
+        joined_ref[i * 32 : i * 32 + 32, :] = block[...]
+    for i, ref in enumerate((mine_ref, other_ref)):
+        for k in range(2):
+            early = early_ref[i * 2 + k]
+            late = lax.dot_general(
                 joined_ref[...],
                 ref[k * 256 : k * 256 + 256, :],
                 (((1,), (1,)), ((), ())),
                 preferred_element_type=F32,
             )
-            most, least = jnp.max(part, axis=0, keepdims=True), jnp.min(part, axis=0, keepdims=True)
+            most = jnp.maximum(jnp.max(early, axis=0, keepdims=True), jnp.max(late, axis=0, keepdims=True))
+            least = jnp.minimum(jnp.min(early, axis=0, keepdims=True), jnp.min(late, axis=0, keepdims=True))
             halves = jnp.round(most + least)
             centre = halves * 0.5
             reach = jnp.maximum(most - centre, centre - least)
             step = jnp.maximum(jnp.ceil(reach * (2.0**17 / 32767)), 1.0)
-            code = jnp.round((part - centre) * (2.0**17 / step))
+            scale = 2.0**17 / step
             row = lax.broadcasted_iota(jnp.int32, (16, 256), 0)
             extra = jnp.where(row == 0, halves, jnp.where(row == 1, step, 0.0))
             for n in range(2):
                 columns = slice(n * 128, n * 128 + 128)
                 at = i * 4 + k * 2 + n
-                out_ref[at, :512, :] = code[:, columns].astype(jnp.int32).astype(jnp.int16)
+                for start, part in ((0, late), (LATE * 32, early)):
+                    code = jnp.round((part[:, columns] - centre[:, columns]) * scale[:, columns])
+                    out_ref[at, start : start + part.shape[0], :] = code.astype(jnp.int32).astype(jnp.int16)
                 out_ref[at, 512:, :] = extra[:, columns].astype(jnp.int32).astype(jnp.int16)
 
 
 def partial_scores(mine, other, blocks):
+    early, joined = pl.pallas_call(
+        early_kernel,
+        out_shape=(shape((4, 512 - LATE * 32, 256), F32), shape((512, 2048), BF16)),
+        in_specs=[VMEM] * (18 - LATE),
+        out_specs=(VMEM, VMEM),
+        compiler_params=PARAMS,
+    )(mine, other, *blocks[LATE:])
     return pl.pallas_call(
         score_kernel,
         out_shape=(shape((8, 528, 128), jnp.int16), shape((512, 2048), BF16)),
-        in_specs=[VMEM] * 18,
-        out_specs=(VMEM, VMEM),
-        compiler_params=PARAMS,
-    )(mine, other, *blocks)
+        grid=(1,),
+        in_specs=[VMEM] * 3 + [ANY] + [VMEM] * LATE,
+        out_specs=(VMEM, pl.BlockSpec((LATE * 32, 2048), lambda j: (0, 0))),
+        input_output_aliases={3: 1},
+        compiler_params=PARAMS,
+    )(mine, other, early, joined, *blocks[:LATE])
 
 
 def grad_kernel(pieces_ref, norm_ref, other_norm_ref, at_ref, other_at_ref, out_ref):
@@ -103,6 +135,7 @@
     place = lax.broadcasted_iota(jnp.int32, (512, 128), 0)
     turn = place >> 6
     ahead = jnp.where((turn & 1) == 0, 4 + (turn >> 1), (7 - turn) >> 1)
+    ahead = jnp.where((z & 1) == 0, ahead, 8 - ahead)
     ident = ((y + (place >> 5)) & 1) * 512 + ((z + ahead) & 7) * 64 + core * 32 + (place & 31)
     onehot = (positive == ident).astype(F32)
     grad = (jnp.exp(scores * FACTOR - norm) - onehot) * (8.0 * FACTOR)
@@ -143,21 +176,25 @@
     )(grad, mine, other)
 
 
-def add_kernel(places, *refs):
-    n = len(places)
-    for i, place in enumerate(places):
-        total = refs[2 * i][place] + refs[2 * i + 1][...].astype(F32)
-        refs[2 * n + i][...] = total.astype(BF16)
+def add_kernel(items, *refs):
+    outs = refs[len(refs) - len(items) :]
+    at = 0
+    for (place, n), out in zip(items, outs):
+        total = refs[at][place]
+        for come in refs[at + 1 : at + 1 + n]:
+            total = total + come[...].astype(F32)
+        out[...] = total.astype(BF16)
+        at += 1 + n
 
 
 def add_blocks(*items):
     return pl.pallas_call(
-        functools.partial(add_kernel, [place for _, place, _ in items]),
+        functools.partial(add_kernel, [(place, len(come)) for _, place, *come in items]),
         out_shape=(shape((32, 2048), BF16),) * len(items),
-        in_specs=[VMEM] * (2 * len(items)),
+        in_specs=[VMEM] * sum(len(item) - 1 for item in items),
         out_specs=(VMEM,) * len(items),
         compiler_params=PARAMS,
-    )(*[a for sums, _, come in items for a in (sums, come)])
+    )(*[a for sums, _, *come in items for a in (sums, *come)])
 
 
 def query_kernel(first, act_ref, own_grad_ref, other_grad_ref, own_ref, other_ref, *refs):
@@ -201,16 +238,16 @@
     blocks = {(0, 0): own, (1, 0): swap(own, "ylo")}
     for d in range(1, 4):
         for s in (0, 1):
-            blocks[s, -d] = shift(blocks[s, 1 - d], 1)
-            blocks[s, d] = shift(blocks[s, d - 1], -1)
-    blocks[0, 4] = shift(blocks[0, -3], 1)
-    blocks[1, 4] = shift(blocks[1, 3], -1)
+            blocks[s, d], blocks[s, -d] = even(blocks[s, 1 - d]), odd(blocks[s, d - 1])
+    blocks[0, 4], blocks[1, 4] = even(blocks[0, -3]), odd(blocks[1, 3])
 
     mine = saturate(query_act)
     other = swap(mine, "core")
     norm, other_norm = normalizer.reshape(4, 128), swap(normalizer, "core").reshape(4, 128)
     at, other_at = positive.reshape(4, 128), swap(positive, "core").reshape(4, 128)
-    other, norm, other_norm, at, other_at = lax.optimization_barrier((other, norm, other_norm, at, other_at))
+    blocks[0, 4], norm, other_norm, at, other_at = lax.optimization_barrier(
+        (blocks[0, 4], norm, other_norm, at, other_at)
+    )
 
     part, joined = partial_scores(mine, other, [blocks[k] for k in KEYS])
     grad = exchange(score_grad(exchange(part), norm, other_norm, at, other_at))
@@ -219,16 +256,18 @@
     query_args = (query_act, grad, swap(grad[4:], "core"), joined, swap(joined, "core"))
     query_begun = query_grads(*query_args)
 
-    far, a0, a1, b0, b1 = passage_sums(grad, mine, other, 0, [0, 1, 4, 3])
+    far, a0, a1, b0, b1 = passage_sums(grad, mine, other, 0, [0, 1, 2, 5])
     (near,) = passage_sums(grad, mine, other, 256, [])
     place = {k: (far, i) if i < 8 else (near, i - 8) for i, k in enumerate(KEYS)}
-    a0, a1, b0, b1 = shift(a0, 1), shift(a1, -1), shift(b0, -1), shift(b1, 1)
-    for d in (3, 2, 1):
+    a0, a1, b0, b1 = even(a0), odd(a1), even(b0), odd(b1)
+    for d in (-3, 2, -1):
+        ways = (odd, even) if d < 0 else (even, odd)
         a0, a1 = add_blocks((*place[0, d], a0), (*place[1, -d], a1))
-        a0, a1 = shift(a0, 1), shift(a1, -1)
-        if d > 1:
-            b0, b1 = add_blocks((*place[0, 1 - d], b0), (*place[1, d - 1], b1))
-            b0, b1 = shift(b0, -1), shift(b1, 1)
+        a0, a1 = ways[0](a0), ways[1](a1)
+        if d != -1:
+            d = -2 if d < 0 else 1
+            b0, b1 = add_blocks((*place[0, d], b0), (*place[1, -d], b1))
+            b0, b1 = ways[0](b0), ways[1](b1)
     sums = [near[place[s, 0][1]] for s in (0, 1)]
     theirs = after(sums[1], query_begun) + a1.astype(F32) + b1.astype(F32)
     theirs = swap(theirs.astype(BF16), "ylo").astype(F32)

time: 119 us -> 116 us (0.975)
  blocking collectives: 36.6 us -> 34.2 us
    ppermute x7, waiting for transfers between devices: 5.15 us -> 0.57 us  [swap(): return lax.ppermute(value, axis, [(0, 1), (1, 0)])]
    ppermute x28, waiting for transfers between devices: 15.2 us -> 19.7 us  [the longest x14 12.5 us: odd(): lax.ppermute(value, 'z', [(i, (i - 1 ^ 1) + 1 & 7) for i in range(8)])]
    all_to_all x2, blocking collectives: 36.6 us -> 34.2 us  [exchange(): return lax.all_to_all(value, REP, split_axis=0, concat_axis=0)]
    pallas_call x5 -> x6, Pallas kernels: 0.23 us -> 1.8 us  [the longest x1 1.56 us: partial_scores(): pl.pallas_call(early_kernel, out_shape=(shape((4, 512 - LATE * 32, 256),...]
  transfers between devices with their start and end apart: 35 -> 35, of which waited for: 14 -> 17; matrix products, arithmetic and copies ran while one was open for 0% -> 0% of each run, Pallas kernels for 7% -> 9%
where the time goes in v5:
time: 116 us
  starting transfers between devices  43.5 us (38%)
  blocking collectives  34.2 us (29%)
  waiting for transfers between devices  20.3 us (18%)
  Pallas kernels  13.1 us (11%)
  other arithmetic  3.99 us (3%)
    all_to_all x2, blocking collectives, exchange(): return lax.all_to_all(value, REP, split_axis=0, concat_axis=0)  34.2 us
    ppermute x14, starting transfers between devices, odd(): lax.ppermute(value, 'z', [(i, (i - 1 ^ 1) + 1 & 7) for i in range(8)])  28.2 us
    ppermute x14, waiting for transfers between devices, odd(): lax.ppermute(value, 'z', [(i, (i - 1 ^ 1) + 1 & 7) for i in range(8)])  12.5 us
    ppermute x14, starting transfers between devices, even(): return lax.ppermute(value, 'z', [(i, i ^ 1) for i in range(8)])  11 us
    ppermute x14, waiting for transfers between devices, even(): return lax.ppermute(value, 'z', [(i, i ^ 1) for i in range(8)])  7.2 us
    pallas_call x2, Pallas kernels, query_grads(): pl.pallas_call(functools.partial(query_kernel, first), out_shape=shape((5...  6.16 us
    ppermute x7, starting transfers between devices, swap(): return lax.ppermute(value, axis, [(0, 1), (1, 0)])  4.31 us
    convert_element_type x2, other arithmetic, saturate(): jnp.where(wide < 2.0 ** (-8), small, jnp.log(1.0 + wide)).astype(BF16)  3.17 us
  transfers between devices with their start and end apart: 35, of which 17 were waited for; matrix products, arithmetic and copies ran while one was open for 0% of the time, Pallas kernels for 9%

profile of v5, /device:TPU:8, one launch (start us, length us, event | category | flops | bytes accessed | tf_op | source)
XLA Modules:
  0.0 116.0 jit_solution(15196208706644150400)
XLA Ops:
  0.7 3.1 %fusion.1.mine_ref = bf16[512,2048]{1,0:T(8,128)(2,1)S(1)} fusion(bf16[512,2048]{1,0:T(8,128)(2,1)} %act_ref.3), kind=kLoop, calls=%fused_computation.2 | loop fusion | flops 9437184 | bytes 4194304 | tf_op jit(solution)/shard_map/convert_element_type | solution.py:30
  4.0 2.3 %collective-permute-start.3 = (bf16[32,2048]{1,0:T(8,128)(2,1)S(1)}, bf16[32,2048]{1,0:T(8,128)(2,1)S(1)}, u32[]{:S(2)}, u32[]{:S(2)}) collective-permute-start(bf16[32,2048]{1,0:T(8,128)(2,1)S(1)} %fusion.8.refs_8_), channel_id=1, source_target_pairs={{0,128},{128,0},{1,129},{129,1},{2,130},{130,2},{3,131},{131,3},{4... | collective-permute-start | bytes 393224 | tf_op jit(solution)/shard_map/ppermute | solution.py:39
  6.2 4.1 %collective-permute-start.1 = (bf16[32,2048]{1,0:T(8,128)(2,1)S(1)}, bf16[32,2048]{1,0:T(8,128)(2,1)S(1)}, u32[]{:S(2)}, u32[]{:S(2)}) collective-permute-start(bf16[32,2048]{1,0:T(8,128)(2,1)S(1)} %fusion.8.refs_8_), channel_id=1, source_target_pairs={{0,112},{16,32},{32,16},{48,64},{64,48},{80,96},{96,80},{112,0},{1... | collective-permute-start | bytes 393224 | tf_op jit(solution)/shard_map/ppermute | solution.py:47
  10.4 1.5 %collective-permute-start.8 = (bf16[32,2048]{1,0:T(8,128)(2,1)S(1)}, bf16[32,2048]{1,0:T(8,128)(2,1)S(1)}, u32[]{:S(2)}, u32[]{:S(2)}) collective-permute-start(bf16[32,2048]{1,0:T(8,128)(2,1)S(1)} %collective-permute-done.3.refs_9_), channel_id=1, source_target_pairs={{0,16},{16,0},{32,48},{48,32},{64,80},{80,64},{96,112},{112,96},{1... | collective-permute-start | bytes 393224 | tf_op jit(solution)/shard_map/ppermute | solution.py:43
  11.9 0.5 collective-permute-start.12
  12.4 1.8 %collective-permute-done.1.refs_6_ = bf16[32,2048]{1,0:T(8,128)(2,1)S(1)} collective-permute-done((bf16[32,2048]{1,0:T(8,128)(2,1)S(1)}, bf16[32,2048]{1,0:T(8,128)(2,1)S(1)}, u32[]{:S(2)}, u32[]{:S(2)}) %collective-permute-start.1) | collective-permute-done | bytes 131104 | tf_op jit(solution)/shard_map/ppermute | solution.py:47
  14.2 2.0 %collective-permute-start.6 = (bf16[32,2048]{1,0:T(8,128)(2,1)S(1)}, bf16[32,2048]{1,0:T(8,128)(2,1)S(1)}, u32[]{:S(2)}, u32[]{:S(2)}) collective-permute-start(bf16[32,2048]{1,0:T(8,128)(2,1)S(1)} %fusion.8.refs_8_), channel_id=1, source_target_pairs={{0,16},{16,0},{32,48},{48,32},{64,80},{80,64},{96,112},{112,96},{1... | collective-permute-start | bytes 393224 | tf_op jit(solution)/shard_map/ppermute | solution.py:43
  16.2 3.1 %collective-permute-start.4 = (bf16[32,2048]{1,0:T(8,128)(2,1)S(1)}, bf16[32,2048]{1,0:T(8,128)(2,1)S(1)}, u32[]{:S(2)}, u32[]{:S(2)}) collective-permute-start(bf16[32,2048]{1,0:T(8,128)(2,1)S(1)} %collective-permute-done.3.refs_9_), channel_id=1, source_target_pairs={{0,112},{16,32},{32,16},{48,64},{64,48},{80,96},{96,80},{112,0},{1... | collective-permute-start | bytes 393224 | tf_op jit(solution)/shard_map/ppermute | solution.py:47
  19.4 2.5 %collective-permute-start.9 = (bf16[32,2048]{1,0:T(8,128)(2,1)S(1)}, bf16[32,2048]{1,0:T(8,128)(2,1)S(1)}, u32[]{:S(2)}, u32[]{:S(2)}) collective-permute-start(bf16[32,2048]{1,0:T(8,128)(2,1)S(1)} %collective-permute-done.8.refs_5_), channel_id=1, source_target_pairs={{0,112},{16,32},{32,16},{48,64},{64,48},{80,96},{96,80},{112,0},{1... | collective-permute-start | bytes 393224 | tf_op jit(solution)/shard_map/ppermute | solution.py:47
  21.8 2.8 %collective-permute-start.10 = (bf16[32,2048]{1,0:T(8,128)(2,1)S(1)}, bf16[32,2048]{1,0:T(8,128)(2,1)S(1)}, u32[]{:S(2)}, u32[]{:S(2)}) collective-permute-start(bf16[32,2048]{1,0:T(8,128)(2,1)S(1)} %collective-permute-done.2.refs_0_), channel_id=1, source_target_pairs={{0,112},{16,32},{32,16},{48,64},{64,48},{80,96},{96,80},{112,0},{1... | collective-permute-start | bytes 393224 | tf_op jit(solution)/shard_map/ppermute | solution.py:47
  24.6 1.9 %collective-permute-start.7 = (bf16[32,2048]{1,0:T(8,128)(2,1)S(1)}, bf16[32,2048]{1,0:T(8,128)(2,1)S(1)}, u32[]{:S(2)}, u32[]{:S(2)}) collective-permute-start(bf16[32,2048]{1,0:T(8,128)(2,1)S(1)} %collective-permute-done.6.refs_4_), channel_id=1, source_target_pairs={{0,112},{16,32},{32,16},{48,64},{64,48},{80,96},{96,80},{112,0},{1... | collective-permute-start | bytes 393224 | tf_op jit(solution)/shard_map/ppermute | solution.py:47
  26.9 1.7 %collective-permute-start.14 = (bf16[32,2048]{1,0:T(8,128)(2,1)S(1)}, bf16[32,2048]{1,0:T(8,128)(2,1)S(1)}, u32[]{:S(2)}, u32[]{:S(2)}) collective-permute-start(bf16[32,2048]{1,0:T(8,128)(2,1)S(1)} %collective-permute-done.9.refs_3_), channel_id=1, source_target_pairs={{0,16},{16,0},{32,48},{48,32},{64,80},{80,64},{96,112},{112,96},{1... | collective-permute-start | bytes 393224 | tf_op jit(solution)/shard_map/ppermute | solution.py:43
  28.6 1.0 collective-permute-done.10.refs_4_
  29.6 1.4 %collective-permute-done.7.refs_2_ = bf16[32,2048]{1,0:T(8,128)(2,1)S(1)} collective-permute-done((bf16[32,2048]{1,0:T(8,128)(2,1)S(1)}, bf16[32,2048]{1,0:T(8,128)(2,1)S(1)}, u32[]{:S(2)}, u32[]{:S(2)}) %collective-permute-start.7) | collective-permute-done | bytes 131104 | tf_op jit(solution)/shard_map/ppermute | solution.py:47
  31.0 0.6 collective-permute-start.16
  31.6 1.4 %collective-permute-done.5.refs_1_ = bf16[32,2048]{1,0:T(8,128)(2,1)S(1)} collective-permute-done((bf16[32,2048]{1,0:T(8,128)(2,1)S(1)}, bf16[32,2048]{1,0:T(8,128)(2,1)S(1)}, u32[]{:S(2)}, u32[]{:S(2)}) %collective-permute-start.5) | collective-permute-done | bytes 131104 | tf_op jit(solution)/shard_map/ppermute | solution.py:43
  33.0 1.6 %collective-permute-start.17 = (bf16[32,2048]{1,0:T(8,128)(2,1)S(1)}, bf16[32,2048]{1,0:T(8,128)(2,1)S(1)}, u32[]{:S(2)}, u32[]{:S(2)}) collective-permute-start(bf16[32,2048]{1,0:T(8,128)(2,1)S(1)} %collective-permute-done.5.refs_1_), channel_id=1, source_target_pairs={{0,112},{16,32},{32,16},{48,64},{64,48},{80,96},{96,80},{112,0},{1... | collective-permute-start | bytes 393224 | tf_op jit(solution)/shard_map/ppermute | solution.py:47
  34.5 1.2 %collective-permute-done.14.refs_3_ = bf16[32,2048]{1,0:T(8,128)(2,1)S(1)} collective-permute-done((bf16[32,2048]{1,0:T(8,128)(2,1)S(1)}, bf16[32,2048]{1,0:T(8,128)(2,1)S(1)}, u32[]{:S(2)}, u32[]{:S(2)}) %collective-permute-start.14) | collective-permute-done | bytes 131104 | tf_op jit(solution)/shard_map/ppermute | solution.py:43
  36.2 1.6 %collective-permute-done.11.refs_0_ = bf16[32,2048]{1,0:T(8,128)(2,1)S(1)} collective-permute-done((bf16[32,2048]{1,0:T(8,128)(2,1)S(1)}, bf16[32,2048]{1,0:T(8,128)(2,1)S(1)}, u32[]{:S(2)}, u32[]{:S(2)}) %collective-permute-start.11) | collective-permute-done | bytes 131104 | tf_op jit(solution)/shard_map/ppermute | solution.py:43
  37.8 1.6 %shard_map.59 = (f32[4,320,256]{2,1,0:T(8,128)S(1)}, bf16[512,2048]{1,0:T(8,128)(2,1)S(1)}) custom-call(bf16[512,2048]{1,0:T(8,128)(2,1)S(1)} %fusion.1.mine_ref, bf16[512,2048]{1,0:T(8,128)(2,1)S(1)} %collective-permute-done.other_ref, bf16[32,2048]{1,0:T(8,128)(2,1)S(1)} %collective-permute-done.2.refs_0_, ...), custom_call_target="tpu_custom_call" | custom-call | tf_op jit(solution)/shard_map/pallas_call | solution.py:104
  39.4 2.5 %collective-permute-done.15.refs_1_ = bf16[32,2048]{1,0:T(8,128)(2,1)S(1)} collective-permute-done((bf16[32,2048]{1,0:T(8,128)(2,1)S(1)}, bf16[32,2048]{1,0:T(8,128)(2,1)S(1)}, u32[]{:S(2)}, u32[]{:S(2)}) %collective-permute-start.15) | collective-permute-done | bytes 131104 | tf_op jit(solution)/shard_map/ppermute | solution.py:47
  41.9 2.0 %shard_map.60 = (s16[8,528,128]{2,1,0:T(8,128)(2,1)S(1)}, bf16[512,2048]{1,0:T(8,128)(2,1)S(1)}) custom-call(bf16[512,2048]{1,0:T(8,128)(2,1)S(1)} %fusion.1.mine_ref, bf16[512,2048]{1,0:T(8,128)(2,1)S(1)} %collective-permute-done.other_ref, f32[4,320,256]{2,1,0:T(8,128)S(1)} %get-tuple-element.29.early_ref, ...), custom_call_target="tpu_custom_call", output_to_operand_aliasing={{1}: (3, {})} | custom-call | tf_op jit(solution)/shard_map/pallas_call | solution.py:111
  44.0 19.2 %all_to_all.10.pieces_ref = s16[8,528,128]{2,1,0:T(8,128)(2,1)S(1)} all-to-all(s16[8,528,128]{2,1,0:T(8,128)(2,1)S(1)} %get-tuple-element.32), channel_id=1, replica_groups=mesh['ylo'=2,'z'=8,'core'=2,'yhi'=2,'x'=4] {'x','yhi'}, dimensions={0} | all-to-all | bytes 2162688 | tf_op jit(solution)/shard_map/all_to_all | solution.py:51
  63.1 0.6 shard_map.61
  63.7 15.1 %all_to_all.11.own_grad_ref.grad_ref = bf16[8,512,128]{2,1,0:T(8,128)(2,1)S(1)} all-to-all(bf16[8,512,128]{2,1,0:T(8,128)(2,1)S(1)} %shard_map.61), channel_id=1, replica_groups=mesh['ylo'=2,'z'=8,'core'=2,'yhi'=2,'x'=4] {'x','yhi'}, dimensions={0} | all-to-all | bytes 2097152 | tf_op jit(solution)/shard_map/all_to_all | solution.py:51
  78.8 1.2 %shard_map.65 = (f32[8,32,2048]{2,1,0:T(8,128)S(1)}, bf16[32,2048]{1,0:T(8,128)(2,1)S(1)}, bf16[32,2048]{1,0:T(8,128)(2,1)S(1)}, bf16[32,2048]{1,0:T(8,128)(2,1)S(1)}, bf16[32,2048]{1,0:T(8,128)(2,1)S(1)}) custom-call(bf16[8,512,128]{2,1,0:T(8,128)(2,1)S(1)} %all_to_all.11.own_grad_ref.grad_ref, bf16[512,2048]{1,0:T(8,128)(2,1)S(1)} %fusion.1.mine_ref, ...), custom_call_target="tpu_custom_call" | custom-call | tf_op jit(solution)/shard_map/pallas_call | solution.py:170
  80.1 1.3 %collective-permute-start.20 = (bf16[32,2048]{1,0:T(8,128)(2,1)S(1)}, bf16[32,2048]{1,0:T(8,128)(2,1)S(1)}, u32[]{:S(2)}, u32[]{:S(2)}) collective-permute-start(bf16[32,2048]{1,0:T(8,128)(2,1)S(1)} %get-tuple-element.41), channel_id=1, source_target_pairs={{0,16},{16,0},{32,48},{48,32},{64,80},{80,64},{96,112},{112,96},{1... | collective-permute-start | bytes 393224 | tf_op jit(solution)/shard_map/ppermute | solution.py:43
  81.3 1.5 %collective-permute-start.21 = (bf16[32,2048]{1,0:T(8,128)(2,1)S(1)}, bf16[32,2048]{1,0:T(8,128)(2,1)S(1)}, u32[]{:S(2)}, u32[]{:S(2)}) collective-permute-start(bf16[32,2048]{1,0:T(8,128)(2,1)S(1)} %get-tuple-element.42), channel_id=1, source_target_pairs={{0,112},{16,32},{32,16},{48,64},{64,48},{80,96},{96,80},{112,0},{1... | collective-permute-start | bytes 393224 | tf_op jit(solution)/shard_map/ppermute | solution.py:47
  83.2 1.5 %collective-permute-start.28 = (bf16[32,2048]{1,0:T(8,128)(2,1)S(1)}, bf16[32,2048]{1,0:T(8,128)(2,1)S(1)}, u32[]{:S(2)}, u32[]{:S(2)}) collective-permute-start(bf16[32,2048]{1,0:T(8,128)(2,1)S(1)} %get-tuple-element.49), channel_id=1, source_target_pairs={{0,112},{16,32},{32,16},{48,64},{64,48},{80,96},{96,80},{112,0},{1... | collective-permute-start | bytes 393224 | tf_op jit(solution)/shard_map/ppermute | solution.py:47
  84.7 1.8 %collective-permute-done.20.refs_1_ = bf16[32,2048]{1,0:T(8,128)(2,1)S(1)} collective-permute-done((bf16[32,2048]{1,0:T(8,128)(2,1)S(1)}, bf16[32,2048]{1,0:T(8,128)(2,1)S(1)}, u32[]{:S(2)}, u32[]{:S(2)}) %collective-permute-start.20) | collective-permute-done | bytes 131104 | tf_op jit(solution)/shard_map/ppermute | solution.py:43
  86.4 2.4 %collective-permute-done.21.refs_3_ = bf16[32,2048]{1,0:T(8,128)(2,1)S(1)} collective-permute-done((bf16[32,2048]{1,0:T(8,128)(2,1)S(1)}, bf16[32,2048]{1,0:T(8,128)(2,1)S(1)}, u32[]{:S(2)}, u32[]{:S(2)}) %collective-permute-start.21) | collective-permute-done | bytes 131104 | tf_op jit(solution)/shard_map/ppermute | solution.py:47
  88.9 1.6 %collective-permute-start.22 = (bf16[32,2048]{1,0:T(8,128)(2,1)S(1)}, bf16[32,2048]{1,0:T(8,128)(2,1)S(1)}, u32[]{:S(2)}, u32[]{:S(2)}) collective-permute-start(bf16[32,2048]{1,0:T(8,128)(2,1)S(1)} %get-tuple-element.43), channel_id=1, source_target_pairs={{0,112},{16,32},{32,16},{48,64},{64,48},{80,96},{96,80},{112,0},{1... | collective-permute-start | bytes 393224 | tf_op jit(solution)/shard_map/ppermute | solution.py:47
  90.5 1.2 %shard_map.64.refs_2_.refs_0_ = f32[8,32,2048]{2,1,0:T(8,128)S(1)} custom-call(bf16[8,512,128]{2,1,0:T(8,128)(2,1)S(1)} %all_to_all.11.own_grad_ref.grad_ref, bf16[512,2048]{1,0:T(8,128)(2,1)S(1)} %fusion.1.mine_ref, bf16[512,2048]{1,0:T(8,128)(2,1)S(1)} %collective-permute-done.other_ref), custom_call_target="tpu_custom_call" | custom-call | tf_op jit(solution)/shard_map/pallas_call | solution.py:170
  91.9 1.8 %collective-permute-start.29 = (bf16[32,2048]{1,0:T(8,128)(2,1)S(1)}, bf16[32,2048]{1,0:T(8,128)(2,1)S(1)}, u32[]{:S(2)}, u32[]{:S(2)}) collective-permute-start(bf16[32,2048]{1,0:T(8,128)(2,1)S(1)} %get-tuple-element.50), channel_id=1, source_target_pairs={{0,112},{16,32},{32,16},{48,64},{64,48},{80,96},{96,80},{112,0},{1... | collective-permute-start | bytes 393224 | tf_op jit(solution)/shard_map/ppermute | solution.py:47
  93.7 1.3 %collective-permute-start.30 = (bf16[32,2048]{1,0:T(8,128)(2,1)S(1)}, bf16[32,2048]{1,0:T(8,128)(2,1)S(1)}, u32[]{:S(2)}, u32[]{:S(2)}) collective-permute-start(bf16[32,2048]{1,0:T(8,128)(2,1)S(1)} %get-tuple-element.51), channel_id=1, source_target_pairs={{0,16},{16,0},{32,48},{48,32},{64,80},{80,64},{96,112},{112,96},{1... | collective-permute-start | bytes 393224 | tf_op jit(solution)/shard_map/ppermute | solution.py:43
  95.0 1.1 collective-permute-done.22.refs_1_
  96.8 1.8 %collective-permute-start.25 = (bf16[32,2048]{1,0:T(8,128)(2,1)S(1)}, bf16[32,2048]{1,0:T(8,128)(2,1)S(1)}, u32[]{:S(2)}, u32[]{:S(2)}) collective-permute-start(bf16[32,2048]{1,0:T(8,128)(2,1)S(1)} %get-tuple-element.46), channel_id=1, source_target_pairs={{0,112},{16,32},{32,16},{48,64},{64,48},{80,96},{96,80},{112,0},{1... | collective-permute-start | bytes 393224 | tf_op jit(solution)/shard_map/ppermute | solution.py:47
  99.1 0.6 collective-permute-done.30.refs_3_
  99.8 1.8 %collective-permute-start.33 = (bf16[32,2048]{1,0:T(8,128)(2,1)S(1)}, bf16[32,2048]{1,0:T(8,128)(2,1)S(1)}, u32[]{:S(2)}, u32[]{:S(2)}) collective-permute-start(bf16[32,2048]{1,0:T(8,128)(2,1)S(1)} %get-tuple-element.55), channel_id=1, source_target_pairs={{0,112},{16,32},{32,16},{48,64},{64,48},{80,96},{96,80},{112,0},{1... | collective-permute-start | bytes 393224 | tf_op jit(solution)/shard_map/ppermute | solution.py:47
  101.7 1.3 %collective-permute-done.25.refs_3_ = bf16[32,2048]{1,0:T(8,128)(2,1)S(1)} collective-permute-done((bf16[32,2048]{1,0:T(8,128)(2,1)S(1)}, bf16[32,2048]{1,0:T(8,128)(2,1)S(1)}, u32[]{:S(2)}, u32[]{:S(2)}) %collective-permute-start.25) | collective-permute-done | bytes 131104 | tf_op jit(solution)/shard_map/ppermute | solution.py:47
  103.1 1.1 collective-permute-start.32
  104.3 1.1 collective-permute-start.31
  105.3 1.8 %collective-permute-start.26 = (bf16[32,2048]{1,0:T(8,128)(2,1)S(1)}, bf16[32,2048]{1,0:T(8,128)(2,1)S(1)}, u32[]{:S(2)}, u32[]{:S(2)}) collective-permute-start(bf16[32,2048]{1,0:T(8,128)(2,1)S(1)} %get-tuple-element.47), channel_id=1, source_target_pairs={{0,112},{16,32},{32,16},{48,64},{64,48},{80,96},{96,80},{112,0},{1... | collective-permute-start | bytes 393224 | tf_op jit(solution)/shard_map/ppermute | solution.py:47
  107.1 3.1 %shard_map.62.refs_0_ = bf16[512,2048]{1,0:T(8,128)(2,1)} custom-call(bf16[512,2048]{1,0:T(8,128)(2,1)S(1)} %copy-done, bf16[8,512,128]{2,1,0:T(8,128)(2,1)S(1)} %all_to_all.11.own_grad_ref.grad_ref, bf16[4,512,128]{2,1,0:T(8,128)(2,1)S(1)} %collective-permute-done.18.other_grad_ref, bf16[512,2048]{1,0:T(8,128)(2,1)S(1)} %get-tuple-element.38.own_ref, ...), custom_call_target="tpu_custom_call" | custom-call | tf_op jit(solution)/shard_map/pallas_call | solution.py:224
  110.2 1.4 %collective-permute-start.34 = (bf16[32,2048]{1,0:T(8,128)(2,1)S(1)}, bf16[32,2048]{1,0:T(8,128)(2,1)S(1)}, u32[]{:S(2)}, u32[]{:S(2)}) collective-permute-start(bf16[32,2048]{1,0:T(8,128)(2,1)S(1)} %add_convert_fusion), channel_id=1, source_target_pairs={{0,128},{128,0},{1,129},{129,1},{2,130},{130,2},{3,131},{131,3},{4... | collective-permute-start | bytes 393224 | tf_op jit(solution)/shard_map/ppermute | solution.py:39
  111.6 3.1 %shard_map.63 = bf16[512,2048]{1,0:T(8,128)(2,1)} custom-call(bf16[512,2048]{1,0:T(8,128)(2,1)S(1)} %copy-done, bf16[8,512,128]{2,1,0:T(8,128)(2,1)S(1)} %all_to_all.11.own_grad_ref.grad_ref, bf16[4,512,128]{2,1,0:T(8,128)(2,1)S(1)} %collective-permute-done.18.other_grad_ref, ...), custom_call_target="tpu_custom_call", output_to_operand_aliasing={{}: (5, {})} | custom-call | tf_op jit(solution)/shard_map/pallas_call | solution.py:224
  114.7 0.5 collective-permute-done.34
  115.3 0.8 fusion.11
  (50 shorter events, 2.9 us)
Async XLA Ops:
  0.6 3.2 %copy-start.3 = (bf16[32,2048]{1,0:T(8,128)(2,1)S(1)}, bf16[32,2048]{1,0:T(8,128)(2,1)}, u32[]{:S(2)}) copy-start(bf16[32,2048]{1,0:T(8,128)(2,1)} %param.5) | copy-start | bytes 393220
  0.6 11.2 %copy-start.2 = (s32[512]{0:T(512)S(1)}, s32[512]{0:T(512)}, u32[]{:S(2)}) copy-start(s32[512]{0:T(512)} %param.6) | copy-start | bytes 6148
  0.7 11.2 %copy-start.1 = (f32[512]{0:T(512)S(1)}, f32[512]{0:T(512)}, u32[]{:S(2)}) copy-start(f32[512]{0:T(512)} %param.7) | copy-start | bytes 6148
  3.7 34.1 %collective-permute-start = (bf16[512,2048]{1,0:T(8,128)(2,1)S(1)}, bf16[512,2048]{1,0:T(8,128)(2,1)S(1)}, u32[]{:S(2)}, u32[]{:S(2)}) collective-permute-start(bf16[512,2048]{1,0:T(8,128)(2,1)S(1)} %fusion.1.mine_ref), channel_id=1, source_target_pairs={{0,8},{8,0},{1,9},{9,1},{2,10},{10,2},{3,11},{11,3},{4,12},{12,4},... | collective-permute-start | bytes 6291464 | tf_op jit(solution)/shard_map/ppermute | solution.py:39
  4.0 6.4 %collective-permute-start.3 = (bf16[32,2048]{1,0:T(8,128)(2,1)S(1)}, bf16[32,2048]{1,0:T(8,128)(2,1)S(1)}, u32[]{:S(2)}, u32[]{:S(2)}) collective-permute-start(bf16[32,2048]{1,0:T(8,128)(2,1)S(1)} %fusion.8.refs_8_), channel_id=1, source_target_pairs={{0,128},{128,0},{1,129},{129,1},{2,130},{130,2},{3,131},{131,3},{4... | collective-permute-start | bytes 393224 | tf_op jit(solution)/shard_map/ppermute | solution.py:39
  6.2 8.0 %collective-permute-start.1 = (bf16[32,2048]{1,0:T(8,128)(2,1)S(1)}, bf16[32,2048]{1,0:T(8,128)(2,1)S(1)}, u32[]{:S(2)}, u32[]{:S(2)}) collective-permute-start(bf16[32,2048]{1,0:T(8,128)(2,1)S(1)} %fusion.8.refs_8_), channel_id=1, source_target_pairs={{0,112},{16,32},{32,16},{48,64},{64,48},{80,96},{96,80},{112,0},{1... | collective-permute-start | bytes 393224 | tf_op jit(solution)/shard_map/ppermute | solution.py:47
  10.4 9.0 %collective-permute-start.8 = (bf16[32,2048]{1,0:T(8,128)(2,1)S(1)}, bf16[32,2048]{1,0:T(8,128)(2,1)S(1)}, u32[]{:S(2)}, u32[]{:S(2)}) collective-permute-start(bf16[32,2048]{1,0:T(8,128)(2,1)S(1)} %collective-permute-done.3.refs_9_), channel_id=1, source_target_pairs={{0,16},{16,0},{32,48},{48,32},{64,80},{80,64},{96,112},{112,96},{1... | collective-permute-start | bytes 393224 | tf_op jit(solution)/shard_map/ppermute | solution.py:43
  11.8 2.4 %collective-permute-start.13 = (s32[512]{0:T(512)S(1)}, s32[512]{0:T(512)S(1)}, u32[]{:S(2)}, u32[]{:S(2)}) collective-permute-start(s32[512]{0:T(512)S(1)} %copy-done.2), channel_id=1, source_target_pairs={{0,8},{8,0},{1,9},{9,1},{2,10},{10,2},{3,11},{11,3},{4,12},{12,4},... | collective-permute-start | bytes 6152 | tf_op jit(solution)/shard_map/ppermute | solution.py:39
  11.9 4.4 %collective-permute-start.12 = (f32[512]{0:T(512)S(1)}, f32[512]{0:T(512)S(1)}, u32[]{:S(2)}, u32[]{:S(2)}) collective-permute-start(f32[512]{0:T(512)S(1)} %copy-done.1), channel_id=1, source_target_pairs={{0,8},{8,0},{1,9},{9,1},{2,10},{10,2},{3,11},{11,3},{4,12},{12,4},... | collective-permute-start | bytes 6152 | tf_op jit(solution)/shard_map/ppermute | solution.py:39
  14.2 7.6 %collective-permute-start.2 = (bf16[32,2048]{1,0:T(8,128)(2,1)S(1)}, bf16[32,2048]{1,0:T(8,128)(2,1)S(1)}, u32[]{:S(2)}, u32[]{:S(2)}) collective-permute-start(bf16[32,2048]{1,0:T(8,128)(2,1)S(1)} %collective-permute-done.1.refs_6_), channel_id=1, source_target_pairs={{0,16},{16,0},{32,48},{48,32},{64,80},{80,64},{96,112},{112,96},{1... | collective-permute-start | bytes 393224 | tf_op jit(solution)/shard_map/ppermute | solution.py:43
  14.2 10.4 %collective-permute-start.6 = (bf16[32,2048]{1,0:T(8,128)(2,1)S(1)}, bf16[32,2048]{1,0:T(8,128)(2,1)S(1)}, u32[]{:S(2)}, u32[]{:S(2)}) collective-permute-start(bf16[32,2048]{1,0:T(8,128)(2,1)S(1)} %fusion.8.refs_8_), channel_id=1, source_target_pairs={{0,16},{16,0},{32,48},{48,32},{64,80},{80,64},{96,112},{112,96},{1... | collective-permute-start | bytes 393224 | tf_op jit(solution)/shard_map/ppermute | solution.py:43
  16.2 10.3 %collective-permute-start.4 = (bf16[32,2048]{1,0:T(8,128)(2,1)S(1)}, bf16[32,2048]{1,0:T(8,128)(2,1)S(1)}, u32[]{:S(2)}, u32[]{:S(2)}) collective-permute-start(bf16[32,2048]{1,0:T(8,128)(2,1)S(1)} %collective-permute-done.3.refs_9_), channel_id=1, source_target_pairs={{0,112},{16,32},{32,16},{48,64},{64,48},{80,96},{96,80},{112,0},{1... | collective-permute-start | bytes 393224 | tf_op jit(solution)/shard_map/ppermute | solution.py:47
  19.4 7.5 %collective-permute-start.9 = (bf16[32,2048]{1,0:T(8,128)(2,1)S(1)}, bf16[32,2048]{1,0:T(8,128)(2,1)S(1)}, u32[]{:S(2)}, u32[]{:S(2)}) collective-permute-start(bf16[32,2048]{1,0:T(8,128)(2,1)S(1)} %collective-permute-done.8.refs_5_), channel_id=1, source_target_pairs={{0,112},{16,32},{32,16},{48,64},{64,48},{80,96},{96,80},{112,0},{1... | collective-permute-start | bytes 393224 | tf_op jit(solution)/shard_map/ppermute | solution.py:47
  21.8 7.7 %collective-permute-start.10 = (bf16[32,2048]{1,0:T(8,128)(2,1)S(1)}, bf16[32,2048]{1,0:T(8,128)(2,1)S(1)}, u32[]{:S(2)}, u32[]{:S(2)}) collective-permute-start(bf16[32,2048]{1,0:T(8,128)(2,1)S(1)} %collective-permute-done.2.refs_0_), channel_id=1, source_target_pairs={{0,112},{16,32},{32,16},{48,64},{64,48},{80,96},{96,80},{112,0},{1... | collective-permute-start | bytes 393224 | tf_op jit(solution)/shard_map/ppermute | solution.py:47
  24.6 6.3 %collective-permute-start.7 = (bf16[32,2048]{1,0:T(8,128)(2,1)S(1)}, bf16[32,2048]{1,0:T(8,128)(2,1)S(1)}, u32[]{:S(2)}, u32[]{:S(2)}) collective-permute-start(bf16[32,2048]{1,0:T(8,128)(2,1)S(1)} %collective-permute-done.6.refs_4_), channel_id=1, source_target_pairs={{0,112},{16,32},{32,16},{48,64},{64,48},{80,96},{96,80},{112,0},{1... | collective-permute-start | bytes 393224 | tf_op jit(solution)/shard_map/ppermute | solution.py:47
  26.5 6.5 %collective-permute-start.5 = (bf16[32,2048]{1,0:T(8,128)(2,1)S(1)}, bf16[32,2048]{1,0:T(8,128)(2,1)S(1)}, u32[]{:S(2)}, u32[]{:S(2)}) collective-permute-start(bf16[32,2048]{1,0:T(8,128)(2,1)S(1)} %collective-permute-done.4.refs_7_), channel_id=1, source_target_pairs={{0,16},{16,0},{32,48},{48,32},{64,80},{80,64},{96,112},{112,96},{1... | collective-permute-start | bytes 393224 | tf_op jit(solution)/shard_map/ppermute | solution.py:43
  26.9 8.9 %collective-permute-start.14 = (bf16[32,2048]{1,0:T(8,128)(2,1)S(1)}, bf16[32,2048]{1,0:T(8,128)(2,1)S(1)}, u32[]{:S(2)}, u32[]{:S(2)}) collective-permute-start(bf16[32,2048]{1,0:T(8,128)(2,1)S(1)} %collective-permute-done.9.refs_3_), channel_id=1, source_target_pairs={{0,16},{16,0},{32,48},{48,32},{64,80},{80,64},{96,112},{112,96},{1... | collective-permute-start | bytes 393224 | tf_op jit(solution)/shard_map/ppermute | solution.py:43
  29.6 8.3 %collective-permute-start.11 = (bf16[32,2048]{1,0:T(8,128)(2,1)S(1)}, bf16[32,2048]{1,0:T(8,128)(2,1)S(1)}, u32[]{:S(2)}, u32[]{:S(2)}) collective-permute-start(bf16[32,2048]{1,0:T(8,128)(2,1)S(1)} %collective-permute-done.10.refs_4_), channel_id=1, source_target_pairs={{0,16},{16,0},{32,48},{48,32},{64,80},{80,64},{96,112},{112,96},{1... | collective-permute-start | bytes 393224 | tf_op jit(solution)/shard_map/ppermute | solution.py:43
  31.0 8.4 %collective-permute-start.16 = (bf16[32,2048]{1,0:T(8,128)(2,1)S(1)}, bf16[32,2048]{1,0:T(8,128)(2,1)S(1)}, u32[]{:S(2)}, u32[]{:S(2)}) collective-permute-start(bf16[32,2048]{1,0:T(8,128)(2,1)S(1)} %collective-permute-done.7.refs_2_), channel_id=1, source_target_pairs={{0,16},{16,0},{32,48},{48,32},{64,80},{80,64},{96,112},{112,96},{1... | collective-permute-start | bytes 393224 | tf_op jit(solution)/shard_map/ppermute | solution.py:43
  33.0 6.5 %collective-permute-start.17 = (bf16[32,2048]{1,0:T(8,128)(2,1)S(1)}, bf16[32,2048]{1,0:T(8,128)(2,1)S(1)}, u32[]{:S(2)}, u32[]{:S(2)}) collective-permute-start(bf16[32,2048]{1,0:T(8,128)(2,1)S(1)} %collective-permute-done.5.refs_1_), channel_id=1, source_target_pairs={{0,112},{16,32},{32,16},{48,64},{64,48},{80,96},{96,80},{112,0},{1... | collective-permute-start | bytes 393224 | tf_op jit(solution)/shard_map/ppermute | solution.py:47
  35.8 6.2 %collective-permute-start.15 = (bf16[32,2048]{1,0:T(8,128)(2,1)S(1)}, bf16[32,2048]{1,0:T(8,128)(2,1)S(1)}, u32[]{:S(2)}, u32[]{:S(2)}) collective-permute-start(bf16[32,2048]{1,0:T(8,128)(2,1)S(1)} %collective-permute-done.14.refs_3_), channel_id=1, source_target_pairs={{0,112},{16,32},{32,16},{48,64},{64,48},{80,96},{96,80},{112,0},{1... | collective-permute-start | bytes 393224 | tf_op jit(solution)/shard_map/ppermute | solution.py:47
  78.8 28.3 %collective-permute-start.19 = (bf16[512,2048]{1,0:T(8,128)(2,1)S(1)}, bf16[512,2048]{1,0:T(8,128)(2,1)S(1)}, u32[]{:S(2)}, u32[]{:S(2)}) collective-permute-start(bf16[512,2048]{1,0:T(8,128)(2,1)S(1)} %get-tuple-element.38.own_ref), channel_id=1, source_target_pairs={{0,8},{8,0},{1,9},{9,1},{2,10},{10,2},{3,11},{11,3},{4,12},{12,4},... | collective-permute-start | bytes 6291464 | tf_op jit(solution)/shard_map/ppermute | solution.py:39
  80.1 6.4 %collective-permute-start.20 = (bf16[32,2048]{1,0:T(8,128)(2,1)S(1)}, bf16[32,2048]{1,0:T(8,128)(2,1)S(1)}, u32[]{:S(2)}, u32[]{:S(2)}) collective-permute-start(bf16[32,2048]{1,0:T(8,128)(2,1)S(1)} %get-tuple-element.41), channel_id=1, source_target_pairs={{0,16},{16,0},{32,48},{48,32},{64,80},{80,64},{96,112},{112,96},{1... | collective-permute-start | bytes 393224 | tf_op jit(solution)/shard_map/ppermute | solution.py:43
  81.3 7.5 %collective-permute-start.21 = (bf16[32,2048]{1,0:T(8,128)(2,1)S(1)}, bf16[32,2048]{1,0:T(8,128)(2,1)S(1)}, u32[]{:S(2)}, u32[]{:S(2)}) collective-permute-start(bf16[32,2048]{1,0:T(8,128)(2,1)S(1)} %get-tuple-element.42), channel_id=1, source_target_pairs={{0,112},{16,32},{32,16},{48,64},{64,48},{80,96},{96,80},{112,0},{1... | collective-permute-start | bytes 393224 | tf_op jit(solution)/shard_map/ppermute | solution.py:47
  82.9 8.9 %collective-permute-start.27 = (bf16[32,2048]{1,0:T(8,128)(2,1)S(1)}, bf16[32,2048]{1,0:T(8,128)(2,1)S(1)}, u32[]{:S(2)}, u32[]{:S(2)}) collective-permute-start(bf16[32,2048]{1,0:T(8,128)(2,1)S(1)} %get-tuple-element.48), channel_id=1, source_target_pairs={{0,16},{16,0},{32,48},{48,32},{64,80},{80,64},{96,112},{112,96},{1... | collective-permute-start | bytes 393224 | tf_op jit(solution)/shard_map/ppermute | solution.py:43
  83.2 8.6 %collective-permute-start.28 = (bf16[32,2048]{1,0:T(8,128)(2,1)S(1)}, bf16[32,2048]{1,0:T(8,128)(2,1)S(1)}, u32[]{:S(2)}, u32[]{:S(2)}) collective-permute-start(bf16[32,2048]{1,0:T(8,128)(2,1)S(1)} %get-tuple-element.49), channel_id=1, source_target_pairs={{0,112},{16,32},{32,16},{48,64},{64,48},{80,96},{96,80},{112,0},{1... | collective-permute-start | bytes 393224 | tf_op jit(solution)/shard_map/ppermute | solution.py:47
  88.9 7.2 %collective-permute-start.22 = (bf16[32,2048]{1,0:T(8,128)(2,1)S(1)}, bf16[32,2048]{1,0:T(8,128)(2,1)S(1)}, u32[]{:S(2)}, u32[]{:S(2)}) collective-permute-start(bf16[32,2048]{1,0:T(8,128)(2,1)S(1)} %get-tuple-element.43), channel_id=1, source_target_pairs={{0,112},{16,32},{32,16},{48,64},{64,48},{80,96},{96,80},{112,0},{1... | collective-permute-start | bytes 393224 | tf_op jit(solution)/shard_map/ppermute | solution.py:47
  90.5 6.1 %collective-permute-start.23 = (bf16[32,2048]{1,0:T(8,128)(2,1)S(1)}, bf16[32,2048]{1,0:T(8,128)(2,1)S(1)}, u32[]{:S(2)}, u32[]{:S(2)}) collective-permute-start(bf16[32,2048]{1,0:T(8,128)(2,1)S(1)} %get-tuple-element.44), channel_id=1, source_target_pairs={{0,16},{16,0},{32,48},{48,32},{64,80},{80,64},{96,112},{112,96},{1... | collective-permute-start | bytes 393224 | tf_op jit(solution)/shard_map/ppermute | solution.py:43
  91.9 7.2 %collective-permute-start.29 = (bf16[32,2048]{1,0:T(8,128)(2,1)S(1)}, bf16[32,2048]{1,0:T(8,128)(2,1)S(1)}, u32[]{:S(2)}, u32[]{:S(2)}) collective-permute-start(bf16[32,2048]{1,0:T(8,128)(2,1)S(1)} %get-tuple-element.50), channel_id=1, source_target_pairs={{0,112},{16,32},{32,16},{48,64},{64,48},{80,96},{96,80},{112,0},{1... | collective-permute-start | bytes 393224 | tf_op jit(solution)/shard_map/ppermute | solution.py:47
  93.7 6.0 %collective-permute-start.30 = (bf16[32,2048]{1,0:T(8,128)(2,1)S(1)}, bf16[32,2048]{1,0:T(8,128)(2,1)S(1)}, u32[]{:S(2)}, u32[]{:S(2)}) collective-permute-start(bf16[32,2048]{1,0:T(8,128)(2,1)S(1)} %get-tuple-element.51), channel_id=1, source_target_pairs={{0,16},{16,0},{32,48},{48,32},{64,80},{80,64},{96,112},{112,96},{1... | collective-permute-start | bytes 393224 | tf_op jit(solution)/shard_map/ppermute | solution.py:43
  96.7 5.1 %collective-permute-start.24 = (bf16[32,2048]{1,0:T(8,128)(2,1)S(1)}, bf16[32,2048]{1,0:T(8,128)(2,1)S(1)}, u32[]{:S(2)}, u32[]{:S(2)}) collective-permute-start(bf16[32,2048]{1,0:T(8,128)(2,1)S(1)} %get-tuple-element.45), channel_id=1, source_target_pairs={{0,16},{16,0},{32,48},{48,32},{64,80},{80,64},{96,112},{112,96},{1... | collective-permute-start | bytes 393224 | tf_op jit(solution)/shard_map/ppermute | solution.py:43
  96.8 6.3 %collective-permute-start.25 = (bf16[32,2048]{1,0:T(8,128)(2,1)S(1)}, bf16[32,2048]{1,0:T(8,128)(2,1)S(1)}, u32[]{:S(2)}, u32[]{:S(2)}) collective-permute-start(bf16[32,2048]{1,0:T(8,128)(2,1)S(1)} %get-tuple-element.46), channel_id=1, source_target_pairs={{0,112},{16,32},{32,16},{48,64},{64,48},{80,96},{96,80},{112,0},{1... | collective-permute-start | bytes 393224 | tf_op jit(solution)/shard_map/ppermute | solution.py:47
  99.1 6.2 %collective-permute-start.18 = (bf16[4,512,128]{2,1,0:T(8,128)(2,1)S(1)}, bf16[4,512,128]{2,1,0:T(8,128)(2,1)S(1)}, u32[]{:S(2)}, u32[]{:S(2)}) collective-permute-start(bf16[4,512,128]{2,1,0:T(8,128)(2,1)S(1)} %slice.12), channel_id=1, source_target_pairs={{0,8},{8,0},{1,9},{9,1},{2,10},{10,2},{3,11},{11,3},{4,12},{12,4},... | collective-permute-start | bytes 1572872 | tf_op jit(solution)/shard_map/ppermute | solution.py:39
  99.8 7.3 %copy-start = (bf16[512,2048]{1,0:T(8,128)(2,1)S(1)}, bf16[512,2048]{1,0:T(8,128)(2,1)}, u32[]{:S(2)}) copy-start(bf16[512,2048]{1,0:T(8,128)(2,1)} %act_ref.3) | copy-start | bytes 6291460
  99.8 10.4 %collective-permute-start.33 = (bf16[32,2048]{1,0:T(8,128)(2,1)S(1)}, bf16[32,2048]{1,0:T(8,128)(2,1)S(1)}, u32[]{:S(2)}, u32[]{:S(2)}) collective-permute-start(bf16[32,2048]{1,0:T(8,128)(2,1)S(1)} %get-tuple-element.55), channel_id=1, source_target_pairs={{0,112},{16,32},{32,16},{48,64},{64,48},{80,96},{96,80},{112,0},{1... | collective-permute-start | bytes 393224 | tf_op jit(solution)/shard_map/ppermute | solution.py:47
  103.1 7.1 %collective-permute-start.32 = (bf16[32,2048]{1,0:T(8,128)(2,1)S(1)}, bf16[32,2048]{1,0:T(8,128)(2,1)S(1)}, u32[]{:S(2)}, u32[]{:S(2)}) collective-permute-start(bf16[32,2048]{1,0:T(8,128)(2,1)S(1)} %get-tuple-element.54), channel_id=1, source_target_pairs={{0,16},{16,0},{32,48},{48,32},{64,80},{80,64},{96,112},{112,96},{1... | collective-permute-start | bytes 393224 | tf_op jit(solution)/shard_map/ppermute | solution.py:43
  104.3 10.5 %collective-permute-start.31 = (bf16[32,2048]{1,0:T(8,128)(2,1)S(1)}, bf16[32,2048]{1,0:T(8,128)(2,1)S(1)}, u32[]{:S(2)}, u32[]{:S(2)}) collective-permute-start(bf16[32,2048]{1,0:T(8,128)(2,1)S(1)} %get-tuple-element.52), channel_id=1, source_target_pairs={{0,16},{16,0},{32,48},{48,32},{64,80},{80,64},{96,112},{112,96},{1... | collective-permute-start | bytes 393224 | tf_op jit(solution)/shard_map/ppermute | solution.py:43
  105.3 9.4 %collective-permute-start.26 = (bf16[32,2048]{1,0:T(8,128)(2,1)S(1)}, bf16[32,2048]{1,0:T(8,128)(2,1)S(1)}, u32[]{:S(2)}, u32[]{:S(2)}) collective-permute-start(bf16[32,2048]{1,0:T(8,128)(2,1)S(1)} %get-tuple-element.47), channel_id=1, source_target_pairs={{0,112},{16,32},{32,16},{48,64},{64,48},{80,96},{96,80},{112,0},{1... | collective-permute-start | bytes 393224 | tf_op jit(solution)/shard_map/ppermute | solution.py:47
  110.2 5.1 %collective-permute-start.34 = (bf16[32,2048]{1,0:T(8,128)(2,1)S(1)}, bf16[32,2048]{1,0:T(8,128)(2,1)S(1)}, u32[]{:S(2)}, u32[]{:S(2)}) collective-permute-start(bf16[32,2048]{1,0:T(8,128)(2,1)S(1)} %add_convert_fusion), channel_id=1, source_target_pairs={{0,128},{128,0},{1,129},{129,1},{2,130},{130,2},{3,131},{131,3},{4... | collective-permute-start | bytes 393224 | tf_op jit(solution)/shard_map/ppermute | solution.py:39

commit v6 on v5

--- a/solution.py
+++ b/solution.py
@@ -45,6 +45,11 @@
 
 def odd(value):
     return lax.ppermute(value, "z", [(i, ((i - 1) ^ 1) + 1 & 7) for i in range(8)])
+
+
+def cross(value, way):
+    to = [i ^ 1 if way is even else ((i - 1) ^ 1) + 1 & 7 for i in range(8)]
+    return lax.ppermute(value, ("ylo", "z"), [(y * 8 + i, (1 - y) * 8 + to[i]) for y in (0, 1) for i in range(8)])
 
 
 def exchange(value):
@@ -197,40 +202,30 @@
     )(*[a for sums, _, *come in items for a in (sums, *come)])
 
 
-def query_kernel(first, act_ref, own_grad_ref, other_grad_ref, own_ref, other_ref, *refs):
-    out_ref, turned_ref = refs[-2:]
-    j = pl.program_id(0)
-
-    @pl.when(j == 0)
-    def _():
-        for i, g in enumerate((own_grad_ref, other_grad_ref)):
-            for k in range(4):
-                turned_ref[k * 128 : k * 128 + 128, i * 512 : i * 512 + 512] = g[k].T
-
-    columns = pl.ds(pl.multiple_of((j + first) * 512, 512), 512)
-    total = jnp.dot(turned_ref[:, :512], own_ref[:, columns], preferred_element_type=F32)
-    total += jnp.dot(turned_ref[:, 512:], other_ref[:, columns], preferred_element_type=F32)
-    wide = act_ref[...].astype(F32)
-    below = 1.0 + jnp.maximum(wide, 0.0)
-    guess = pl.reciprocal(below, approx=True)
-    inverse = guess * (2.0 - below * guess)
-    out_ref[...] = jnp.where(wide > 0.0, total * inverse, 0.0).astype(BF16)
-
-
-def query_grads(act, grad, other_grad, own, other, begun=None):
-    first = 0 if begun is None else 2
-    column = pl.BlockSpec((512, 512), lambda j: (0, j + first))
-    rest = () if begun is None else (begun,)
-    return pl.pallas_call(
-        functools.partial(query_kernel, first),
+def query_kernel(act_ref, own_grad_ref, other_grad_ref, own_ref, other_ref, out_ref, turned_ref):
+    for i, g in enumerate((own_grad_ref, other_grad_ref)):
+        for k in range(4):
+            turned_ref[k * 128 : k * 128 + 128, i * 512 : i * 512 + 512] = g[k].T
+    for j in range(4):
+        columns = slice(j * 512, j * 512 + 512)
+        total = jnp.dot(turned_ref[:, :512], own_ref[:, columns], preferred_element_type=F32)
+        total += jnp.dot(turned_ref[:, 512:], other_ref[:, columns], preferred_element_type=F32)
+        wide = act_ref[:, columns].astype(F32)
+        below = 1.0 + jnp.maximum(wide, 0.0)
+        guess = pl.reciprocal(below, approx=True)
+        inverse = guess * (2.0 - below * guess)
+        out_ref[:, columns] = jnp.where(wide > 0.0, total * inverse, 0.0).astype(BF16)
+
+
+def query_grads(act, grad, other_grad, own, other):
+    return pl.pallas_call(
+        query_kernel,
         out_shape=shape((512, 2048), BF16),
-        grid=(2,),
-        in_specs=[column] + [VMEM] * 4 + [ANY] * len(rest),
-        out_specs=column,
+        in_specs=[VMEM] * 5,
+        out_specs=VMEM,
         scratch_shapes=[pltpu.VMEM((512, 1024), BF16)],
-        input_output_aliases={5: 0} if rest else {},
-        compiler_params=PARAMS,
-    )(act, grad, other_grad, own, other, *rest)
+        compiler_params=PARAMS,
+    )(act, grad[:4], other_grad, own, other)
 
 
 def shards(query_act, passage_act, positive, normalizer):
@@ -253,8 +248,7 @@
     grad = exchange(score_grad(exchange(part), norm, other_norm, at, other_at))
 
     joined = after(joined, grad)
-    query_args = (query_act, grad, swap(grad[4:], "core"), joined, swap(joined, "core"))
-    query_begun = query_grads(*query_args)
+    query_grad = query_grads(query_act, grad, swap(grad[4:], "core"), joined, swap(joined, "core"))
 
     far, a0, a1, b0, b1 = passage_sums(grad, mine, other, 0, [0, 1, 2, 5])
     (near,) = passage_sums(grad, mine, other, 256, [])
@@ -262,17 +256,15 @@
     a0, a1, b0, b1 = even(a0), odd(a1), even(b0), odd(b1)
     for d in (-3, 2, -1):
         ways = (odd, even) if d < 0 else (even, odd)
-        a0, a1 = add_blocks((*place[0, d], a0), (*place[1, -d], a1))
-        a0, a1 = ways[0](a0), ways[1](a1)
+        (a0,), (a1,) = add_blocks((*place[0, d], a0)), add_blocks((*place[1, -d], a1))
+        a0, a1 = ways[0](a0), cross(a1, even) if d == -1 else ways[1](a1)
         if d != -1:
             d = -2 if d < 0 else 1
-            b0, b1 = add_blocks((*place[0, d], b0), (*place[1, -d], b1))
+            (b0,), (b1,) = add_blocks((*place[0, d], b0)), add_blocks((*place[1, -d], b1))
             b0, b1 = ways[0](b0), ways[1](b1)
     sums = [near[place[s, 0][1]] for s in (0, 1)]
-    theirs = after(sums[1], query_begun) + a1.astype(F32) + b1.astype(F32)
-    theirs = swap(theirs.astype(BF16), "ylo").astype(F32)
-    query_grad = query_grads(*query_args, query_begun)
-    total = after(sums[0], query_grad) + a0.astype(F32) + b0.astype(F32) + theirs
+    theirs = swap((sums[1] + b1.astype(F32)).astype(BF16), "ylo").astype(F32)
+    total = after(sums[0], query_grad) + a0.astype(F32) + a1.astype(F32) + b0.astype(F32) + theirs
     passage_grad = (total * slope(passage_act)).astype(BF16)
     return (query_grad, passage_grad)
 

time: 116 us -> 114 us (0.983)
  Pallas kernels: 13.1 us -> 11.5 us
  starting transfers between devices: 43.5 us -> 42.3 us
    pallas_call x2 -> x1, Pallas kernels: 6.16 us -> 4.57 us  [query_grads(): pl.pallas_call(query_kernel, out_shape=shape((512, 2048), BF16), in_specs...]
    ppermute x14 -> x13, waiting for transfers between devices: 7.2 us -> 5.71 us  [even(): return lax.ppermute(value, 'z', [(i, i ^ 1) for i in range(8)])]
    ppermute x14 -> x13, starting transfers between devices: 11 us -> 9.91 us  [even(): return lax.ppermute(value, 'z', [(i, i ^ 1) for i in range(8)])]
  transfers between devices with their start and end apart: 35 -> 35, of which waited for: 17 -> 14; matrix products, arithmetic and copies ran while one was open for 0% -> 0% of each run, Pallas kernels for 9% -> 8%
where the time goes in v6:
time: 114 us
  starting transfers between devices  42.3 us (37%)
  blocking collectives  34.2 us (30%)
  waiting for transfers between devices  20.6 us (18%)
  Pallas kernels  11.5 us (10%)
  other arithmetic  3.99 us (4%)
    all_to_all x2, blocking collectives, exchange(): return lax.all_to_all(value, REP, split_axis=0, concat_axis=0)  34.2 us
    ppermute x14, starting transfers between devices, odd(): lax.ppermute(value, 'z', [(i, (i - 1 ^ 1) + 1 & 7) for i in range(8)])  28 us
    ppermute x14, waiting for transfers between devices, odd(): lax.ppermute(value, 'z', [(i, (i - 1 ^ 1) + 1 & 7) for i in range(8)])  13.4 us
    ppermute x13, starting transfers between devices, even(): return lax.ppermute(value, 'z', [(i, i ^ 1) for i in range(8)])  9.91 us
    ppermute x13, waiting for transfers between devices, even(): return lax.ppermute(value, 'z', [(i, i ^ 1) for i in range(8)])  5.71 us
    pallas_call x1, Pallas kernels, query_grads(): pl.pallas_call(query_kernel, out_shape=shape((512, 2048), BF16), in_specs...  4.57 us
    ppermute x7, starting transfers between devices, swap(): return lax.ppermute(value, axis, [(0, 1), (1, 0)])  3.99 us
    convert_element_type x2, other arithmetic, saturate(): jnp.where(wide < 2.0 ** (-8), small, jnp.log(1.0 + wide)).astype(BF16)  3.17 us
  transfers between devices with their start and end apart: 35, of which 14 were waited for; matrix products, arithmetic and copies ran while one was open for 0% of the time, Pallas kernels for 8%

profile of v6, /device:TPU:8, one launch (start us, length us, event | category | flops | bytes accessed | tf_op | source)
XLA Modules:
  0.0 113.6 jit_solution(12746274595550365334)
XLA Ops:
  0.7 3.1 %fusion.1.mine_ref = bf16[512,2048]{1,0:T(8,128)(2,1)S(1)} fusion(bf16[512,2048]{1,0:T(8,128)(2,1)} %act_ref.1), kind=kLoop, calls=%fused_computation.2 | loop fusion | flops 9437184 | bytes 4194304 | tf_op jit(solution)/shard_map/convert_element_type | solution.py:30
  4.0 2.3 %collective-permute-start.3 = (bf16[32,2048]{1,0:T(8,128)(2,1)S(1)}, bf16[32,2048]{1,0:T(8,128)(2,1)S(1)}, u32[]{:S(2)}, u32[]{:S(2)}) collective-permute-start(bf16[32,2048]{1,0:T(8,128)(2,1)S(1)} %fusion.8.refs_8_), channel_id=1, source_target_pairs={{0,128},{128,0},{1,129},{129,1},{2,130},{130,2},{3,131},{131,3},{4... | collective-permute-start | bytes 393224 | tf_op jit(solution)/shard_map/ppermute | solution.py:39
  6.2 4.1 %collective-permute-start.1 = (bf16[32,2048]{1,0:T(8,128)(2,1)S(1)}, bf16[32,2048]{1,0:T(8,128)(2,1)S(1)}, u32[]{:S(2)}, u32[]{:S(2)}) collective-permute-start(bf16[32,2048]{1,0:T(8,128)(2,1)S(1)} %fusion.8.refs_8_), channel_id=1, source_target_pairs={{0,112},{16,32},{32,16},{48,64},{64,48},{80,96},{96,80},{112,0},{1... | collective-permute-start | bytes 393224 | tf_op jit(solution)/shard_map/ppermute | solution.py:47
  10.4 1.5 %collective-permute-start.8 = (bf16[32,2048]{1,0:T(8,128)(2,1)S(1)}, bf16[32,2048]{1,0:T(8,128)(2,1)S(1)}, u32[]{:S(2)}, u32[]{:S(2)}) collective-permute-start(bf16[32,2048]{1,0:T(8,128)(2,1)S(1)} %collective-permute-done.3.refs_9_), channel_id=1, source_target_pairs={{0,16},{16,0},{32,48},{48,32},{64,80},{80,64},{96,112},{112,96},{1... | collective-permute-start | bytes 393224 | tf_op jit(solution)/shard_map/ppermute | solution.py:43
  11.9 0.5 collective-permute-start.13
  12.4 1.8 %collective-permute-done.1.refs_6_ = bf16[32,2048]{1,0:T(8,128)(2,1)S(1)} collective-permute-done((bf16[32,2048]{1,0:T(8,128)(2,1)S(1)}, bf16[32,2048]{1,0:T(8,128)(2,1)S(1)}, u32[]{:S(2)}, u32[]{:S(2)}) %collective-permute-start.1) | collective-permute-done | bytes 131104 | tf_op jit(solution)/shard_map/ppermute | solution.py:47
  14.2 2.0 %collective-permute-start.6 = (bf16[32,2048]{1,0:T(8,128)(2,1)S(1)}, bf16[32,2048]{1,0:T(8,128)(2,1)S(1)}, u32[]{:S(2)}, u32[]{:S(2)}) collective-permute-start(bf16[32,2048]{1,0:T(8,128)(2,1)S(1)} %fusion.8.refs_8_), channel_id=1, source_target_pairs={{0,16},{16,0},{32,48},{48,32},{64,80},{80,64},{96,112},{112,96},{1... | collective-permute-start | bytes 393224 | tf_op jit(solution)/shard_map/ppermute | solution.py:43
  16.2 3.1 %collective-permute-start.4 = (bf16[32,2048]{1,0:T(8,128)(2,1)S(1)}, bf16[32,2048]{1,0:T(8,128)(2,1)S(1)}, u32[]{:S(2)}, u32[]{:S(2)}) collective-permute-start(bf16[32,2048]{1,0:T(8,128)(2,1)S(1)} %collective-permute-done.3.refs_9_), channel_id=1, source_target_pairs={{0,112},{16,32},{32,16},{48,64},{64,48},{80,96},{96,80},{112,0},{1... | collective-permute-start | bytes 393224 | tf_op jit(solution)/shard_map/ppermute | solution.py:47
  19.4 2.5 %collective-permute-start.9 = (bf16[32,2048]{1,0:T(8,128)(2,1)S(1)}, bf16[32,2048]{1,0:T(8,128)(2,1)S(1)}, u32[]{:S(2)}, u32[]{:S(2)}) collective-permute-start(bf16[32,2048]{1,0:T(8,128)(2,1)S(1)} %collective-permute-done.8.refs_5_), channel_id=1, source_target_pairs={{0,112},{16,32},{32,16},{48,64},{64,48},{80,96},{96,80},{112,0},{1... | collective-permute-start | bytes 393224 | tf_op jit(solution)/shard_map/ppermute | solution.py:47
  21.8 2.8 %collective-permute-start.10 = (bf16[32,2048]{1,0:T(8,128)(2,1)S(1)}, bf16[32,2048]{1,0:T(8,128)(2,1)S(1)}, u32[]{:S(2)}, u32[]{:S(2)}) collective-permute-start(bf16[32,2048]{1,0:T(8,128)(2,1)S(1)} %collective-permute-done.2.refs_0_), channel_id=1, source_target_pairs={{0,112},{16,32},{32,16},{48,64},{64,48},{80,96},{96,80},{112,0},{1... | collective-permute-start | bytes 393224 | tf_op jit(solution)/shard_map/ppermute | solution.py:47
  24.6 1.9 %collective-permute-start.7 = (bf16[32,2048]{1,0:T(8,128)(2,1)S(1)}, bf16[32,2048]{1,0:T(8,128)(2,1)S(1)}, u32[]{:S(2)}, u32[]{:S(2)}) collective-permute-start(bf16[32,2048]{1,0:T(8,128)(2,1)S(1)} %collective-permute-done.6.refs_4_), channel_id=1, source_target_pairs={{0,112},{16,32},{32,16},{48,64},{64,48},{80,96},{96,80},{112,0},{1... | collective-permute-start | bytes 393224 | tf_op jit(solution)/shard_map/ppermute | solution.py:47
  26.9 1.7 %collective-permute-start.14 = (bf16[32,2048]{1,0:T(8,128)(2,1)S(1)}, bf16[32,2048]{1,0:T(8,128)(2,1)S(1)}, u32[]{:S(2)}, u32[]{:S(2)}) collective-permute-start(bf16[32,2048]{1,0:T(8,128)(2,1)S(1)} %collective-permute-done.9.refs_3_), channel_id=1, source_target_pairs={{0,16},{16,0},{32,48},{48,32},{64,80},{80,64},{96,112},{112,96},{1... | collective-permute-start | bytes 393224 | tf_op jit(solution)/shard_map/ppermute | solution.py:43
  28.6 1.0 collective-permute-done.10.refs_4_
  29.6 1.4 %collective-permute-done.7.refs_2_ = bf16[32,2048]{1,0:T(8,128)(2,1)S(1)} collective-permute-done((bf16[32,2048]{1,0:T(8,128)(2,1)S(1)}, bf16[32,2048]{1,0:T(8,128)(2,1)S(1)}, u32[]{:S(2)}, u32[]{:S(2)}) %collective-permute-start.7) | collective-permute-done | bytes 131104 | tf_op jit(solution)/shard_map/ppermute | solution.py:47
  31.0 0.6 collective-permute-start.16
  31.6 1.4 %collective-permute-done.5.refs_1_ = bf16[32,2048]{1,0:T(8,128)(2,1)S(1)} collective-permute-done((bf16[32,2048]{1,0:T(8,128)(2,1)S(1)}, bf16[32,2048]{1,0:T(8,128)(2,1)S(1)}, u32[]{:S(2)}, u32[]{:S(2)}) %collective-permute-start.5) | collective-permute-done | bytes 131104 | tf_op jit(solution)/shard_map/ppermute | solution.py:43
  33.0 1.6 %collective-permute-start.17 = (bf16[32,2048]{1,0:T(8,128)(2,1)S(1)}, bf16[32,2048]{1,0:T(8,128)(2,1)S(1)}, u32[]{:S(2)}, u32[]{:S(2)}) collective-permute-start(bf16[32,2048]{1,0:T(8,128)(2,1)S(1)} %collective-permute-done.5.refs_1_), channel_id=1, source_target_pairs={{0,112},{16,32},{32,16},{48,64},{64,48},{80,96},{96,80},{112,0},{1... | collective-permute-start | bytes 393224 | tf_op jit(solution)/shard_map/ppermute | solution.py:47
  34.5 1.2 %collective-permute-done.14.refs_3_ = bf16[32,2048]{1,0:T(8,128)(2,1)S(1)} collective-permute-done((bf16[32,2048]{1,0:T(8,128)(2,1)S(1)}, bf16[32,2048]{1,0:T(8,128)(2,1)S(1)}, u32[]{:S(2)}, u32[]{:S(2)}) %collective-permute-start.14) | collective-permute-done | bytes 131104 | tf_op jit(solution)/shard_map/ppermute | solution.py:43
  35.8 0.4 collective-permute-start.15
  36.2 1.6 %collective-permute-done.11.refs_0_ = bf16[32,2048]{1,0:T(8,128)(2,1)S(1)} collective-permute-done((bf16[32,2048]{1,0:T(8,128)(2,1)S(1)}, bf16[32,2048]{1,0:T(8,128)(2,1)S(1)}, u32[]{:S(2)}, u32[]{:S(2)}) %collective-permute-start.11) | collective-permute-done | bytes 131104 | tf_op jit(solution)/shard_map/ppermute | solution.py:43
  37.8 1.6 %shard_map.59 = (f32[4,320,256]{2,1,0:T(8,128)S(1)}, bf16[512,2048]{1,0:T(8,128)(2,1)S(1)}) custom-call(bf16[512,2048]{1,0:T(8,128)(2,1)S(1)} %fusion.1.mine_ref, bf16[512,2048]{1,0:T(8,128)(2,1)S(1)} %collective-permute-done.other_ref, bf16[32,2048]{1,0:T(8,128)(2,1)S(1)} %collective-permute-done.2.refs_0_, ...), custom_call_target="tpu_custom_call" | custom-call | tf_op jit(solution)/shard_map/pallas_call | solution.py:109
  39.4 2.5 %collective-permute-done.15.refs_1_ = bf16[32,2048]{1,0:T(8,128)(2,1)S(1)} collective-permute-done((bf16[32,2048]{1,0:T(8,128)(2,1)S(1)}, bf16[32,2048]{1,0:T(8,128)(2,1)S(1)}, u32[]{:S(2)}, u32[]{:S(2)}) %collective-permute-start.15) | collective-permute-done | bytes 131104 | tf_op jit(solution)/shard_map/ppermute | solution.py:47
  41.9 2.0 %shard_map.60 = (s16[8,528,128]{2,1,0:T(8,128)(2,1)S(1)}, bf16[512,2048]{1,0:T(8,128)(2,1)S(1)}) custom-call(bf16[512,2048]{1,0:T(8,128)(2,1)S(1)} %fusion.1.mine_ref, bf16[512,2048]{1,0:T(8,128)(2,1)S(1)} %collective-permute-done.other_ref, f32[4,320,256]{2,1,0:T(8,128)S(1)} %get-tuple-element.18.early_ref, ...), custom_call_target="tpu_custom_call", output_to_operand_aliasing={{1}: (3, {})} | custom-call | tf_op jit(solution)/shard_map/pallas_call | solution.py:116
  44.0 19.2 %all_to_all.10.pieces_ref = s16[8,528,128]{2,1,0:T(8,128)(2,1)S(1)} all-to-all(s16[8,528,128]{2,1,0:T(8,128)(2,1)S(1)} %get-tuple-element.21), channel_id=1, replica_groups=mesh['ylo'=2,'z'=8,'core'=2,'yhi'=2,'x'=4] {'x','yhi'}, dimensions={0} | all-to-all | bytes 2162688 | tf_op jit(solution)/shard_map/all_to_all | solution.py:56
  63.1 0.6 shard_map.61
  63.7 15.1 %all_to_all.11.grad_ref = bf16[8,512,128]{2,1,0:T(8,128)(2,1)S(1)} all-to-all(bf16[8,512,128]{2,1,0:T(8,128)(2,1)S(1)} %shard_map.61), channel_id=1, replica_groups=mesh['ylo'=2,'z'=8,'core'=2,'yhi'=2,'x'=4] {'x','yhi'}, dimensions={0} | all-to-all | bytes 2097152 | tf_op jit(solution)/shard_map/all_to_all | solution.py:56
  78.8 1.2 %shard_map.64 = (f32[8,32,2048]{2,1,0:T(8,128)S(1)}, bf16[32,2048]{1,0:T(8,128)(2,1)S(1)}, bf16[32,2048]{1,0:T(8,128)(2,1)S(1)}, bf16[32,2048]{1,0:T(8,128)(2,1)S(1)}, bf16[32,2048]{1,0:T(8,128)(2,1)S(1)}) custom-call(bf16[8,512,128]{2,1,0:T(8,128)(2,1)S(1)} %all_to_all.11.grad_ref, bf16[512,2048]{1,0:T(8,128)(2,1)S(1)} %fusion.1.mine_ref, ...), custom_call_target="tpu_custom_call" | custom-call | tf_op jit(solution)/shard_map/pallas_call | solution.py:175
  80.1 1.3 %collective-permute-start.20 = (bf16[32,2048]{1,0:T(8,128)(2,1)S(1)}, bf16[32,2048]{1,0:T(8,128)(2,1)S(1)}, u32[]{:S(2)}, u32[]{:S(2)}) collective-permute-start(bf16[32,2048]{1,0:T(8,128)(2,1)S(1)} %get-tuple-element.30), channel_id=1, source_target_pairs={{0,16},{16,0},{32,48},{48,32},{64,80},{80,64},{96,112},{112,96},{1... | collective-permute-start | bytes 393224 | tf_op jit(solution)/shard_map/ppermute | solution.py:43
  81.3 1.5 %collective-permute-start.24 = (bf16[32,2048]{1,0:T(8,128)(2,1)S(1)}, bf16[32,2048]{1,0:T(8,128)(2,1)S(1)}, u32[]{:S(2)}, u32[]{:S(2)}) collective-permute-start(bf16[32,2048]{1,0:T(8,128)(2,1)S(1)} %get-tuple-element.31), channel_id=1, source_target_pairs={{0,112},{16,32},{32,16},{48,64},{64,48},{80,96},{96,80},{112,0},{1... | collective-permute-start | bytes 393224 | tf_op jit(solution)/shard_map/ppermute | solution.py:47
  82.9 1.7 %collective-permute-start.31 = (bf16[32,2048]{1,0:T(8,128)(2,1)S(1)}, bf16[32,2048]{1,0:T(8,128)(2,1)S(1)}, u32[]{:S(2)}, u32[]{:S(2)}) collective-permute-start(bf16[32,2048]{1,0:T(8,128)(2,1)S(1)} %get-tuple-element.33), channel_id=1, source_target_pairs={{0,112},{16,32},{32,16},{48,64},{64,48},{80,96},{96,80},{112,0},{1... | collective-permute-start | bytes 393224 | tf_op jit(solution)/shard_map/ppermute | solution.py:47
  84.6 1.5 %collective-permute-done.20.refs_1_ = bf16[32,2048]{1,0:T(8,128)(2,1)S(1)} collective-permute-done((bf16[32,2048]{1,0:T(8,128)(2,1)S(1)}, bf16[32,2048]{1,0:T(8,128)(2,1)S(1)}, u32[]{:S(2)}, u32[]{:S(2)}) %collective-permute-start.20) | collective-permute-done | bytes 131104 | tf_op jit(solution)/shard_map/ppermute | solution.py:43
  86.1 1.6 %collective-permute-start.21 = (bf16[32,2048]{1,0:T(8,128)(2,1)S(1)}, bf16[32,2048]{1,0:T(8,128)(2,1)S(1)}, u32[]{:S(2)}, u32[]{:S(2)}) collective-permute-start(bf16[32,2048]{1,0:T(8,128)(2,1)S(1)} %shard_map.65), channel_id=1, source_target_pairs={{0,112},{16,32},{32,16},{48,64},{64,48},{80,96},{96,80},{112,0},{1... | collective-permute-start | bytes 393224 | tf_op jit(solution)/shard_map/ppermute | solution.py:47
  87.7 1.2 %collective-permute-done.24.refs_1_ = bf16[32,2048]{1,0:T(8,128)(2,1)S(1)} collective-permute-done((bf16[32,2048]{1,0:T(8,128)(2,1)S(1)}, bf16[32,2048]{1,0:T(8,128)(2,1)S(1)}, u32[]{:S(2)}, u32[]{:S(2)}) %collective-permute-start.24) | collective-permute-done | bytes 131104 | tf_op jit(solution)/shard_map/ppermute | solution.py:47
  89.0 2.7 %collective-permute-done.31.refs_1_ = bf16[32,2048]{1,0:T(8,128)(2,1)S(1)} collective-permute-done((bf16[32,2048]{1,0:T(8,128)(2,1)S(1)}, bf16[32,2048]{1,0:T(8,128)(2,1)S(1)}, u32[]{:S(2)}, u32[]{:S(2)}) %collective-permute-start.31) | collective-permute-done | bytes 131104 | tf_op jit(solution)/shard_map/ppermute | solution.py:47
  91.8 1.2 %shard_map.63.refs_0_ = f32[8,32,2048]{2,1,0:T(8,128)S(1)} custom-call(bf16[8,512,128]{2,1,0:T(8,128)(2,1)S(1)} %all_to_all.11.grad_ref, bf16[512,2048]{1,0:T(8,128)(2,1)S(1)} %fusion.1.mine_ref, bf16[512,2048]{1,0:T(8,128)(2,1)S(1)} %collective-permute-done.other_ref), custom_call_target="tpu_custom_call" | custom-call | tf_op jit(solution)/shard_map/pallas_call | solution.py:175
  93.1 1.6 %collective-permute-start.29 = (bf16[32,2048]{1,0:T(8,128)(2,1)S(1)}, bf16[32,2048]{1,0:T(8,128)(2,1)S(1)}, u32[]{:S(2)}, u32[]{:S(2)}) collective-permute-start(bf16[32,2048]{1,0:T(8,128)(2,1)S(1)} %shard_map.71), channel_id=1, source_target_pairs={{0,112},{16,32},{32,16},{48,64},{64,48},{80,96},{96,80},{112,0},{1... | collective-permute-start | bytes 393224 | tf_op jit(solution)/shard_map/ppermute | solution.py:47
  94.8 1.6 %collective-permute-start.22 = (bf16[32,2048]{1,0:T(8,128)(2,1)S(1)}, bf16[32,2048]{1,0:T(8,128)(2,1)S(1)}, u32[]{:S(2)}, u32[]{:S(2)}) collective-permute-start(bf16[32,2048]{1,0:T(8,128)(2,1)S(1)} %shard_map.66), channel_id=1, source_target_pairs={{0,16},{16,0},{32,48},{48,32},{64,80},{80,64},{96,112},{112,96},{1... | collective-permute-start | bytes 393224 | tf_op jit(solution)/shard_map/ppermute | solution.py:43
  96.4 1.6 %collective-permute-start.26 = (bf16[32,2048]{1,0:T(8,128)(2,1)S(1)}, bf16[32,2048]{1,0:T(8,128)(2,1)S(1)}, u32[]{:S(2)}, u32[]{:S(2)}) collective-permute-start(bf16[32,2048]{1,0:T(8,128)(2,1)S(1)} %shard_map.69), channel_id=1, source_target_pairs={{0,112},{16,32},{32,16},{48,64},{64,48},{80,96},{96,80},{112,0},{1... | collective-permute-start | bytes 393224 | tf_op jit(solution)/shard_map/ppermute | solution.py:47
  98.0 2.0 %collective-permute-start.33 = (bf16[32,2048]{1,0:T(8,128)(2,1)S(1)}, bf16[32,2048]{1,0:T(8,128)(2,1)S(1)}, u32[]{:S(2)}, u32[]{:S(2)}) collective-permute-start(bf16[32,2048]{1,0:T(8,128)(2,1)S(1)} %shard_map.74), channel_id=1, source_target_pairs={{0,112},{16,32},{32,16},{48,64},{64,48},{80,96},{96,80},{112,0},{1... | collective-permute-start | bytes 393224 | tf_op jit(solution)/shard_map/ppermute | solution.py:47
  100.1 0.5 collective-permute-done.29.refs_1_
  100.7 1.1 collective-permute-start.30
  101.8 1.8 %collective-permute-done.26.refs_1_ = bf16[32,2048]{1,0:T(8,128)(2,1)S(1)} collective-permute-done((bf16[32,2048]{1,0:T(8,128)(2,1)S(1)}, bf16[32,2048]{1,0:T(8,128)(2,1)S(1)}, u32[]{:S(2)}, u32[]{:S(2)}) %collective-permute-start.26) | collective-permute-done | bytes 131104 | tf_op jit(solution)/shard_map/ppermute | solution.py:47
  103.6 1.5 %collective-permute-start.23 = (bf16[32,2048]{1,0:T(8,128)(2,1)S(1)}, bf16[32,2048]{1,0:T(8,128)(2,1)S(1)}, u32[]{:S(2)}, u32[]{:S(2)}) collective-permute-start(bf16[32,2048]{1,0:T(8,128)(2,1)S(1)} %shard_map.67), channel_id=1, source_target_pairs={{0,112},{16,32},{32,16},{48,64},{64,48},{80,96},{96,80},{112,0},{1... | collective-permute-start | bytes 393224 | tf_op jit(solution)/shard_map/ppermute | solution.py:47
  105.2 0.4 collective-permute-start.27
  105.6 1.1 collective-permute-start.34
  106.8 4.6 %shard_map.62 = bf16[512,2048]{1,0:T(8,128)(2,1)} custom-call(bf16[512,2048]{1,0:T(8,128)(2,1)S(1)} %copy-done, bf16[4,512,128]{2,1,0:T(8,128)(2,1)S(1)} %get-tuple-element.35.own_grad_ref, bf16[4,512,128]{2,1,0:T(8,128)(2,1)S(1)} %collective-permute-done.18.other_grad_ref, bf16[512,2048]{1,0:T(8,128)(2,1)S(1)} %get-tuple-element.27.own_ref, ...), custom_call_target="tpu_custom_call" | custom-call | tf_op jit(solution)/shard_map/pallas_call | solution.py:221
  111.4 1.4 %collective-permute-done.34 = bf16[32,2048]{1,0:T(8,128)(2,1)S(1)} collective-permute-done((bf16[32,2048]{1,0:T(8,128)(2,1)S(1)}, bf16[32,2048]{1,0:T(8,128)(2,1)S(1)}, u32[]{:S(2)}, u32[]{:S(2)}) %collective-permute-start.34) | collective-permute-done | bytes 131104 | tf_op jit(solution)/shard_map/ppermute | solution.py:39
  112.8 0.8 fusion.13
  (54 shorter events, 1.2 us)
Async XLA Ops:
  0.6 3.2 %copy-start.3 = (bf16[32,2048]{1,0:T(8,128)(2,1)S(1)}, bf16[32,2048]{1,0:T(8,128)(2,1)}, u32[]{:S(2)}) copy-start(bf16[32,2048]{1,0:T(8,128)(2,1)} %param.5) | copy-start | bytes 393220
  0.6 11.2 %copy-start.1 = (f32[512]{0:T(512)S(1)}, f32[512]{0:T(512)}, u32[]{:S(2)}) copy-start(f32[512]{0:T(512)} %param.7) | copy-start | bytes 6148
  0.7 11.2 %copy-start.2 = (s32[512]{0:T(512)S(1)}, s32[512]{0:T(512)}, u32[]{:S(2)}) copy-start(s32[512]{0:T(512)} %param.6) | copy-start | bytes 6148
  3.7 34.1 %collective-permute-start = (bf16[512,2048]{1,0:T(8,128)(2,1)S(1)}, bf16[512,2048]{1,0:T(8,128)(2,1)S(1)}, u32[]{:S(2)}, u32[]{:S(2)}) collective-permute-start(bf16[512,2048]{1,0:T(8,128)(2,1)S(1)} %fusion.1.mine_ref), channel_id=1, source_target_pairs={{0,8},{8,0},{1,9},{9,1},{2,10},{10,2},{3,11},{11,3},{4,12},{12,4},... | collective-permute-start | bytes 6291464 | tf_op jit(solution)/shard_map/ppermute | solution.py:39
  4.0 6.4 %collective-permute-start.3 = (bf16[32,2048]{1,0:T(8,128)(2,1)S(1)}, bf16[32,2048]{1,0:T(8,128)(2,1)S(1)}, u32[]{:S(2)}, u32[]{:S(2)}) collective-permute-start(bf16[32,2048]{1,0:T(8,128)(2,1)S(1)} %fusion.8.refs_8_), channel_id=1, source_target_pairs={{0,128},{128,0},{1,129},{129,1},{2,130},{130,2},{3,131},{131,3},{4... | collective-permute-start | bytes 393224 | tf_op jit(solution)/shard_map/ppermute | solution.py:39
  6.2 8.0 %collective-permute-start.1 = (bf16[32,2048]{1,0:T(8,128)(2,1)S(1)}, bf16[32,2048]{1,0:T(8,128)(2,1)S(1)}, u32[]{:S(2)}, u32[]{:S(2)}) collective-permute-start(bf16[32,2048]{1,0:T(8,128)(2,1)S(1)} %fusion.8.refs_8_), channel_id=1, source_target_pairs={{0,112},{16,32},{32,16},{48,64},{64,48},{80,96},{96,80},{112,0},{1... | collective-permute-start | bytes 393224 | tf_op jit(solution)/shard_map/ppermute | solution.py:47
  10.4 9.0 %collective-permute-start.8 = (bf16[32,2048]{1,0:T(8,128)(2,1)S(1)}, bf16[32,2048]{1,0:T(8,128)(2,1)S(1)}, u32[]{:S(2)}, u32[]{:S(2)}) collective-permute-start(bf16[32,2048]{1,0:T(8,128)(2,1)S(1)} %collective-permute-done.3.refs_9_), channel_id=1, source_target_pairs={{0,16},{16,0},{32,48},{48,32},{64,80},{80,64},{96,112},{112,96},{1... | collective-permute-start | bytes 393224 | tf_op jit(solution)/shard_map/ppermute | solution.py:43
  11.8 2.4 %collective-permute-start.12 = (f32[512]{0:T(512)S(1)}, f32[512]{0:T(512)S(1)}, u32[]{:S(2)}, u32[]{:S(2)}) collective-permute-start(f32[512]{0:T(512)S(1)} %copy-done.1), channel_id=1, source_target_pairs={{0,8},{8,0},{1,9},{9,1},{2,10},{10,2},{3,11},{11,3},{4,12},{12,4},... | collective-permute-start | bytes 6152 | tf_op jit(solution)/shard_map/ppermute | solution.py:39
  11.9 4.4 %collective-permute-start.13 = (s32[512]{0:T(512)S(1)}, s32[512]{0:T(512)S(1)}, u32[]{:S(2)}, u32[]{:S(2)}) collective-permute-start(s32[512]{0:T(512)S(1)} %copy-done.2), channel_id=1, source_target_pairs={{0,8},{8,0},{1,9},{9,1},{2,10},{10,2},{3,11},{11,3},{4,12},{12,4},... | collective-permute-start | bytes 6152 | tf_op jit(solution)/shard_map/ppermute | solution.py:39
  14.2 7.6 %collective-permute-start.2 = (bf16[32,2048]{1,0:T(8,128)(2,1)S(1)}, bf16[32,2048]{1,0:T(8,128)(2,1)S(1)}, u32[]{:S(2)}, u32[]{:S(2)}) collective-permute-start(bf16[32,2048]{1,0:T(8,128)(2,1)S(1)} %collective-permute-done.1.refs_6_), channel_id=1, source_target_pairs={{0,16},{16,0},{32,48},{48,32},{64,80},{80,64},{96,112},{112,96},{1... | collective-permute-start | bytes 393224 | tf_op jit(solution)/shard_map/ppermute | solution.py:43
  14.2 10.4 %collective-permute-start.6 = (bf16[32,2048]{1,0:T(8,128)(2,1)S(1)}, bf16[32,2048]{1,0:T(8,128)(2,1)S(1)}, u32[]{:S(2)}, u32[]{:S(2)}) collective-permute-start(bf16[32,2048]{1,0:T(8,128)(2,1)S(1)} %fusion.8.refs_8_), channel_id=1, source_target_pairs={{0,16},{16,0},{32,48},{48,32},{64,80},{80,64},{96,112},{112,96},{1... | collective-permute-start | bytes 393224 | tf_op jit(solution)/shard_map/ppermute | solution.py:43
  16.2 10.3 %collective-permute-start.4 = (bf16[32,2048]{1,0:T(8,128)(2,1)S(1)}, bf16[32,2048]{1,0:T(8,128)(2,1)S(1)}, u32[]{:S(2)}, u32[]{:S(2)}) collective-permute-start(bf16[32,2048]{1,0:T(8,128)(2,1)S(1)} %collective-permute-done.3.refs_9_), channel_id=1, source_target_pairs={{0,112},{16,32},{32,16},{48,64},{64,48},{80,96},{96,80},{112,0},{1... | collective-permute-start | bytes 393224 | tf_op jit(solution)/shard_map/ppermute | solution.py:47
  19.4 7.5 %collective-permute-start.9 = (bf16[32,2048]{1,0:T(8,128)(2,1)S(1)}, bf16[32,2048]{1,0:T(8,128)(2,1)S(1)}, u32[]{:S(2)}, u32[]{:S(2)}) collective-permute-start(bf16[32,2048]{1,0:T(8,128)(2,1)S(1)} %collective-permute-done.8.refs_5_), channel_id=1, source_target_pairs={{0,112},{16,32},{32,16},{48,64},{64,48},{80,96},{96,80},{112,0},{1... | collective-permute-start | bytes 393224 | tf_op jit(solution)/shard_map/ppermute | solution.py:47
  21.8 7.7 %collective-permute-start.10 = (bf16[32,2048]{1,0:T(8,128)(2,1)S(1)}, bf16[32,2048]{1,0:T(8,128)(2,1)S(1)}, u32[]{:S(2)}, u32[]{:S(2)}) collective-permute-start(bf16[32,2048]{1,0:T(8,128)(2,1)S(1)} %collective-permute-done.2.refs_0_), channel_id=1, source_target_pairs={{0,112},{16,32},{32,16},{48,64},{64,48},{80,96},{96,80},{112,0},{1... | collective-permute-start | bytes 393224 | tf_op jit(solution)/shard_map/ppermute | solution.py:47
  24.6 6.3 %collective-permute-start.7 = (bf16[32,2048]{1,0:T(8,128)(2,1)S(1)}, bf16[32,2048]{1,0:T(8,128)(2,1)S(1)}, u32[]{:S(2)}, u32[]{:S(2)}) collective-permute-start(bf16[32,2048]{1,0:T(8,128)(2,1)S(1)} %collective-permute-done.6.refs_4_), channel_id=1, source_target_pairs={{0,112},{16,32},{32,16},{48,64},{64,48},{80,96},{96,80},{112,0},{1... | collective-permute-start | bytes 393224 | tf_op jit(solution)/shard_map/ppermute | solution.py:47
  26.5 6.5 %collective-permute-start.5 = (bf16[32,2048]{1,0:T(8,128)(2,1)S(1)}, bf16[32,2048]{1,0:T(8,128)(2,1)S(1)}, u32[]{:S(2)}, u32[]{:S(2)}) collective-permute-start(bf16[32,2048]{1,0:T(8,128)(2,1)S(1)} %collective-permute-done.4.refs_7_), channel_id=1, source_target_pairs={{0,16},{16,0},{32,48},{48,32},{64,80},{80,64},{96,112},{112,96},{1... | collective-permute-start | bytes 393224 | tf_op jit(solution)/shard_map/ppermute | solution.py:43
  26.9 8.9 %collective-permute-start.14 = (bf16[32,2048]{1,0:T(8,128)(2,1)S(1)}, bf16[32,2048]{1,0:T(8,128)(2,1)S(1)}, u32[]{:S(2)}, u32[]{:S(2)}) collective-permute-start(bf16[32,2048]{1,0:T(8,128)(2,1)S(1)} %collective-permute-done.9.refs_3_), channel_id=1, source_target_pairs={{0,16},{16,0},{32,48},{48,32},{64,80},{80,64},{96,112},{112,96},{1... | collective-permute-start | bytes 393224 | tf_op jit(solution)/shard_map/ppermute | solution.py:43
  29.6 8.3 %collective-permute-start.11 = (bf16[32,2048]{1,0:T(8,128)(2,1)S(1)}, bf16[32,2048]{1,0:T(8,128)(2,1)S(1)}, u32[]{:S(2)}, u32[]{:S(2)}) collective-permute-start(bf16[32,2048]{1,0:T(8,128)(2,1)S(1)} %collective-permute-done.10.refs_4_), channel_id=1, source_target_pairs={{0,16},{16,0},{32,48},{48,32},{64,80},{80,64},{96,112},{112,96},{1... | collective-permute-start | bytes 393224 | tf_op jit(solution)/shard_map/ppermute | solution.py:43
  31.0 8.4 %collective-permute-start.16 = (bf16[32,2048]{1,0:T(8,128)(2,1)S(1)}, bf16[32,2048]{1,0:T(8,128)(2,1)S(1)}, u32[]{:S(2)}, u32[]{:S(2)}) collective-permute-start(bf16[32,2048]{1,0:T(8,128)(2,1)S(1)} %collective-permute-done.7.refs_2_), channel_id=1, source_target_pairs={{0,16},{16,0},{32,48},{48,32},{64,80},{80,64},{96,112},{112,96},{1... | collective-permute-start | bytes 393224 | tf_op jit(solution)/shard_map/ppermute | solution.py:43
  33.0 6.5 %collective-permute-start.17 = (bf16[32,2048]{1,0:T(8,128)(2,1)S(1)}, bf16[32,2048]{1,0:T(8,128)(2,1)S(1)}, u32[]{:S(2)}, u32[]{:S(2)}) collective-permute-start(bf16[32,2048]{1,0:T(8,128)(2,1)S(1)} %collective-permute-done.5.refs_1_), channel_id=1, source_target_pairs={{0,112},{16,32},{32,16},{48,64},{64,48},{80,96},{96,80},{112,0},{1... | collective-permute-start | bytes 393224 | tf_op jit(solution)/shard_map/ppermute | solution.py:47
  35.8 6.2 %collective-permute-start.15 = (bf16[32,2048]{1,0:T(8,128)(2,1)S(1)}, bf16[32,2048]{1,0:T(8,128)(2,1)S(1)}, u32[]{:S(2)}, u32[]{:S(2)}) collective-permute-start(bf16[32,2048]{1,0:T(8,128)(2,1)S(1)} %collective-permute-done.14.refs_3_), channel_id=1, source_target_pairs={{0,112},{16,32},{32,16},{48,64},{64,48},{80,96},{96,80},{112,0},{1... | collective-permute-start | bytes 393224 | tf_op jit(solution)/shard_map/ppermute | solution.py:47
  78.8 28.0 %collective-permute-start.19 = (bf16[512,2048]{1,0:T(8,128)(2,1)S(1)}, bf16[512,2048]{1,0:T(8,128)(2,1)S(1)}, u32[]{:S(2)}, u32[]{:S(2)}) collective-permute-start(bf16[512,2048]{1,0:T(8,128)(2,1)S(1)} %get-tuple-element.27.own_ref), channel_id=1, source_target_pairs={{0,8},{8,0},{1,9},{9,1},{2,10},{10,2},{3,11},{11,3},{4,12},{12,4},... | collective-permute-start | bytes 6291464 | tf_op jit(solution)/shard_map/ppermute | solution.py:39
  80.1 6.0 %collective-permute-start.20 = (bf16[32,2048]{1,0:T(8,128)(2,1)S(1)}, bf16[32,2048]{1,0:T(8,128)(2,1)S(1)}, u32[]{:S(2)}, u32[]{:S(2)}) collective-permute-start(bf16[32,2048]{1,0:T(8,128)(2,1)S(1)} %get-tuple-element.30), channel_id=1, source_target_pairs={{0,16},{16,0},{32,48},{48,32},{64,80},{80,64},{96,112},{112,96},{1... | collective-permute-start | bytes 393224 | tf_op jit(solution)/shard_map/ppermute | solution.py:43
  81.3 7.5 %collective-permute-start.24 = (bf16[32,2048]{1,0:T(8,128)(2,1)S(1)}, bf16[32,2048]{1,0:T(8,128)(2,1)S(1)}, u32[]{:S(2)}, u32[]{:S(2)}) collective-permute-start(bf16[32,2048]{1,0:T(8,128)(2,1)S(1)} %get-tuple-element.31), channel_id=1, source_target_pairs={{0,112},{16,32},{32,16},{48,64},{64,48},{80,96},{96,80},{112,0},{1... | collective-permute-start | bytes 393224 | tf_op jit(solution)/shard_map/ppermute | solution.py:47
  82.9 8.8 %collective-permute-start.31 = (bf16[32,2048]{1,0:T(8,128)(2,1)S(1)}, bf16[32,2048]{1,0:T(8,128)(2,1)S(1)}, u32[]{:S(2)}, u32[]{:S(2)}) collective-permute-start(bf16[32,2048]{1,0:T(8,128)(2,1)S(1)} %get-tuple-element.33), channel_id=1, source_target_pairs={{0,112},{16,32},{32,16},{48,64},{64,48},{80,96},{96,80},{112,0},{1... | collective-permute-start | bytes 393224 | tf_op jit(solution)/shard_map/ppermute | solution.py:47
  84.6 8.5 %collective-permute-start.28 = (bf16[32,2048]{1,0:T(8,128)(2,1)S(1)}, bf16[32,2048]{1,0:T(8,128)(2,1)S(1)}, u32[]{:S(2)}, u32[]{:S(2)}) collective-permute-start(bf16[32,2048]{1,0:T(8,128)(2,1)S(1)} %get-tuple-element.32), channel_id=1, source_target_pairs={{0,16},{16,0},{32,48},{48,32},{64,80},{80,64},{96,112},{112,96},{1... | collective-permute-start | bytes 393224 | tf_op jit(solution)/shard_map/ppermute | solution.py:43
  86.1 8.6 %collective-permute-start.21 = (bf16[32,2048]{1,0:T(8,128)(2,1)S(1)}, bf16[32,2048]{1,0:T(8,128)(2,1)S(1)}, u32[]{:S(2)}, u32[]{:S(2)}) collective-permute-start(bf16[32,2048]{1,0:T(8,128)(2,1)S(1)} %shard_map.65), channel_id=1, source_target_pairs={{0,112},{16,32},{32,16},{48,64},{64,48},{80,96},{96,80},{112,0},{1... | collective-permute-start | bytes 393224 | tf_op jit(solution)/shard_map/ppermute | solution.py:47
  88.9 7.4 %collective-permute-start.25 = (bf16[32,2048]{1,0:T(8,128)(2,1)S(1)}, bf16[32,2048]{1,0:T(8,128)(2,1)S(1)}, u32[]{:S(2)}, u32[]{:S(2)}) collective-permute-start(bf16[32,2048]{1,0:T(8,128)(2,1)S(1)} %shard_map.68), channel_id=1, source_target_pairs={{0,16},{16,0},{32,48},{48,32},{64,80},{80,64},{96,112},{112,96},{1... | collective-permute-start | bytes 393224 | tf_op jit(solution)/shard_map/ppermute | solution.py:43
  91.7 6.3 %collective-permute-start.32 = (bf16[32,2048]{1,0:T(8,128)(2,1)S(1)}, bf16[32,2048]{1,0:T(8,128)(2,1)S(1)}, u32[]{:S(2)}, u32[]{:S(2)}) collective-permute-start(bf16[32,2048]{1,0:T(8,128)(2,1)S(1)} %shard_map.73), channel_id=1, source_target_pairs={{0,16},{16,0},{32,48},{48,32},{64,80},{80,64},{96,112},{112,96},{1... | collective-permute-start | bytes 393224 | tf_op jit(solution)/shard_map/ppermute | solution.py:43
  93.1 7.5 %collective-permute-start.29 = (bf16[32,2048]{1,0:T(8,128)(2,1)S(1)}, bf16[32,2048]{1,0:T(8,128)(2,1)S(1)}, u32[]{:S(2)}, u32[]{:S(2)}) collective-permute-start(bf16[32,2048]{1,0:T(8,128)(2,1)S(1)} %shard_map.71), channel_id=1, source_target_pairs={{0,112},{16,32},{32,16},{48,64},{64,48},{80,96},{96,80},{112,0},{1... | collective-permute-start | bytes 393224 | tf_op jit(solution)/shard_map/ppermute | solution.py:47
  94.8 5.9 %collective-permute-start.22 = (bf16[32,2048]{1,0:T(8,128)(2,1)S(1)}, bf16[32,2048]{1,0:T(8,128)(2,1)S(1)}, u32[]{:S(2)}, u32[]{:S(2)}) collective-permute-start(bf16[32,2048]{1,0:T(8,128)(2,1)S(1)} %shard_map.66), channel_id=1, source_target_pairs={{0,16},{16,0},{32,48},{48,32},{64,80},{80,64},{96,112},{112,96},{1... | collective-permute-start | bytes 393224 | tf_op jit(solution)/shard_map/ppermute | solution.py:43
  96.4 7.2 %collective-permute-start.26 = (bf16[32,2048]{1,0:T(8,128)(2,1)S(1)}, bf16[32,2048]{1,0:T(8,128)(2,1)S(1)}, u32[]{:S(2)}, u32[]{:S(2)}) collective-permute-start(bf16[32,2048]{1,0:T(8,128)(2,1)S(1)} %shard_map.69), channel_id=1, source_target_pairs={{0,112},{16,32},{32,16},{48,64},{64,48},{80,96},{96,80},{112,0},{1... | collective-permute-start | bytes 393224 | tf_op jit(solution)/shard_map/ppermute | solution.py:47
  98.0 7.1 %collective-permute-start.33 = (bf16[32,2048]{1,0:T(8,128)(2,1)S(1)}, bf16[32,2048]{1,0:T(8,128)(2,1)S(1)}, u32[]{:S(2)}, u32[]{:S(2)}) collective-permute-start(bf16[32,2048]{1,0:T(8,128)(2,1)S(1)} %shard_map.74), channel_id=1, source_target_pairs={{0,112},{16,32},{32,16},{48,64},{64,48},{80,96},{96,80},{112,0},{1... | collective-permute-start | bytes 393224 | tf_op jit(solution)/shard_map/ppermute | solution.py:47
  100.6 5.0 %collective-permute-start.18 = (bf16[4,512,128]{2,1,0:T(8,128)(2,1)S(1)}, bf16[4,512,128]{2,1,0:T(8,128)(2,1)S(1)}, u32[]{:S(2)}, u32[]{:S(2)}) collective-permute-start(bf16[4,512,128]{2,1,0:T(8,128)(2,1)S(1)} %get-tuple-element.34), channel_id=1, source_target_pairs={{0,8},{8,0},{1,9},{9,1},{2,10},{10,2},{3,11},{11,3},{4,12},{12,4},... | collective-permute-start | bytes 1572872 | tf_op jit(solution)/shard_map/ppermute | solution.py:39
  100.7 10.7 %collective-permute-start.30 = (bf16[32,2048]{1,0:T(8,128)(2,1)S(1)}, bf16[32,2048]{1,0:T(8,128)(2,1)S(1)}, u32[]{:S(2)}, u32[]{:S(2)}) collective-permute-start(bf16[32,2048]{1,0:T(8,128)(2,1)S(1)} %shard_map.72), channel_id=1, source_target_pairs={{0,16},{16,0},{32,48},{48,32},{64,80},{80,64},{96,112},{112,96},{1... | collective-permute-start | bytes 393224 | tf_op jit(solution)/shard_map/ppermute | solution.py:43
  101.7 5.0 %copy-start = (bf16[512,2048]{1,0:T(8,128)(2,1)S(1)}, bf16[512,2048]{1,0:T(8,128)(2,1)}, u32[]{:S(2)}) copy-start(bf16[512,2048]{1,0:T(8,128)(2,1)} %act_ref.1) | copy-start | bytes 6291460
  103.6 7.8 %collective-permute-start.23 = (bf16[32,2048]{1,0:T(8,128)(2,1)S(1)}, bf16[32,2048]{1,0:T(8,128)(2,1)S(1)}, u32[]{:S(2)}, u32[]{:S(2)}) collective-permute-start(bf16[32,2048]{1,0:T(8,128)(2,1)S(1)} %shard_map.67), channel_id=1, source_target_pairs={{0,112},{16,32},{32,16},{48,64},{64,48},{80,96},{96,80},{112,0},{1... | collective-permute-start | bytes 393224 | tf_op jit(solution)/shard_map/ppermute | solution.py:47
  105.2 6.2 %collective-permute-start.27 = (bf16[32,2048]{1,0:T(8,128)(2,1)S(1)}, bf16[32,2048]{1,0:T(8,128)(2,1)S(1)}, u32[]{:S(2)}, u32[]{:S(2)}) collective-permute-start(bf16[32,2048]{1,0:T(8,128)(2,1)S(1)} %shard_map.70), channel_id=1, source_target_pairs={{0,144},{16,128},{32,176},{48,160},{64,208},{80,192},{96,240},{112... | collective-permute-start | bytes 393224 | tf_op jit(solution)/shard_map/ppermute | solution.py:52
  105.6 7.1 %collective-permute-start.34 = (bf16[32,2048]{1,0:T(8,128)(2,1)S(1)}, bf16[32,2048]{1,0:T(8,128)(2,1)S(1)}, u32[]{:S(2)}, u32[]{:S(2)}) collective-permute-start(bf16[32,2048]{1,0:T(8,128)(2,1)S(1)} %fusion.12), channel_id=1, source_target_pairs={{0,128},{128,0},{1,129},{129,1},{2,130},{130,2},{3,131},{131,3},{4... | collective-permute-start | bytes 393224 | tf_op jit(solution)/shard_map/ppermute | solution.py:39

commit v7 on v6

--- a/solution.py
+++ b/solution.py
@@ -14,7 +14,7 @@
 BF16, F32 = jnp.bfloat16, jnp.float32
 ORDER = [4, 3, -3, 2, -2, 1, -1, 0]
 KEYS = [(s, d) for d in ORDER for s in (0, 1)]
-LATE = 6
+LATE = 4
 VMEM = pl.BlockSpec(memory_space=pltpu.VMEM)
 ANY = pl.BlockSpec(memory_space=pl.ANY)
 PARAMS = pltpu.CompilerParams(vmem_limit_bytes=16 * 1024 * 1024)

time: 114 us -> 113 us (level)
  waiting for transfers between devices: 20.6 us -> 16.4 us
  starting transfers between devices: 42.3 us -> 44 us
    ppermute x14, starting transfers between devices: 28 us -> 34 us  [odd(): lax.ppermute(value, 'z', [(i, (i - 1 ^ 1) + 1 & 7) for i in range(8)])]
    ppermute x13, starting transfers between devices: 9.91 us -> 5.55 us  [even(): return lax.ppermute(value, 'z', [(i, i ^ 1) for i in range(8)])]
    ppermute x14, waiting for transfers between devices: 13.4 us -> 9.83 us  [odd(): lax.ppermute(value, 'z', [(i, (i - 1 ^ 1) + 1 & 7) for i in range(8)])]
  transfers between devices with their start and end apart: 35 -> 35, of which waited for: 14 -> 13; matrix products, arithmetic and copies ran while one was open for 0% -> 0% of each run, Pallas kernels for 8% -> 8%
where the time goes in v7:
time: 113 us; the launch traced here: 112 us
  starting transfers between devices  44 us (39%)
  blocking collectives  35.1 us (31%)
  waiting for transfers between devices  16.4 us (15%)
  Pallas kernels  11.7 us (10%)
  other arithmetic  3.99 us (4%)
    all_to_all x2, blocking collectives, exchange(): return lax.all_to_all(value, REP, split_axis=0, concat_axis=0)  35.1 us
    ppermute x14, starting transfers between devices, odd(): lax.ppermute(value, 'z', [(i, (i - 1 ^ 1) + 1 & 7) for i in range(8)])  34 us
    ppermute x14, waiting for transfers between devices, odd(): lax.ppermute(value, 'z', [(i, (i - 1 ^ 1) + 1 & 7) for i in range(8)])  9.83 us
    ppermute x13, waiting for transfers between devices, even(): return lax.ppermute(value, 'z', [(i, i ^ 1) for i in range(8)])  5.89 us
    ppermute x13, starting transfers between devices, even(): return lax.ppermute(value, 'z', [(i, i ^ 1) for i in range(8)])  5.55 us
    pallas_call x1, Pallas kernels, query_grads(): pl.pallas_call(query_kernel, out_shape=shape((512, 2048), BF16), in_specs...  4.57 us
    ppermute x7, starting transfers between devices, swap(): return lax.ppermute(value, axis, [(0, 1), (1, 0)])  4.11 us
    convert_element_type x2, other arithmetic, saturate(): jnp.where(wide < 2.0 ** (-8), small, jnp.log(1.0 + wide)).astype(BF16)  3.17 us
  transfers between devices with their start and end apart: 35, of which 13 were waited for; matrix products, arithmetic and copies ran while one was open for 0% of the time, Pallas kernels for 8%

profile of v7, /device:TPU:8, one launch (start us, length us, event | category | flops | bytes accessed | tf_op | source)
XLA Modules:
  0.0 112.2 jit_solution(2760048984535158952)
XLA Ops:
  0.7 3.1 %fusion.1.mine_ref = bf16[512,2048]{1,0:T(8,128)(2,1)S(1)} fusion(bf16[512,2048]{1,0:T(8,128)(2,1)} %act_ref.1), kind=kLoop, calls=%fused_computation.2 | loop fusion | flops 9437184 | bytes 4194304 | tf_op jit(solution)/shard_map/convert_element_type | solution.py:30
  4.0 2.3 %collective-permute-start.4 = (bf16[32,2048]{1,0:T(8,128)(2,1)S(1)}, bf16[32,2048]{1,0:T(8,128)(2,1)S(1)}, u32[]{:S(2)}, u32[]{:S(2)}) collective-permute-start(bf16[32,2048]{1,0:T(8,128)(2,1)S(1)} %fusion.8.refs_10_), channel_id=1, source_target_pairs={{0,128},{128,0},{1,129},{129,1},{2,130},{130,2},{3,131},{131,3},{4... | collective-permute-start | bytes 393224 | tf_op jit(solution)/shard_map/ppermute | solution.py:39
  6.2 4.1 %collective-permute-start.1 = (bf16[32,2048]{1,0:T(8,128)(2,1)S(1)}, bf16[32,2048]{1,0:T(8,128)(2,1)S(1)}, u32[]{:S(2)}, u32[]{:S(2)}) collective-permute-start(bf16[32,2048]{1,0:T(8,128)(2,1)S(1)} %fusion.8.refs_10_), channel_id=1, source_target_pairs={{0,112},{16,32},{32,16},{48,64},{64,48},{80,96},{96,80},{112,0},{1... | collective-permute-start | bytes 393224 | tf_op jit(solution)/shard_map/ppermute | solution.py:47
  10.4 1.5 %collective-permute-start.10 = (bf16[32,2048]{1,0:T(8,128)(2,1)S(1)}, bf16[32,2048]{1,0:T(8,128)(2,1)S(1)}, u32[]{:S(2)}, u32[]{:S(2)}) collective-permute-start(bf16[32,2048]{1,0:T(8,128)(2,1)S(1)} %collective-permute-done.4.refs_11_), channel_id=1, source_target_pairs={{0,16},{16,0},{32,48},{48,32},{64,80},{80,64},{96,112},{112,96},{1... | collective-permute-start | bytes 393224 | tf_op jit(solution)/shard_map/ppermute | solution.py:43
  11.9 0.5 collective-permute-start.14
  12.4 1.8 %collective-permute-done.1.refs_8_ = bf16[32,2048]{1,0:T(8,128)(2,1)S(1)} collective-permute-done((bf16[32,2048]{1,0:T(8,128)(2,1)S(1)}, bf16[32,2048]{1,0:T(8,128)(2,1)S(1)}, u32[]{:S(2)}, u32[]{:S(2)}) %collective-permute-start.1) | collective-permute-done | bytes 131104 | tf_op jit(solution)/shard_map/ppermute | solution.py:47
  14.2 4.1 %collective-permute-start.5 = (bf16[32,2048]{1,0:T(8,128)(2,1)S(1)}, bf16[32,2048]{1,0:T(8,128)(2,1)S(1)}, u32[]{:S(2)}, u32[]{:S(2)}) collective-permute-start(bf16[32,2048]{1,0:T(8,128)(2,1)S(1)} %collective-permute-done.4.refs_11_), channel_id=1, source_target_pairs={{0,112},{16,32},{32,16},{48,64},{64,48},{80,96},{96,80},{112,0},{1... | collective-permute-start | bytes 393224 | tf_op jit(solution)/shard_map/ppermute | solution.py:47
  18.3 3.5 %collective-permute-start.11 = (bf16[32,2048]{1,0:T(8,128)(2,1)S(1)}, bf16[32,2048]{1,0:T(8,128)(2,1)S(1)}, u32[]{:S(2)}, u32[]{:S(2)}) collective-permute-start(bf16[32,2048]{1,0:T(8,128)(2,1)S(1)} %collective-permute-done.10.refs_7_), channel_id=1, source_target_pairs={{0,112},{16,32},{32,16},{48,64},{64,48},{80,96},{96,80},{112,0},{1... | collective-permute-start | bytes 393224 | tf_op jit(solution)/shard_map/ppermute | solution.py:47
  21.8 2.8 %collective-permute-start.3 = (bf16[32,2048]{1,0:T(8,128)(2,1)S(1)}, bf16[32,2048]{1,0:T(8,128)(2,1)S(1)}, u32[]{:S(2)}, u32[]{:S(2)}) collective-permute-start(bf16[32,2048]{1,0:T(8,128)(2,1)S(1)} %collective-permute-done.2.refs_2_), channel_id=1, source_target_pairs={{0,112},{16,32},{32,16},{48,64},{64,48},{80,96},{96,80},{112,0},{1... | collective-permute-start | bytes 393224 | tf_op jit(solution)/shard_map/ppermute | solution.py:47
  24.6 2.0 %collective-permute-start.9 = (bf16[32,2048]{1,0:T(8,128)(2,1)S(1)}, bf16[32,2048]{1,0:T(8,128)(2,1)S(1)}, u32[]{:S(2)}, u32[]{:S(2)}) collective-permute-start(bf16[32,2048]{1,0:T(8,128)(2,1)S(1)} %collective-permute-done.8.refs_6_), channel_id=1, source_target_pairs={{0,112},{16,32},{32,16},{48,64},{64,48},{80,96},{96,80},{112,0},{1... | collective-permute-start | bytes 393224 | tf_op jit(solution)/shard_map/ppermute | solution.py:47
  26.7 1.0 collective-permute-start.15
  27.7 1.7 %collective-permute-done.3.refs_0_ = bf16[32,2048]{1,0:T(8,128)(2,1)S(1)} collective-permute-done((bf16[32,2048]{1,0:T(8,128)(2,1)S(1)}, bf16[32,2048]{1,0:T(8,128)(2,1)S(1)}, u32[]{:S(2)}, u32[]{:S(2)}) %collective-permute-start.3) | collective-permute-done | bytes 131104 | tf_op jit(solution)/shard_map/ppermute | solution.py:47
  29.3 1.7 %collective-permute-done.6.refs_3_ = bf16[32,2048]{1,0:T(8,128)(2,1)S(1)} collective-permute-done((bf16[32,2048]{1,0:T(8,128)(2,1)S(1)}, bf16[32,2048]{1,0:T(8,128)(2,1)S(1)}, u32[]{:S(2)}, u32[]{:S(2)}) %collective-permute-start.6) | collective-permute-done | bytes 131104 | tf_op jit(solution)/shard_map/ppermute | solution.py:43
  31.0 1.1 %collective-permute-start.7 = (bf16[32,2048]{1,0:T(8,128)(2,1)S(1)}, bf16[32,2048]{1,0:T(8,128)(2,1)S(1)}, u32[]{:S(2)}, u32[]{:S(2)}) collective-permute-start(bf16[32,2048]{1,0:T(8,128)(2,1)S(1)} %collective-permute-done.6.refs_3_), channel_id=1, source_target_pairs={{0,112},{16,32},{32,16},{48,64},{64,48},{80,96},{96,80},{112,0},{1... | collective-permute-start | bytes 393224 | tf_op jit(solution)/shard_map/ppermute | solution.py:47
  32.2 0.7 collective-permute-start.17
  32.9 0.9 collective-permute-done.15.refs_3_
  33.8 1.3 %collective-permute-start.16 = (bf16[32,2048]{1,0:T(8,128)(2,1)S(1)}, bf16[32,2048]{1,0:T(8,128)(2,1)S(1)}, u32[]{:S(2)}, u32[]{:S(2)}) collective-permute-start(bf16[32,2048]{1,0:T(8,128)(2,1)S(1)} %collective-permute-done.15.refs_3_), channel_id=1, source_target_pairs={{0,112},{16,32},{32,16},{48,64},{64,48},{80,96},{96,80},{112,0},{1... | collective-permute-start | bytes 393224 | tf_op jit(solution)/shard_map/ppermute | solution.py:47
  35.1 1.3 %collective-permute-done.12.refs_0_ = bf16[32,2048]{1,0:T(8,128)(2,1)S(1)} collective-permute-done((bf16[32,2048]{1,0:T(8,128)(2,1)S(1)}, bf16[32,2048]{1,0:T(8,128)(2,1)S(1)}, u32[]{:S(2)}, u32[]{:S(2)}) %collective-permute-start.12) | collective-permute-done | bytes 131104 | tf_op jit(solution)/shard_map/ppermute | solution.py:43
  36.4 0.9 collective-permute-done.7.refs_1_
  37.3 1.8 %shard_map.59 = (f32[4,384,256]{2,1,0:T(8,128)S(1)}, bf16[512,2048]{1,0:T(8,128)(2,1)S(1)}) custom-call(bf16[512,2048]{1,0:T(8,128)(2,1)S(1)} %fusion.1.mine_ref, bf16[512,2048]{1,0:T(8,128)(2,1)S(1)} %collective-permute-done.other_ref, bf16[32,2048]{1,0:T(8,128)(2,1)S(1)} %collective-permute-done.3.refs_0_, ...), custom_call_target="tpu_custom_call" | custom-call | tf_op jit(solution)/shard_map/pallas_call | solution.py:109
  39.2 0.8 collective-permute-done.16.refs_1_
  40.0 2.0 %shard_map.60 = (s16[8,528,128]{2,1,0:T(8,128)(2,1)S(1)}, bf16[512,2048]{1,0:T(8,128)(2,1)S(1)}) custom-call(bf16[512,2048]{1,0:T(8,128)(2,1)S(1)} %fusion.1.mine_ref, bf16[512,2048]{1,0:T(8,128)(2,1)S(1)} %collective-permute-done.other_ref, f32[4,384,256]{2,1,0:T(8,128)S(1)} %get-tuple-element.18.early_ref, ...), custom_call_target="tpu_custom_call", output_to_operand_aliasing={{1}: (3, {})} | custom-call | tf_op jit(solution)/shard_map/pallas_call | solution.py:116
  42.0 20.0 %all_to_all.10.pieces_ref = s16[8,528,128]{2,1,0:T(8,128)(2,1)S(1)} all-to-all(s16[8,528,128]{2,1,0:T(8,128)(2,1)S(1)} %get-tuple-element.21), channel_id=1, replica_groups=mesh['ylo'=2,'z'=8,'core'=2,'yhi'=2,'x'=4] {'x','yhi'}, dimensions={0} | all-to-all | bytes 2162688 | tf_op jit(solution)/shard_map/all_to_all | solution.py:56
  62.0 0.6 shard_map.61
  62.7 15.1 %all_to_all.11.grad_ref = bf16[8,512,128]{2,1,0:T(8,128)(2,1)S(1)} all-to-all(bf16[8,512,128]{2,1,0:T(8,128)(2,1)S(1)} %shard_map.61), channel_id=1, replica_groups=mesh['ylo'=2,'z'=8,'core'=2,'yhi'=2,'x'=4] {'x','yhi'}, dimensions={0} | all-to-all | bytes 2097152 | tf_op jit(solution)/shard_map/all_to_all | solution.py:56
  77.7 1.2 %shard_map.64 = (f32[8,32,2048]{2,1,0:T(8,128)S(1)}, bf16[32,2048]{1,0:T(8,128)(2,1)S(1)}, bf16[32,2048]{1,0:T(8,128)(2,1)S(1)}, bf16[32,2048]{1,0:T(8,128)(2,1)S(1)}, bf16[32,2048]{1,0:T(8,128)(2,1)S(1)}) custom-call(bf16[8,512,128]{2,1,0:T(8,128)(2,1)S(1)} %all_to_all.11.grad_ref, bf16[512,2048]{1,0:T(8,128)(2,1)S(1)} %fusion.1.mine_ref, ...), custom_call_target="tpu_custom_call" | custom-call | tf_op jit(solution)/shard_map/pallas_call | solution.py:175
  79.0 0.9 collective-permute-start.20
  79.9 2.2 %collective-permute-start.24 = (bf16[32,2048]{1,0:T(8,128)(2,1)S(1)}, bf16[32,2048]{1,0:T(8,128)(2,1)S(1)}, u32[]{:S(2)}, u32[]{:S(2)}) collective-permute-start(bf16[32,2048]{1,0:T(8,128)(2,1)S(1)} %get-tuple-element.31), channel_id=1, source_target_pairs={{0,112},{16,32},{32,16},{48,64},{64,48},{80,96},{96,80},{112,0},{1... | collective-permute-start | bytes 393224 | tf_op jit(solution)/shard_map/ppermute | solution.py:47
  82.1 1.0 collective-permute-start.31
  83.1 1.9 %collective-permute-done.20.refs_1_ = bf16[32,2048]{1,0:T(8,128)(2,1)S(1)} collective-permute-done((bf16[32,2048]{1,0:T(8,128)(2,1)S(1)}, bf16[32,2048]{1,0:T(8,128)(2,1)S(1)}, u32[]{:S(2)}, u32[]{:S(2)}) %collective-permute-start.20) | collective-permute-done | bytes 131104 | tf_op jit(solution)/shard_map/ppermute | solution.py:43
  85.0 2.7 %collective-permute-start.21 = (bf16[32,2048]{1,0:T(8,128)(2,1)S(1)}, bf16[32,2048]{1,0:T(8,128)(2,1)S(1)}, u32[]{:S(2)}, u32[]{:S(2)}) collective-permute-start(bf16[32,2048]{1,0:T(8,128)(2,1)S(1)} %shard_map.65), channel_id=1, source_target_pairs={{0,112},{16,32},{32,16},{48,64},{64,48},{80,96},{96,80},{112,0},{1... | collective-permute-start | bytes 393224 | tf_op jit(solution)/shard_map/ppermute | solution.py:47
  87.8 2.4 %collective-permute-done.31.refs_1_ = bf16[32,2048]{1,0:T(8,128)(2,1)S(1)} collective-permute-done((bf16[32,2048]{1,0:T(8,128)(2,1)S(1)}, bf16[32,2048]{1,0:T(8,128)(2,1)S(1)}, u32[]{:S(2)}, u32[]{:S(2)}) %collective-permute-start.31) | collective-permute-done | bytes 131104 | tf_op jit(solution)/shard_map/ppermute | solution.py:47
  90.2 0.1 collective-permute-start.32
  90.4 1.2 %shard_map.63.refs_0_ = f32[8,32,2048]{2,1,0:T(8,128)S(1)} custom-call(bf16[8,512,128]{2,1,0:T(8,128)(2,1)S(1)} %all_to_all.11.grad_ref, bf16[512,2048]{1,0:T(8,128)(2,1)S(1)} %fusion.1.mine_ref, bf16[512,2048]{1,0:T(8,128)(2,1)S(1)} %collective-permute-done.other_ref), custom_call_target="tpu_custom_call" | custom-call | tf_op jit(solution)/shard_map/pallas_call | solution.py:175
  91.7 2.7 %collective-permute-start.29 = (bf16[32,2048]{1,0:T(8,128)(2,1)S(1)}, bf16[32,2048]{1,0:T(8,128)(2,1)S(1)}, u32[]{:S(2)}, u32[]{:S(2)}) collective-permute-start(bf16[32,2048]{1,0:T(8,128)(2,1)S(1)} %shard_map.71), channel_id=1, source_target_pairs={{0,112},{16,32},{32,16},{48,64},{64,48},{80,96},{96,80},{112,0},{1... | collective-permute-start | bytes 393224 | tf_op jit(solution)/shard_map/ppermute | solution.py:47
  94.4 0.4 collective-permute-start.22
  94.8 2.1 %collective-permute-start.26 = (bf16[32,2048]{1,0:T(8,128)(2,1)S(1)}, bf16[32,2048]{1,0:T(8,128)(2,1)S(1)}, u32[]{:S(2)}, u32[]{:S(2)}) collective-permute-start(bf16[32,2048]{1,0:T(8,128)(2,1)S(1)} %shard_map.69), channel_id=1, source_target_pairs={{0,112},{16,32},{32,16},{48,64},{64,48},{80,96},{96,80},{112,0},{1... | collective-permute-start | bytes 393224 | tf_op jit(solution)/shard_map/ppermute | solution.py:47
  97.0 1.8 %collective-permute-start.33 = (bf16[32,2048]{1,0:T(8,128)(2,1)S(1)}, bf16[32,2048]{1,0:T(8,128)(2,1)S(1)}, u32[]{:S(2)}, u32[]{:S(2)}) collective-permute-start(bf16[32,2048]{1,0:T(8,128)(2,1)S(1)} %shard_map.74), channel_id=1, source_target_pairs={{0,112},{16,32},{32,16},{48,64},{64,48},{80,96},{96,80},{112,0},{1... | collective-permute-start | bytes 393224 | tf_op jit(solution)/shard_map/ppermute | solution.py:47
  98.9 0.3 collective-permute-done.29.refs_1_
  99.3 0.2 collective-permute-done.22.refs_1_
  99.4 0.8 collective-permute-start.30
  100.3 1.9 %collective-permute-done.26.refs_1_ = bf16[32,2048]{1,0:T(8,128)(2,1)S(1)} collective-permute-done((bf16[32,2048]{1,0:T(8,128)(2,1)S(1)}, bf16[32,2048]{1,0:T(8,128)(2,1)S(1)}, u32[]{:S(2)}, u32[]{:S(2)}) %collective-permute-start.26) | collective-permute-done | bytes 131104 | tf_op jit(solution)/shard_map/ppermute | solution.py:47
  102.1 2.4 %collective-permute-start.23 = (bf16[32,2048]{1,0:T(8,128)(2,1)S(1)}, bf16[32,2048]{1,0:T(8,128)(2,1)S(1)}, u32[]{:S(2)}, u32[]{:S(2)}) collective-permute-start(bf16[32,2048]{1,0:T(8,128)(2,1)S(1)} %shard_map.67), channel_id=1, source_target_pairs={{0,112},{16,32},{32,16},{48,64},{64,48},{80,96},{96,80},{112,0},{1... | collective-permute-start | bytes 393224 | tf_op jit(solution)/shard_map/ppermute | solution.py:47
  104.6 0.3 collective-permute-start.27
  104.9 1.2 %collective-permute-start.34 = (bf16[32,2048]{1,0:T(8,128)(2,1)S(1)}, bf16[32,2048]{1,0:T(8,128)(2,1)S(1)}, u32[]{:S(2)}, u32[]{:S(2)}) collective-permute-start(bf16[32,2048]{1,0:T(8,128)(2,1)S(1)} %fusion.12), channel_id=1, source_target_pairs={{0,128},{128,0},{1,129},{129,1},{2,130},{130,2},{3,131},{131,3},{4... | collective-permute-start | bytes 393224 | tf_op jit(solution)/shard_map/ppermute | solution.py:39
  106.2 4.6 %shard_map.62 = bf16[512,2048]{1,0:T(8,128)(2,1)} custom-call(bf16[512,2048]{1,0:T(8,128)(2,1)S(1)} %copy-done, bf16[4,512,128]{2,1,0:T(8,128)(2,1)S(1)} %get-tuple-element.35.own_grad_ref, bf16[4,512,128]{2,1,0:T(8,128)(2,1)S(1)} %collective-permute-done.18.other_grad_ref, bf16[512,2048]{1,0:T(8,128)(2,1)S(1)} %get-tuple-element.27.own_ref, ...), custom_call_target="tpu_custom_call" | custom-call | tf_op jit(solution)/shard_map/pallas_call | solution.py:221
  110.8 0.7 collective-permute-done.34
  111.4 0.8 fusion.13
  (54 shorter events, 0.8 us)
Async XLA Ops:
  0.6 3.2 %copy-start.3 = (bf16[32,2048]{1,0:T(8,128)(2,1)S(1)}, bf16[32,2048]{1,0:T(8,128)(2,1)}, u32[]{:S(2)}) copy-start(bf16[32,2048]{1,0:T(8,128)(2,1)} %param.5) | copy-start | bytes 393220
  0.6 11.2 %copy-start.1 = (f32[512]{0:T(512)S(1)}, f32[512]{0:T(512)}, u32[]{:S(2)}) copy-start(f32[512]{0:T(512)} %param.7) | copy-start | bytes 6148
  0.7 11.2 %copy-start.2 = (s32[512]{0:T(512)S(1)}, s32[512]{0:T(512)}, u32[]{:S(2)}) copy-start(s32[512]{0:T(512)} %param.6) | copy-start | bytes 6148
  3.7 33.6 %collective-permute-start = (bf16[512,2048]{1,0:T(8,128)(2,1)S(1)}, bf16[512,2048]{1,0:T(8,128)(2,1)S(1)}, u32[]{:S(2)}, u32[]{:S(2)}) collective-permute-start(bf16[512,2048]{1,0:T(8,128)(2,1)S(1)} %fusion.1.mine_ref), channel_id=1, source_target_pairs={{0,8},{8,0},{1,9},{9,1},{2,10},{10,2},{3,11},{11,3},{4,12},{12,4},... | collective-permute-start | bytes 6291464 | tf_op jit(solution)/shard_map/ppermute | solution.py:39
  4.0 6.4 %collective-permute-start.4 = (bf16[32,2048]{1,0:T(8,128)(2,1)S(1)}, bf16[32,2048]{1,0:T(8,128)(2,1)S(1)}, u32[]{:S(2)}, u32[]{:S(2)}) collective-permute-start(bf16[32,2048]{1,0:T(8,128)(2,1)S(1)} %fusion.8.refs_10_), channel_id=1, source_target_pairs={{0,128},{128,0},{1,129},{129,1},{2,130},{130,2},{3,131},{131,3},{4... | collective-permute-start | bytes 393224 | tf_op jit(solution)/shard_map/ppermute | solution.py:39
  6.2 8.0 %collective-permute-start.1 = (bf16[32,2048]{1,0:T(8,128)(2,1)S(1)}, bf16[32,2048]{1,0:T(8,128)(2,1)S(1)}, u32[]{:S(2)}, u32[]{:S(2)}) collective-permute-start(bf16[32,2048]{1,0:T(8,128)(2,1)S(1)} %fusion.8.refs_10_), channel_id=1, source_target_pairs={{0,112},{16,32},{32,16},{48,64},{64,48},{80,96},{96,80},{112,0},{1... | collective-permute-start | bytes 393224 | tf_op jit(solution)/shard_map/ppermute | solution.py:47
  10.4 8.0 %collective-permute-start.10 = (bf16[32,2048]{1,0:T(8,128)(2,1)S(1)}, bf16[32,2048]{1,0:T(8,128)(2,1)S(1)}, u32[]{:S(2)}, u32[]{:S(2)}) collective-permute-start(bf16[32,2048]{1,0:T(8,128)(2,1)S(1)} %collective-permute-done.4.refs_11_), channel_id=1, source_target_pairs={{0,16},{16,0},{32,48},{48,32},{64,80},{80,64},{96,112},{112,96},{1... | collective-permute-start | bytes 393224 | tf_op jit(solution)/shard_map/ppermute | solution.py:43
  11.8 2.4 %collective-permute-start.13 = (f32[512]{0:T(512)S(1)}, f32[512]{0:T(512)S(1)}, u32[]{:S(2)}, u32[]{:S(2)}) collective-permute-start(f32[512]{0:T(512)S(1)} %copy-done.1), channel_id=1, source_target_pairs={{0,8},{8,0},{1,9},{9,1},{2,10},{10,2},{3,11},{11,3},{4,12},{12,4},... | collective-permute-start | bytes 6152 | tf_op jit(solution)/shard_map/ppermute | solution.py:39
  11.9 6.5 %collective-permute-start.14 = (s32[512]{0:T(512)S(1)}, s32[512]{0:T(512)S(1)}, u32[]{:S(2)}, u32[]{:S(2)}) collective-permute-start(s32[512]{0:T(512)S(1)} %copy-done.2), channel_id=1, source_target_pairs={{0,8},{8,0},{1,9},{9,1},{2,10},{10,2},{3,11},{11,3},{4,12},{12,4},... | collective-permute-start | bytes 6152 | tf_op jit(solution)/shard_map/ppermute | solution.py:39
  14.2 7.6 %collective-permute-start.2 = (bf16[32,2048]{1,0:T(8,128)(2,1)S(1)}, bf16[32,2048]{1,0:T(8,128)(2,1)S(1)}, u32[]{:S(2)}, u32[]{:S(2)}) collective-permute-start(bf16[32,2048]{1,0:T(8,128)(2,1)S(1)} %collective-permute-done.1.refs_8_), channel_id=1, source_target_pairs={{0,16},{16,0},{32,48},{48,32},{64,80},{80,64},{96,112},{112,96},{1... | collective-permute-start | bytes 393224 | tf_op jit(solution)/shard_map/ppermute | solution.py:43
  14.2 10.4 %collective-permute-start.5 = (bf16[32,2048]{1,0:T(8,128)(2,1)S(1)}, bf16[32,2048]{1,0:T(8,128)(2,1)S(1)}, u32[]{:S(2)}, u32[]{:S(2)}) collective-permute-start(bf16[32,2048]{1,0:T(8,128)(2,1)S(1)} %collective-permute-done.4.refs_11_), channel_id=1, source_target_pairs={{0,112},{16,32},{32,16},{48,64},{64,48},{80,96},{96,80},{112,0},{1... | collective-permute-start | bytes 393224 | tf_op jit(solution)/shard_map/ppermute | solution.py:47
  18.3 6.3 %collective-permute-start.8 = (bf16[32,2048]{1,0:T(8,128)(2,1)S(1)}, bf16[32,2048]{1,0:T(8,128)(2,1)S(1)}, u32[]{:S(2)}, u32[]{:S(2)}) collective-permute-start(bf16[32,2048]{1,0:T(8,128)(2,1)S(1)} %fusion.8.refs_10_), channel_id=1, source_target_pairs={{0,16},{16,0},{32,48},{48,32},{64,80},{80,64},{96,112},{112,96},{1... | collective-permute-start | bytes 393224 | tf_op jit(solution)/shard_map/ppermute | solution.py:43
  18.3 8.3 %collective-permute-start.11 = (bf16[32,2048]{1,0:T(8,128)(2,1)S(1)}, bf16[32,2048]{1,0:T(8,128)(2,1)S(1)}, u32[]{:S(2)}, u32[]{:S(2)}) collective-permute-start(bf16[32,2048]{1,0:T(8,128)(2,1)S(1)} %collective-permute-done.10.refs_7_), channel_id=1, source_target_pairs={{0,112},{16,32},{32,16},{48,64},{64,48},{80,96},{96,80},{112,0},{1... | collective-permute-start | bytes 393224 | tf_op jit(solution)/shard_map/ppermute | solution.py:47
  21.8 7.5 %collective-permute-start.3 = (bf16[32,2048]{1,0:T(8,128)(2,1)S(1)}, bf16[32,2048]{1,0:T(8,128)(2,1)S(1)}, u32[]{:S(2)}, u32[]{:S(2)}) collective-permute-start(bf16[32,2048]{1,0:T(8,128)(2,1)S(1)} %collective-permute-done.2.refs_2_), channel_id=1, source_target_pairs={{0,112},{16,32},{32,16},{48,64},{64,48},{80,96},{96,80},{112,0},{1... | collective-permute-start | bytes 393224 | tf_op jit(solution)/shard_map/ppermute | solution.py:47
  24.6 6.4 %collective-permute-start.6 = (bf16[32,2048]{1,0:T(8,128)(2,1)S(1)}, bf16[32,2048]{1,0:T(8,128)(2,1)S(1)}, u32[]{:S(2)}, u32[]{:S(2)}) collective-permute-start(bf16[32,2048]{1,0:T(8,128)(2,1)S(1)} %collective-permute-done.5.refs_9_), channel_id=1, source_target_pairs={{0,16},{16,0},{32,48},{48,32},{64,80},{80,64},{96,112},{112,96},{1... | collective-permute-start | bytes 393224 | tf_op jit(solution)/shard_map/ppermute | solution.py:43
  24.6 7.5 %collective-permute-start.9 = (bf16[32,2048]{1,0:T(8,128)(2,1)S(1)}, bf16[32,2048]{1,0:T(8,128)(2,1)S(1)}, u32[]{:S(2)}, u32[]{:S(2)}) collective-permute-start(bf16[32,2048]{1,0:T(8,128)(2,1)S(1)} %collective-permute-done.8.refs_6_), channel_id=1, source_target_pairs={{0,112},{16,32},{32,16},{48,64},{64,48},{80,96},{96,80},{112,0},{1... | collective-permute-start | bytes 393224 | tf_op jit(solution)/shard_map/ppermute | solution.py:47
  26.7 7.2 %collective-permute-start.15 = (bf16[32,2048]{1,0:T(8,128)(2,1)S(1)}, bf16[32,2048]{1,0:T(8,128)(2,1)S(1)}, u32[]{:S(2)}, u32[]{:S(2)}) collective-permute-start(bf16[32,2048]{1,0:T(8,128)(2,1)S(1)} %collective-permute-done.11.refs_5_), channel_id=1, source_target_pairs={{0,16},{16,0},{32,48},{48,32},{64,80},{80,64},{96,112},{112,96},{1... | collective-permute-start | bytes 393224 | tf_op jit(solution)/shard_map/ppermute | solution.py:43
  29.3 7.1 %collective-permute-start.12 = (bf16[32,2048]{1,0:T(8,128)(2,1)S(1)}, bf16[32,2048]{1,0:T(8,128)(2,1)S(1)}, u32[]{:S(2)}, u32[]{:S(2)}) collective-permute-start(bf16[32,2048]{1,0:T(8,128)(2,1)S(1)} %collective-permute-done.3.refs_0_), channel_id=1, source_target_pairs={{0,16},{16,0},{32,48},{48,32},{64,80},{80,64},{96,112},{112,96},{1... | collective-permute-start | bytes 393224 | tf_op jit(solution)/shard_map/ppermute | solution.py:43
  31.0 6.3 %collective-permute-start.7 = (bf16[32,2048]{1,0:T(8,128)(2,1)S(1)}, bf16[32,2048]{1,0:T(8,128)(2,1)S(1)}, u32[]{:S(2)}, u32[]{:S(2)}) collective-permute-start(bf16[32,2048]{1,0:T(8,128)(2,1)S(1)} %collective-permute-done.6.refs_3_), channel_id=1, source_target_pairs={{0,112},{16,32},{32,16},{48,64},{64,48},{80,96},{96,80},{112,0},{1... | collective-permute-start | bytes 393224 | tf_op jit(solution)/shard_map/ppermute | solution.py:47
  32.2 7.0 %collective-permute-start.17 = (bf16[32,2048]{1,0:T(8,128)(2,1)S(1)}, bf16[32,2048]{1,0:T(8,128)(2,1)S(1)}, u32[]{:S(2)}, u32[]{:S(2)}) collective-permute-start(bf16[32,2048]{1,0:T(8,128)(2,1)S(1)} %collective-permute-done.9.refs_4_), channel_id=1, source_target_pairs={{0,16},{16,0},{32,48},{48,32},{64,80},{80,64},{96,112},{112,96},{1... | collective-permute-start | bytes 393224 | tf_op jit(solution)/shard_map/ppermute | solution.py:43
  33.8 6.2 %collective-permute-start.16 = (bf16[32,2048]{1,0:T(8,128)(2,1)S(1)}, bf16[32,2048]{1,0:T(8,128)(2,1)S(1)}, u32[]{:S(2)}, u32[]{:S(2)}) collective-permute-start(bf16[32,2048]{1,0:T(8,128)(2,1)S(1)} %collective-permute-done.15.refs_3_), channel_id=1, source_target_pairs={{0,112},{16,32},{32,16},{48,64},{64,48},{80,96},{96,80},{112,0},{1... | collective-permute-start | bytes 393224 | tf_op jit(solution)/shard_map/ppermute | solution.py:47
  77.7 28.4 %collective-permute-start.19 = (bf16[512,2048]{1,0:T(8,128)(2,1)S(1)}, bf16[512,2048]{1,0:T(8,128)(2,1)S(1)}, u32[]{:S(2)}, u32[]{:S(2)}) collective-permute-start(bf16[512,2048]{1,0:T(8,128)(2,1)S(1)} %get-tuple-element.27.own_ref), channel_id=1, source_target_pairs={{0,8},{8,0},{1,9},{9,1},{2,10},{10,2},{3,11},{11,3},{4,12},{12,4},... | collective-permute-start | bytes 6291464 | tf_op jit(solution)/shard_map/ppermute | solution.py:39
  79.0 6.0 %collective-permute-start.20 = (bf16[32,2048]{1,0:T(8,128)(2,1)S(1)}, bf16[32,2048]{1,0:T(8,128)(2,1)S(1)}, u32[]{:S(2)}, u32[]{:S(2)}) collective-permute-start(bf16[32,2048]{1,0:T(8,128)(2,1)S(1)} %get-tuple-element.30), channel_id=1, source_target_pairs={{0,16},{16,0},{32,48},{48,32},{64,80},{80,64},{96,112},{112,96},{1... | collective-permute-start | bytes 393224 | tf_op jit(solution)/shard_map/ppermute | solution.py:43
  79.9 7.9 %collective-permute-start.24 = (bf16[32,2048]{1,0:T(8,128)(2,1)S(1)}, bf16[32,2048]{1,0:T(8,128)(2,1)S(1)}, u32[]{:S(2)}, u32[]{:S(2)}) collective-permute-start(bf16[32,2048]{1,0:T(8,128)(2,1)S(1)} %get-tuple-element.31), channel_id=1, source_target_pairs={{0,112},{16,32},{32,16},{48,64},{64,48},{80,96},{96,80},{112,0},{1... | collective-permute-start | bytes 393224 | tf_op jit(solution)/shard_map/ppermute | solution.py:47
  82.1 8.1 %collective-permute-start.31 = (bf16[32,2048]{1,0:T(8,128)(2,1)S(1)}, bf16[32,2048]{1,0:T(8,128)(2,1)S(1)}, u32[]{:S(2)}, u32[]{:S(2)}) collective-permute-start(bf16[32,2048]{1,0:T(8,128)(2,1)S(1)} %get-tuple-element.33), channel_id=1, source_target_pairs={{0,112},{16,32},{32,16},{48,64},{64,48},{80,96},{96,80},{112,0},{1... | collective-permute-start | bytes 393224 | tf_op jit(solution)/shard_map/ppermute | solution.py:47
  83.1 8.5 %collective-permute-start.28 = (bf16[32,2048]{1,0:T(8,128)(2,1)S(1)}, bf16[32,2048]{1,0:T(8,128)(2,1)S(1)}, u32[]{:S(2)}, u32[]{:S(2)}) collective-permute-start(bf16[32,2048]{1,0:T(8,128)(2,1)S(1)} %get-tuple-element.32), channel_id=1, source_target_pairs={{0,16},{16,0},{32,48},{48,32},{64,80},{80,64},{96,112},{112,96},{1... | collective-permute-start | bytes 393224 | tf_op jit(solution)/shard_map/ppermute | solution.py:43
  85.0 9.3 %collective-permute-start.21 = (bf16[32,2048]{1,0:T(8,128)(2,1)S(1)}, bf16[32,2048]{1,0:T(8,128)(2,1)S(1)}, u32[]{:S(2)}, u32[]{:S(2)}) collective-permute-start(bf16[32,2048]{1,0:T(8,128)(2,1)S(1)} %shard_map.65), channel_id=1, source_target_pairs={{0,112},{16,32},{32,16},{48,64},{64,48},{80,96},{96,80},{112,0},{1... | collective-permute-start | bytes 393224 | tf_op jit(solution)/shard_map/ppermute | solution.py:47
  87.7 7.0 %collective-permute-start.25 = (bf16[32,2048]{1,0:T(8,128)(2,1)S(1)}, bf16[32,2048]{1,0:T(8,128)(2,1)S(1)}, u32[]{:S(2)}, u32[]{:S(2)}) collective-permute-start(bf16[32,2048]{1,0:T(8,128)(2,1)S(1)} %shard_map.68), channel_id=1, source_target_pairs={{0,16},{16,0},{32,48},{48,32},{64,80},{80,64},{96,112},{112,96},{1... | collective-permute-start | bytes 393224 | tf_op jit(solution)/shard_map/ppermute | solution.py:43
  90.2 6.7 %collective-permute-start.32 = (bf16[32,2048]{1,0:T(8,128)(2,1)S(1)}, bf16[32,2048]{1,0:T(8,128)(2,1)S(1)}, u32[]{:S(2)}, u32[]{:S(2)}) collective-permute-start(bf16[32,2048]{1,0:T(8,128)(2,1)S(1)} %shard_map.73), channel_id=1, source_target_pairs={{0,16},{16,0},{32,48},{48,32},{64,80},{80,64},{96,112},{112,96},{1... | collective-permute-start | bytes 393224 | tf_op jit(solution)/shard_map/ppermute | solution.py:43
  91.7 7.6 %collective-permute-start.29 = (bf16[32,2048]{1,0:T(8,128)(2,1)S(1)}, bf16[32,2048]{1,0:T(8,128)(2,1)S(1)}, u32[]{:S(2)}, u32[]{:S(2)}) collective-permute-start(bf16[32,2048]{1,0:T(8,128)(2,1)S(1)} %shard_map.71), channel_id=1, source_target_pairs={{0,112},{16,32},{32,16},{48,64},{64,48},{80,96},{96,80},{112,0},{1... | collective-permute-start | bytes 393224 | tf_op jit(solution)/shard_map/ppermute | solution.py:47
  94.4 5.1 %collective-permute-start.22 = (bf16[32,2048]{1,0:T(8,128)(2,1)S(1)}, bf16[32,2048]{1,0:T(8,128)(2,1)S(1)}, u32[]{:S(2)}, u32[]{:S(2)}) collective-permute-start(bf16[32,2048]{1,0:T(8,128)(2,1)S(1)} %shard_map.66), channel_id=1, source_target_pairs={{0,16},{16,0},{32,48},{48,32},{64,80},{80,64},{96,112},{112,96},{1... | collective-permute-start | bytes 393224 | tf_op jit(solution)/shard_map/ppermute | solution.py:43
  94.8 7.3 %collective-permute-start.26 = (bf16[32,2048]{1,0:T(8,128)(2,1)S(1)}, bf16[32,2048]{1,0:T(8,128)(2,1)S(1)}, u32[]{:S(2)}, u32[]{:S(2)}) collective-permute-start(bf16[32,2048]{1,0:T(8,128)(2,1)S(1)} %shard_map.69), channel_id=1, source_target_pairs={{0,112},{16,32},{32,16},{48,64},{64,48},{80,96},{96,80},{112,0},{1... | collective-permute-start | bytes 393224 | tf_op jit(solution)/shard_map/ppermute | solution.py:47
  97.0 7.6 %collective-permute-start.33 = (bf16[32,2048]{1,0:T(8,128)(2,1)S(1)}, bf16[32,2048]{1,0:T(8,128)(2,1)S(1)}, u32[]{:S(2)}, u32[]{:S(2)}) collective-permute-start(bf16[32,2048]{1,0:T(8,128)(2,1)S(1)} %shard_map.74), channel_id=1, source_target_pairs={{0,112},{16,32},{32,16},{48,64},{64,48},{80,96},{96,80},{112,0},{1... | collective-permute-start | bytes 393224 | tf_op jit(solution)/shard_map/ppermute | solution.py:47
  99.2 5.7 %collective-permute-start.18 = (bf16[4,512,128]{2,1,0:T(8,128)(2,1)S(1)}, bf16[4,512,128]{2,1,0:T(8,128)(2,1)S(1)}, u32[]{:S(2)}, u32[]{:S(2)}) collective-permute-start(bf16[4,512,128]{2,1,0:T(8,128)(2,1)S(1)} %get-tuple-element.34), channel_id=1, source_target_pairs={{0,8},{8,0},{1,9},{9,1},{2,10},{10,2},{3,11},{11,3},{4,12},{12,4},... | collective-permute-start | bytes 1572872 | tf_op jit(solution)/shard_map/ppermute | solution.py:39
  99.4 11.3 %collective-permute-start.30 = (bf16[32,2048]{1,0:T(8,128)(2,1)S(1)}, bf16[32,2048]{1,0:T(8,128)(2,1)S(1)}, u32[]{:S(2)}, u32[]{:S(2)}) collective-permute-start(bf16[32,2048]{1,0:T(8,128)(2,1)S(1)} %shard_map.72), channel_id=1, source_target_pairs={{0,16},{16,0},{32,48},{48,32},{64,80},{80,64},{96,112},{112,96},{1... | collective-permute-start | bytes 393224 | tf_op jit(solution)/shard_map/ppermute | solution.py:43
  100.3 5.9 %copy-start = (bf16[512,2048]{1,0:T(8,128)(2,1)S(1)}, bf16[512,2048]{1,0:T(8,128)(2,1)}, u32[]{:S(2)}) copy-start(bf16[512,2048]{1,0:T(8,128)(2,1)} %act_ref.1) | copy-start | bytes 6291460
  102.1 8.6 %collective-permute-start.23 = (bf16[32,2048]{1,0:T(8,128)(2,1)S(1)}, bf16[32,2048]{1,0:T(8,128)(2,1)S(1)}, u32[]{:S(2)}, u32[]{:S(2)}) collective-permute-start(bf16[32,2048]{1,0:T(8,128)(2,1)S(1)} %shard_map.67), channel_id=1, source_target_pairs={{0,112},{16,32},{32,16},{48,64},{64,48},{80,96},{96,80},{112,0},{1... | collective-permute-start | bytes 393224 | tf_op jit(solution)/shard_map/ppermute | solution.py:47
  104.6 6.2 %collective-permute-start.27 = (bf16[32,2048]{1,0:T(8,128)(2,1)S(1)}, bf16[32,2048]{1,0:T(8,128)(2,1)S(1)}, u32[]{:S(2)}, u32[]{:S(2)}) collective-permute-start(bf16[32,2048]{1,0:T(8,128)(2,1)S(1)} %shard_map.70), channel_id=1, source_target_pairs={{0,144},{16,128},{32,176},{48,160},{64,208},{80,192},{96,240},{112... | collective-permute-start | bytes 393224 | tf_op jit(solution)/shard_map/ppermute | solution.py:52
  104.9 6.5 %collective-permute-start.34 = (bf16[32,2048]{1,0:T(8,128)(2,1)S(1)}, bf16[32,2048]{1,0:T(8,128)(2,1)S(1)}, u32[]{:S(2)}, u32[]{:S(2)}) collective-permute-start(bf16[32,2048]{1,0:T(8,128)(2,1)S(1)} %fusion.12), channel_id=1, source_target_pairs={{0,128},{128,0},{1,129},{129,1},{2,130},{130,2},{3,131},{131,3},{4... | collective-permute-start | bytes 393224 | tf_op jit(solution)/shard_map/ppermute | solution.py:39

commit v8 on v7

--- a/solution.py
+++ b/solution.py
@@ -250,21 +250,21 @@
     joined = after(joined, grad)
     query_grad = query_grads(query_act, grad, swap(grad[4:], "core"), joined, swap(joined, "core"))
 
-    far, a0, a1, b0, b1 = passage_sums(grad, mine, other, 0, [0, 1, 2, 5])
+    far, a0, a1, b0, b1 = passage_sums(grad, mine, other, 0, [1, 0, 3, 4])
     (near,) = passage_sums(grad, mine, other, 256, [])
     place = {k: (far, i) if i < 8 else (near, i - 8) for i, k in enumerate(KEYS)}
     a0, a1, b0, b1 = even(a0), odd(a1), even(b0), odd(b1)
     for d in (-3, 2, -1):
         ways = (odd, even) if d < 0 else (even, odd)
-        (a0,), (a1,) = add_blocks((*place[0, d], a0)), add_blocks((*place[1, -d], a1))
-        a0, a1 = ways[0](a0), cross(a1, even) if d == -1 else ways[1](a1)
+        (a0,), (a1,) = add_blocks((*place[1, d], a0)), add_blocks((*place[0, -d], a1))
+        a0, a1 = cross(a0, odd) if d == -1 else ways[0](a0), ways[1](a1)
         if d != -1:
             d = -2 if d < 0 else 1
-            (b0,), (b1,) = add_blocks((*place[0, d], b0)), add_blocks((*place[1, -d], b1))
+            (b0,), (b1,) = add_blocks((*place[1, d], b0)), add_blocks((*place[0, -d], b1))
             b0, b1 = ways[0](b0), ways[1](b1)
     sums = [near[place[s, 0][1]] for s in (0, 1)]
-    theirs = swap((sums[1] + b1.astype(F32)).astype(BF16), "ylo").astype(F32)
-    total = after(sums[0], query_grad) + a0.astype(F32) + a1.astype(F32) + b0.astype(F32) + theirs
+    theirs = swap((sums[1] + b0.astype(F32)).astype(BF16), "ylo").astype(F32)
+    total = after(sums[0], query_grad) + a0.astype(F32) + a1.astype(F32) + b1.astype(F32) + theirs
     passage_grad = (total * slope(passage_act)).astype(BF16)
     return (query_grad, passage_grad)
 

time: 113 us -> 112 us (level)
  waiting for transfers between devices: 16.4 us -> 14 us
    ppermute x1, starting transfers between devices: 0.31 us -> 3.26 us  [cross(): lax.ppermute(value, ('ylo', 'z'), [(y * 8 + i, (1 - y) * 8 + to[i]) for y...]
    ppermute x14 -> x13, starting transfers between devices: 34 us -> 31.2 us  [odd(): lax.ppermute(value, 'z', [(i, (i - 1 ^ 1) + 1 & 7) for i in range(8)])]
    ppermute x14 -> x13, waiting for transfers between devices: 9.83 us -> 7.16 us  [odd(): lax.ppermute(value, 'z', [(i, (i - 1 ^ 1) + 1 & 7) for i in range(8)])]
    ppermute x13 -> x14, starting transfers between devices: 5.55 us -> 6.49 us  [even(): return lax.ppermute(value, 'z', [(i, i ^ 1) for i in range(8)])]
    ppermute x13 -> x14, waiting for transfers between devices: 5.89 us -> 6.78 us  [even(): return lax.ppermute(value, 'z', [(i, i ^ 1) for i in range(8)])]
  transfers between devices with their start and end apart: 35 -> 35, of which waited for: 13 -> 10; matrix products, arithmetic and copies ran while one was open for 0% -> 0% of each run, Pallas kernels for 8% -> 8%
where the time goes in v8:
time: 112 us; the launch traced here: 111 us
  starting transfers between devices  44.6 us (40%)
  blocking collectives  35.1 us (31%)
  waiting for transfers between devices  14 us (12%)
  Pallas kernels  11.7 us (10%)
  other arithmetic  3.99 us (4%)
    all_to_all x2, blocking collectives, exchange(): return lax.all_to_all(value, REP, split_axis=0, concat_axis=0)  35.1 us
    ppermute x13, starting transfers between devices, odd(): lax.ppermute(value, 'z', [(i, (i - 1 ^ 1) + 1 & 7) for i in range(8)])  31.2 us
    ppermute x13, waiting for transfers between devices, odd(): lax.ppermute(value, 'z', [(i, (i - 1 ^ 1) + 1 & 7) for i in range(8)])  7.16 us
    ppermute x14, waiting for transfers between devices, even(): return lax.ppermute(value, 'z', [(i, i ^ 1) for i in range(8)])  6.78 us
    ppermute x14, starting transfers between devices, even(): return lax.ppermute(value, 'z', [(i, i ^ 1) for i in range(8)])  6.49 us
    pallas_call x1, Pallas kernels, query_grads(): pl.pallas_call(query_kernel, out_shape=shape((512, 2048), BF16), in_specs...  4.56 us
    ppermute x7, starting transfers between devices, swap(): return lax.ppermute(value, axis, [(0, 1), (1, 0)])  3.74 us
    ppermute x1, starting transfers between devices, cross(): lax.ppermute(value, ('ylo', 'z'), [(y * 8 + i, (1 - y) * 8 + to[i]) for y...  3.26 us
  transfers between devices with their start and end apart: 35, of which 10 were waited for; matrix products, arithmetic and copies ran while one was open for 0% of the time, Pallas kernels for 8%

profile of v8, /device:TPU:8, one launch (start us, length us, event | category | flops | bytes accessed | tf_op | source)
XLA Modules:
  0.0 110.5 jit_solution(12464102306520514481)
XLA Ops:
  0.7 3.1 %fusion.1.mine_ref = bf16[512,2048]{1,0:T(8,128)(2,1)S(1)} fusion(bf16[512,2048]{1,0:T(8,128)(2,1)} %act_ref.1), kind=kLoop, calls=%fused_computation.2 | loop fusion | flops 9437184 | bytes 4194304 | tf_op jit(solution)/shard_map/convert_element_type | solution.py:30
  3.7 0.1 collective-permute-start
  3.8 0.1 fusion.8.refs_10_
  4.0 2.3 %collective-permute-start.4 = (bf16[32,2048]{1,0:T(8,128)(2,1)S(1)}, bf16[32,2048]{1,0:T(8,128)(2,1)S(1)}, u32[]{:S(2)}, u32[]{:S(2)}) collective-permute-start(bf16[32,2048]{1,0:T(8,128)(2,1)S(1)} %fusion.8.refs_10_), channel_id=1, source_target_pairs={{0,128},{128,0},{1,129},{129,1},{2,130},{130,2},{3,131},{131,3},{4... | collective-permute-start | bytes 393224 | tf_op jit(solution)/shard_map/ppermute | solution.py:39
  6.2 4.1 %collective-permute-start.1 = (bf16[32,2048]{1,0:T(8,128)(2,1)S(1)}, bf16[32,2048]{1,0:T(8,128)(2,1)S(1)}, u32[]{:S(2)}, u32[]{:S(2)}) collective-permute-start(bf16[32,2048]{1,0:T(8,128)(2,1)S(1)} %fusion.8.refs_10_), channel_id=1, source_target_pairs={{0,112},{16,32},{32,16},{48,64},{64,48},{80,96},{96,80},{112,0},{1... | collective-permute-start | bytes 393224 | tf_op jit(solution)/shard_map/ppermute | solution.py:47
  10.4 1.5 %collective-permute-start.10 = (bf16[32,2048]{1,0:T(8,128)(2,1)S(1)}, bf16[32,2048]{1,0:T(8,128)(2,1)S(1)}, u32[]{:S(2)}, u32[]{:S(2)}) collective-permute-start(bf16[32,2048]{1,0:T(8,128)(2,1)S(1)} %collective-permute-done.4.refs_11_), channel_id=1, source_target_pairs={{0,16},{16,0},{32,48},{48,32},{64,80},{80,64},{96,112},{112,96},{1... | collective-permute-start | bytes 393224 | tf_op jit(solution)/shard_map/ppermute | solution.py:43
  11.9 0.5 collective-permute-start.14
  12.4 1.8 %collective-permute-done.1.refs_8_ = bf16[32,2048]{1,0:T(8,128)(2,1)S(1)} collective-permute-done((bf16[32,2048]{1,0:T(8,128)(2,1)S(1)}, bf16[32,2048]{1,0:T(8,128)(2,1)S(1)}, u32[]{:S(2)}, u32[]{:S(2)}) %collective-permute-start.1) | collective-permute-done | bytes 131104 | tf_op jit(solution)/shard_map/ppermute | solution.py:47
  14.2 4.1 %collective-permute-start.5 = (bf16[32,2048]{1,0:T(8,128)(2,1)S(1)}, bf16[32,2048]{1,0:T(8,128)(2,1)S(1)}, u32[]{:S(2)}, u32[]{:S(2)}) collective-permute-start(bf16[32,2048]{1,0:T(8,128)(2,1)S(1)} %collective-permute-done.4.refs_11_), channel_id=1, source_target_pairs={{0,112},{16,32},{32,16},{48,64},{64,48},{80,96},{96,80},{112,0},{1... | collective-permute-start | bytes 393224 | tf_op jit(solution)/shard_map/ppermute | solution.py:47
  18.3 3.5 %collective-permute-start.11 = (bf16[32,2048]{1,0:T(8,128)(2,1)S(1)}, bf16[32,2048]{1,0:T(8,128)(2,1)S(1)}, u32[]{:S(2)}, u32[]{:S(2)}) collective-permute-start(bf16[32,2048]{1,0:T(8,128)(2,1)S(1)} %collective-permute-done.10.refs_7_), channel_id=1, source_target_pairs={{0,112},{16,32},{32,16},{48,64},{64,48},{80,96},{96,80},{112,0},{1... | collective-permute-start | bytes 393224 | tf_op jit(solution)/shard_map/ppermute | solution.py:47
  21.8 2.8 %collective-permute-start.3 = (bf16[32,2048]{1,0:T(8,128)(2,1)S(1)}, bf16[32,2048]{1,0:T(8,128)(2,1)S(1)}, u32[]{:S(2)}, u32[]{:S(2)}) collective-permute-start(bf16[32,2048]{1,0:T(8,128)(2,1)S(1)} %collective-permute-done.2.refs_2_), channel_id=1, source_target_pairs={{0,112},{16,32},{32,16},{48,64},{64,48},{80,96},{96,80},{112,0},{1... | collective-permute-start | bytes 393224 | tf_op jit(solution)/shard_map/ppermute | solution.py:47
  24.6 2.0 %collective-permute-start.9 = (bf16[32,2048]{1,0:T(8,128)(2,1)S(1)}, bf16[32,2048]{1,0:T(8,128)(2,1)S(1)}, u32[]{:S(2)}, u32[]{:S(2)}) collective-permute-start(bf16[32,2048]{1,0:T(8,128)(2,1)S(1)} %collective-permute-done.8.refs_6_), channel_id=1, source_target_pairs={{0,112},{16,32},{32,16},{48,64},{64,48},{80,96},{96,80},{112,0},{1... | collective-permute-start | bytes 393224 | tf_op jit(solution)/shard_map/ppermute | solution.py:47
  26.7 1.0 collective-permute-start.15
  27.7 1.7 %collective-permute-done.3.refs_0_ = bf16[32,2048]{1,0:T(8,128)(2,1)S(1)} collective-permute-done((bf16[32,2048]{1,0:T(8,128)(2,1)S(1)}, bf16[32,2048]{1,0:T(8,128)(2,1)S(1)}, u32[]{:S(2)}, u32[]{:S(2)}) %collective-permute-start.3) | collective-permute-done | bytes 131104 | tf_op jit(solution)/shard_map/ppermute | solution.py:47
  29.3 1.7 %collective-permute-done.6.refs_3_ = bf16[32,2048]{1,0:T(8,128)(2,1)S(1)} collective-permute-done((bf16[32,2048]{1,0:T(8,128)(2,1)S(1)}, bf16[32,2048]{1,0:T(8,128)(2,1)S(1)}, u32[]{:S(2)}, u32[]{:S(2)}) %collective-permute-start.6) | collective-permute-done | bytes 131104 | tf_op jit(solution)/shard_map/ppermute | solution.py:43
  31.0 1.1 %collective-permute-start.7 = (bf16[32,2048]{1,0:T(8,128)(2,1)S(1)}, bf16[32,2048]{1,0:T(8,128)(2,1)S(1)}, u32[]{:S(2)}, u32[]{:S(2)}) collective-permute-start(bf16[32,2048]{1,0:T(8,128)(2,1)S(1)} %collective-permute-done.6.refs_3_), channel_id=1, source_target_pairs={{0,112},{16,32},{32,16},{48,64},{64,48},{80,96},{96,80},{112,0},{1... | collective-permute-start | bytes 393224 | tf_op jit(solution)/shard_map/ppermute | solution.py:47
  32.2 0.7 collective-permute-start.17
  32.9 0.9 collective-permute-done.15.refs_3_
  33.8 1.3 %collective-permute-start.16 = (bf16[32,2048]{1,0:T(8,128)(2,1)S(1)}, bf16[32,2048]{1,0:T(8,128)(2,1)S(1)}, u32[]{:S(2)}, u32[]{:S(2)}) collective-permute-start(bf16[32,2048]{1,0:T(8,128)(2,1)S(1)} %collective-permute-done.15.refs_3_), channel_id=1, source_target_pairs={{0,112},{16,32},{32,16},{48,64},{64,48},{80,96},{96,80},{112,0},{1... | collective-permute-start | bytes 393224 | tf_op jit(solution)/shard_map/ppermute | solution.py:47
  35.1 1.3 %collective-permute-done.12.refs_0_ = bf16[32,2048]{1,0:T(8,128)(2,1)S(1)} collective-permute-done((bf16[32,2048]{1,0:T(8,128)(2,1)S(1)}, bf16[32,2048]{1,0:T(8,128)(2,1)S(1)}, u32[]{:S(2)}, u32[]{:S(2)}) %collective-permute-start.12) | collective-permute-done | bytes 131104 | tf_op jit(solution)/shard_map/ppermute | solution.py:43
  36.4 0.9 collective-permute-done.7.refs_1_
  37.3 1.8 %shard_map.59 = (f32[4,384,256]{2,1,0:T(8,128)S(1)}, bf16[512,2048]{1,0:T(8,128)(2,1)S(1)}) custom-call(bf16[512,2048]{1,0:T(8,128)(2,1)S(1)} %fusion.1.mine_ref, bf16[512,2048]{1,0:T(8,128)(2,1)S(1)} %collective-permute-done.other_ref, bf16[32,2048]{1,0:T(8,128)(2,1)S(1)} %collective-permute-done.3.refs_0_, ...), custom_call_target="tpu_custom_call" | custom-call | tf_op jit(solution)/shard_map/pallas_call | solution.py:109
  39.2 0.8 collective-permute-done.16.refs_1_
  40.0 2.0 %shard_map.60 = (s16[8,528,128]{2,1,0:T(8,128)(2,1)S(1)}, bf16[512,2048]{1,0:T(8,128)(2,1)S(1)}) custom-call(bf16[512,2048]{1,0:T(8,128)(2,1)S(1)} %fusion.1.mine_ref, bf16[512,2048]{1,0:T(8,128)(2,1)S(1)} %collective-permute-done.other_ref, f32[4,384,256]{2,1,0:T(8,128)S(1)} %get-tuple-element.18.early_ref, ...), custom_call_target="tpu_custom_call", output_to_operand_aliasing={{1}: (3, {})} | custom-call | tf_op jit(solution)/shard_map/pallas_call | solution.py:116
  42.0 20.0 %all_to_all.10.pieces_ref = s16[8,528,128]{2,1,0:T(8,128)(2,1)S(1)} all-to-all(s16[8,528,128]{2,1,0:T(8,128)(2,1)S(1)} %get-tuple-element.21), channel_id=1, replica_groups=mesh['ylo'=2,'z'=8,'core'=2,'yhi'=2,'x'=4] {'x','yhi'}, dimensions={0} | all-to-all | bytes 2162688 | tf_op jit(solution)/shard_map/all_to_all | solution.py:56
  62.0 0.6 shard_map.61
  62.7 15.1 %all_to_all.11.grad_ref = bf16[8,512,128]{2,1,0:T(8,128)(2,1)S(1)} all-to-all(bf16[8,512,128]{2,1,0:T(8,128)(2,1)S(1)} %shard_map.61), channel_id=1, replica_groups=mesh['ylo'=2,'z'=8,'core'=2,'yhi'=2,'x'=4] {'x','yhi'}, dimensions={0} | all-to-all | bytes 2097152 | tf_op jit(solution)/shard_map/all_to_all | solution.py:56
  77.7 1.2 %shard_map.64 = (f32[8,32,2048]{2,1,0:T(8,128)S(1)}, bf16[32,2048]{1,0:T(8,128)(2,1)S(1)}, bf16[32,2048]{1,0:T(8,128)(2,1)S(1)}, bf16[32,2048]{1,0:T(8,128)(2,1)S(1)}, bf16[32,2048]{1,0:T(8,128)(2,1)S(1)}) custom-call(bf16[8,512,128]{2,1,0:T(8,128)(2,1)S(1)} %all_to_all.11.grad_ref, bf16[512,2048]{1,0:T(8,128)(2,1)S(1)} %fusion.1.mine_ref, ...), custom_call_target="tpu_custom_call" | custom-call | tf_op jit(solution)/shard_map/pallas_call | solution.py:175
  79.0 0.9 collective-permute-start.20
  79.9 2.2 %collective-permute-start.24 = (bf16[32,2048]{1,0:T(8,128)(2,1)S(1)}, bf16[32,2048]{1,0:T(8,128)(2,1)S(1)}, u32[]{:S(2)}, u32[]{:S(2)}) collective-permute-start(bf16[32,2048]{1,0:T(8,128)(2,1)S(1)} %get-tuple-element.31), channel_id=1, source_target_pairs={{0,112},{16,32},{32,16},{48,64},{64,48},{80,96},{96,80},{112,0},{1... | collective-permute-start | bytes 393224 | tf_op jit(solution)/shard_map/ppermute | solution.py:47
  82.1 2.6 %collective-permute-start.28 = (bf16[32,2048]{1,0:T(8,128)(2,1)S(1)}, bf16[32,2048]{1,0:T(8,128)(2,1)S(1)}, u32[]{:S(2)}, u32[]{:S(2)}) collective-permute-start(bf16[32,2048]{1,0:T(8,128)(2,1)S(1)} %get-tuple-element.32), channel_id=1, source_target_pairs={{0,112},{16,32},{32,16},{48,64},{64,48},{80,96},{96,80},{112,0},{1... | collective-permute-start | bytes 393224 | tf_op jit(solution)/shard_map/ppermute | solution.py:47
  84.8 1.2 %shard_map.63.refs_0_ = f32[8,32,2048]{2,1,0:T(8,128)S(1)} custom-call(bf16[8,512,128]{2,1,0:T(8,128)(2,1)S(1)} %all_to_all.11.grad_ref, bf16[512,2048]{1,0:T(8,128)(2,1)S(1)} %fusion.1.mine_ref, bf16[512,2048]{1,0:T(8,128)(2,1)S(1)} %collective-permute-done.other_ref), custom_call_target="tpu_custom_call" | custom-call | tf_op jit(solution)/shard_map/pallas_call | solution.py:175
  86.1 2.0 %collective-permute-start.21 = (bf16[32,2048]{1,0:T(8,128)(2,1)S(1)}, bf16[32,2048]{1,0:T(8,128)(2,1)S(1)}, u32[]{:S(2)}, u32[]{:S(2)}) collective-permute-start(bf16[32,2048]{1,0:T(8,128)(2,1)S(1)} %shard_map.65), channel_id=1, source_target_pairs={{0,112},{16,32},{32,16},{48,64},{64,48},{80,96},{96,80},{112,0},{1... | collective-permute-start | bytes 393224 | tf_op jit(solution)/shard_map/ppermute | solution.py:47
  88.1 0.1 collective-permute-start.25
  88.3 2.2 %collective-permute-start.32 = (bf16[32,2048]{1,0:T(8,128)(2,1)S(1)}, bf16[32,2048]{1,0:T(8,128)(2,1)S(1)}, u32[]{:S(2)}, u32[]{:S(2)}) collective-permute-start(bf16[32,2048]{1,0:T(8,128)(2,1)S(1)} %shard_map.73), channel_id=1, source_target_pairs={{0,112},{16,32},{32,16},{48,64},{64,48},{80,96},{96,80},{112,0},{1... | collective-permute-start | bytes 393224 | tf_op jit(solution)/shard_map/ppermute | solution.py:47
  90.5 1.0 collective-permute-start.29
  91.5 1.9 %collective-permute-done.21.refs_1_ = bf16[32,2048]{1,0:T(8,128)(2,1)S(1)} collective-permute-done((bf16[32,2048]{1,0:T(8,128)(2,1)S(1)}, bf16[32,2048]{1,0:T(8,128)(2,1)S(1)}, u32[]{:S(2)}, u32[]{:S(2)}) %collective-permute-start.21) | collective-permute-done | bytes 131104 | tf_op jit(solution)/shard_map/ppermute | solution.py:47
  93.5 0.1 collective-permute-start.22
  93.6 0.1 collective-permute-done.25.refs_1_
  93.7 2.2 %collective-permute-start.26 = (bf16[32,2048]{1,0:T(8,128)(2,1)S(1)}, bf16[32,2048]{1,0:T(8,128)(2,1)S(1)}, u32[]{:S(2)}, u32[]{:S(2)}) collective-permute-start(bf16[32,2048]{1,0:T(8,128)(2,1)S(1)} %shard_map.69), channel_id=1, source_target_pairs={{0,112},{16,32},{32,16},{48,64},{64,48},{80,96},{96,80},{112,0},{1... | collective-permute-start | bytes 393224 | tf_op jit(solution)/shard_map/ppermute | solution.py:47
  95.9 1.1 collective-permute-start.33
  97.2 2.8 %collective-permute-done.22.refs_1_ = bf16[32,2048]{1,0:T(8,128)(2,1)S(1)} collective-permute-done((bf16[32,2048]{1,0:T(8,128)(2,1)S(1)}, bf16[32,2048]{1,0:T(8,128)(2,1)S(1)}, u32[]{:S(2)}, u32[]{:S(2)}) %collective-permute-start.22) | collective-permute-done | bytes 131104 | tf_op jit(solution)/shard_map/ppermute | solution.py:43
  100.0 0.8 collective-permute-start.30
  100.9 3.3 %collective-permute-start.23 = (bf16[32,2048]{1,0:T(8,128)(2,1)S(1)}, bf16[32,2048]{1,0:T(8,128)(2,1)S(1)}, u32[]{:S(2)}, u32[]{:S(2)}) collective-permute-start(bf16[32,2048]{1,0:T(8,128)(2,1)S(1)} %shard_map.67), channel_id=1, source_target_pairs={{0,240},{16,160},{32,144},{48,192},{64,176},{80,224},{96,208},{112... | collective-permute-start | bytes 393224 | tf_op jit(solution)/shard_map/ppermute | solution.py:52
  104.2 0.1 collective-permute-start.27
  104.3 0.8 collective-permute-start.34
  105.1 4.6 %shard_map.62 = bf16[512,2048]{1,0:T(8,128)(2,1)} custom-call(bf16[512,2048]{1,0:T(8,128)(2,1)S(1)} %copy-done, bf16[4,512,128]{2,1,0:T(8,128)(2,1)S(1)} %get-tuple-element.35.own_grad_ref, bf16[4,512,128]{2,1,0:T(8,128)(2,1)S(1)} %collective-permute-done.18.other_grad_ref, bf16[512,2048]{1,0:T(8,128)(2,1)S(1)} %get-tuple-element.27.own_ref, ...), custom_call_target="tpu_custom_call" | custom-call | tf_op jit(solution)/shard_map/pallas_call | solution.py:221
  109.7 0.8 fusion.13
  (54 shorter events, 0.7 us)
Async XLA Ops:
  0.6 3.2 %copy-start.3 = (bf16[32,2048]{1,0:T(8,128)(2,1)S(1)}, bf16[32,2048]{1,0:T(8,128)(2,1)}, u32[]{:S(2)}) copy-start(bf16[32,2048]{1,0:T(8,128)(2,1)} %param.5) | copy-start | bytes 393220
  0.6 11.2 %copy-start.1 = (f32[512]{0:T(512)S(1)}, f32[512]{0:T(512)}, u32[]{:S(2)}) copy-start(f32[512]{0:T(512)} %param.7) | copy-start | bytes 6148
  0.7 11.2 %copy-start.2 = (s32[512]{0:T(512)S(1)}, s32[512]{0:T(512)}, u32[]{:S(2)}) copy-start(s32[512]{0:T(512)} %param.6) | copy-start | bytes 6148
  3.7 33.6 %collective-permute-start = (bf16[512,2048]{1,0:T(8,128)(2,1)S(1)}, bf16[512,2048]{1,0:T(8,128)(2,1)S(1)}, u32[]{:S(2)}, u32[]{:S(2)}) collective-permute-start(bf16[512,2048]{1,0:T(8,128)(2,1)S(1)} %fusion.1.mine_ref), channel_id=1, source_target_pairs={{0,8},{8,0},{1,9},{9,1},{2,10},{10,2},{3,11},{11,3},{4,12},{12,4},... | collective-permute-start | bytes 6291464 | tf_op jit(solution)/shard_map/ppermute | solution.py:39
  4.0 6.4 %collective-permute-start.4 = (bf16[32,2048]{1,0:T(8,128)(2,1)S(1)}, bf16[32,2048]{1,0:T(8,128)(2,1)S(1)}, u32[]{:S(2)}, u32[]{:S(2)}) collective-permute-start(bf16[32,2048]{1,0:T(8,128)(2,1)S(1)} %fusion.8.refs_10_), channel_id=1, source_target_pairs={{0,128},{128,0},{1,129},{129,1},{2,130},{130,2},{3,131},{131,3},{4... | collective-permute-start | bytes 393224 | tf_op jit(solution)/shard_map/ppermute | solution.py:39
  6.2 8.0 %collective-permute-start.1 = (bf16[32,2048]{1,0:T(8,128)(2,1)S(1)}, bf16[32,2048]{1,0:T(8,128)(2,1)S(1)}, u32[]{:S(2)}, u32[]{:S(2)}) collective-permute-start(bf16[32,2048]{1,0:T(8,128)(2,1)S(1)} %fusion.8.refs_10_), channel_id=1, source_target_pairs={{0,112},{16,32},{32,16},{48,64},{64,48},{80,96},{96,80},{112,0},{1... | collective-permute-start | bytes 393224 | tf_op jit(solution)/shard_map/ppermute | solution.py:47
  10.4 8.0 %collective-permute-start.10 = (bf16[32,2048]{1,0:T(8,128)(2,1)S(1)}, bf16[32,2048]{1,0:T(8,128)(2,1)S(1)}, u32[]{:S(2)}, u32[]{:S(2)}) collective-permute-start(bf16[32,2048]{1,0:T(8,128)(2,1)S(1)} %collective-permute-done.4.refs_11_), channel_id=1, source_target_pairs={{0,16},{16,0},{32,48},{48,32},{64,80},{80,64},{96,112},{112,96},{1... | collective-permute-start | bytes 393224 | tf_op jit(solution)/shard_map/ppermute | solution.py:43
  11.8 2.4 %collective-permute-start.13 = (f32[512]{0:T(512)S(1)}, f32[512]{0:T(512)S(1)}, u32[]{:S(2)}, u32[]{:S(2)}) collective-permute-start(f32[512]{0:T(512)S(1)} %copy-done.1), channel_id=1, source_target_pairs={{0,8},{8,0},{1,9},{9,1},{2,10},{10,2},{3,11},{11,3},{4,12},{12,4},... | collective-permute-start | bytes 6152 | tf_op jit(solution)/shard_map/ppermute | solution.py:39
  11.9 6.5 %collective-permute-start.14 = (s32[512]{0:T(512)S(1)}, s32[512]{0:T(512)S(1)}, u32[]{:S(2)}, u32[]{:S(2)}) collective-permute-start(s32[512]{0:T(512)S(1)} %copy-done.2), channel_id=1, source_target_pairs={{0,8},{8,0},{1,9},{9,1},{2,10},{10,2},{3,11},{11,3},{4,12},{12,4},... | collective-permute-start | bytes 6152 | tf_op jit(solution)/shard_map/ppermute | solution.py:39
  14.2 7.6 %collective-permute-start.2 = (bf16[32,2048]{1,0:T(8,128)(2,1)S(1)}, bf16[32,2048]{1,0:T(8,128)(2,1)S(1)}, u32[]{:S(2)}, u32[]{:S(2)}) collective-permute-start(bf16[32,2048]{1,0:T(8,128)(2,1)S(1)} %collective-permute-done.1.refs_8_), channel_id=1, source_target_pairs={{0,16},{16,0},{32,48},{48,32},{64,80},{80,64},{96,112},{112,96},{1... | collective-permute-start | bytes 393224 | tf_op jit(solution)/shard_map/ppermute | solution.py:43
  14.2 10.4 %collective-permute-start.5 = (bf16[32,2048]{1,0:T(8,128)(2,1)S(1)}, bf16[32,2048]{1,0:T(8,128)(2,1)S(1)}, u32[]{:S(2)}, u32[]{:S(2)}) collective-permute-start(bf16[32,2048]{1,0:T(8,128)(2,1)S(1)} %collective-permute-done.4.refs_11_), channel_id=1, source_target_pairs={{0,112},{16,32},{32,16},{48,64},{64,48},{80,96},{96,80},{112,0},{1... | collective-permute-start | bytes 393224 | tf_op jit(solution)/shard_map/ppermute | solution.py:47
  18.3 6.3 %collective-permute-start.8 = (bf16[32,2048]{1,0:T(8,128)(2,1)S(1)}, bf16[32,2048]{1,0:T(8,128)(2,1)S(1)}, u32[]{:S(2)}, u32[]{:S(2)}) collective-permute-start(bf16[32,2048]{1,0:T(8,128)(2,1)S(1)} %fusion.8.refs_10_), channel_id=1, source_target_pairs={{0,16},{16,0},{32,48},{48,32},{64,80},{80,64},{96,112},{112,96},{1... | collective-permute-start | bytes 393224 | tf_op jit(solution)/shard_map/ppermute | solution.py:43
  18.3 8.3 %collective-permute-start.11 = (bf16[32,2048]{1,0:T(8,128)(2,1)S(1)}, bf16[32,2048]{1,0:T(8,128)(2,1)S(1)}, u32[]{:S(2)}, u32[]{:S(2)}) collective-permute-start(bf16[32,2048]{1,0:T(8,128)(2,1)S(1)} %collective-permute-done.10.refs_7_), channel_id=1, source_target_pairs={{0,112},{16,32},{32,16},{48,64},{64,48},{80,96},{96,80},{112,0},{1... | collective-permute-start | bytes 393224 | tf_op jit(solution)/shard_map/ppermute | solution.py:47
  21.8 7.5 %collective-permute-start.3 = (bf16[32,2048]{1,0:T(8,128)(2,1)S(1)}, bf16[32,2048]{1,0:T(8,128)(2,1)S(1)}, u32[]{:S(2)}, u32[]{:S(2)}) collective-permute-start(bf16[32,2048]{1,0:T(8,128)(2,1)S(1)} %collective-permute-done.2.refs_2_), channel_id=1, source_target_pairs={{0,112},{16,32},{32,16},{48,64},{64,48},{80,96},{96,80},{112,0},{1... | collective-permute-start | bytes 393224 | tf_op jit(solution)/shard_map/ppermute | solution.py:47
  24.6 6.4 %collective-permute-start.6 = (bf16[32,2048]{1,0:T(8,128)(2,1)S(1)}, bf16[32,2048]{1,0:T(8,128)(2,1)S(1)}, u32[]{:S(2)}, u32[]{:S(2)}) collective-permute-start(bf16[32,2048]{1,0:T(8,128)(2,1)S(1)} %collective-permute-done.5.refs_9_), channel_id=1, source_target_pairs={{0,16},{16,0},{32,48},{48,32},{64,80},{80,64},{96,112},{112,96},{1... | collective-permute-start | bytes 393224 | tf_op jit(solution)/shard_map/ppermute | solution.py:43
  24.6 7.5 %collective-permute-start.9 = (bf16[32,2048]{1,0:T(8,128)(2,1)S(1)}, bf16[32,2048]{1,0:T(8,128)(2,1)S(1)}, u32[]{:S(2)}, u32[]{:S(2)}) collective-permute-start(bf16[32,2048]{1,0:T(8,128)(2,1)S(1)} %collective-permute-done.8.refs_6_), channel_id=1, source_target_pairs={{0,112},{16,32},{32,16},{48,64},{64,48},{80,96},{96,80},{112,0},{1... | collective-permute-start | bytes 393224 | tf_op jit(solution)/shard_map/ppermute | solution.py:47
  26.7 7.2 %collective-permute-start.15 = (bf16[32,2048]{1,0:T(8,128)(2,1)S(1)}, bf16[32,2048]{1,0:T(8,128)(2,1)S(1)}, u32[]{:S(2)}, u32[]{:S(2)}) collective-permute-start(bf16[32,2048]{1,0:T(8,128)(2,1)S(1)} %collective-permute-done.11.refs_5_), channel_id=1, source_target_pairs={{0,16},{16,0},{32,48},{48,32},{64,80},{80,64},{96,112},{112,96},{1... | collective-permute-start | bytes 393224 | tf_op jit(solution)/shard_map/ppermute | solution.py:43
  29.3 7.1 %collective-permute-start.12 = (bf16[32,2048]{1,0:T(8,128)(2,1)S(1)}, bf16[32,2048]{1,0:T(8,128)(2,1)S(1)}, u32[]{:S(2)}, u32[]{:S(2)}) collective-permute-start(bf16[32,2048]{1,0:T(8,128)(2,1)S(1)} %collective-permute-done.3.refs_0_), channel_id=1, source_target_pairs={{0,16},{16,0},{32,48},{48,32},{64,80},{80,64},{96,112},{112,96},{1... | collective-permute-start | bytes 393224 | tf_op jit(solution)/shard_map/ppermute | solution.py:43
  31.0 6.3 %collective-permute-start.7 = (bf16[32,2048]{1,0:T(8,128)(2,1)S(1)}, bf16[32,2048]{1,0:T(8,128)(2,1)S(1)}, u32[]{:S(2)}, u32[]{:S(2)}) collective-permute-start(bf16[32,2048]{1,0:T(8,128)(2,1)S(1)} %collective-permute-done.6.refs_3_), channel_id=1, source_target_pairs={{0,112},{16,32},{32,16},{48,64},{64,48},{80,96},{96,80},{112,0},{1... | collective-permute-start | bytes 393224 | tf_op jit(solution)/shard_map/ppermute | solution.py:47
  32.2 7.0 %collective-permute-start.17 = (bf16[32,2048]{1,0:T(8,128)(2,1)S(1)}, bf16[32,2048]{1,0:T(8,128)(2,1)S(1)}, u32[]{:S(2)}, u32[]{:S(2)}) collective-permute-start(bf16[32,2048]{1,0:T(8,128)(2,1)S(1)} %collective-permute-done.9.refs_4_), channel_id=1, source_target_pairs={{0,16},{16,0},{32,48},{48,32},{64,80},{80,64},{96,112},{112,96},{1... | collective-permute-start | bytes 393224 | tf_op jit(solution)/shard_map/ppermute | solution.py:43
  33.8 6.2 %collective-permute-start.16 = (bf16[32,2048]{1,0:T(8,128)(2,1)S(1)}, bf16[32,2048]{1,0:T(8,128)(2,1)S(1)}, u32[]{:S(2)}, u32[]{:S(2)}) collective-permute-start(bf16[32,2048]{1,0:T(8,128)(2,1)S(1)} %collective-permute-done.15.refs_3_), channel_id=1, source_target_pairs={{0,112},{16,32},{32,16},{48,64},{64,48},{80,96},{96,80},{112,0},{1... | collective-permute-start | bytes 393224 | tf_op jit(solution)/shard_map/ppermute | solution.py:47
  77.7 27.4 %collective-permute-start.19 = (bf16[512,2048]{1,0:T(8,128)(2,1)S(1)}, bf16[512,2048]{1,0:T(8,128)(2,1)S(1)}, u32[]{:S(2)}, u32[]{:S(2)}) collective-permute-start(bf16[512,2048]{1,0:T(8,128)(2,1)S(1)} %get-tuple-element.27.own_ref), channel_id=1, source_target_pairs={{0,8},{8,0},{1,9},{9,1},{2,10},{10,2},{3,11},{11,3},{4,12},{12,4},... | collective-permute-start | bytes 6291464 | tf_op jit(solution)/shard_map/ppermute | solution.py:39
  79.0 7.0 %collective-permute-start.20 = (bf16[32,2048]{1,0:T(8,128)(2,1)S(1)}, bf16[32,2048]{1,0:T(8,128)(2,1)S(1)}, u32[]{:S(2)}, u32[]{:S(2)}) collective-permute-start(bf16[32,2048]{1,0:T(8,128)(2,1)S(1)} %get-tuple-element.30), channel_id=1, source_target_pairs={{0,16},{16,0},{32,48},{48,32},{64,80},{80,64},{96,112},{112,96},{1... | collective-permute-start | bytes 393224 | tf_op jit(solution)/shard_map/ppermute | solution.py:43
  79.9 8.2 %collective-permute-start.24 = (bf16[32,2048]{1,0:T(8,128)(2,1)S(1)}, bf16[32,2048]{1,0:T(8,128)(2,1)S(1)}, u32[]{:S(2)}, u32[]{:S(2)}) collective-permute-start(bf16[32,2048]{1,0:T(8,128)(2,1)S(1)} %get-tuple-element.31), channel_id=1, source_target_pairs={{0,112},{16,32},{32,16},{48,64},{64,48},{80,96},{96,80},{112,0},{1... | collective-permute-start | bytes 393224 | tf_op jit(solution)/shard_map/ppermute | solution.py:47
  82.1 6.2 %collective-permute-start.31 = (bf16[32,2048]{1,0:T(8,128)(2,1)S(1)}, bf16[32,2048]{1,0:T(8,128)(2,1)S(1)}, u32[]{:S(2)}, u32[]{:S(2)}) collective-permute-start(bf16[32,2048]{1,0:T(8,128)(2,1)S(1)} %get-tuple-element.33), channel_id=1, source_target_pairs={{0,16},{16,0},{32,48},{48,32},{64,80},{80,64},{96,112},{112,96},{1... | collective-permute-start | bytes 393224 | tf_op jit(solution)/shard_map/ppermute | solution.py:43
  82.1 8.4 %collective-permute-start.28 = (bf16[32,2048]{1,0:T(8,128)(2,1)S(1)}, bf16[32,2048]{1,0:T(8,128)(2,1)S(1)}, u32[]{:S(2)}, u32[]{:S(2)}) collective-permute-start(bf16[32,2048]{1,0:T(8,128)(2,1)S(1)} %get-tuple-element.32), channel_id=1, source_target_pairs={{0,112},{16,32},{32,16},{48,64},{64,48},{80,96},{96,80},{112,0},{1... | collective-permute-start | bytes 393224 | tf_op jit(solution)/shard_map/ppermute | solution.py:47
  86.1 7.4 %collective-permute-start.21 = (bf16[32,2048]{1,0:T(8,128)(2,1)S(1)}, bf16[32,2048]{1,0:T(8,128)(2,1)S(1)}, u32[]{:S(2)}, u32[]{:S(2)}) collective-permute-start(bf16[32,2048]{1,0:T(8,128)(2,1)S(1)} %shard_map.65), channel_id=1, source_target_pairs={{0,112},{16,32},{32,16},{48,64},{64,48},{80,96},{96,80},{112,0},{1... | collective-permute-start | bytes 393224 | tf_op jit(solution)/shard_map/ppermute | solution.py:47
  88.1 5.6 %collective-permute-start.25 = (bf16[32,2048]{1,0:T(8,128)(2,1)S(1)}, bf16[32,2048]{1,0:T(8,128)(2,1)S(1)}, u32[]{:S(2)}, u32[]{:S(2)}) collective-permute-start(bf16[32,2048]{1,0:T(8,128)(2,1)S(1)} %shard_map.68), channel_id=1, source_target_pairs={{0,16},{16,0},{32,48},{48,32},{64,80},{80,64},{96,112},{112,96},{1... | collective-permute-start | bytes 393224 | tf_op jit(solution)/shard_map/ppermute | solution.py:43
  88.3 7.6 %collective-permute-start.32 = (bf16[32,2048]{1,0:T(8,128)(2,1)S(1)}, bf16[32,2048]{1,0:T(8,128)(2,1)S(1)}, u32[]{:S(2)}, u32[]{:S(2)}) collective-permute-start(bf16[32,2048]{1,0:T(8,128)(2,1)S(1)} %shard_map.73), channel_id=1, source_target_pairs={{0,112},{16,32},{32,16},{48,64},{64,48},{80,96},{96,80},{112,0},{1... | collective-permute-start | bytes 393224 | tf_op jit(solution)/shard_map/ppermute | solution.py:47
  90.5 6.5 %collective-permute-start.29 = (bf16[32,2048]{1,0:T(8,128)(2,1)S(1)}, bf16[32,2048]{1,0:T(8,128)(2,1)S(1)}, u32[]{:S(2)}, u32[]{:S(2)}) collective-permute-start(bf16[32,2048]{1,0:T(8,128)(2,1)S(1)} %shard_map.71), channel_id=1, source_target_pairs={{0,16},{16,0},{32,48},{48,32},{64,80},{80,64},{96,112},{112,96},{1... | collective-permute-start | bytes 393224 | tf_op jit(solution)/shard_map/ppermute | solution.py:43
  93.5 6.5 %collective-permute-start.22 = (bf16[32,2048]{1,0:T(8,128)(2,1)S(1)}, bf16[32,2048]{1,0:T(8,128)(2,1)S(1)}, u32[]{:S(2)}, u32[]{:S(2)}) collective-permute-start(bf16[32,2048]{1,0:T(8,128)(2,1)S(1)} %shard_map.66), channel_id=1, source_target_pairs={{0,16},{16,0},{32,48},{48,32},{64,80},{80,64},{96,112},{112,96},{1... | collective-permute-start | bytes 393224 | tf_op jit(solution)/shard_map/ppermute | solution.py:43
  93.7 7.1 %collective-permute-start.26 = (bf16[32,2048]{1,0:T(8,128)(2,1)S(1)}, bf16[32,2048]{1,0:T(8,128)(2,1)S(1)}, u32[]{:S(2)}, u32[]{:S(2)}) collective-permute-start(bf16[32,2048]{1,0:T(8,128)(2,1)S(1)} %shard_map.69), channel_id=1, source_target_pairs={{0,112},{16,32},{32,16},{48,64},{64,48},{80,96},{96,80},{112,0},{1... | collective-permute-start | bytes 393224 | tf_op jit(solution)/shard_map/ppermute | solution.py:47
  95.9 8.2 %collective-permute-start.33 = (bf16[32,2048]{1,0:T(8,128)(2,1)S(1)}, bf16[32,2048]{1,0:T(8,128)(2,1)S(1)}, u32[]{:S(2)}, u32[]{:S(2)}) collective-permute-start(bf16[32,2048]{1,0:T(8,128)(2,1)S(1)} %shard_map.74), channel_id=1, source_target_pairs={{0,16},{16,0},{32,48},{48,32},{64,80},{80,64},{96,112},{112,96},{1... | collective-permute-start | bytes 393224 | tf_op jit(solution)/shard_map/ppermute | solution.py:43
  97.1 7.2 %collective-permute-start.18 = (bf16[4,512,128]{2,1,0:T(8,128)(2,1)S(1)}, bf16[4,512,128]{2,1,0:T(8,128)(2,1)S(1)}, u32[]{:S(2)}, u32[]{:S(2)}) collective-permute-start(bf16[4,512,128]{2,1,0:T(8,128)(2,1)S(1)} %get-tuple-element.34), channel_id=1, source_target_pairs={{0,8},{8,0},{1,9},{9,1},{2,10},{10,2},{3,11},{11,3},{4,12},{12,4},... | collective-permute-start | bytes 1572872 | tf_op jit(solution)/shard_map/ppermute | solution.py:39
  100.0 9.7 %collective-permute-start.30 = (bf16[32,2048]{1,0:T(8,128)(2,1)S(1)}, bf16[32,2048]{1,0:T(8,128)(2,1)S(1)}, u32[]{:S(2)}, u32[]{:S(2)}) collective-permute-start(bf16[32,2048]{1,0:T(8,128)(2,1)S(1)} %shard_map.72), channel_id=1, source_target_pairs={{0,112},{16,32},{32,16},{48,64},{64,48},{80,96},{96,80},{112,0},{1... | collective-permute-start | bytes 393224 | tf_op jit(solution)/shard_map/ppermute | solution.py:47
  100.9 4.3 %copy-start = (bf16[512,2048]{1,0:T(8,128)(2,1)S(1)}, bf16[512,2048]{1,0:T(8,128)(2,1)}, u32[]{:S(2)}) copy-start(bf16[512,2048]{1,0:T(8,128)(2,1)} %act_ref.1) | copy-start | bytes 6291460
  100.9 8.8 %collective-permute-start.23 = (bf16[32,2048]{1,0:T(8,128)(2,1)S(1)}, bf16[32,2048]{1,0:T(8,128)(2,1)S(1)}, u32[]{:S(2)}, u32[]{:S(2)}) collective-permute-start(bf16[32,2048]{1,0:T(8,128)(2,1)S(1)} %shard_map.67), channel_id=1, source_target_pairs={{0,240},{16,160},{32,144},{48,192},{64,176},{80,224},{96,208},{112... | collective-permute-start | bytes 393224 | tf_op jit(solution)/shard_map/ppermute | solution.py:52
  104.2 5.5 %collective-permute-start.27 = (bf16[32,2048]{1,0:T(8,128)(2,1)S(1)}, bf16[32,2048]{1,0:T(8,128)(2,1)S(1)}, u32[]{:S(2)}, u32[]{:S(2)}) collective-permute-start(bf16[32,2048]{1,0:T(8,128)(2,1)S(1)} %shard_map.70), channel_id=1, source_target_pairs={{0,16},{16,0},{32,48},{48,32},{64,80},{80,64},{96,112},{112,96},{1... | collective-permute-start | bytes 393224 | tf_op jit(solution)/shard_map/ppermute | solution.py:43
  104.3 5.4 %collective-permute-start.34 = (bf16[32,2048]{1,0:T(8,128)(2,1)S(1)}, bf16[32,2048]{1,0:T(8,128)(2,1)S(1)}, u32[]{:S(2)}, u32[]{:S(2)}) collective-permute-start(bf16[32,2048]{1,0:T(8,128)(2,1)S(1)} %fusion.12), channel_id=1, source_target_pairs={{0,128},{128,0},{1,129},{129,1},{2,130},{130,2},{3,131},{131,3},{4... | collective-permute-start | bytes 393224 | tf_op jit(solution)/shard_map/ppermute | solution.py:39

commit v9 on v8

--- a/solution.py
+++ b/solution.py
@@ -14,7 +14,7 @@
 BF16, F32 = jnp.bfloat16, jnp.float32
 ORDER = [4, 3, -3, 2, -2, 1, -1, 0]
 KEYS = [(s, d) for d in ORDER for s in (0, 1)]
-LATE = 4
+LATE = 3
 VMEM = pl.BlockSpec(memory_space=pltpu.VMEM)
 ANY = pl.BlockSpec(memory_space=pl.ANY)
 PARAMS = pltpu.CompilerParams(vmem_limit_bytes=16 * 1024 * 1024)
@@ -202,7 +202,8 @@
     )(*[a for sums, _, *come in items for a in (sums, *come)])
 
 
-def query_kernel(act_ref, own_grad_ref, other_grad_ref, own_ref, other_ref, out_ref, turned_ref):
+def query_kernel(act_ref, own_grad_ref, other_grad_ref, own_ref, other_ref, out_ref, turned_ref, held_ref, sems):
+    copies = []
     for i, g in enumerate((own_grad_ref, other_grad_ref)):
         for k in range(4):
             turned_ref[k * 128 : k * 128 + 128, i * 512 : i * 512 + 512] = g[k].T
@@ -214,7 +215,11 @@
         below = 1.0 + jnp.maximum(wide, 0.0)
         guess = pl.reciprocal(below, approx=True)
         inverse = guess * (2.0 - below * guess)
-        out_ref[:, columns] = jnp.where(wide > 0.0, total * inverse, 0.0).astype(BF16)
+        held_ref[:, columns] = jnp.where(wide > 0.0, total * inverse, 0.0).astype(BF16)
+        copies.append(pltpu.make_async_copy(held_ref.at[:, columns], out_ref.at[:, columns], sems.at[j]))
+        copies[-1].start()
+    for copy in copies:
+        copy.wait()
 
 
 def query_grads(act, grad, other_grad, own, other):
@@ -222,8 +227,12 @@
         query_kernel,
         out_shape=shape((512, 2048), BF16),
         in_specs=[VMEM] * 5,
-        out_specs=VMEM,
-        scratch_shapes=[pltpu.VMEM((512, 1024), BF16)],
+        out_specs=ANY,
+        scratch_shapes=[
+            pltpu.VMEM((512, 1024), BF16),
+            pltpu.VMEM((512, 2048), BF16),
+            pltpu.SemaphoreType.DMA((4,)),
+        ],
         compiler_params=PARAMS,
     )(act, grad[:4], other_grad, own, other)
 
@@ -256,8 +265,8 @@
     a0, a1, b0, b1 = even(a0), odd(a1), even(b0), odd(b1)
     for d in (-3, 2, -1):
         ways = (odd, even) if d < 0 else (even, odd)
-        (a0,), (a1,) = add_blocks((*place[1, d], a0)), add_blocks((*place[0, -d], a1))
-        a0, a1 = cross(a0, odd) if d == -1 else ways[0](a0), ways[1](a1)
+        (a1,), (a0,) = add_blocks((*place[0, -d], a1)), add_blocks((*place[1, d], a0))
+        a1, a0 = ways[1](a1), cross(a0, odd) if d == -1 else ways[0](a0)
         if d != -1:
             d = -2 if d < 0 else 1
             (b0,), (b1,) = add_blocks((*place[1, d], b0)), add_blocks((*place[0, -d], b1))

time: 112 us -> 111 us (level)
  transfers between devices with their start and end apart: 35 -> 35, of which waited for: 10 -> 11; matrix products, arithmetic and copies ran while one was open for 0% -> 0% of each run, Pallas kernels for 8% -> 8%
where the time goes in v9:
time: 111 us; the launch traced here: 110 us
  starting transfers between devices  44.6 us (40%)
  blocking collectives  35.1 us (32%)
  waiting for transfers between devices  14.3 us (13%)
  Pallas kernels  11.3 us (10%)
  other arithmetic  3.99 us (4%)
    all_to_all x2, blocking collectives, exchange(): return lax.all_to_all(value, REP, split_axis=0, concat_axis=0)  35.1 us
    ppermute x13, starting transfers between devices, odd(): lax.ppermute(value, 'z', [(i, (i - 1 ^ 1) + 1 & 7) for i in range(8)])  30.8 us
    ppermute x13, waiting for transfers between devices, odd(): lax.ppermute(value, 'z', [(i, (i - 1 ^ 1) + 1 & 7) for i in range(8)])  6.94 us
    ppermute x14, waiting for transfers between devices, even(): return lax.ppermute(value, 'z', [(i, i ^ 1) for i in range(8)])  6.77 us
    ppermute x14, starting transfers between devices, even(): return lax.ppermute(value, 'z', [(i, i ^ 1) for i in range(8)])  6.68 us
    pallas_call x1, Pallas kernels, query_grads(): pl.pallas_call(query_kernel, out_shape=shape((512, 2048), BF16), in_specs...  4.06 us
    ppermute x7, starting transfers between devices, swap(): return lax.ppermute(value, axis, [(0, 1), (1, 0)])  3.73 us
    ppermute x1, starting transfers between devices, cross(): lax.ppermute(value, ('ylo', 'z'), [(y * 8 + i, (1 - y) * 8 + to[i]) for y...  3.39 us
  transfers between devices with their start and end apart: 35, of which 11 were waited for; matrix products, arithmetic and copies ran while one was open for 0% of the time, Pallas kernels for 8%

profile of v9, /device:TPU:8, one launch (start us, length us, event | category | flops | bytes accessed | tf_op | source)
XLA Modules:
  0.0 110.3 jit_solution(13032021238360298662)
XLA Ops:
  0.7 3.1 %fusion.1.mine_ref = bf16[512,2048]{1,0:T(8,128)(2,1)S(1)} fusion(bf16[512,2048]{1,0:T(8,128)(2,1)} %act_ref.1), kind=kLoop, calls=%fused_computation.2 | loop fusion | flops 9437184 | bytes 4194304 | tf_op jit(solution)/shard_map/convert_element_type | solution.py:30
  3.8 0.1 fusion.8.refs_11_
  4.0 2.3 %collective-permute-start.1 = (bf16[32,2048]{1,0:T(8,128)(2,1)S(1)}, bf16[32,2048]{1,0:T(8,128)(2,1)S(1)}, u32[]{:S(2)}, u32[]{:S(2)}) collective-permute-start(bf16[32,2048]{1,0:T(8,128)(2,1)S(1)} %fusion.8.refs_11_), channel_id=1, source_target_pairs={{0,128},{128,0},{1,129},{129,1},{2,130},{130,2},{3,131},{131,3},{4... | collective-permute-start | bytes 393224 | tf_op jit(solution)/shard_map/ppermute | solution.py:39
  6.2 4.1 %collective-permute-start.5 = (bf16[32,2048]{1,0:T(8,128)(2,1)S(1)}, bf16[32,2048]{1,0:T(8,128)(2,1)S(1)}, u32[]{:S(2)}, u32[]{:S(2)}) collective-permute-start(bf16[32,2048]{1,0:T(8,128)(2,1)S(1)} %fusion.8.refs_11_), channel_id=1, source_target_pairs={{0,112},{16,32},{32,16},{48,64},{64,48},{80,96},{96,80},{112,0},{1... | collective-permute-start | bytes 393224 | tf_op jit(solution)/shard_map/ppermute | solution.py:47
  10.4 1.5 %collective-permute-start.2 = (bf16[32,2048]{1,0:T(8,128)(2,1)S(1)}, bf16[32,2048]{1,0:T(8,128)(2,1)S(1)}, u32[]{:S(2)}, u32[]{:S(2)}) collective-permute-start(bf16[32,2048]{1,0:T(8,128)(2,1)S(1)} %collective-permute-done.1.refs_12_), channel_id=1, source_target_pairs={{0,16},{16,0},{32,48},{48,32},{64,80},{80,64},{96,112},{112,96},{1... | collective-permute-start | bytes 393224 | tf_op jit(solution)/shard_map/ppermute | solution.py:43
  11.9 0.5 collective-permute-start.15
  12.4 1.8 %collective-permute-done.5.refs_9_ = bf16[32,2048]{1,0:T(8,128)(2,1)S(1)} collective-permute-done((bf16[32,2048]{1,0:T(8,128)(2,1)S(1)}, bf16[32,2048]{1,0:T(8,128)(2,1)S(1)}, u32[]{:S(2)}, u32[]{:S(2)}) %collective-permute-start.5) | collective-permute-done | bytes 131104 | tf_op jit(solution)/shard_map/ppermute | solution.py:47
  14.2 4.1 %collective-permute-start.8 = (bf16[32,2048]{1,0:T(8,128)(2,1)S(1)}, bf16[32,2048]{1,0:T(8,128)(2,1)S(1)}, u32[]{:S(2)}, u32[]{:S(2)}) collective-permute-start(bf16[32,2048]{1,0:T(8,128)(2,1)S(1)} %collective-permute-done.1.refs_12_), channel_id=1, source_target_pairs={{0,112},{16,32},{32,16},{48,64},{64,48},{80,96},{96,80},{112,0},{1... | collective-permute-start | bytes 393224 | tf_op jit(solution)/shard_map/ppermute | solution.py:47
  18.3 3.5 %collective-permute-start.3 = (bf16[32,2048]{1,0:T(8,128)(2,1)S(1)}, bf16[32,2048]{1,0:T(8,128)(2,1)S(1)}, u32[]{:S(2)}, u32[]{:S(2)}) collective-permute-start(bf16[32,2048]{1,0:T(8,128)(2,1)S(1)} %collective-permute-done.2.refs_8_), channel_id=1, source_target_pairs={{0,112},{16,32},{32,16},{48,64},{64,48},{80,96},{96,80},{112,0},{1... | collective-permute-start | bytes 393224 | tf_op jit(solution)/shard_map/ppermute | solution.py:47
  21.8 2.8 %collective-permute-start.7 = (bf16[32,2048]{1,0:T(8,128)(2,1)S(1)}, bf16[32,2048]{1,0:T(8,128)(2,1)S(1)}, u32[]{:S(2)}, u32[]{:S(2)}) collective-permute-start(bf16[32,2048]{1,0:T(8,128)(2,1)S(1)} %collective-permute-done.6.refs_3_), channel_id=1, source_target_pairs={{0,112},{16,32},{32,16},{48,64},{64,48},{80,96},{96,80},{112,0},{1... | collective-permute-start | bytes 393224 | tf_op jit(solution)/shard_map/ppermute | solution.py:47
  24.6 2.0 %collective-permute-start.12 = (bf16[32,2048]{1,0:T(8,128)(2,1)S(1)}, bf16[32,2048]{1,0:T(8,128)(2,1)S(1)}, u32[]{:S(2)}, u32[]{:S(2)}) collective-permute-start(bf16[32,2048]{1,0:T(8,128)(2,1)S(1)} %collective-permute-done.11.refs_7_), channel_id=1, source_target_pairs={{0,112},{16,32},{32,16},{48,64},{64,48},{80,96},{96,80},{112,0},{1... | collective-permute-start | bytes 393224 | tf_op jit(solution)/shard_map/ppermute | solution.py:47
  26.7 1.0 collective-permute-start.4
  27.7 1.7 %collective-permute-done.7.refs_1_ = bf16[32,2048]{1,0:T(8,128)(2,1)S(1)} collective-permute-done((bf16[32,2048]{1,0:T(8,128)(2,1)S(1)}, bf16[32,2048]{1,0:T(8,128)(2,1)S(1)}, u32[]{:S(2)}, u32[]{:S(2)}) %collective-permute-start.7) | collective-permute-done | bytes 131104 | tf_op jit(solution)/shard_map/ppermute | solution.py:47
  29.3 1.7 %collective-permute-done.9.refs_4_ = bf16[32,2048]{1,0:T(8,128)(2,1)S(1)} collective-permute-done((bf16[32,2048]{1,0:T(8,128)(2,1)S(1)}, bf16[32,2048]{1,0:T(8,128)(2,1)S(1)}, u32[]{:S(2)}, u32[]{:S(2)}) %collective-permute-start.9) | collective-permute-done | bytes 131104 | tf_op jit(solution)/shard_map/ppermute | solution.py:43
  31.0 1.1 %collective-permute-start.10 = (bf16[32,2048]{1,0:T(8,128)(2,1)S(1)}, bf16[32,2048]{1,0:T(8,128)(2,1)S(1)}, u32[]{:S(2)}, u32[]{:S(2)}) collective-permute-start(bf16[32,2048]{1,0:T(8,128)(2,1)S(1)} %collective-permute-done.9.refs_4_), channel_id=1, source_target_pairs={{0,112},{16,32},{32,16},{48,64},{64,48},{80,96},{96,80},{112,0},{1... | collective-permute-start | bytes 393224 | tf_op jit(solution)/shard_map/ppermute | solution.py:47
  32.2 0.7 collective-permute-start.17
  32.9 0.9 collective-permute-done.4.refs_0_
  33.8 1.3 %collective-permute-start.16 = (bf16[32,2048]{1,0:T(8,128)(2,1)S(1)}, bf16[32,2048]{1,0:T(8,128)(2,1)S(1)}, u32[]{:S(2)}, u32[]{:S(2)}) collective-permute-start(bf16[32,2048]{1,0:T(8,128)(2,1)S(1)} %collective-permute-done.4.refs_0_), channel_id=1, source_target_pairs={{0,112},{16,32},{32,16},{48,64},{64,48},{80,96},{96,80},{112,0},{1... | collective-permute-start | bytes 393224 | tf_op jit(solution)/shard_map/ppermute | solution.py:47
  35.1 1.3 %collective-permute-done.13.refs_0_ = bf16[32,2048]{1,0:T(8,128)(2,1)S(1)} collective-permute-done((bf16[32,2048]{1,0:T(8,128)(2,1)S(1)}, bf16[32,2048]{1,0:T(8,128)(2,1)S(1)}, u32[]{:S(2)}, u32[]{:S(2)}) %collective-permute-start.13) | collective-permute-done | bytes 131104 | tf_op jit(solution)/shard_map/ppermute | solution.py:43
  36.4 0.9 collective-permute-done.10.refs_2_
  37.3 2.0 %shard_map.59 = (f32[4,416,256]{2,1,0:T(8,128)S(1)}, bf16[512,2048]{1,0:T(8,128)(2,1)S(1)}) custom-call(bf16[512,2048]{1,0:T(8,128)(2,1)S(1)} %fusion.1.mine_ref, bf16[512,2048]{1,0:T(8,128)(2,1)S(1)} %collective-permute-done.other_ref, bf16[32,2048]{1,0:T(8,128)(2,1)S(1)} %collective-permute-done.4.refs_0_, ...), custom_call_target="tpu_custom_call" | custom-call | tf_op jit(solution)/shard_map/pallas_call | solution.py:109
  39.3 0.7 collective-permute-done.16.refs_1_
  40.0 1.9 %shard_map.60 = (s16[8,528,128]{2,1,0:T(8,128)(2,1)S(1)}, bf16[512,2048]{1,0:T(8,128)(2,1)S(1)}) custom-call(bf16[512,2048]{1,0:T(8,128)(2,1)S(1)} %fusion.1.mine_ref, bf16[512,2048]{1,0:T(8,128)(2,1)S(1)} %collective-permute-done.other_ref, f32[4,416,256]{2,1,0:T(8,128)S(1)} %get-tuple-element.18.early_ref, ...), custom_call_target="tpu_custom_call", output_to_operand_aliasing={{1}: (3, {})} | custom-call | tf_op jit(solution)/shard_map/pallas_call | solution.py:116
  41.9 20.0 %all_to_all.10.pieces_ref = s16[8,528,128]{2,1,0:T(8,128)(2,1)S(1)} all-to-all(s16[8,528,128]{2,1,0:T(8,128)(2,1)S(1)} %get-tuple-element.21), channel_id=1, replica_groups=mesh['ylo'=2,'z'=8,'core'=2,'yhi'=2,'x'=4] {'x','yhi'}, dimensions={0} | all-to-all | bytes 2162688 | tf_op jit(solution)/shard_map/all_to_all | solution.py:56
  61.9 0.6 shard_map.61
  62.5 15.1 %all_to_all.11.grad_ref = bf16[8,512,128]{2,1,0:T(8,128)(2,1)S(1)} all-to-all(bf16[8,512,128]{2,1,0:T(8,128)(2,1)S(1)} %shard_map.61), channel_id=1, replica_groups=mesh['ylo'=2,'z'=8,'core'=2,'yhi'=2,'x'=4] {'x','yhi'}, dimensions={0} | all-to-all | bytes 2097152 | tf_op jit(solution)/shard_map/all_to_all | solution.py:56
  77.6 1.2 %shard_map.64 = (f32[8,32,2048]{2,1,0:T(8,128)S(1)}, bf16[32,2048]{1,0:T(8,128)(2,1)S(1)}, bf16[32,2048]{1,0:T(8,128)(2,1)S(1)}, bf16[32,2048]{1,0:T(8,128)(2,1)S(1)}, bf16[32,2048]{1,0:T(8,128)(2,1)S(1)}) custom-call(bf16[8,512,128]{2,1,0:T(8,128)(2,1)S(1)} %all_to_all.11.grad_ref, bf16[512,2048]{1,0:T(8,128)(2,1)S(1)} %fusion.1.mine_ref, ...), custom_call_target="tpu_custom_call" | custom-call | tf_op jit(solution)/shard_map/pallas_call | solution.py:175
  78.9 0.9 collective-permute-start.20
  79.7 2.0 %collective-permute-start.24 = (bf16[32,2048]{1,0:T(8,128)(2,1)S(1)}, bf16[32,2048]{1,0:T(8,128)(2,1)S(1)}, u32[]{:S(2)}, u32[]{:S(2)}) collective-permute-start(bf16[32,2048]{1,0:T(8,128)(2,1)S(1)} %get-tuple-element.31), channel_id=1, source_target_pairs={{0,112},{16,32},{32,16},{48,64},{64,48},{80,96},{96,80},{112,0},{1... | collective-permute-start | bytes 393224 | tf_op jit(solution)/shard_map/ppermute | solution.py:47
  81.8 0.2 collective-permute-start.31
  82.0 2.6 %collective-permute-start.28 = (bf16[32,2048]{1,0:T(8,128)(2,1)S(1)}, bf16[32,2048]{1,0:T(8,128)(2,1)S(1)}, u32[]{:S(2)}, u32[]{:S(2)}) collective-permute-start(bf16[32,2048]{1,0:T(8,128)(2,1)S(1)} %get-tuple-element.32), channel_id=1, source_target_pairs={{0,112},{16,32},{32,16},{48,64},{64,48},{80,96},{96,80},{112,0},{1... | collective-permute-start | bytes 393224 | tf_op jit(solution)/shard_map/ppermute | solution.py:47
  84.7 1.2 %shard_map.63.refs_0_ = f32[8,32,2048]{2,1,0:T(8,128)S(1)} custom-call(bf16[8,512,128]{2,1,0:T(8,128)(2,1)S(1)} %all_to_all.11.grad_ref, bf16[512,2048]{1,0:T(8,128)(2,1)S(1)} %fusion.1.mine_ref, bf16[512,2048]{1,0:T(8,128)(2,1)S(1)} %collective-permute-done.other_ref), custom_call_target="tpu_custom_call" | custom-call | tf_op jit(solution)/shard_map/pallas_call | solution.py:175
  85.9 2.0 %collective-permute-start.21 = (bf16[32,2048]{1,0:T(8,128)(2,1)S(1)}, bf16[32,2048]{1,0:T(8,128)(2,1)S(1)}, u32[]{:S(2)}, u32[]{:S(2)}) collective-permute-start(bf16[32,2048]{1,0:T(8,128)(2,1)S(1)} %shard_map.65), channel_id=1, source_target_pairs={{0,112},{16,32},{32,16},{48,64},{64,48},{80,96},{96,80},{112,0},{1... | collective-permute-start | bytes 393224 | tf_op jit(solution)/shard_map/ppermute | solution.py:47
  88.0 0.1 collective-permute-start.25
  88.1 2.2 %collective-permute-start.32 = (bf16[32,2048]{1,0:T(8,128)(2,1)S(1)}, bf16[32,2048]{1,0:T(8,128)(2,1)S(1)}, u32[]{:S(2)}, u32[]{:S(2)}) collective-permute-start(bf16[32,2048]{1,0:T(8,128)(2,1)S(1)} %shard_map.73), channel_id=1, source_target_pairs={{0,112},{16,32},{32,16},{48,64},{64,48},{80,96},{96,80},{112,0},{1... | collective-permute-start | bytes 393224 | tf_op jit(solution)/shard_map/ppermute | solution.py:47
  90.4 1.0 collective-permute-start.29
  91.4 1.8 %collective-permute-done.21.refs_1_ = bf16[32,2048]{1,0:T(8,128)(2,1)S(1)} collective-permute-done((bf16[32,2048]{1,0:T(8,128)(2,1)S(1)}, bf16[32,2048]{1,0:T(8,128)(2,1)S(1)}, u32[]{:S(2)}, u32[]{:S(2)}) %collective-permute-start.21) | collective-permute-done | bytes 131104 | tf_op jit(solution)/shard_map/ppermute | solution.py:47
  93.3 0.1 collective-permute-start.22
  93.4 0.2 collective-permute-done.25.refs_1_
  93.6 2.2 %collective-permute-start.26 = (bf16[32,2048]{1,0:T(8,128)(2,1)S(1)}, bf16[32,2048]{1,0:T(8,128)(2,1)S(1)}, u32[]{:S(2)}, u32[]{:S(2)}) collective-permute-start(bf16[32,2048]{1,0:T(8,128)(2,1)S(1)} %shard_map.69), channel_id=1, source_target_pairs={{0,112},{16,32},{32,16},{48,64},{64,48},{80,96},{96,80},{112,0},{1... | collective-permute-start | bytes 393224 | tf_op jit(solution)/shard_map/ppermute | solution.py:47
  95.8 1.1 collective-permute-start.33
  97.1 2.7 %collective-permute-done.22.refs_1_ = bf16[32,2048]{1,0:T(8,128)(2,1)S(1)} collective-permute-done((bf16[32,2048]{1,0:T(8,128)(2,1)S(1)}, bf16[32,2048]{1,0:T(8,128)(2,1)S(1)}, u32[]{:S(2)}, u32[]{:S(2)}) %collective-permute-start.22) | collective-permute-done | bytes 131104 | tf_op jit(solution)/shard_map/ppermute | solution.py:43
  99.8 0.7 collective-permute-start.30
  100.5 3.4 %collective-permute-start.23 = (bf16[32,2048]{1,0:T(8,128)(2,1)S(1)}, bf16[32,2048]{1,0:T(8,128)(2,1)S(1)}, u32[]{:S(2)}, u32[]{:S(2)}) collective-permute-start(bf16[32,2048]{1,0:T(8,128)(2,1)S(1)} %shard_map.67), channel_id=1, source_target_pairs={{0,240},{16,160},{32,144},{48,192},{64,176},{80,224},{96,208},{112... | collective-permute-start | bytes 393224 | tf_op jit(solution)/shard_map/ppermute | solution.py:52
  104.1 0.8 collective-permute-start.34
  104.9 4.1 %shard_map.62 = bf16[512,2048]{1,0:T(8,128)(2,1)} custom-call(bf16[512,2048]{1,0:T(8,128)(2,1)S(1)} %copy-done, bf16[4,512,128]{2,1,0:T(8,128)(2,1)S(1)} %get-tuple-element.35.own_grad_ref, bf16[4,512,128]{2,1,0:T(8,128)(2,1)S(1)} %collective-permute-done.18.other_grad_ref, bf16[512,2048]{1,0:T(8,128)(2,1)S(1)} %get-tuple-element.27.own_ref, ...), custom_call_target="tpu_custom_call" | custom-call | tf_op jit(solution)/shard_map/pallas_call | solution.py:226
  109.0 0.5 collective-permute-done.34
  109.5 0.8 fusion.13
  (54 shorter events, 0.8 us)
Async XLA Ops:
  0.6 3.2 %copy-start.3 = (bf16[32,2048]{1,0:T(8,128)(2,1)S(1)}, bf16[32,2048]{1,0:T(8,128)(2,1)}, u32[]{:S(2)}) copy-start(bf16[32,2048]{1,0:T(8,128)(2,1)} %param.5) | copy-start | bytes 393220
  0.6 11.2 %copy-start.1 = (f32[512]{0:T(512)S(1)}, f32[512]{0:T(512)}, u32[]{:S(2)}) copy-start(f32[512]{0:T(512)} %param.7) | copy-start | bytes 6148
  0.7 11.2 %copy-start.2 = (s32[512]{0:T(512)S(1)}, s32[512]{0:T(512)}, u32[]{:S(2)}) copy-start(s32[512]{0:T(512)} %param.6) | copy-start | bytes 6148
  3.7 33.6 %collective-permute-start = (bf16[512,2048]{1,0:T(8,128)(2,1)S(1)}, bf16[512,2048]{1,0:T(8,128)(2,1)S(1)}, u32[]{:S(2)}, u32[]{:S(2)}) collective-permute-start(bf16[512,2048]{1,0:T(8,128)(2,1)S(1)} %fusion.1.mine_ref), channel_id=1, source_target_pairs={{0,8},{8,0},{1,9},{9,1},{2,10},{10,2},{3,11},{11,3},{4,12},{12,4},... | collective-permute-start | bytes 6291464 | tf_op jit(solution)/shard_map/ppermute | solution.py:39
  4.0 6.4 %collective-permute-start.1 = (bf16[32,2048]{1,0:T(8,128)(2,1)S(1)}, bf16[32,2048]{1,0:T(8,128)(2,1)S(1)}, u32[]{:S(2)}, u32[]{:S(2)}) collective-permute-start(bf16[32,2048]{1,0:T(8,128)(2,1)S(1)} %fusion.8.refs_11_), channel_id=1, source_target_pairs={{0,128},{128,0},{1,129},{129,1},{2,130},{130,2},{3,131},{131,3},{4... | collective-permute-start | bytes 393224 | tf_op jit(solution)/shard_map/ppermute | solution.py:39
  6.2 8.0 %collective-permute-start.5 = (bf16[32,2048]{1,0:T(8,128)(2,1)S(1)}, bf16[32,2048]{1,0:T(8,128)(2,1)S(1)}, u32[]{:S(2)}, u32[]{:S(2)}) collective-permute-start(bf16[32,2048]{1,0:T(8,128)(2,1)S(1)} %fusion.8.refs_11_), channel_id=1, source_target_pairs={{0,112},{16,32},{32,16},{48,64},{64,48},{80,96},{96,80},{112,0},{1... | collective-permute-start | bytes 393224 | tf_op jit(solution)/shard_map/ppermute | solution.py:47
  10.4 8.0 %collective-permute-start.2 = (bf16[32,2048]{1,0:T(8,128)(2,1)S(1)}, bf16[32,2048]{1,0:T(8,128)(2,1)S(1)}, u32[]{:S(2)}, u32[]{:S(2)}) collective-permute-start(bf16[32,2048]{1,0:T(8,128)(2,1)S(1)} %collective-permute-done.1.refs_12_), channel_id=1, source_target_pairs={{0,16},{16,0},{32,48},{48,32},{64,80},{80,64},{96,112},{112,96},{1... | collective-permute-start | bytes 393224 | tf_op jit(solution)/shard_map/ppermute | solution.py:43
  11.8 2.4 %collective-permute-start.14 = (f32[512]{0:T(512)S(1)}, f32[512]{0:T(512)S(1)}, u32[]{:S(2)}, u32[]{:S(2)}) collective-permute-start(f32[512]{0:T(512)S(1)} %copy-done.1), channel_id=1, source_target_pairs={{0,8},{8,0},{1,9},{9,1},{2,10},{10,2},{3,11},{11,3},{4,12},{12,4},... | collective-permute-start | bytes 6152 | tf_op jit(solution)/shard_map/ppermute | solution.py:39
  11.9 6.5 %collective-permute-start.15 = (s32[512]{0:T(512)S(1)}, s32[512]{0:T(512)S(1)}, u32[]{:S(2)}, u32[]{:S(2)}) collective-permute-start(s32[512]{0:T(512)S(1)} %copy-done.2), channel_id=1, source_target_pairs={{0,8},{8,0},{1,9},{9,1},{2,10},{10,2},{3,11},{11,3},{4,12},{12,4},... | collective-permute-start | bytes 6152 | tf_op jit(solution)/shard_map/ppermute | solution.py:39
  14.2 7.6 %collective-permute-start.6 = (bf16[32,2048]{1,0:T(8,128)(2,1)S(1)}, bf16[32,2048]{1,0:T(8,128)(2,1)S(1)}, u32[]{:S(2)}, u32[]{:S(2)}) collective-permute-start(bf16[32,2048]{1,0:T(8,128)(2,1)S(1)} %collective-permute-done.5.refs_9_), channel_id=1, source_target_pairs={{0,16},{16,0},{32,48},{48,32},{64,80},{80,64},{96,112},{112,96},{1... | collective-permute-start | bytes 393224 | tf_op jit(solution)/shard_map/ppermute | solution.py:43
  14.2 10.4 %collective-permute-start.8 = (bf16[32,2048]{1,0:T(8,128)(2,1)S(1)}, bf16[32,2048]{1,0:T(8,128)(2,1)S(1)}, u32[]{:S(2)}, u32[]{:S(2)}) collective-permute-start(bf16[32,2048]{1,0:T(8,128)(2,1)S(1)} %collective-permute-done.1.refs_12_), channel_id=1, source_target_pairs={{0,112},{16,32},{32,16},{48,64},{64,48},{80,96},{96,80},{112,0},{1... | collective-permute-start | bytes 393224 | tf_op jit(solution)/shard_map/ppermute | solution.py:47
  18.3 6.3 %collective-permute-start.11 = (bf16[32,2048]{1,0:T(8,128)(2,1)S(1)}, bf16[32,2048]{1,0:T(8,128)(2,1)S(1)}, u32[]{:S(2)}, u32[]{:S(2)}) collective-permute-start(bf16[32,2048]{1,0:T(8,128)(2,1)S(1)} %fusion.8.refs_11_), channel_id=1, source_target_pairs={{0,16},{16,0},{32,48},{48,32},{64,80},{80,64},{96,112},{112,96},{1... | collective-permute-start | bytes 393224 | tf_op jit(solution)/shard_map/ppermute | solution.py:43
  18.3 8.3 %collective-permute-start.3 = (bf16[32,2048]{1,0:T(8,128)(2,1)S(1)}, bf16[32,2048]{1,0:T(8,128)(2,1)S(1)}, u32[]{:S(2)}, u32[]{:S(2)}) collective-permute-start(bf16[32,2048]{1,0:T(8,128)(2,1)S(1)} %collective-permute-done.2.refs_8_), channel_id=1, source_target_pairs={{0,112},{16,32},{32,16},{48,64},{64,48},{80,96},{96,80},{112,0},{1... | collective-permute-start | bytes 393224 | tf_op jit(solution)/shard_map/ppermute | solution.py:47
  21.8 7.5 %collective-permute-start.7 = (bf16[32,2048]{1,0:T(8,128)(2,1)S(1)}, bf16[32,2048]{1,0:T(8,128)(2,1)S(1)}, u32[]{:S(2)}, u32[]{:S(2)}) collective-permute-start(bf16[32,2048]{1,0:T(8,128)(2,1)S(1)} %collective-permute-done.6.refs_3_), channel_id=1, source_target_pairs={{0,112},{16,32},{32,16},{48,64},{64,48},{80,96},{96,80},{112,0},{1... | collective-permute-start | bytes 393224 | tf_op jit(solution)/shard_map/ppermute | solution.py:47
  24.6 6.4 %collective-permute-start.9 = (bf16[32,2048]{1,0:T(8,128)(2,1)S(1)}, bf16[32,2048]{1,0:T(8,128)(2,1)S(1)}, u32[]{:S(2)}, u32[]{:S(2)}) collective-permute-start(bf16[32,2048]{1,0:T(8,128)(2,1)S(1)} %collective-permute-done.8.refs_10_), channel_id=1, source_target_pairs={{0,16},{16,0},{32,48},{48,32},{64,80},{80,64},{96,112},{112,96},{1... | collective-permute-start | bytes 393224 | tf_op jit(solution)/shard_map/ppermute | solution.py:43
  24.6 7.5 %collective-permute-start.12 = (bf16[32,2048]{1,0:T(8,128)(2,1)S(1)}, bf16[32,2048]{1,0:T(8,128)(2,1)S(1)}, u32[]{:S(2)}, u32[]{:S(2)}) collective-permute-start(bf16[32,2048]{1,0:T(8,128)(2,1)S(1)} %collective-permute-done.11.refs_7_), channel_id=1, source_target_pairs={{0,112},{16,32},{32,16},{48,64},{64,48},{80,96},{96,80},{112,0},{1... | collective-permute-start | bytes 393224 | tf_op jit(solution)/shard_map/ppermute | solution.py:47
  26.7 7.2 %collective-permute-start.4 = (bf16[32,2048]{1,0:T(8,128)(2,1)S(1)}, bf16[32,2048]{1,0:T(8,128)(2,1)S(1)}, u32[]{:S(2)}, u32[]{:S(2)}) collective-permute-start(bf16[32,2048]{1,0:T(8,128)(2,1)S(1)} %collective-permute-done.3.refs_6_), channel_id=1, source_target_pairs={{0,16},{16,0},{32,48},{48,32},{64,80},{80,64},{96,112},{112,96},{1... | collective-permute-start | bytes 393224 | tf_op jit(solution)/shard_map/ppermute | solution.py:43
  29.3 7.1 %collective-permute-start.13 = (bf16[32,2048]{1,0:T(8,128)(2,1)S(1)}, bf16[32,2048]{1,0:T(8,128)(2,1)S(1)}, u32[]{:S(2)}, u32[]{:S(2)}) collective-permute-start(bf16[32,2048]{1,0:T(8,128)(2,1)S(1)} %collective-permute-done.7.refs_1_), channel_id=1, source_target_pairs={{0,16},{16,0},{32,48},{48,32},{64,80},{80,64},{96,112},{112,96},{1... | collective-permute-start | bytes 393224 | tf_op jit(solution)/shard_map/ppermute | solution.py:43
  31.0 6.3 %collective-permute-start.10 = (bf16[32,2048]{1,0:T(8,128)(2,1)S(1)}, bf16[32,2048]{1,0:T(8,128)(2,1)S(1)}, u32[]{:S(2)}, u32[]{:S(2)}) collective-permute-start(bf16[32,2048]{1,0:T(8,128)(2,1)S(1)} %collective-permute-done.9.refs_4_), channel_id=1, source_target_pairs={{0,112},{16,32},{32,16},{48,64},{64,48},{80,96},{96,80},{112,0},{1... | collective-permute-start | bytes 393224 | tf_op jit(solution)/shard_map/ppermute | solution.py:47
  32.2 7.2 %collective-permute-start.17 = (bf16[32,2048]{1,0:T(8,128)(2,1)S(1)}, bf16[32,2048]{1,0:T(8,128)(2,1)S(1)}, u32[]{:S(2)}, u32[]{:S(2)}) collective-permute-start(bf16[32,2048]{1,0:T(8,128)(2,1)S(1)} %collective-permute-done.12.refs_5_), channel_id=1, source_target_pairs={{0,16},{16,0},{32,48},{48,32},{64,80},{80,64},{96,112},{112,96},{1... | collective-permute-start | bytes 393224 | tf_op jit(solution)/shard_map/ppermute | solution.py:43
  33.8 6.2 %collective-permute-start.16 = (bf16[32,2048]{1,0:T(8,128)(2,1)S(1)}, bf16[32,2048]{1,0:T(8,128)(2,1)S(1)}, u32[]{:S(2)}, u32[]{:S(2)}) collective-permute-start(bf16[32,2048]{1,0:T(8,128)(2,1)S(1)} %collective-permute-done.4.refs_0_), channel_id=1, source_target_pairs={{0,112},{16,32},{32,16},{48,64},{64,48},{80,96},{96,80},{112,0},{1... | collective-permute-start | bytes 393224 | tf_op jit(solution)/shard_map/ppermute | solution.py:47
  77.6 27.3 %collective-permute-start.19 = (bf16[512,2048]{1,0:T(8,128)(2,1)S(1)}, bf16[512,2048]{1,0:T(8,128)(2,1)S(1)}, u32[]{:S(2)}, u32[]{:S(2)}) collective-permute-start(bf16[512,2048]{1,0:T(8,128)(2,1)S(1)} %get-tuple-element.27.own_ref), channel_id=1, source_target_pairs={{0,8},{8,0},{1,9},{9,1},{2,10},{10,2},{3,11},{11,3},{4,12},{12,4},... | collective-permute-start | bytes 6291464 | tf_op jit(solution)/shard_map/ppermute | solution.py:39
  78.9 7.0 %collective-permute-start.20 = (bf16[32,2048]{1,0:T(8,128)(2,1)S(1)}, bf16[32,2048]{1,0:T(8,128)(2,1)S(1)}, u32[]{:S(2)}, u32[]{:S(2)}) collective-permute-start(bf16[32,2048]{1,0:T(8,128)(2,1)S(1)} %get-tuple-element.30), channel_id=1, source_target_pairs={{0,16},{16,0},{32,48},{48,32},{64,80},{80,64},{96,112},{112,96},{1... | collective-permute-start | bytes 393224 | tf_op jit(solution)/shard_map/ppermute | solution.py:43
  79.7 8.2 %collective-permute-start.24 = (bf16[32,2048]{1,0:T(8,128)(2,1)S(1)}, bf16[32,2048]{1,0:T(8,128)(2,1)S(1)}, u32[]{:S(2)}, u32[]{:S(2)}) collective-permute-start(bf16[32,2048]{1,0:T(8,128)(2,1)S(1)} %get-tuple-element.31), channel_id=1, source_target_pairs={{0,112},{16,32},{32,16},{48,64},{64,48},{80,96},{96,80},{112,0},{1... | collective-permute-start | bytes 393224 | tf_op jit(solution)/shard_map/ppermute | solution.py:47
  81.8 6.3 %collective-permute-start.31 = (bf16[32,2048]{1,0:T(8,128)(2,1)S(1)}, bf16[32,2048]{1,0:T(8,128)(2,1)S(1)}, u32[]{:S(2)}, u32[]{:S(2)}) collective-permute-start(bf16[32,2048]{1,0:T(8,128)(2,1)S(1)} %get-tuple-element.33), channel_id=1, source_target_pairs={{0,16},{16,0},{32,48},{48,32},{64,80},{80,64},{96,112},{112,96},{1... | collective-permute-start | bytes 393224 | tf_op jit(solution)/shard_map/ppermute | solution.py:43
  82.0 8.4 %collective-permute-start.28 = (bf16[32,2048]{1,0:T(8,128)(2,1)S(1)}, bf16[32,2048]{1,0:T(8,128)(2,1)S(1)}, u32[]{:S(2)}, u32[]{:S(2)}) collective-permute-start(bf16[32,2048]{1,0:T(8,128)(2,1)S(1)} %get-tuple-element.32), channel_id=1, source_target_pairs={{0,112},{16,32},{32,16},{48,64},{64,48},{80,96},{96,80},{112,0},{1... | collective-permute-start | bytes 393224 | tf_op jit(solution)/shard_map/ppermute | solution.py:47
  85.9 7.3 %collective-permute-start.21 = (bf16[32,2048]{1,0:T(8,128)(2,1)S(1)}, bf16[32,2048]{1,0:T(8,128)(2,1)S(1)}, u32[]{:S(2)}, u32[]{:S(2)}) collective-permute-start(bf16[32,2048]{1,0:T(8,128)(2,1)S(1)} %shard_map.65), channel_id=1, source_target_pairs={{0,112},{16,32},{32,16},{48,64},{64,48},{80,96},{96,80},{112,0},{1... | collective-permute-start | bytes 393224 | tf_op jit(solution)/shard_map/ppermute | solution.py:47
  88.0 5.6 %collective-permute-start.25 = (bf16[32,2048]{1,0:T(8,128)(2,1)S(1)}, bf16[32,2048]{1,0:T(8,128)(2,1)S(1)}, u32[]{:S(2)}, u32[]{:S(2)}) collective-permute-start(bf16[32,2048]{1,0:T(8,128)(2,1)S(1)} %shard_map.68), channel_id=1, source_target_pairs={{0,16},{16,0},{32,48},{48,32},{64,80},{80,64},{96,112},{112,96},{1... | collective-permute-start | bytes 393224 | tf_op jit(solution)/shard_map/ppermute | solution.py:43
  88.1 7.6 %collective-permute-start.32 = (bf16[32,2048]{1,0:T(8,128)(2,1)S(1)}, bf16[32,2048]{1,0:T(8,128)(2,1)S(1)}, u32[]{:S(2)}, u32[]{:S(2)}) collective-permute-start(bf16[32,2048]{1,0:T(8,128)(2,1)S(1)} %shard_map.73), channel_id=1, source_target_pairs={{0,112},{16,32},{32,16},{48,64},{64,48},{80,96},{96,80},{112,0},{1... | collective-permute-start | bytes 393224 | tf_op jit(solution)/shard_map/ppermute | solution.py:47
  90.4 6.5 %collective-permute-start.29 = (bf16[32,2048]{1,0:T(8,128)(2,1)S(1)}, bf16[32,2048]{1,0:T(8,128)(2,1)S(1)}, u32[]{:S(2)}, u32[]{:S(2)}) collective-permute-start(bf16[32,2048]{1,0:T(8,128)(2,1)S(1)} %shard_map.71), channel_id=1, source_target_pairs={{0,16},{16,0},{32,48},{48,32},{64,80},{80,64},{96,112},{112,96},{1... | collective-permute-start | bytes 393224 | tf_op jit(solution)/shard_map/ppermute | solution.py:43
  93.3 6.5 %collective-permute-start.22 = (bf16[32,2048]{1,0:T(8,128)(2,1)S(1)}, bf16[32,2048]{1,0:T(8,128)(2,1)S(1)}, u32[]{:S(2)}, u32[]{:S(2)}) collective-permute-start(bf16[32,2048]{1,0:T(8,128)(2,1)S(1)} %shard_map.66), channel_id=1, source_target_pairs={{0,16},{16,0},{32,48},{48,32},{64,80},{80,64},{96,112},{112,96},{1... | collective-permute-start | bytes 393224 | tf_op jit(solution)/shard_map/ppermute | solution.py:43
  93.6 6.9 %collective-permute-start.26 = (bf16[32,2048]{1,0:T(8,128)(2,1)S(1)}, bf16[32,2048]{1,0:T(8,128)(2,1)S(1)}, u32[]{:S(2)}, u32[]{:S(2)}) collective-permute-start(bf16[32,2048]{1,0:T(8,128)(2,1)S(1)} %shard_map.69), channel_id=1, source_target_pairs={{0,112},{16,32},{32,16},{48,64},{64,48},{80,96},{96,80},{112,0},{1... | collective-permute-start | bytes 393224 | tf_op jit(solution)/shard_map/ppermute | solution.py:47
  95.8 8.1 %collective-permute-start.33 = (bf16[32,2048]{1,0:T(8,128)(2,1)S(1)}, bf16[32,2048]{1,0:T(8,128)(2,1)S(1)}, u32[]{:S(2)}, u32[]{:S(2)}) collective-permute-start(bf16[32,2048]{1,0:T(8,128)(2,1)S(1)} %shard_map.74), channel_id=1, source_target_pairs={{0,16},{16,0},{32,48},{48,32},{64,80},{80,64},{96,112},{112,96},{1... | collective-permute-start | bytes 393224 | tf_op jit(solution)/shard_map/ppermute | solution.py:43
  96.9 7.1 %collective-permute-start.18 = (bf16[4,512,128]{2,1,0:T(8,128)(2,1)S(1)}, bf16[4,512,128]{2,1,0:T(8,128)(2,1)S(1)}, u32[]{:S(2)}, u32[]{:S(2)}) collective-permute-start(bf16[4,512,128]{2,1,0:T(8,128)(2,1)S(1)} %get-tuple-element.34), channel_id=1, source_target_pairs={{0,8},{8,0},{1,9},{9,1},{2,10},{10,2},{3,11},{11,3},{4,12},{12,4},... | collective-permute-start | bytes 1572872 | tf_op jit(solution)/shard_map/ppermute | solution.py:39
  99.8 9.2 %collective-permute-start.30 = (bf16[32,2048]{1,0:T(8,128)(2,1)S(1)}, bf16[32,2048]{1,0:T(8,128)(2,1)S(1)}, u32[]{:S(2)}, u32[]{:S(2)}) collective-permute-start(bf16[32,2048]{1,0:T(8,128)(2,1)S(1)} %shard_map.72), channel_id=1, source_target_pairs={{0,112},{16,32},{32,16},{48,64},{64,48},{80,96},{96,80},{112,0},{1... | collective-permute-start | bytes 393224 | tf_op jit(solution)/shard_map/ppermute | solution.py:47
  100.5 4.4 %copy-start = (bf16[512,2048]{1,0:T(8,128)(2,1)S(1)}, bf16[512,2048]{1,0:T(8,128)(2,1)}, u32[]{:S(2)}) copy-start(bf16[512,2048]{1,0:T(8,128)(2,1)} %act_ref.1) | copy-start | bytes 6291460
  100.5 8.5 %collective-permute-start.23 = (bf16[32,2048]{1,0:T(8,128)(2,1)S(1)}, bf16[32,2048]{1,0:T(8,128)(2,1)S(1)}, u32[]{:S(2)}, u32[]{:S(2)}) collective-permute-start(bf16[32,2048]{1,0:T(8,128)(2,1)S(1)} %shard_map.67), channel_id=1, source_target_pairs={{0,240},{16,160},{32,144},{48,192},{64,176},{80,224},{96,208},{112... | collective-permute-start | bytes 393224 | tf_op jit(solution)/shard_map/ppermute | solution.py:52
  104.0 5.1 %collective-permute-start.27 = (bf16[32,2048]{1,0:T(8,128)(2,1)S(1)}, bf16[32,2048]{1,0:T(8,128)(2,1)S(1)}, u32[]{:S(2)}, u32[]{:S(2)}) collective-permute-start(bf16[32,2048]{1,0:T(8,128)(2,1)S(1)} %shard_map.70), channel_id=1, source_target_pairs={{0,16},{16,0},{32,48},{48,32},{64,80},{80,64},{96,112},{112,96},{1... | collective-permute-start | bytes 393224 | tf_op jit(solution)/shard_map/ppermute | solution.py:43
  104.1 5.4 %collective-permute-start.34 = (bf16[32,2048]{1,0:T(8,128)(2,1)S(1)}, bf16[32,2048]{1,0:T(8,128)(2,1)S(1)}, u32[]{:S(2)}, u32[]{:S(2)}) collective-permute-start(bf16[32,2048]{1,0:T(8,128)(2,1)S(1)} %fusion.12), channel_id=1, source_target_pairs={{0,128},{128,0},{1,129},{129,1},{2,130},{130,2},{3,131},{131,3},{4... | collective-permute-start | bytes 393224 | tf_op jit(solution)/shard_map/ppermute | solution.py:39
